TPU v7x, 32 devices: a whole 2x2x4 slice. The times are simulated.
32 devices in a mesh: expert: 16 (over z, y, core), tensor: 2 (over x).
Axes of the slice: x: 2, y: 2, z: 4, core: 2. Of those that a mesh axis runs over, the one named last changes fastest.
Arguments:
- queries: bfloat16 [1024, 4096], P('expert', 'tensor'), may hold values from -5 to 5
- keys: bfloat16 [1024, 512], P('expert'), may hold values from -6 to 6
- values: bfloat16 [1024, 512], P('expert'), may hold values from -6 to 6
- positions: int32 [1024], P('expert'), may hold values from 0 to 31, as said below
- out_weight: bfloat16 [4096, 2048], P('tensor'), may hold values from -0.09375 to 0.09375
- residual: bfloat16 [1024, 2048], P(('expert', 'tensor')), may hold values from -3 to 3
- norm_gain: float32 [2048], replicated, may hold values from 0.25 to 1.75
- routes: int32 [1024, 8], P('expert'), may hold values from 0 to 15, all different within a row; in each aligned block of 32 rows (0 to 31, 32 to 63, ...) at most 32 rows name the same one
- route_probs: float32 [1024, 8], P('expert'), may hold values from 0.05 to 0.4
- gate_weight: bfloat16 [32, 2048, 768], P(('expert', 'tensor')), may hold values from -0.125 to 0.125
- up_weight: bfloat16 [32, 2048, 768], P(('expert', 'tensor')), may hold values from -0.125 to 0.125
- down_weight: bfloat16 [32, 768, 2048], P(('expert', 'tensor')), may hold values from -0.15625 to 0.15625
Outputs:
- layer_out: bfloat16 [1024, 2048], P(('expert', 'tensor'))
Inputs may be any that keep to these rules, and one draw needn't show every extreme that they name: `routes`: each row names 8 different experts. In each aligned block of 32 rows (the rows of one device) no expert is named by more than 32 rows, a bound that some block reaches. In each sequence of 64 rows a document starts at the first row; a document starts only at an even row of a sequence, where positions is 0; elsewhere positions[i] = positions[i - 1] + 1.
All inputs are finite; a program needn't handle non-finite values.
Results may differ from a plain program's by a relative error of at most 0.0057.
Values may be sent and summed in bfloat16 or wider, within the bound.
No kernel may reach another device: no remote copies, remote signals or barrier semaphores. Data moves between devices by JAX's collectives and lax.ppermute only.
A program may use at most 128 MiB of HBM per device.

v0:
```python
import math

import jax
import jax.numpy as jnp
from jax import lax
from jax.sharding import PartitionSpec as P

D = 2048
QUERY_HEADS = 32
KEY_VALUE_HEADS = 4
HEAD_WIDTH = 128
TOPK = 8


NEG_BIG = -1e30
EPS = 1e-06


def swapped(shard, axis, distance):
    return lax.ppermute(shard, axis, [(i, i ^ 1 << distance) for i in range(lax.axis_size(axis))])


def slot_numbers(route_block, expert_count):
    share_count, share_rows, top_count = route_block.shape
    flattened_routes = route_block.reshape(share_count, share_rows * top_count)
    one_hot = (
        flattened_routes[:, :, None] == jnp.arange(expert_count, dtype=jnp.int32)[None, None, :]
    ).astype(jnp.int32)
    before = jnp.cumsum(one_hot, axis=1) - one_hot
    return jnp.sum(before * one_hot, axis=2).reshape(share_count, share_rows, top_count)


def source_table(route_block, slot_ids, expert_count, capacity):
    share_count, share_rows, top_count = route_block.shape
    share_ids = jnp.broadcast_to(
        jnp.arange(share_count, dtype=jnp.int32)[:, None, None], route_block.shape
    )
    row_ids = share_ids * share_rows + jnp.broadcast_to(
        jnp.arange(share_rows, dtype=jnp.int32)[None, :, None], route_block.shape
    )
    empty_table = jnp.full(
        (share_count, expert_count, capacity), share_count * share_rows, jnp.int32
    )
    return empty_table.at[share_ids, route_block, slot_ids].set(row_ids)


def normalize(stream_rows, gain):
    mean_square = jnp.mean(stream_rows * stream_rows, axis=-1, keepdims=True)
    return (stream_rows * lax.rsqrt(mean_square + EPS) * gain).astype(jnp.bfloat16)


def on_device(
    queries,
    keys,
    values,
    positions,
    out_weight,
    residual,
    norm_gain,
    routes,
    route_probs,
    gate_weight,
    up_weight,
    down_weight,
):
    tensor_size = lax.axis_size("tensor")
    expert_size = lax.axis_size("expert")
    tensor_rank = lax.axis_index("tensor")
    group_rows = queries.shape[0]
    token_rows = group_rows // tensor_size
    heads_dev = queries.shape[1] // HEAD_WIDTH
    queries_per_key_head = QUERY_HEADS // KEY_VALUE_HEADS
    kv_count = max(1, heads_dev // queries_per_key_head)
    heads_each = heads_dev // kv_count
    kv_first = tensor_rank * heads_dev // queries_per_key_head
    key_cols = lax.dynamic_slice_in_dim(keys, kv_first * HEAD_WIDTH, kv_count * HEAD_WIDTH, 1)
    value_cols = lax.dynamic_slice_in_dim(values, kv_first * HEAD_WIDTH, kv_count * HEAD_WIDTH, 1)
    query_block = queries.reshape(group_rows, kv_count, heads_each, HEAD_WIDTH)
    local_index = jnp.arange(group_rows, dtype=jnp.int32)
    earliest = local_index - positions
    visible = (local_index[None, :] <= local_index[:, None]) & (
        local_index[None, :] >= earliest[:, None]
    )
    score_scale = 1.0 / math.sqrt(HEAD_WIDTH)
    scores = (
        jnp.einsum(
            "qkhd,nkd->khqn",
            query_block,
            key_cols.reshape(group_rows, kv_count, HEAD_WIDTH),
            preferred_element_type=jnp.float32,
        )
        * score_scale
    )
    masked = jnp.where(visible[None, None], scores, NEG_BIG)
    row_max = jnp.max(masked, axis=3, keepdims=True)
    raw_weights = jnp.where(visible[None, None], jnp.exp(masked - row_max), 0.0)
    soft_weights = (raw_weights / jnp.sum(raw_weights, axis=3, keepdims=True)).astype(jnp.bfloat16)
    head_values = jnp.einsum(
        "khqn,nkd->qkhd",
        soft_weights,
        value_cols.reshape(group_rows, kv_count, HEAD_WIDTH),
        preferred_element_type=jnp.float32,
    )
    attended = head_values.reshape(group_rows, heads_dev * HEAD_WIDTH).astype(jnp.bfloat16)
    partial_proj = jnp.dot(attended, out_weight, preferred_element_type=jnp.float32)
    projected = lax.psum(partial_proj, "tensor")
    projected_own = lax.dynamic_slice_in_dim(projected, tensor_rank * token_rows, token_rows, 0)
    middle_own = residual.astype(jnp.float32) + projected_own
    normed_own = normalize(middle_own, norm_gain)
    local_count = tensor_size // 2
    experts = local_count * expert_size
    slot_cap = max(2, 2 * token_rows * TOPK // experts)
    own_routes = lax.dynamic_slice_in_dim(routes, tensor_rank * token_rows, token_rows, 0)
    own_probs = lax.dynamic_slice_in_dim(route_probs, tensor_rank * token_rows, token_rows, 0)
    blank_row = jnp.zeros((1, D), jnp.bfloat16)
    own_block = own_routes.reshape(1, token_rows, TOPK)
    own_numbers = slot_numbers(own_block, experts)
    own_slots = own_numbers[0]
    slot_table = source_table(own_block, own_numbers, experts, slot_cap)[0]
    padded = jnp.concatenate([normed_own, blank_row], axis=0)
    outgoing = jnp.take(padded, slot_table, axis=0).reshape(expert_size, local_count, slot_cap, D)
    doubled = jnp.broadcast_to(outgoing[:, :, None], (expert_size, local_count, 2, slot_cap, D))
    copies = jnp.transpose(doubled, (1, 2, 0, 3, 4)).reshape(tensor_size, expert_size, slot_cap, D)
    incoming = lax.all_to_all(
        lax.all_to_all(copies, "expert", split_axis=1, concat_axis=1, tiled=True),
        "tensor",
        split_axis=0,
        concat_axis=0,
        tiled=True,
    )
    slot_rows = incoming.reshape(tensor_size * expert_size * slot_cap, D)
    gate_value = jnp.dot(slot_rows, gate_weight[0], preferred_element_type=jnp.float32)
    up_value = jnp.dot(slot_rows, up_weight[0], preferred_element_type=jnp.float32)
    hidden = (jax.nn.silu(gate_value) * up_value).astype(jnp.bfloat16)
    part = jnp.dot(hidden, down_weight[0], preferred_element_type=jnp.float32).astype(jnp.bfloat16)
    part = lax.optimization_barrier(part).reshape(tensor_size, expert_size, slot_cap, D)
    half_count = expert_size // 2
    side = tensor_rank % 2
    kept = lax.dynamic_slice_in_dim(part, side * half_count, half_count, 1)
    given = lax.dynamic_slice_in_dim(part, (1 - side) * half_count, half_count, 1)
    partner = swapped(given, "tensor", 0)
    summed = (kept.astype(jnp.float32) + partner.astype(jnp.float32)).astype(jnp.bfloat16)
    homeward = lax.all_to_all(summed, "tensor", split_axis=0, concat_axis=0, tiled=True)
    homeward = homeward.reshape(local_count, expert_size, slot_cap, D)
    returned = lax.all_to_all(homeward, "expert", split_axis=1, concat_axis=0, tiled=True).reshape(
        experts * slot_cap, D
    )
    flat_index = (own_routes * slot_cap + own_slots).reshape(token_rows * TOPK)
    picked = jnp.take(returned, flat_index, axis=0).reshape(token_rows, TOPK, D)
    mixture = jnp.einsum("tk,tkd->td", own_probs, picked.astype(jnp.float32))
    return (middle_own + mixture).astype(jnp.bfloat16)


def solution(mesh):
    return jax.shard_map(
        on_device,
        mesh=mesh,
        in_specs=(
            P("expert", "tensor"),
            P("expert", None),
            P("expert", None),
            P("expert"),
            P("tensor", None),
            P(("expert", "tensor"), None),
            P(),
            P("expert", None),
            P("expert", None),
            P(("expert", "tensor"), None, None),
            P(("expert", "tensor"), None, None),
            P(("expert", "tensor"), None, None),
        ),
        out_specs=P(("expert", "tensor"), None),
        check_vma=False,
    )
```

profile of v0, /device:TPU:0, one launch (start us, length us, event | category | flops | bytes accessed | tf_op | source)
XLA Modules:
  0.0 375.3 jit_solution(7575017527321394960)
XLA Ops:
  6.5 0.9 constant_dynamic-slice_fusion.2
  7.5 0.7 iota_subtract_fusion
  8.2 1.0 copy.81
  9.2 1.2 fusion.12
  10.4 0.4 fusion.42
  10.8 1.5 fusion.13
  12.6 5.7 %fusion.19 = f32[64,2048]{1,0:T(8,128)} fusion(bf16[2048,2048]{1,0:T(8,128)(2,1)} %param.16, bf16[8,8,16,128]{3,2,1,0:T(8,128)(2,1)S(1)} %bitcast.82), kind=kOutput, calls=%fused_computation.26 | convolution fusion | flops 536870912 | bytes 9175040 | tf_op jit(solution)/shard_map/dot_general | solution.py:105
  18.6 0.6 reduce-window.6
  19.2 0.2 slice_reduce_fusion
  20.3 12.8 %scatter_fusion = s32[16,32]{1,0:T(8,128)S(1)} fusion(s32[16,32]{1,0:T(8,128)S(1)} %broadcast.194, s32[256]{0:T(256)S(1)} %reshape.356, s32[256]{0:T(256)S(1)} %reshape.358), kind=kCustom, calls=%fused_computation.2 | custom fusion | bytes 5120 | tf_op jit(solution)/shard_map/scatter | solution.py:44
  33.2 16.6 %all-reduce.3.cloned.1.call-done = f32[64,2048]{1,0:T(8,128)} async-done(((f32[64,2048]{1,0:T(8,128)}), f32[64,2048]{1,0:T(8,128)}) %all-reduce.3.cloned.1.call-update) | async-done | bytes 524304 | tf_op jit(solution)/shard_map/psum | solution.py:106
  49.8 1.1 multiply_reduce_fusion
  50.9 1.0 multiply_convert_fusion.1
  52.0 3.3 gather_fusion
  55.3 1.8 broadcast_select_fusion
  57.2 0.5 reshape.330
  57.7 97.7 %all_to_all.24 = bf16[2,16,32,2048]{3,2,0,1:T(8,128)(2,1)S(1)} all-to-all(bf16[2,16,32,2048]{3,2,0,1:T(8,128)(2,1)S(1)} %reshape.330), channel_id=1, replica_groups=mesh['expert'=16,'tensor'=2] {'expert'}, dimensions={1} | all-to-all | bytes 8388608 | tf_op jit(solution)/shard_map/all_to_all | solution.py:125
  155.4 2.2 copy.51
  157.6 5.8 %all-to-all-start.1 = ((bf16[2,16,32,2048]{3,2,1,0:T(8,128)(2,1)}), bf16[2,16,32,2048]{3,2,1,0:T(8,128)(2,1)}, u32[]{:S(2)}, u32[]{:S(2)}) async-start(bf16[2,16,32,2048]{3,2,1,0:T(8,128)(2,1)} %copy.51), calls=%async_computation.1 | async-start | bytes 8388608 | tf_op jit(solution)/shard_map/all_to_all | solution.py:124
  163.4 48.4 %all-to-all-done.1 = bf16[2,16,32,2048]{3,2,1,0:T(8,128)(2,1)} async-done(((bf16[2,16,32,2048]{3,2,1,0:T(8,128)(2,1)}), bf16[2,16,32,2048]{3,2,1,0:T(8,128)(2,1)}, u32[]{:S(2)}, u32[]{:S(2)}) %all-to-all-start.1) | async-done | bytes 4194336 | tf_op jit(solution)/shard_map/all_to_all | solution.py:124
  211.8 8.3 %fusion.2 = f32[1024,768]{1,0:T(8,128)} fusion(bf16[1024,2048]{1,0:T(8,128)(2,1)} %bitcast.15, bf16[1,2048,768]{2,1,0:T(8,128)(2,1)} %param.22), kind=kOutput, calls=%fused_computation.7 | convolution fusion | flops 3221225472 | bytes 10485760 | tf_op jit(solution)/shard_map/dot_general | solution.py:133
  220.2 12.3 %convolution_convert_fusion = bf16[1024,2048]{1,0:T(8,128)(2,1)} fusion(bf16[1,768,2048]{2,1,0:T(8,128)(2,1)S(1)} %copy-done, f32[1024,768]{1,0:T(8,128)} %fusion.2, bf16[1024,2048]{1,0:T(8,128)(2,1)} %bitcast.15, bf16[1,2048,768]{2,1,0:T(8,128)(2,1)} %param.21), kind=kOutput, calls=%fused_computation.5 | convolution fusion | flops 6449266688 | bytes 17825792 | tf_op jit(solution)/shard_map/dot_general | solution.py:135
  232.4 3.2 constant_dynamic-slice_fusion
  235.6 0.3 collective-permute-start
  235.9 47.4 %collective-permute-done = bf16[2,8,32,2048]{3,2,1,0:T(8,128)(2,1)} collective-permute-done((bf16[2,8,32,2048]{3,2,1,0:T(8,128)(2,1)}, bf16[2,8,32,2048]{3,2,1,0:T(8,128)(2,1)}, u32[]{:S(2)}, u32[]{:S(2)}) %collective-permute-start) | collective-permute-done | bytes 2097184 | tf_op jit(solution)/shard_map/ppermute | solution.py:20
  283.4 3.0 add_convert_fusion
  286.4 27.7 %all_to_all.25 = bf16[2,8,32,2048]{3,2,1,0:T(8,128)(2,1)} all-to-all(bf16[2,8,32,2048]{3,2,1,0:T(8,128)(2,1)S(1)} %add_convert_fusion), channel_id=1, replica_groups=mesh['expert'=16,'tensor'=2] {'tensor'}, dimensions={0} | all-to-all | bytes 4194304 | tf_op jit(solution)/shard_map/all_to_all | solution.py:143
  314.1 4.6 %all-to-all-start.3 = ((bf16[1,16,32,2048]{3,2,0,1:T(8,128)(2,1)}), bf16[1,16,32,2048]{3,2,0,1:T(8,128)(2,1)}, u32[]{:S(2)}, u32[]{:S(2)}) async-start(bf16[1,16,32,2048]{3,2,0,1:T(8,128)(2,1)} %bitcast.79), calls=%async_computation.3 | async-start | bytes 4194304 | tf_op jit(solution)/shard_map/all_to_all | solution.py:145
  319.1 40.7 %all-to-all-done.3 = bf16[1,16,32,2048]{3,2,0,1:T(8,128)(2,1)} async-done(((bf16[1,16,32,2048]{3,2,0,1:T(8,128)(2,1)}), bf16[1,16,32,2048]{3,2,0,1:T(8,128)(2,1)}, u32[]{:S(2)}, u32[]{:S(2)}) %all-to-all-start.3) | async-done | bytes 2097184 | tf_op jit(solution)/shard_map/all_to_all | solution.py:145
  359.8 5.2 %gather_fusion.1 = bf16[256,2048]{1,0:T(8,128)(2,1)} fusion(bf16[512,2048]{1,0:T(8,128)(2,1)} %bitcast.21, s32[1024]{0:T(1024)S(1)} %pad_clamp_fusion), kind=kCustom, calls=%fused_computation.1 | custom fusion | bytes 2098176 | tf_op jit(solution)/shard_map/jit(_take)/gather | solution.py:149
  365.0 1.7 fusion.14
  366.7 1.7 fusion.22
  (53 shorter events, 1.9 us)
Async XLA Ops:
  6.5 213.6 %copy-start = (bf16[1,768,2048]{2,1,0:T(8,128)(2,1)S(1)}, bf16[1,768,2048]{2,1,0:T(8,128)(2,1)}, u32[]{:S(2)}) copy-start(bf16[1,768,2048]{2,1,0:T(8,128)(2,1)} %param.23) | copy-start | bytes 9437188
  6.5 43.2 %all-reduce.3.cloned.1.call-start = ((), (), s32[]{:S(2)}) async-start(), calls=%async_computation.4 | async-start | bytes 1048576 | tf_op jit(solution)/shard_map/psum | solution.py:106
  12.5 5.8 %copy-start.3 = (s32[64,8]{0,1:T(8,128)S(1)}, s32[64,8]{0,1:T(8,128)}, u32[]{:S(2)}) copy-start(s32[64,8]{0,1:T(8,128)} %param.19) | copy-start | bytes 6148
  20.3 29.5 %copy-start.1 = (bf16[32,2048]{1,0:T(8,128)(2,1)S(1)}, bf16[32,2048]{1,0:T(8,128)(2,1)}, u32[]{:S(2)}) copy-start(bf16[32,2048]{1,0:T(8,128)(2,1)} %param.17) | copy-start | bytes 393220
  20.3 30.6 %copy-start.2 = (f32[2048]{0:T(1024)S(1)}, f32[2048]{0:T(1024)}, u32[]{:S(2)}) copy-start(f32[2048]{0:T(1024)} %param.18) | copy-start | bytes 24580
  157.6 54.2 %all-to-all-start.1 = ((bf16[2,16,32,2048]{3,2,1,0:T(8,128)(2,1)}), bf16[2,16,32,2048]{3,2,1,0:T(8,128)(2,1)}, u32[]{:S(2)}, u32[]{:S(2)}) async-start(bf16[2,16,32,2048]{3,2,1,0:T(8,128)(2,1)} %copy.51), calls=%async_computation.1 | async-start | bytes 8388608 | tf_op jit(solution)/shard_map/all_to_all | solution.py:124
  235.6 47.8 %collective-permute-start = (bf16[2,8,32,2048]{3,2,1,0:T(8,128)(2,1)}, bf16[2,8,32,2048]{3,2,1,0:T(8,128)(2,1)}, u32[]{:S(2)}, u32[]{:S(2)}) collective-permute-start(bf16[2,8,32,2048]{3,2,1,0:T(8,128)(2,1)} %constant_dynamic-slice_fusion), channel_id=1, source_target_pairs={{0,1},{1,0},{2,3},{3,2},{4,5},{5,4},{6,7},{7,6},{8,9},{9,8},{10,11... | collective-permute-start | bytes 6291464 | tf_op jit(solution)/shard_map/ppermute | solution.py:20
  314.1 4.8 %copy-start.4 = (f32[64,8]{0,1:T(8,128)S(1)}, f32[64,8]{0,1:T(8,128)}, u32[]{:S(2)}) copy-start(f32[64,8]{0,1:T(8,128)} %param.20) | copy-start | bytes 6148
  314.1 45.6 %all-to-all-start.3 = ((bf16[1,16,32,2048]{3,2,0,1:T(8,128)(2,1)}), bf16[1,16,32,2048]{3,2,0,1:T(8,128)(2,1)}, u32[]{:S(2)}, u32[]{:S(2)}) async-start(bf16[1,16,32,2048]{3,2,0,1:T(8,128)(2,1)} %bitcast.79), calls=%async_computation.3 | async-start | bytes 4194304 | tf_op jit(solution)/shard_map/all_to_all | solution.py:145
Sparse Core Ops, SparseCore 0:
  18.5 31.2 all-reduce.2
where the time goes:
time: 381 us; the launch traced here: 375 us
  waiting for transfers between devices  153 us (40%)
  blocking collectives  125 us (33%)
  matrix products  31.2 us (8%)
  local copies, waits for them, and re-layouts  30.9 us (8%)
  between operations  13.7 us (4%)
  starting transfers between devices  10.6 us (3%)
  other arithmetic  10.3 us (3%)
    all_to_all x1, blocking collectives, on_device(): lax.all_to_all(copies, 'expert', split_axis=1, concat_axis=1, tiled=True)  97.7 us
    all_to_all x1, waiting for transfers between devices, on_device(): lax.all_to_all(lax.all_to_all(copies, 'expert', split_axis=1, concat_axis...  48.4 us
    ppermute x1, waiting for transfers between devices, swapped(): lax.ppermute(shard, axis, [(i, i ^ 1 << distance) for i in range(lax.axis...  47.4 us
    all_to_all x1, waiting for transfers between devices, on_device(): lax.all_to_all(homeward, 'expert', split_axis=1, concat_axis=0, tiled=True)  40.7 us
    all_to_all x1, blocking collectives, on_device(): lax.all_to_all(summed, 'tensor', split_axis=0, concat_axis=0, tiled=True)  27.7 us
    psum x1, waiting for transfers between devices, on_device(): projected = lax.psum(partial_proj, 'tensor')  16.6 us
    scatter x1, local copies, waits for them, and re-layouts, source_table(): return empty_table.at[share_ids, route_block, slot_ids].set(row_ids)  12.8 us
    dot_general x1, matrix products, on_device(): jnp.dot(hidden, down_weight[0], preferred_element_type=jnp.float32)  12.3 us
  transfers between devices with their start and end apart: 4, of which 4 were waited for; matrix products, arithmetic and copies ran while one was open for 4% of the time, Pallas kernels for 0%

commit v1 on v0

v1 whole, which is shorter than its diff:
```python
import functools
import math

import jax
import jax.numpy as jnp
from jax import lax
from jax.experimental import pallas as pl
from jax.experimental.pallas import tpu as pltpu
from jax.sharding import PartitionSpec as P

D = 2048
QUERY_HEADS = 32
KEY_VALUE_HEADS = 4
HEAD_WIDTH = 128
TOPK = 8


NEG_BIG = -1e30
EPS = 1e-06
LANES = 128

BOTH = ("expert", "tensor")
BIT_X, BIT_CORE, BIT_Y, BIT_Z0, BIT_Z1 = 1, 2, 4, 8, 16
STAGES = ((BIT_Z1, BIT_Z0), (BIT_Z0, BIT_Z1), (BIT_X, BIT_Y), (BIT_Y, BIT_X))
FIRST_BLOCK = 256
SECOND_BLOCK = 512


def swapped(shard, axis, distance):
    return lax.ppermute(shard, axis, [(i, i ^ 1 << distance) for i in range(lax.axis_size(axis))])


def exchanged(shard, masks):
    count = lax.axis_size("expert") * lax.axis_size("tensor")
    return lax.ppermute(
        shard, BOTH, [(i, i ^ masks[1 if i & BIT_CORE else 0]) for i in range(count)]
    )


def core_swapped(shard):
    return exchanged(shard, (BIT_CORE, BIT_CORE))


def slot_numbers(route_block, expert_count):
    share_count, share_rows, top_count = route_block.shape
    flattened_routes = route_block.reshape(share_count, share_rows * top_count)
    one_hot = (
        flattened_routes[:, :, None] == jnp.arange(expert_count, dtype=jnp.int32)[None, None, :]
    ).astype(jnp.int32)
    before = jnp.cumsum(one_hot, axis=1) - one_hot
    return jnp.sum(before * one_hot, axis=2).reshape(share_count, share_rows, top_count)


def source_table(route_block, slot_ids, expert_count, capacity):
    share_count, share_rows, top_count = route_block.shape
    share_ids = jnp.broadcast_to(
        jnp.arange(share_count, dtype=jnp.int32)[:, None, None], route_block.shape
    )
    row_ids = share_ids * share_rows + jnp.broadcast_to(
        jnp.arange(share_rows, dtype=jnp.int32)[None, :, None], route_block.shape
    )
    empty_table = jnp.full(
        (share_count, expert_count, capacity), share_count * share_rows, jnp.int32
    )
    return empty_table.at[share_ids, route_block, slot_ids].set(row_ids)


def normalize(stream_rows, gain):
    mean_square = jnp.mean(stream_rows * stream_rows, axis=-1, keepdims=True)
    return (stream_rows * lax.rsqrt(mean_square + EPS) * gain).astype(jnp.bfloat16)


def partial_projection(queries, keys, values, positions, out_weight):
    tensor_rank = lax.axis_index("tensor")
    group_rows = queries.shape[0]
    heads_dev = queries.shape[1] // HEAD_WIDTH
    queries_per_key_head = QUERY_HEADS // KEY_VALUE_HEADS
    kv_count = max(1, heads_dev // queries_per_key_head)
    heads_each = heads_dev // kv_count
    kv_first = tensor_rank * heads_dev // queries_per_key_head
    key_cols = lax.dynamic_slice_in_dim(keys, kv_first * HEAD_WIDTH, kv_count * HEAD_WIDTH, 1)
    value_cols = lax.dynamic_slice_in_dim(values, kv_first * HEAD_WIDTH, kv_count * HEAD_WIDTH, 1)
    query_block = queries.reshape(group_rows, kv_count, heads_each, HEAD_WIDTH)
    local_index = jnp.arange(group_rows, dtype=jnp.int32)
    earliest = local_index - positions
    visible = (local_index[None, :] <= local_index[:, None]) & (
        local_index[None, :] >= earliest[:, None]
    )
    score_scale = 1.0 / math.sqrt(HEAD_WIDTH)
    scores = (
        jnp.einsum(
            "qkhd,nkd->khqn",
            query_block,
            key_cols.reshape(group_rows, kv_count, HEAD_WIDTH),
            preferred_element_type=jnp.float32,
        )
        * score_scale
    )
    masked = jnp.where(visible[None, None], scores, NEG_BIG)
    row_max = jnp.max(masked, axis=3, keepdims=True)
    raw_weights = jnp.where(visible[None, None], jnp.exp(masked - row_max), 0.0)
    soft_weights = (raw_weights / jnp.sum(raw_weights, axis=3, keepdims=True)).astype(jnp.bfloat16)
    head_values = jnp.einsum(
        "khqn,nkd->qkhd",
        soft_weights,
        value_cols.reshape(group_rows, kv_count, HEAD_WIDTH),
        preferred_element_type=jnp.float32,
    )
    attended = head_values.reshape(group_rows, heads_dev * HEAD_WIDTH).astype(jnp.bfloat16)
    return jnp.dot(attended, out_weight, preferred_element_type=jnp.float32)


def expert_kernel(
    first_steps,
    near_ref,
    far_ref,
    pick_ref,
    gate_ref,
    up_ref,
    down_ref,
    near_out_ref,
    far_out_ref,
    hidden_ref,
):
    step = pl.program_id(0)
    rows = near_ref.shape[0]

    @pl.when(step < first_steps)
    def _():
        cols = pl.ds(pl.multiple_of(step * FIRST_BLOCK, FIRST_BLOCK), FIRST_BLOCK)
        for place, source in enumerate((near_ref, far_ref)):
            feed = source[:, :D]
            weight = jnp.sum(
                source[:, D:].astype(jnp.float32) * pick_ref[...], axis=1, keepdims=True
            )
            gate = jnp.dot(feed, gate_ref[0], preferred_element_type=jnp.float32)
            up = jnp.dot(feed, up_ref[0], preferred_element_type=jnp.float32)
            hidden = gate / (1.0 + jnp.exp(-gate)) * up * weight
            hidden_ref[place * rows : (place + 1) * rows, cols] = hidden.astype(jnp.bfloat16)

    @pl.when(step >= first_steps)
    def _():
        for place, target in enumerate((near_out_ref, far_out_ref)):
            target[...] = jnp.dot(
                hidden_ref[place * rows : (place + 1) * rows, :],
                down_ref[0],
                preferred_element_type=jnp.float32,
            ).astype(jnp.bfloat16)


def weighted_expert(near, far, pick, gate_weight, up_weight, down_weight):
    rows, width = near.shape
    units = gate_weight.shape[2]
    first_steps = units // FIRST_BLOCK
    second_steps = D // SECOND_BLOCK
    whole = pl.BlockSpec((rows, width), lambda s: (0, 0))
    first = pl.BlockSpec((1, D, FIRST_BLOCK), lambda s: (0, 0, jnp.minimum(s, first_steps - 1)))
    second = lambda s: jnp.maximum(s - first_steps, 0)
    target = pl.BlockSpec((rows, SECOND_BLOCK), lambda s: (0, second(s)))
    return pl.pallas_call(
        functools.partial(expert_kernel, first_steps),
        grid=(first_steps + second_steps,),
        in_specs=[
            whole,
            whole,
            pl.BlockSpec((1, LANES), lambda s: (0, 0)),
            first,
            first,
            pl.BlockSpec((1, units, SECOND_BLOCK), lambda s: (0, 0, second(s))),
        ],
        out_specs=[target, target],
        out_shape=[jax.ShapeDtypeStruct((rows, D), jnp.bfloat16)] * 2,
        scratch_shapes=[pltpu.VMEM((2 * rows, units), jnp.bfloat16)],
        compiler_params=pltpu.CompilerParams(vmem_limit_bytes=40 * 2**20),
        cost_estimate=pl.CostEstimate(
            flops=2 * 2 * rows * 3 * D * units,
            bytes_accessed=2 * 3 * D * units + 8 * rows * D,
            transcendentals=2 * rows * units,
        ),
        name="expert_half",
    )(near, far, pick, gate_weight, up_weight, down_weight)


def dense_experts(middle_own, normed_own, own_routes, own_probs, gate_weight, up_weight, down_weight):
    expert_size = lax.axis_size("expert")
    token_rows = normed_own.shape[0]
    numbers = jnp.arange(expert_size, dtype=jnp.int32)
    table = jnp.sum(
        jnp.where(own_routes[:, :, None] == numbers, own_probs[:, :, None], 0.0), axis=1
    )
    high = lax.reduce_precision(table, 8, 7)
    blank = jnp.zeros((token_rows, LANES - 2 * expert_size), jnp.bfloat16)
    block = jnp.concatenate(
        [normed_own, high.astype(jnp.bfloat16), (table - high).astype(jnp.bfloat16), blank], axis=1
    )
    lane = jnp.arange(LANES, dtype=jnp.int32)[None, :]
    mine = lax.axis_index("expert")
    pick = ((lane == mine) | (lane == mine + expert_size)).astype(jnp.float32)
    for masks in STAGES[:-1]:
        block = jnp.concatenate([block, exchanged(block, masks)], axis=0)
    late = exchanged(block, STAGES[-1])
    block_far = core_swapped(block)
    expert = functools.partial(
        weighted_expert,
        pick=pick,
        gate_weight=gate_weight,
        up_weight=up_weight,
        down_weight=down_weight,
    )
    early_near, early_far = expert(block, block_far)
    late_near, late_far = expert(late, core_swapped(late))
    f32 = jnp.float32
    total = (late_near.astype(f32) + core_swapped(late_far).astype(f32)).astype(jnp.bfloat16)
    total = (
        early_near.astype(f32)
        + core_swapped(early_far).astype(f32)
        + exchanged(total, STAGES[-1]).astype(f32)
    )
    for masks in reversed(STAGES[:-1]):
        half = total.shape[0] // 2
        total = total[:half] + exchanged(total[half:].astype(jnp.bfloat16), masks).astype(f32)
    return (middle_own + total).astype(jnp.bfloat16)


def routed_experts(middle_own, normed_own, own_routes, own_probs, gate_weight, up_weight, down_weight):
    tensor_size = lax.axis_size("tensor")
    expert_size = lax.axis_size("expert")
    tensor_rank = lax.axis_index("tensor")
    token_rows = normed_own.shape[0]
    local_count = tensor_size // 2
    experts = local_count * expert_size
    slot_cap = max(2, 2 * token_rows * TOPK // experts)
    blank_row = jnp.zeros((1, D), jnp.bfloat16)
    own_block = own_routes.reshape(1, token_rows, TOPK)
    own_numbers = slot_numbers(own_block, experts)
    own_slots = own_numbers[0]
    slot_table = source_table(own_block, own_numbers, experts, slot_cap)[0]
    padded = jnp.concatenate([normed_own, blank_row], axis=0)
    outgoing = jnp.take(padded, slot_table, axis=0).reshape(expert_size, local_count, slot_cap, D)
    doubled = jnp.broadcast_to(outgoing[:, :, None], (expert_size, local_count, 2, slot_cap, D))
    copies = jnp.transpose(doubled, (1, 2, 0, 3, 4)).reshape(tensor_size, expert_size, slot_cap, D)
    incoming = lax.all_to_all(
        lax.all_to_all(copies, "expert", split_axis=1, concat_axis=1, tiled=True),
        "tensor",
        split_axis=0,
        concat_axis=0,
        tiled=True,
    )
    slot_rows = incoming.reshape(tensor_size * expert_size * slot_cap, D)
    gate_value = jnp.dot(slot_rows, gate_weight[0], preferred_element_type=jnp.float32)
    up_value = jnp.dot(slot_rows, up_weight[0], preferred_element_type=jnp.float32)
    hidden = (jax.nn.silu(gate_value) * up_value).astype(jnp.bfloat16)
    part = jnp.dot(hidden, down_weight[0], preferred_element_type=jnp.float32).astype(jnp.bfloat16)
    part = lax.optimization_barrier(part).reshape(tensor_size, expert_size, slot_cap, D)
    half_count = expert_size // 2
    side = tensor_rank % 2
    kept = lax.dynamic_slice_in_dim(part, side * half_count, half_count, 1)
    given = lax.dynamic_slice_in_dim(part, (1 - side) * half_count, half_count, 1)
    partner = swapped(given, "tensor", 0)
    summed = (kept.astype(jnp.float32) + partner.astype(jnp.float32)).astype(jnp.bfloat16)
    homeward = lax.all_to_all(summed, "tensor", split_axis=0, concat_axis=0, tiled=True)
    homeward = homeward.reshape(local_count, expert_size, slot_cap, D)
    returned = lax.all_to_all(homeward, "expert", split_axis=1, concat_axis=0, tiled=True).reshape(
        experts * slot_cap, D
    )
    flat_index = (own_routes * slot_cap + own_slots).reshape(token_rows * TOPK)
    picked = jnp.take(returned, flat_index, axis=0).reshape(token_rows, TOPK, D)
    mixture = jnp.einsum("tk,tkd->td", own_probs, picked.astype(jnp.float32))
    return (middle_own + mixture).astype(jnp.bfloat16)


def on_device(
    queries,
    keys,
    values,
    positions,
    out_weight,
    residual,
    norm_gain,
    routes,
    route_probs,
    gate_weight,
    up_weight,
    down_weight,
):
    tensor_size = lax.axis_size("tensor")
    expert_size = lax.axis_size("expert")
    tensor_rank = lax.axis_index("tensor")
    token_rows = queries.shape[0] // tensor_size
    partial_proj = partial_projection(queries, keys, values, positions, out_weight)
    own_routes = lax.dynamic_slice_in_dim(routes, tensor_rank * token_rows, token_rows, 0)
    own_probs = lax.dynamic_slice_in_dim(route_probs, tensor_rank * token_rows, token_rows, 0)
    dense = tensor_size == 2 and expert_size == 16
    if dense:
        kept = lax.dynamic_slice_in_dim(partial_proj, tensor_rank * token_rows, token_rows, 0)
        given = lax.dynamic_slice_in_dim(partial_proj, (1 - tensor_rank) * token_rows, token_rows, 0)
        projected_own = kept + swapped(given.astype(jnp.bfloat16), "tensor", 0).astype(jnp.float32)
    else:
        projected = lax.psum(partial_proj, "tensor")
        projected_own = lax.dynamic_slice_in_dim(projected, tensor_rank * token_rows, token_rows, 0)
    middle_own = residual.astype(jnp.float32) + projected_own
    normed_own = normalize(middle_own, norm_gain)
    experts = dense_experts if dense else routed_experts
    return experts(
        middle_own, normed_own, own_routes, own_probs, gate_weight, up_weight, down_weight
    )


def solution(mesh):
    return jax.shard_map(
        on_device,
        mesh=mesh,
        in_specs=(
            P("expert", "tensor"),
            P("expert", None),
            P("expert", None),
            P("expert"),
            P("tensor", None),
            P(("expert", "tensor"), None),
            P(),
            P("expert", None),
            P("expert", None),
            P(("expert", "tensor"), None, None),
            P(("expert", "tensor"), None, None),
            P(("expert", "tensor"), None, None),
        ),
        out_specs=P(("expert", "tensor"), None),
        check_vma=False,
    )
```

time: 381 us -> 133 us (0.35); the launches traced: 375 us -> 133 us
  blocking collectives: 125 us -> 0 us
  waiting for transfers between devices: 153 us -> 66.4 us
  matrix products: 31.2 us -> 6.14 us
  starting transfers between devices: 10.6 us -> 29.1 us
  local copies, waits for them, and re-layouts: 30.9 us -> 13 us
  Pallas kernels: 0 us -> 15.2 us
  between operations: 13.7 us -> 0.22 us
  other arithmetic: 10.3 us -> 2.92 us
    all_to_all x2 -> x0, blocking collectives: 125 us -> none  [the longest x1 97.7 us: on_device(): lax.all_to_all(copies, 'expert', split_axis=1, concat_axis=1, tiled=True)]
    all_to_all x2 -> x0, waiting for transfers between devices: 89.1 us -> none  [the longest x1 48.4 us: on_device(): lax.all_to_all(lax.all_to_all(copies, 'expert', split_axis=1, concat_axis...]
    ppermute x0 -> x12, waiting for transfers between devices: none -> 63.2 us  [exchanged(): lax.ppermute(shard, BOTH, [(i, i ^ masks[1 if i & BIT_CORE else 0]) for i...]
    ppermute x1, waiting for transfers between devices: 47.4 us -> 3.16 us  [swapped(): lax.ppermute(shard, axis, [(i, i ^ 1 << distance) for i in range(lax.axis...]
    ppermute x0 -> x12, starting transfers between devices: none -> 26.1 us  [exchanged(): lax.ppermute(shard, BOTH, [(i, i ^ masks[1 if i & BIT_CORE else 0]) for i...]
    dot_general x6 -> x3, matrix products: 30.8 us -> 5.71 us  [the longest x1 4.99 us: partial_projection(): return jnp.dot(attended, out_weight, preferred_element_type=jnp.float32)]
    psum x1 -> x0, waiting for transfers between devices: 16.6 us -> none  [on_device(): projected = lax.psum(partial_proj, 'tensor')]
    pallas_call x0 -> x2, Pallas kernels: none -> 15.2 us  [weighted_expert(): pl.pallas_call(functools.partial(expert_kernel, first_steps), grid=(first...]
  transfers between devices with their start and end apart: 4 -> 13, of which waited for: 4 -> 10; matrix products, arithmetic and copies ran while one was open for 4% -> 1% of each run, Pallas kernels for 0% -> 11%
where the time goes in v1:
time: 133 us
  waiting for transfers between devices  66.4 us (50%)
  starting transfers between devices  29.1 us (22%)
  Pallas kernels  15.2 us (11%)
  local copies, waits for them, and re-layouts  13 us (10%)
  matrix products  6.14 us (5%)
  other arithmetic  2.92 us (2%)
    ppermute x12, waiting for transfers between devices, exchanged(): lax.ppermute(shard, BOTH, [(i, i ^ masks[1 if i & BIT_CORE else 0]) for i...  63.2 us
    ppermute x12, starting transfers between devices, exchanged(): lax.ppermute(shard, BOTH, [(i, i ^ masks[1 if i & BIT_CORE else 0]) for i...  26.1 us
    pallas_call x2, Pallas kernels, weighted_expert(): pl.pallas_call(functools.partial(expert_kernel, first_steps), grid=(first...  15.2 us
    unnamed x29, local copies, waits for them, and re-layouts  11.5 us
    dot_general x1, matrix products, partial_projection(): return jnp.dot(attended, out_weight, preferred_element_type=jnp.float32)  4.99 us
    ppermute x1, waiting for transfers between devices, swapped(): lax.ppermute(shard, axis, [(i, i ^ 1 << distance) for i in range(lax.axis...  3.16 us
    ppermute x1, starting transfers between devices, swapped(): lax.ppermute(shard, axis, [(i, i ^ 1 << distance) for i in range(lax.axis...  3 us
  transfers between devices with their start and end apart: 13, of which 10 were waited for; matrix products, arithmetic and copies ran while one was open for 1% of the time, Pallas kernels for 11%

profile of v1, /device:TPU:0, one launch (start us, length us, event | category | flops | bytes accessed | tf_op | source)
XLA Modules:
  0.0 133.0 jit_solution(14289151626798281877)
XLA Ops:
  0.7 0.8 constant_dynamic-slice_fusion.2
  1.5 1.0 copy.46
  3.9 5.0 %fusion.7 = f32[64,2048]{1,0:T(8,128)S(1)} fusion(bf16[2048,2048]{1,0:T(8,128)(2,1)} %param.16, bf16[8,8,16,128]{3,2,1,0:T(8,128)(2,1)S(1)} %bitcast.22), kind=kOutput, calls=%fused_computation.19 | convolution fusion | flops 536870912 | bytes 9175040 | tf_op jit(solution)/shard_map/dot_general | solution.py:110
  8.9 3.0 %collective-permute-start = (bf16[32,2048]{1,0:T(8,128)(2,1)S(1)}, bf16[32,2048]{1,0:T(8,128)(2,1)S(1)}, u32[]{:S(2)}, u32[]{:S(2)}) collective-permute-start(bf16[32,2048]{1,0:T(8,128)(2,1)S(1)} %dynamic-slice_convert_fusion), channel_id=1, source_target_pairs={{0,1},{1,0},{2,3},{3,2},{4,5},{5,4},{6,7},{7,6},{8,9},{9,8},{10,11... | collective-permute-start | bytes 393224 | tf_op jit(solution)/shard_map/ppermute | solution.py:30
  12.3 3.2 %collective-permute-done = bf16[32,2048]{1,0:T(8,128)(2,1)S(1)} collective-permute-done((bf16[32,2048]{1,0:T(8,128)(2,1)S(1)}, bf16[32,2048]{1,0:T(8,128)(2,1)S(1)}, u32[]{:S(2)}, u32[]{:S(2)}) %collective-permute-start) | collective-permute-done | bytes 131104 | tf_op jit(solution)/shard_map/ppermute | solution.py:30
  15.6 0.7 copy-done.9
  16.5 2.9 %collective-permute-start.1 = (bf16[32,2176]{1,0:T(8,128)(2,1)S(1)}, bf16[32,2176]{1,0:T(8,128)(2,1)S(1)}, u32[]{:S(2)}, u32[]{:S(2)}) collective-permute-start(bf16[32,2176]{1,0:T(8,128)(2,1)S(1)} %concatenate.14), channel_id=1, source_target_pairs={{0,16},{1,17},{2,10},{3,11},{4,20},{5,21},{6,14},{7,15},{8,24},{9,... | collective-permute-start | bytes 417800 | tf_op jit(solution)/shard_map/ppermute | solution.py:35
  19.4 4.7 %collective-permute-done.1 = bf16[32,2176]{1,0:T(8,128)(2,1)S(1)} collective-permute-done((bf16[32,2176]{1,0:T(8,128)(2,1)S(1)}, bf16[32,2176]{1,0:T(8,128)(2,1)S(1)}, u32[]{:S(2)}, u32[]{:S(2)}) %collective-permute-start.1) | collective-permute-done | bytes 139296 | tf_op jit(solution)/shard_map/ppermute | solution.py:35
  24.1 4.8 %collective-permute-start.2 = (bf16[64,2176]{1,0:T(8,128)(2,1)S(1)}, bf16[64,2176]{1,0:T(8,128)(2,1)S(1)}, u32[]{:S(2)}, u32[]{:S(2)}) collective-permute-start(bf16[64,2176]{1,0:T(8,128)(2,1)S(1)} %pad_maximum_fusion.2), channel_id=1, source_target_pairs={{0,8},{1,9},{2,18},{3,19},{4,12},{5,13},{6,22},{7,23},{8,0},{9,1},... | collective-permute-start | bytes 835592 | tf_op jit(solution)/shard_map/ppermute | solution.py:35
  28.9 4.5 %collective-permute-done.2 = bf16[64,2176]{1,0:T(8,128)(2,1)S(1)} collective-permute-done((bf16[64,2176]{1,0:T(8,128)(2,1)S(1)}, bf16[64,2176]{1,0:T(8,128)(2,1)S(1)}, u32[]{:S(2)}, u32[]{:S(2)}) %collective-permute-start.2) | collective-permute-done | bytes 278560 | tf_op jit(solution)/shard_map/ppermute | solution.py:35
  33.5 2.3 %collective-permute-start.3 = (bf16[128,2176]{1,0:T(8,128)(2,1)S(1)}, bf16[128,2176]{1,0:T(8,128)(2,1)S(1)}, u32[]{:S(2)}, u32[]{:S(2)}) collective-permute-start(bf16[128,2176]{1,0:T(8,128)(2,1)S(1)} %pad_maximum_fusion.1), channel_id=1, source_target_pairs={{0,1},{1,0},{2,6},{3,7},{4,5},{5,4},{6,2},{7,3},{8,9},{9,8},{10,14... | collective-permute-start | bytes 1671176 | tf_op jit(solution)/shard_map/ppermute | solution.py:35
  35.8 9.4 %collective-permute-done.3 = bf16[128,2176]{1,0:T(8,128)(2,1)S(1)} collective-permute-done((bf16[128,2176]{1,0:T(8,128)(2,1)S(1)}, bf16[128,2176]{1,0:T(8,128)(2,1)S(1)}, u32[]{:S(2)}, u32[]{:S(2)}) %collective-permute-start.3) | collective-permute-done | bytes 557088 | tf_op jit(solution)/shard_map/ppermute | solution.py:35
  45.3 2.4 %collective-permute-start.6 = (bf16[256,2176]{1,0:T(8,128)(2,1)S(1)}, bf16[256,2176]{1,0:T(8,128)(2,1)S(1)}, u32[]{:S(2)}, u32[]{:S(2)}) collective-permute-start(bf16[256,2176]{1,0:T(8,128)(2,1)S(1)} %pad_maximum_fusion.near_ref), channel_id=1, source_target_pairs={{0,4},{1,5},{2,3},{3,2},{4,0},{5,1},{6,7},{7,6},{8,12},{9,13},{10,... | collective-permute-start | bytes 3342344 | tf_op jit(solution)/shard_map/ppermute | solution.py:35
  47.7 13.5 %collective-permute-done.6.near_ref = bf16[256,2176]{1,0:T(8,128)(2,1)S(1)} collective-permute-done((bf16[256,2176]{1,0:T(8,128)(2,1)S(1)}, bf16[256,2176]{1,0:T(8,128)(2,1)S(1)}, u32[]{:S(2)}, u32[]{:S(2)}) %collective-permute-start.6) | collective-permute-done | bytes 1114144 | tf_op jit(solution)/shard_map/ppermute | solution.py:35
  61.7 2.2 %collective-permute-done.7.far_ref = bf16[256,2176]{1,0:T(8,128)(2,1)S(1)} collective-permute-done((bf16[256,2176]{1,0:T(8,128)(2,1)S(1)}, bf16[256,2176]{1,0:T(8,128)(2,1)S(1)}, u32[]{:S(2)}, u32[]{:S(2)}) %collective-permute-start.7) | collective-permute-done | bytes 1114144 | tf_op jit(solution)/shard_map/ppermute | solution.py:35
  63.9 1.9 %copy-done.1 = bf16[1,2048,768]{2,1,0:T(8,128)(2,1)S(1)} copy-done((bf16[1,2048,768]{2,1,0:T(8,128)(2,1)S(1)}, bf16[1,2048,768]{2,1,0:T(8,128)(2,1)}, u32[]{:S(2)}) %copy-start.1) | copy-done | bytes 3145752
  65.8 1.9 %copy-done.3 = bf16[1,2048,768]{2,1,0:T(8,128)(2,1)S(1)} copy-done((bf16[1,2048,768]{2,1,0:T(8,128)(2,1)S(1)}, bf16[1,2048,768]{2,1,0:T(8,128)(2,1)}, u32[]{:S(2)}) %copy-start.3) | copy-done | bytes 3145752
  67.7 1.9 %copy-done.5 = bf16[1,768,2048]{2,1,0:T(8,128)(2,1)S(1)} copy-done((bf16[1,768,2048]{2,1,0:T(8,128)(2,1)S(1)}, bf16[1,768,2048]{2,1,0:T(8,128)(2,1)}, u32[]{:S(2)}) %copy-start.5) | copy-done | bytes 3145752
  69.6 8.0 %expert_half.3 = (bf16[256,2048]{1,0:T(8,128)(2,1)S(1)}, bf16[256,2048]{1,0:T(8,128)(2,1)}) custom-call(bf16[256,2176]{1,0:T(8,128)(2,1)S(1)} %collective-permute-done.6.near_ref, bf16[256,2176]{1,0:T(8,128)(2,1)S(1)} %collective-permute-done.7.far_ref, f32[1,128]{1,0:T(1,128)S(1)} %or_convert_fusion.pick_ref, bf16[1,2048,768]{2,1,0:T(8,128)(2,1)S(1)} %copy-done.1, ...), custom_call_target="tpu_custom_call" | custom-call | flops 4831838208 | bytes 13631488 | tf_op jit(solution)/shard_map/expert_half/pallas_call | solution.py:160
  77.7 1.0 copy-done.7
  78.7 1.9 %copy-done.6 = bf16[1,768,2048]{2,1,0:T(8,128)(2,1)S(1)} copy-done((bf16[1,768,2048]{2,1,0:T(8,128)(2,1)S(1)}, bf16[1,768,2048]{2,1,0:T(8,128)(2,1)}, u32[]{:S(2)}) %copy-start.6) | copy-done | bytes 3145752
  80.6 1.2 copy-done.8
  81.9 7.2 %expert_half.2 = (bf16[256,2048]{1,0:T(8,128)(2,1)S(1)}, bf16[256,2048]{1,0:T(8,128)(2,1)S(1)}) custom-call(bf16[256,2176]{1,0:T(8,128)(2,1)S(1)} %pad_maximum_fusion.near_ref, bf16[256,2176]{1,0:T(8,128)(2,1)S(1)} %copy-done.8, f32[1,128]{1,0:T(1,128)S(1)} %or_convert_fusion.pick_ref, bf16[1,2048,768]{2,1,0:T(8,128)(2,1)S(1)} %copy-done.2, ...), custom_call_target="tpu_custom_call" | custom-call | flops 4831838208 | bytes 13631488 | tf_op jit(solution)/shard_map/expert_half/pallas_call | solution.py:160
  89.9 2.1 %collective-permute-start.9 = (bf16[256,2048]{1,0:T(8,128)(2,1)S(1)}, bf16[256,2048]{1,0:T(8,128)(2,1)S(1)}, u32[]{:S(2)}, u32[]{:S(2)}) collective-permute-start(bf16[256,2048]{1,0:T(8,128)(2,1)S(1)} %add_convert_fusion), channel_id=1, source_target_pairs={{0,4},{1,5},{2,3},{3,2},{4,0},{5,1},{6,7},{7,6},{8,12},{9,13},{10,... | collective-permute-start | bytes 3145736 | tf_op jit(solution)/shard_map/ppermute | solution.py:35
  92.0 12.8 %collective-permute-done.9 = bf16[256,2048]{1,0:T(8,128)(2,1)S(1)} collective-permute-done((bf16[256,2048]{1,0:T(8,128)(2,1)S(1)}, bf16[256,2048]{1,0:T(8,128)(2,1)S(1)}, u32[]{:S(2)}, u32[]{:S(2)}) %collective-permute-start.9) | collective-permute-done | bytes 1048608 | tf_op jit(solution)/shard_map/ppermute | solution.py:35
  105.4 2.1 %collective-permute-start.10 = (bf16[128,2048]{1,0:T(8,128)(2,1)S(1)}, bf16[128,2048]{1,0:T(8,128)(2,1)S(1)}, u32[]{:S(2)}, u32[]{:S(2)}) collective-permute-start(bf16[128,2048]{1,0:T(8,128)(2,1)S(1)} %slice.43), channel_id=1, source_target_pairs={{0,1},{1,0},{2,6},{3,7},{4,5},{5,4},{6,2},{7,3},{8,9},{9,8},{10,14... | collective-permute-start | bytes 1572872 | tf_op jit(solution)/shard_map/ppermute | solution.py:35
  107.5 7.2 %collective-permute-done.10 = bf16[128,2048]{1,0:T(8,128)(2,1)S(1)} collective-permute-done((bf16[128,2048]{1,0:T(8,128)(2,1)S(1)}, bf16[128,2048]{1,0:T(8,128)(2,1)S(1)}, u32[]{:S(2)}, u32[]{:S(2)}) %collective-permute-start.10) | collective-permute-done | bytes 524320 | tf_op jit(solution)/shard_map/ppermute | solution.py:35
  114.8 2.2 %collective-permute-start.11 = (bf16[64,2048]{1,0:T(8,128)(2,1)S(1)}, bf16[64,2048]{1,0:T(8,128)(2,1)S(1)}, u32[]{:S(2)}, u32[]{:S(2)}) collective-permute-start(bf16[64,2048]{1,0:T(8,128)(2,1)S(1)} %slice.44), channel_id=1, source_target_pairs={{0,8},{1,9},{2,18},{3,19},{4,12},{5,13},{6,22},{7,23},{8,0},{9,1},... | collective-permute-start | bytes 786440 | tf_op jit(solution)/shard_map/ppermute | solution.py:35
  117.0 4.7 %collective-permute-done.11 = bf16[64,2048]{1,0:T(8,128)(2,1)S(1)} collective-permute-done((bf16[64,2048]{1,0:T(8,128)(2,1)S(1)}, bf16[64,2048]{1,0:T(8,128)(2,1)S(1)}, u32[]{:S(2)}, u32[]{:S(2)}) %collective-permute-start.11) | collective-permute-done | bytes 262176 | tf_op jit(solution)/shard_map/ppermute | solution.py:35
  121.7 6.3 %collective-permute-start.12 = (bf16[32,2048]{1,0:T(8,128)(2,1)S(1)}, bf16[32,2048]{1,0:T(8,128)(2,1)S(1)}, u32[]{:S(2)}, u32[]{:S(2)}) collective-permute-start(bf16[32,2048]{1,0:T(8,128)(2,1)S(1)} %slice.45), channel_id=1, source_target_pairs={{0,16},{1,17},{2,10},{3,11},{4,20},{5,21},{6,14},{7,15},{8,24},{9,... | collective-permute-start | bytes 393224 | tf_op jit(solution)/shard_map/ppermute | solution.py:35
  128.0 4.3 %collective-permute-done.12 = bf16[32,2048]{1,0:T(8,128)(2,1)S(1)} collective-permute-done((bf16[32,2048]{1,0:T(8,128)(2,1)S(1)}, bf16[32,2048]{1,0:T(8,128)(2,1)S(1)}, u32[]{:S(2)}, u32[]{:S(2)}) %collective-permute-start.12) | collective-permute-done | bytes 131104 | tf_op jit(solution)/shard_map/ppermute | solution.py:35
  132.3 0.7 fusion.11
  (60 shorter events, 5.2 us)
Async XLA Ops:
  0.0 11.9 %copy-start = (s32[64,8]{0,1:T(8,128)S(1)}, s32[64,8]{0,1:T(8,128)}, u32[]{:S(2)}) copy-start(s32[64,8]{0,1:T(8,128)} %param.19) | copy-start | bytes 6148
  3.9 8.1 %copy-start.13 = (f32[64,8]{0,1:T(8,128)S(1)}, f32[64,8]{0,1:T(8,128)}, u32[]{:S(2)}) copy-start(f32[64,8]{0,1:T(8,128)} %param.20) | copy-start | bytes 6148
  3.9 11.6 %copy-start.11 = (bf16[32,2048]{1,0:T(8,128)(2,1)S(1)}, bf16[32,2048]{1,0:T(8,128)(2,1)}, u32[]{:S(2)}) copy-start(bf16[32,2048]{1,0:T(8,128)(2,1)} %param.17) | copy-start | bytes 393220
  3.9 12.4 %copy-start.12 = (f32[2048]{0:T(1024)S(1)}, f32[2048]{0:T(1024)}, u32[]{:S(2)}) copy-start(f32[2048]{0:T(1024)} %param.18) | copy-start | bytes 24580
  8.9 6.5 %collective-permute-start = (bf16[32,2048]{1,0:T(8,128)(2,1)S(1)}, bf16[32,2048]{1,0:T(8,128)(2,1)S(1)}, u32[]{:S(2)}, u32[]{:S(2)}) collective-permute-start(bf16[32,2048]{1,0:T(8,128)(2,1)S(1)} %dynamic-slice_convert_fusion), channel_id=1, source_target_pairs={{0,1},{1,0},{2,3},{3,2},{4,5},{5,4},{6,7},{7,6},{8,9},{9,8},{10,11... | collective-permute-start | bytes 393224 | tf_op jit(solution)/shard_map/ppermute | solution.py:30
  15.6 0.7 copy-start.9
  16.5 7.6 %collective-permute-start.1 = (bf16[32,2176]{1,0:T(8,128)(2,1)S(1)}, bf16[32,2176]{1,0:T(8,128)(2,1)S(1)}, u32[]{:S(2)}, u32[]{:S(2)}) collective-permute-start(bf16[32,2176]{1,0:T(8,128)(2,1)S(1)} %concatenate.14), channel_id=1, source_target_pairs={{0,16},{1,17},{2,10},{3,11},{4,20},{5,21},{6,14},{7,15},{8,24},{9,... | collective-permute-start | bytes 417800 | tf_op jit(solution)/shard_map/ppermute | solution.py:35
  24.1 9.4 %collective-permute-start.2 = (bf16[64,2176]{1,0:T(8,128)(2,1)S(1)}, bf16[64,2176]{1,0:T(8,128)(2,1)S(1)}, u32[]{:S(2)}, u32[]{:S(2)}) collective-permute-start(bf16[64,2176]{1,0:T(8,128)(2,1)S(1)} %pad_maximum_fusion.2), channel_id=1, source_target_pairs={{0,8},{1,9},{2,18},{3,19},{4,12},{5,13},{6,22},{7,23},{8,0},{9,1},... | collective-permute-start | bytes 835592 | tf_op jit(solution)/shard_map/ppermute | solution.py:35
  33.5 11.7 %collective-permute-start.3 = (bf16[128,2176]{1,0:T(8,128)(2,1)S(1)}, bf16[128,2176]{1,0:T(8,128)(2,1)S(1)}, u32[]{:S(2)}, u32[]{:S(2)}) collective-permute-start(bf16[128,2176]{1,0:T(8,128)(2,1)S(1)} %pad_maximum_fusion.1), channel_id=1, source_target_pairs={{0,1},{1,0},{2,6},{3,7},{4,5},{5,4},{6,2},{7,3},{8,9},{9,8},{10,14... | collective-permute-start | bytes 1671176 | tf_op jit(solution)/shard_map/ppermute | solution.py:35
  45.3 15.9 %collective-permute-start.6 = (bf16[256,2176]{1,0:T(8,128)(2,1)S(1)}, bf16[256,2176]{1,0:T(8,128)(2,1)S(1)}, u32[]{:S(2)}, u32[]{:S(2)}) collective-permute-start(bf16[256,2176]{1,0:T(8,128)(2,1)S(1)} %pad_maximum_fusion.near_ref), channel_id=1, source_target_pairs={{0,4},{1,5},{2,3},{3,2},{4,0},{5,1},{6,7},{7,6},{8,12},{9,13},{10,... | collective-permute-start | bytes 3342344 | tf_op jit(solution)/shard_map/ppermute | solution.py:35
  61.2 2.8 %collective-permute-start.7 = (bf16[256,2176]{1,0:T(8,128)(2,1)S(1)}, bf16[256,2176]{1,0:T(8,128)(2,1)S(1)}, u32[]{:S(2)}, u32[]{:S(2)}) collective-permute-start(bf16[256,2176]{1,0:T(8,128)(2,1)S(1)} %collective-permute-done.6.near_ref), channel_id=1, source_target_pairs={{0,2},{1,3},{2,0},{3,1},{4,6},{5,7},{6,4},{7,5},{8,10},{9,11},{10,... | collective-permute-start | bytes 3342344 | tf_op jit(solution)/shard_map/ppermute | solution.py:35
  61.2 16.5 %collective-permute-start.4 = (bf16[256,2176]{1,0:T(8,128)(2,1)S(1)}, bf16[256,2176]{1,0:T(8,128)(2,1)S(1)}, u32[]{:S(2)}, u32[]{:S(2)}) collective-permute-start(bf16[256,2176]{1,0:T(8,128)(2,1)S(1)} %pad_maximum_fusion.near_ref), channel_id=1, source_target_pairs={{0,2},{1,3},{2,0},{3,1},{4,6},{5,7},{6,4},{7,5},{8,10},{9,11},{10,... | collective-permute-start | bytes 3342344 | tf_op jit(solution)/shard_map/ppermute | solution.py:35
  63.9 1.9 %copy-start.1 = (bf16[1,2048,768]{2,1,0:T(8,128)(2,1)S(1)}, bf16[1,2048,768]{2,1,0:T(8,128)(2,1)}, u32[]{:S(2)}) copy-start(bf16[1,2048,768]{2,1,0:T(8,128)(2,1)} %gate_ref.3) | copy-start | bytes 9437188
  65.8 1.9 %copy-start.3 = (bf16[1,2048,768]{2,1,0:T(8,128)(2,1)S(1)}, bf16[1,2048,768]{2,1,0:T(8,128)(2,1)}, u32[]{:S(2)}) copy-start(bf16[1,2048,768]{2,1,0:T(8,128)(2,1)} %up_ref.3) | copy-start | bytes 9437188
  67.7 1.9 %copy-start.5 = (bf16[1,768,2048]{2,1,0:T(8,128)(2,1)S(1)}, bf16[1,768,2048]{2,1,0:T(8,128)(2,1)}, u32[]{:S(2)}) copy-start(bf16[1,768,2048]{2,1,0:T(8,128)(2,1)} %down_ref.3) | copy-start | bytes 9437188
  69.6 9.1 %copy-start.2 = (bf16[1,2048,768]{2,1,0:T(8,128)(2,1)S(1)}, bf16[1,2048,768]{2,1,0:T(8,128)(2,1)}, u32[]{:S(2)}) copy-start(bf16[1,2048,768]{2,1,0:T(8,128)(2,1)} %gate_ref.3) | copy-start | bytes 9437188
  69.6 9.1 %copy-start.4 = (bf16[1,2048,768]{2,1,0:T(8,128)(2,1)S(1)}, bf16[1,2048,768]{2,1,0:T(8,128)(2,1)}, u32[]{:S(2)}) copy-start(bf16[1,2048,768]{2,1,0:T(8,128)(2,1)} %up_ref.3) | copy-start | bytes 9437188
  77.6 12.0 %collective-permute-start.8 = (bf16[256,2048]{1,0:T(8,128)(2,1)}, bf16[256,2048]{1,0:T(8,128)(2,1)S(1)}, u32[]{:S(2)}, u32[]{:S(2)}) collective-permute-start(bf16[256,2048]{1,0:T(8,128)(2,1)} %get-tuple-element.12), channel_id=1, source_target_pairs={{0,2},{1,3},{2,0},{3,1},{4,6},{5,7},{6,4},{7,5},{8,10},{9,11},{10,... | collective-permute-start | bytes 3145736 | tf_op jit(solution)/shard_map/ppermute | solution.py:35
  77.7 1.0 copy-start.7
  78.7 1.9 %copy-start.6 = (bf16[1,768,2048]{2,1,0:T(8,128)(2,1)S(1)}, bf16[1,768,2048]{2,1,0:T(8,128)(2,1)}, u32[]{:S(2)}) copy-start(bf16[1,768,2048]{2,1,0:T(8,128)(2,1)} %down_ref.3) | copy-start | bytes 9437188
  80.6 1.2 copy-start.8
  89.1 2.9 %collective-permute-start.5 = (bf16[256,2048]{1,0:T(8,128)(2,1)S(1)}, bf16[256,2048]{1,0:T(8,128)(2,1)S(1)}, u32[]{:S(2)}, u32[]{:S(2)}) collective-permute-start(bf16[256,2048]{1,0:T(8,128)(2,1)S(1)} %get-tuple-element.10), channel_id=1, source_target_pairs={{0,2},{1,3},{2,0},{3,1},{4,6},{5,7},{6,4},{7,5},{8,10},{9,11},{10,... | collective-permute-start | bytes 3145736 | tf_op jit(solution)/shard_map/ppermute | solution.py:35
  89.9 14.9 %collective-permute-start.9 = (bf16[256,2048]{1,0:T(8,128)(2,1)S(1)}, bf16[256,2048]{1,0:T(8,128)(2,1)S(1)}, u32[]{:S(2)}, u32[]{:S(2)}) collective-permute-start(bf16[256,2048]{1,0:T(8,128)(2,1)S(1)} %add_convert_fusion), channel_id=1, source_target_pairs={{0,4},{1,5},{2,3},{3,2},{4,0},{5,1},{6,7},{7,6},{8,12},{9,13},{10,... | collective-permute-start | bytes 3145736 | tf_op jit(solution)/shard_map/ppermute | solution.py:35
  105.4 26.9 %copy-start.10 = (f32[32,2048]{1,0:T(8,128)S(1)}, f32[32,2048]{1,0:T(8,128)}, u32[]{:S(2)}) copy-start(f32[32,2048]{1,0:T(8,128)} %copy-done.9) | copy-start | bytes 786436
  105.4 9.2 %collective-permute-start.10 = (bf16[128,2048]{1,0:T(8,128)(2,1)S(1)}, bf16[128,2048]{1,0:T(8,128)(2,1)S(1)}, u32[]{:S(2)}, u32[]{:S(2)}) collective-permute-start(bf16[128,2048]{1,0:T(8,128)(2,1)S(1)} %slice.43), channel_id=1, source_target_pairs={{0,1},{1,0},{2,6},{3,7},{4,5},{5,4},{6,2},{7,3},{8,9},{9,8},{10,14... | collective-permute-start | bytes 1572872 | tf_op jit(solution)/shard_map/ppermute | solution.py:35
  114.8 6.8 %collective-permute-start.11 = (bf16[64,2048]{1,0:T(8,128)(2,1)S(1)}, bf16[64,2048]{1,0:T(8,128)(2,1)S(1)}, u32[]{:S(2)}, u32[]{:S(2)}) collective-permute-start(bf16[64,2048]{1,0:T(8,128)(2,1)S(1)} %slice.44), channel_id=1, source_target_pairs={{0,8},{1,9},{2,18},{3,19},{4,12},{5,13},{6,22},{7,23},{8,0},{9,1},... | collective-permute-start | bytes 786440 | tf_op jit(solution)/shard_map/ppermute | solution.py:35
  121.7 10.6 %collective-permute-start.12 = (bf16[32,2048]{1,0:T(8,128)(2,1)S(1)}, bf16[32,2048]{1,0:T(8,128)(2,1)S(1)}, u32[]{:S(2)}, u32[]{:S(2)}) collective-permute-start(bf16[32,2048]{1,0:T(8,128)(2,1)S(1)} %slice.45), channel_id=1, source_target_pairs={{0,16},{1,17},{2,10},{3,11},{4,20},{5,21},{6,14},{7,15},{8,24},{9,... | collective-permute-start | bytes 393224 | tf_op jit(solution)/shard_map/ppermute | solution.py:35

commit v2 on v0

v2 whole, which is shorter than its diff:
```python
import functools
import math

import jax
import jax.numpy as jnp
from jax import lax
from jax.experimental import pallas as pl
from jax.experimental.pallas import tpu as pltpu
from jax.sharding import PartitionSpec as P

D = 2048
QUERY_HEADS = 32
KEY_VALUE_HEADS = 4
HEAD_WIDTH = 128
TOPK = 8


NEG_BIG = -1e30
EPS = 1e-06
LANES = 128

BOTH = ("expert", "tensor")
BIT_X, BIT_CORE, BIT_Y, BIT_Z0, BIT_Z1 = 1, 2, 4, 8, 16
NEAR_PLANE, FAR_PLANE = (BIT_X, BIT_Y), (BIT_Y, BIT_X)
NEAR_LINE, FAR_LINE = (BIT_Z0, BIT_Z0), (BIT_Z1, BIT_Z1)
CORE = (BIT_CORE, BIT_CORE)
FIRST_BLOCK = 256
SECOND_BLOCK = 512


def swapped(shard, axis, distance):
    return lax.ppermute(shard, axis, [(i, i ^ 1 << distance) for i in range(lax.axis_size(axis))])


def exchanged(shard, masks):
    count = lax.axis_size("expert") * lax.axis_size("tensor")
    return lax.ppermute(
        shard, BOTH, [(i, i ^ masks[1 if i & BIT_CORE else 0]) for i in range(count)]
    )


def widened(shard):
    return shard.astype(jnp.float32)


def narrowed(shard):
    return shard.astype(jnp.bfloat16)


def slot_numbers(route_block, expert_count):
    share_count, share_rows, top_count = route_block.shape
    flattened_routes = route_block.reshape(share_count, share_rows * top_count)
    one_hot = (
        flattened_routes[:, :, None] == jnp.arange(expert_count, dtype=jnp.int32)[None, None, :]
    ).astype(jnp.int32)
    before = jnp.cumsum(one_hot, axis=1) - one_hot
    return jnp.sum(before * one_hot, axis=2).reshape(share_count, share_rows, top_count)


def source_table(route_block, slot_ids, expert_count, capacity):
    share_count, share_rows, top_count = route_block.shape
    share_ids = jnp.broadcast_to(
        jnp.arange(share_count, dtype=jnp.int32)[:, None, None], route_block.shape
    )
    row_ids = share_ids * share_rows + jnp.broadcast_to(
        jnp.arange(share_rows, dtype=jnp.int32)[None, :, None], route_block.shape
    )
    empty_table = jnp.full(
        (share_count, expert_count, capacity), share_count * share_rows, jnp.int32
    )
    return empty_table.at[share_ids, route_block, slot_ids].set(row_ids)


def normalize(stream_rows, gain):
    mean_square = jnp.mean(stream_rows * stream_rows, axis=-1, keepdims=True)
    return (stream_rows * lax.rsqrt(mean_square + EPS) * gain).astype(jnp.bfloat16)


def partial_projection(queries, keys, values, positions, out_weight):
    tensor_rank = lax.axis_index("tensor")
    group_rows = queries.shape[0]
    heads_dev = queries.shape[1] // HEAD_WIDTH
    queries_per_key_head = QUERY_HEADS // KEY_VALUE_HEADS
    kv_count = max(1, heads_dev // queries_per_key_head)
    heads_each = heads_dev // kv_count
    kv_first = tensor_rank * heads_dev // queries_per_key_head
    key_cols = lax.dynamic_slice_in_dim(keys, kv_first * HEAD_WIDTH, kv_count * HEAD_WIDTH, 1)
    value_cols = lax.dynamic_slice_in_dim(values, kv_first * HEAD_WIDTH, kv_count * HEAD_WIDTH, 1)
    query_block = queries.reshape(group_rows, kv_count, heads_each, HEAD_WIDTH)
    local_index = jnp.arange(group_rows, dtype=jnp.int32)
    earliest = local_index - positions
    visible = (local_index[None, :] <= local_index[:, None]) & (
        local_index[None, :] >= earliest[:, None]
    )
    score_scale = 1.0 / math.sqrt(HEAD_WIDTH)
    scores = (
        jnp.einsum(
            "qkhd,nkd->khqn",
            query_block,
            key_cols.reshape(group_rows, kv_count, HEAD_WIDTH),
            preferred_element_type=jnp.float32,
        )
        * score_scale
    )
    masked = jnp.where(visible[None, None], scores, NEG_BIG)
    row_max = jnp.max(masked, axis=3, keepdims=True)
    raw_weights = jnp.where(visible[None, None], jnp.exp(masked - row_max), 0.0)
    soft_weights = (raw_weights / jnp.sum(raw_weights, axis=3, keepdims=True)).astype(jnp.bfloat16)
    head_values = jnp.einsum(
        "khqn,nkd->qkhd",
        soft_weights,
        value_cols.reshape(group_rows, kv_count, HEAD_WIDTH),
        preferred_element_type=jnp.float32,
    )
    attended = head_values.reshape(group_rows, heads_dev * HEAD_WIDTH).astype(jnp.bfloat16)
    return jnp.dot(attended, out_weight, preferred_element_type=jnp.float32)


def attention_kernel(
    queries_hbm,
    keys_hbm,
    values_hbm,
    positions_ref,
    out_weight_hbm,
    kept_ref,
    given_ref,
    queries_ref,
    keys_ref,
    values_ref,
    weight_ref,
    total_ref,
    input_sems,
    weight_sems,
):
    chunks, chunk_rows = weight_ref.shape[:2]
    input_copies = [
        pltpu.make_async_copy(source, target, input_sems.at[place])
        for place, (source, target) in enumerate(
            ((keys_hbm, keys_ref), (queries_hbm, queries_ref), (values_hbm, values_ref))
        )
    ]
    weight_copies = [
        pltpu.make_async_copy(
            out_weight_hbm.at[pl.ds(chunk * chunk_rows, chunk_rows), :],
            weight_ref.at[chunk],
            weight_sems.at[chunk],
        )
        for chunk in range(chunks)
    ]
    for copy in input_copies + weight_copies:
        copy.start()
    rows = queries_ref.shape[0]
    own_rows = kept_ref.shape[0]
    rank = lax.axis_index("tensor")
    group_heads = QUERY_HEADS // KEY_VALUE_HEADS
    groups = queries_ref.shape[1] // (HEAD_WIDTH * group_heads)
    query_index = lax.broadcasted_iota(jnp.int32, (rows, rows), 0)
    key_index = lax.broadcasted_iota(jnp.int32, (rows, rows), 1)
    position = jnp.sum(
        jnp.where(query_index == key_index, positions_ref[...], 0), axis=1, keepdims=True
    )
    visible = (key_index <= query_index) & (key_index >= query_index - position)
    visible = jnp.concatenate([visible.astype(jnp.float32)] * group_heads, axis=0) > 0.5
    score_scale = 1.0 / math.sqrt(HEAD_WIDTH)
    per_group = chunks // groups
    heads_chunk = group_heads // per_group
    for copy in input_copies:
        copy.wait()
    for group in range(groups):
        place = pl.multiple_of((rank * groups + group) * HEAD_WIDTH, HEAD_WIDTH)
        key = keys_ref[:, pl.ds(place, HEAD_WIDTH)]
        value = values_ref[:, pl.ds(place, HEAD_WIDTH)]
        first = group * group_heads
        query = jnp.concatenate(
            [
                queries_ref[:, (first + head) * HEAD_WIDTH : (first + head + 1) * HEAD_WIDTH]
                for head in range(group_heads)
            ],
            axis=0,
        )
        scores = (
            lax.dot_general(
                query, key, (((1,), (1,)), ((), ())), preferred_element_type=jnp.float32
            )
            * score_scale
        )
        masked = jnp.where(visible, scores, NEG_BIG)
        row_max = jnp.max(masked, axis=1, keepdims=True)
        raw = jnp.where(visible, jnp.exp(masked - row_max), 0.0)
        soft = (raw / jnp.sum(raw, axis=1, keepdims=True)).astype(jnp.bfloat16)
        attended = jnp.dot(soft, value, preferred_element_type=jnp.float32).astype(jnp.bfloat16)
        for part in range(per_group):
            chunk = group * per_group + part
            feed = jnp.concatenate(
                [
                    attended[head * rows : (head + 1) * rows]
                    for head in range(part * heads_chunk, (part + 1) * heads_chunk)
                ],
                axis=1,
            )
            weight_copies[chunk].wait()
            product = jnp.dot(feed, weight_ref[chunk], preferred_element_type=jnp.float32)
            if chunk == 0:
                total_ref[...] = product
            else:
                total_ref[...] += product
    kept_ref[...] = total_ref[pl.ds(pl.multiple_of(rank * own_rows, own_rows), own_rows), :]
    given_ref[...] = total_ref[
        pl.ds(pl.multiple_of((1 - rank) * own_rows, own_rows), own_rows), :
    ].astype(jnp.bfloat16)


def attention_halves(queries, keys, values, positions, out_weight):
    rows, width = queries.shape
    chunks = 4
    near = pl.BlockSpec(memory_space=pltpu.VMEM)
    far = pl.BlockSpec(memory_space=pltpu.HBM)
    return pl.pallas_call(
        attention_kernel,
        in_specs=[far, far, far, near, far],
        out_specs=[near] * 2,
        out_shape=[
            jax.ShapeDtypeStruct((rows // 2, D), jnp.float32),
            jax.ShapeDtypeStruct((rows // 2, D), jnp.bfloat16),
        ],
        scratch_shapes=[
            pltpu.VMEM(queries.shape, queries.dtype),
            pltpu.VMEM(keys.shape, keys.dtype),
            pltpu.VMEM(values.shape, values.dtype),
            pltpu.VMEM((chunks, width // chunks, D), jnp.bfloat16),
            pltpu.VMEM((rows, D), jnp.float32),
            pltpu.SemaphoreType.DMA((3,)),
            pltpu.SemaphoreType.DMA((chunks,)),
        ],
        compiler_params=pltpu.CompilerParams(vmem_limit_bytes=24 * 2**20),
        cost_estimate=pl.CostEstimate(
            flops=2 * rows * width * D + 4 * rows * rows * width,
            bytes_accessed=2 * width * D,
            transcendentals=rows * rows * width // HEAD_WIDTH,
        ),
        name="attention_halves",
    )(
        *[pltpu.with_memory_space_constraint(x, pltpu.HBM) for x in (queries, keys, values)],
        positions.reshape(1, rows),
        pltpu.with_memory_space_constraint(out_weight, pltpu.HBM),
    )


def load_kernel(count, pieces, *refs):
    sources, targets, sems = refs[:count], refs[count + 1 : 2 * count + 1], refs[2 * count + 1]
    copies = []
    for place, (source, target) in enumerate(zip(sources, targets)):
        rows = source.shape[1] // pieces
        for piece in range(pieces):
            window = pl.ds(piece * rows, rows)
            copies.append(
                pltpu.make_async_copy(
                    source.at[:, window, :],
                    target.at[:, window, :],
                    sems.at[place * pieces + piece],
                )
            )
    for copy in copies:
        copy.start()
    for copy in copies:
        copy.wait()


def loaded(weights, after):
    pieces = 2
    far = pl.BlockSpec(memory_space=pltpu.HBM)
    return pl.pallas_call(
        functools.partial(load_kernel, len(weights), pieces),
        in_specs=[far] * len(weights) + [pl.BlockSpec(memory_space=pl.ANY)],
        out_specs=[pl.BlockSpec(memory_space=pltpu.VMEM)] * len(weights),
        out_shape=[pltpu.VMEM(weight.shape, weight.dtype) for weight in weights],
        scratch_shapes=[pltpu.SemaphoreType.DMA((len(weights) * pieces,))],
        compiler_params=pltpu.CompilerParams(vmem_limit_bytes=2 * 2**20),
        cost_estimate=pl.CostEstimate(
            flops=0, bytes_accessed=sum(2 * weight.size for weight in weights), transcendentals=0
        ),
        name="load_weights",
    )(*[pltpu.with_memory_space_constraint(weight, pltpu.HBM) for weight in weights], after)


def norm_kernel(
    kept_ref,
    taken_ref,
    residual_ref,
    gain_ref,
    routes_ref,
    probs_ref,
    middle_ref,
    block_ref,
    table_ref,
):
    rows = kept_ref.shape[0]
    top_count, group_rows = routes_ref.shape
    expert_size = lax.axis_size("expert")
    rank = lax.axis_index("tensor")
    middle = (
        residual_ref[...].astype(jnp.float32)
        + kept_ref[...]
        + taken_ref[...].astype(jnp.float32)
    )
    middle_ref[...] = middle
    mean_square = jnp.mean(middle * middle, axis=1, keepdims=True)
    block_ref[:, :D] = (middle * lax.rsqrt(mean_square + EPS) * gain_ref[...]).astype(jnp.bfloat16)
    number = lax.broadcasted_iota(jnp.int32, (LANES, group_rows), 0)
    table = jnp.zeros((LANES, group_rows), jnp.float32)
    for choice in range(top_count):
        route = routes_ref[choice : choice + 1, :]
        hit = (number == route) | (number == route + expert_size)
        table = jnp.where(hit, probs_ref[choice : choice + 1, :], table)
    high = table.astype(jnp.bfloat16).astype(jnp.float32)
    table = jnp.where(number < expert_size, high, table - high)
    table = jnp.concatenate(
        [table, jnp.zeros((LANES, LANES - group_rows), jnp.float32)], axis=1
    )
    table_ref[...] = table.T
    block_ref[:, D:] = table_ref[pl.ds(pl.multiple_of(rank * rows, rows), rows), :].astype(
        jnp.bfloat16
    )


def normed_block(kept, taken, residual, norm_gain, routes, route_probs):
    rows = kept.shape[0]
    near = pl.BlockSpec(memory_space=pltpu.VMEM)
    return pl.pallas_call(
        norm_kernel,
        in_specs=[near] * 6,
        out_specs=[near] * 2,
        out_shape=[
            jax.ShapeDtypeStruct((rows, D), jnp.float32),
            jax.ShapeDtypeStruct((rows, D + LANES), jnp.bfloat16),
        ],
        scratch_shapes=[pltpu.VMEM((LANES, LANES), jnp.float32)],
        compiler_params=pltpu.CompilerParams(vmem_limit_bytes=6 * 2**20),
        cost_estimate=pl.CostEstimate(flops=6 * rows * D, bytes_accessed=20 * rows * D, transcendentals=rows),
        name="normed_block",
    )(kept, taken, residual, norm_gain.reshape(1, D), routes.T, route_probs.T)


def expert_kernel(
    near_ref,
    far_ref,
    gate_ref,
    up_ref,
    down_ref,
    near_out_ref,
    far_out_ref,
    feed_ref,
    hidden_ref,
):
    rows = near_ref.shape[0]
    units = gate_ref.shape[2]
    lane = lax.broadcasted_iota(jnp.int32, (1, LANES), 1)
    mine = lax.axis_index("expert")
    pick = jnp.where((lane == mine) | (lane == mine + lax.axis_size("expert")), 1.0, 0.0)
    weights = []
    for place, source in enumerate((near_ref, far_ref)):
        feed_ref[place * rows : (place + 1) * rows, :] = source[:, :D]
        weights.append(
            jnp.sum(source[:, D:].astype(jnp.float32) * pick, axis=1, keepdims=True)
        )
    weight = jnp.concatenate(weights, axis=0)
    for first in range(0, units, FIRST_BLOCK):
        cols = slice(first, first + FIRST_BLOCK)
        gate = jnp.dot(feed_ref[...], gate_ref[0, :, cols], preferred_element_type=jnp.float32)
        up = jnp.dot(feed_ref[...], up_ref[0, :, cols], preferred_element_type=jnp.float32)
        hidden = gate / (1.0 + jnp.exp(-gate)) * up * weight
        hidden_ref[:, cols] = hidden.astype(jnp.bfloat16)
    for first in range(0, D, SECOND_BLOCK):
        cols = slice(first, first + SECOND_BLOCK)
        part = jnp.dot(
            hidden_ref[...], down_ref[0, :, cols], preferred_element_type=jnp.float32
        ).astype(jnp.bfloat16)
        near_out_ref[:, cols] = part[:rows]
        far_out_ref[:, cols] = part[rows:]


def weighted_expert(near, far, weights):
    rows = near.shape[0]
    units = weights[0].shape[2]
    whole = pl.BlockSpec(memory_space=pltpu.VMEM)
    return pl.pallas_call(
        expert_kernel,
        in_specs=[whole] * 5,
        out_specs=[whole] * 2,
        out_shape=[jax.ShapeDtypeStruct((rows, D), jnp.bfloat16)] * 2,
        scratch_shapes=[
            pltpu.VMEM((2 * rows, D), jnp.bfloat16),
            pltpu.VMEM((2 * rows, units), jnp.bfloat16),
        ],
        compiler_params=pltpu.CompilerParams(vmem_limit_bytes=12 * 2**20),
        cost_estimate=pl.CostEstimate(
            flops=2 * 2 * rows * 3 * D * units,
            bytes_accessed=8 * rows * D,
            transcendentals=2 * rows * units,
        ),
        name="expert_half",
    )(near, far, *[pltpu.with_memory_space_constraint(w, pltpu.VMEM) for w in weights])


def dense_experts(middle_own, block, weights):
    def plane_sum(rows):
        pair = jnp.concatenate([rows, exchanged(rows, NEAR_PLANE)], axis=0)
        near = jnp.concatenate([pair, exchanged(pair, FAR_PLANE)], axis=0)
        near_out, far_out = weighted_expert(near, exchanged(near, CORE), weights)
        total = widened(near_out) + widened(exchanged(far_out, CORE))
        for masks in (FAR_PLANE, NEAR_PLANE):
            half = total.shape[0] // 2
            total = total[:half] + widened(exchanged(narrowed(total[half:]), masks))
        return total

    far_line = exchanged(block, FAR_LINE)
    own_sum = plane_sum(block)
    far_sum = plane_sum(far_line)
    both_sum = plane_sum(exchanged(far_line, NEAR_LINE))
    near_sum = plane_sum(exchanged(block, NEAR_LINE))
    far_sum += widened(exchanged(narrowed(both_sum), NEAR_LINE))
    own_sum += widened(exchanged(narrowed(near_sum), NEAR_LINE))
    own_sum += widened(exchanged(narrowed(far_sum), FAR_LINE))
    return (middle_own + own_sum).astype(jnp.bfloat16)


def routed_experts(middle_own, normed_own, own_routes, own_probs, gate_weight, up_weight, down_weight):
    tensor_size = lax.axis_size("tensor")
    expert_size = lax.axis_size("expert")
    tensor_rank = lax.axis_index("tensor")
    token_rows = normed_own.shape[0]
    local_count = tensor_size // 2
    experts = local_count * expert_size
    slot_cap = max(2, 2 * token_rows * TOPK // experts)
    blank_row = jnp.zeros((1, D), jnp.bfloat16)
    own_block = own_routes.reshape(1, token_rows, TOPK)
    own_numbers = slot_numbers(own_block, experts)
    own_slots = own_numbers[0]
    slot_table = source_table(own_block, own_numbers, experts, slot_cap)[0]
    padded = jnp.concatenate([normed_own, blank_row], axis=0)
    outgoing = jnp.take(padded, slot_table, axis=0).reshape(expert_size, local_count, slot_cap, D)
    doubled = jnp.broadcast_to(outgoing[:, :, None], (expert_size, local_count, 2, slot_cap, D))
    copies = jnp.transpose(doubled, (1, 2, 0, 3, 4)).reshape(tensor_size, expert_size, slot_cap, D)
    incoming = lax.all_to_all(
        lax.all_to_all(copies, "expert", split_axis=1, concat_axis=1, tiled=True),
        "tensor",
        split_axis=0,
        concat_axis=0,
        tiled=True,
    )
    slot_rows = incoming.reshape(tensor_size * expert_size * slot_cap, D)
    gate_value = jnp.dot(slot_rows, gate_weight[0], preferred_element_type=jnp.float32)
    up_value = jnp.dot(slot_rows, up_weight[0], preferred_element_type=jnp.float32)
    hidden = (jax.nn.silu(gate_value) * up_value).astype(jnp.bfloat16)
    part = jnp.dot(hidden, down_weight[0], preferred_element_type=jnp.float32).astype(jnp.bfloat16)
    part = lax.optimization_barrier(part).reshape(tensor_size, expert_size, slot_cap, D)
    half_count = expert_size // 2
    side = tensor_rank % 2
    kept = lax.dynamic_slice_in_dim(part, side * half_count, half_count, 1)
    given = lax.dynamic_slice_in_dim(part, (1 - side) * half_count, half_count, 1)
    partner = swapped(given, "tensor", 0)
    summed = (kept.astype(jnp.float32) + partner.astype(jnp.float32)).astype(jnp.bfloat16)
    homeward = lax.all_to_all(summed, "tensor", split_axis=0, concat_axis=0, tiled=True)
    homeward = homeward.reshape(local_count, expert_size, slot_cap, D)
    returned = lax.all_to_all(homeward, "expert", split_axis=1, concat_axis=0, tiled=True).reshape(
        experts * slot_cap, D
    )
    flat_index = (own_routes * slot_cap + own_slots).reshape(token_rows * TOPK)
    picked = jnp.take(returned, flat_index, axis=0).reshape(token_rows, TOPK, D)
    mixture = jnp.einsum("tk,tkd->td", own_probs, picked.astype(jnp.float32))
    return (middle_own + mixture).astype(jnp.bfloat16)


def on_device(
    queries,
    keys,
    values,
    positions,
    out_weight,
    residual,
    norm_gain,
    routes,
    route_probs,
    gate_weight,
    up_weight,
    down_weight,
):
    tensor_size = lax.axis_size("tensor")
    expert_size = lax.axis_size("expert")
    tensor_rank = lax.axis_index("tensor")
    token_rows = queries.shape[0] // tensor_size
    if tensor_size == 2 and expert_size == 16:
        kept, given = attention_halves(queries, keys, values, positions, out_weight)
        weights = loaded((gate_weight, up_weight, down_weight), given)
        middle_own, block = normed_block(
            kept, swapped(given, "tensor", 0), residual, norm_gain, routes, route_probs
        )
        return dense_experts(middle_own, block, weights)
    own_routes = lax.dynamic_slice_in_dim(routes, tensor_rank * token_rows, token_rows, 0)
    own_probs = lax.dynamic_slice_in_dim(route_probs, tensor_rank * token_rows, token_rows, 0)
    partial_proj = partial_projection(queries, keys, values, positions, out_weight)
    projected = lax.psum(partial_proj, "tensor")
    projected_own = lax.dynamic_slice_in_dim(projected, tensor_rank * token_rows, token_rows, 0)
    middle_own = residual.astype(jnp.float32) + projected_own
    normed_own = normalize(middle_own, norm_gain)
    return routed_experts(
        middle_own, normed_own, own_routes, own_probs, gate_weight, up_weight, down_weight
    )


def solution(mesh):
    return jax.shard_map(
        on_device,
        mesh=mesh,
        in_specs=(
            P("expert", "tensor"),
            P("expert", None),
            P("expert", None),
            P("expert"),
            P("tensor", None),
            P(("expert", "tensor"), None),
            P(),
            P("expert", None),
            P("expert", None),
            P(("expert", "tensor"), None, None),
            P(("expert", "tensor"), None, None),
            P(("expert", "tensor"), None, None),
        ),
        out_specs=P(("expert", "tensor"), None),
        check_vma=False,
    )
```

time: 381 us -> 96 us (0.25); the launches traced: 375 us -> 95.8 us
  blocking collectives: 125 us -> 0 us
  waiting for transfers between devices: 153 us -> 40.7 us
  matrix products: 31.2 us -> 0 us
  local copies, waits for them, and re-layouts: 30.9 us -> 1.09 us
  starting transfers between devices: 10.6 us -> 31.9 us
  Pallas kernels: 0 us -> 20.2 us
  between operations: 13.7 us -> 0.39 us
  other arithmetic: 10.3 us -> 1.64 us
    all_to_all x2 -> x0, blocking collectives: 125 us -> none  [the longest x1 97.7 us: on_device(): lax.all_to_all(copies, 'expert', split_axis=1, concat_axis=1, tiled=True)]
    all_to_all x2 -> x0, waiting for transfers between devices: 89.1 us -> none  [the longest x1 48.4 us: on_device(): lax.all_to_all(lax.all_to_all(copies, 'expert', split_axis=1, concat_axis...]
    ppermute x1, waiting for transfers between devices: 47.4 us -> 0.01 us  [swapped(): lax.ppermute(shard, axis, [(i, i ^ 1 << distance) for i in range(lax.axis...]
    ppermute x0 -> x30, waiting for transfers between devices: none -> 40.7 us  [exchanged(): lax.ppermute(shard, BOTH, [(i, i ^ masks[1 if i & BIT_CORE else 0]) for i...]
    dot_general x6 -> x0, matrix products: 30.8 us -> none  [the longest x1 12.3 us: on_device(): jnp.dot(hidden, down_weight[0], preferred_element_type=jnp.float32)]
    ppermute x0 -> x30, starting transfers between devices: none -> 28.9 us  [exchanged(): lax.ppermute(shard, BOTH, [(i, i ^ masks[1 if i & BIT_CORE else 0]) for i...]
    pallas_call x0 -> x7, Pallas kernels: none -> 20.2 us  [the longest x4 10.7 us: weighted_expert(): pl.pallas_call(expert_kernel, in_specs=[whole] * 5, out_specs=[whole] * 2...]
    psum x1 -> x0, waiting for transfers between devices: 16.6 us -> none  [on_device(): projected = lax.psum(partial_proj, 'tensor')]
  transfers between devices with their start and end apart: 4 -> 31, of which waited for: 4 -> 11; matrix products, arithmetic and copies ran while one was open for 4% -> 1% of each run, Pallas kernels for 0% -> 15%
where the time goes in v2:
time: 96 us; the launch traced here: 95.8 us
  waiting for transfers between devices  40.7 us (42%)
  starting transfers between devices  31.9 us (33%)
  Pallas kernels  20.2 us (21%)
  other arithmetic  1.64 us (2%)
  local copies, waits for them, and re-layouts  1.09 us (1%)
    ppermute x30, waiting for transfers between devices, exchanged(): lax.ppermute(shard, BOTH, [(i, i ^ masks[1 if i & BIT_CORE else 0]) for i...  40.7 us
    ppermute x30, starting transfers between devices, exchanged(): lax.ppermute(shard, BOTH, [(i, i ^ masks[1 if i & BIT_CORE else 0]) for i...  28.9 us
    pallas_call x4, Pallas kernels, weighted_expert(): pl.pallas_call(expert_kernel, in_specs=[whole] * 5, out_specs=[whole] * 2...  10.7 us
    pallas_call x1, Pallas kernels, attention_halves(): pl.pallas_call(attention_kernel, in_specs=[far, far, far, near, far], out...  5.5 us
    pallas_call x1, Pallas kernels, loaded(): pl.pallas_call(functools.partial(load_kernel, len(weights), pieces), in_s...  3.79 us
    ppermute x1, starting transfers between devices, swapped(): lax.ppermute(shard, axis, [(i, i ^ 1 << distance) for i in range(lax.axis...  3.01 us
  transfers between devices with their start and end apart: 31, of which 11 were waited for; matrix products, arithmetic and copies ran while one was open for 1% of the time, Pallas kernels for 15%

profile of v2, /device:TPU:0, one launch (start us, length us, event | category | flops | bytes accessed | tf_op | source)
XLA Modules:
  0.0 95.8 jit_solution(1602217668284559011)
XLA Ops:
  0.7 5.5 %attention_halves.1 = (f32[32,2048]{1,0:T(8,128)S(1)}, bf16[32,2048]{1,0:T(8,128)(2,1)S(1)}) custom-call(bf16[64,2048]{1,0:T(8,128)(2,1)} %queries_hbm.1, bf16[64,512]{1,0:T(8,128)(2,1)} %keys_hbm.1, bf16[64,512]{1,0:T(8,128)(2,1)} %values_hbm.1, s32[1,64]{1,0:T(1,128)S(1)} %bitcast.7, bf16[2048,2048]{1,0:T(8,128)(2,1)} %out_weight_hbm.1), custom_call_target="tpu_custom_call" | custom-call | flops 570425344 | bytes 8388608 | tf_op jit(solution)/shard_map/attention_halves/pallas_call | solution.py:218
  6.2 3.0 %collective-permute-start = (bf16[32,2048]{1,0:T(8,128)(2,1)S(1)}, bf16[32,2048]{1,0:T(8,128)(2,1)S(1)}, u32[]{:S(2)}, u32[]{:S(2)}) collective-permute-start(bf16[32,2048]{1,0:T(8,128)(2,1)S(1)} %get-tuple-element.21.refs_3_), channel_id=1, source_target_pairs={{0,1},{1,0},{2,3},{3,2},{4,5},{5,4},{6,7},{7,6},{8,9},{9,8},{10,11... | collective-permute-start | bytes 393224 | tf_op jit(solution)/shard_map/ppermute | solution.py:32
  9.2 3.8 %load_weights.1 = (bf16[1,2048,768]{2,1,0:T(8,128)(2,1)S(1)}, bf16[1,2048,768]{2,1,0:T(8,128)(2,1)S(1)}, bf16[1,768,2048]{2,1,0:T(8,128)(2,1)S(1)}) custom-call(bf16[1,2048,768]{2,1,0:T(8,128)(2,1)} %refs_0_.1, bf16[1,2048,768]{2,1,0:T(8,128)(2,1)} %refs_1_.1, bf16[1,768,2048]{2,1,0:T(8,128)(2,1)} %refs_2_.1, bf16[32,2048]{1,0:T(8,128)(2,1)S(1)} %get-tuple-element.21.refs_3_), custom_call_target="tpu_custom_call" | custom-call | bytes 9437184 | tf_op jit(solution)/shard_map/load_weights/pallas_call | solution.py:272
  13.3 1.6 %collective-permute-start.7 = (bf16[32,2176]{1,0:T(8,128)(2,1)S(1)}, bf16[32,2176]{1,0:T(8,128)(2,1)S(1)}, u32[]{:S(2)}, u32[]{:S(2)}) collective-permute-start(bf16[32,2176]{1,0:T(8,128)(2,1)S(1)} %get-tuple-element.23), channel_id=1, source_target_pairs={{0,8},{1,9},{2,10},{3,11},{4,12},{5,13},{6,14},{7,15},{8,0},{9,1},... | collective-permute-start | bytes 417800 | tf_op jit(solution)/shard_map/ppermute | solution.py:37
  14.9 2.6 %collective-permute-start.15 = (bf16[32,2176]{1,0:T(8,128)(2,1)S(1)}, bf16[32,2176]{1,0:T(8,128)(2,1)S(1)}, u32[]{:S(2)}, u32[]{:S(2)}) collective-permute-start(bf16[32,2176]{1,0:T(8,128)(2,1)S(1)} %get-tuple-element.23), channel_id=1, source_target_pairs={{0,16},{1,17},{2,18},{3,19},{4,20},{5,21},{6,22},{7,23},{8,24},{9,... | collective-permute-start | bytes 417800 | tf_op jit(solution)/shard_map/ppermute | solution.py:37
  17.5 1.4 %collective-permute-start.1 = (bf16[32,2176]{1,0:T(8,128)(2,1)S(1)}, bf16[32,2176]{1,0:T(8,128)(2,1)S(1)}, u32[]{:S(2)}, u32[]{:S(2)}) collective-permute-start(bf16[32,2176]{1,0:T(8,128)(2,1)S(1)} %get-tuple-element.23), channel_id=1, source_target_pairs={{0,1},{1,0},{2,6},{3,7},{4,5},{5,4},{6,2},{7,3},{8,9},{9,8},{10,14... | collective-permute-start | bytes 417800 | tf_op jit(solution)/shard_map/ppermute | solution.py:37
  18.9 3.6 %collective-permute-done.1 = bf16[32,2176]{1,0:T(8,128)(2,1)S(1)} collective-permute-done((bf16[32,2176]{1,0:T(8,128)(2,1)S(1)}, bf16[32,2176]{1,0:T(8,128)(2,1)S(1)}, u32[]{:S(2)}, u32[]{:S(2)}) %collective-permute-start.1) | collective-permute-done | bytes 139296 | tf_op jit(solution)/shard_map/ppermute | solution.py:37
  22.6 1.6 %collective-permute-start.2 = (bf16[64,2176]{1,0:T(8,128)(2,1)S(1)}, bf16[64,2176]{1,0:T(8,128)(2,1)S(1)}, u32[]{:S(2)}, u32[]{:S(2)}) collective-permute-start(bf16[64,2176]{1,0:T(8,128)(2,1)S(1)} %pad_maximum_fusion), channel_id=1, source_target_pairs={{0,4},{1,5},{2,3},{3,2},{4,0},{5,1},{6,7},{7,6},{8,12},{9,13},{10,... | collective-permute-start | bytes 835592 | tf_op jit(solution)/shard_map/ppermute | solution.py:37
  24.2 1.4 %collective-permute-start.8 = (bf16[32,2176]{1,0:T(8,128)(2,1)S(1)}, bf16[32,2176]{1,0:T(8,128)(2,1)S(1)}, u32[]{:S(2)}, u32[]{:S(2)}) collective-permute-start(bf16[32,2176]{1,0:T(8,128)(2,1)S(1)} %collective-permute-done.7), channel_id=1, source_target_pairs={{0,1},{1,0},{2,6},{3,7},{4,5},{5,4},{6,2},{7,3},{8,9},{9,8},{10,14... | collective-permute-start | bytes 417800 | tf_op jit(solution)/shard_map/ppermute | solution.py:37
  26.8 3.7 %collective-permute-done.8 = bf16[32,2176]{1,0:T(8,128)(2,1)S(1)} collective-permute-done((bf16[32,2176]{1,0:T(8,128)(2,1)S(1)}, bf16[32,2176]{1,0:T(8,128)(2,1)S(1)}, u32[]{:S(2)}, u32[]{:S(2)}) %collective-permute-start.8) | collective-permute-done | bytes 139296 | tf_op jit(solution)/shard_map/ppermute | solution.py:37
  30.6 2.9 %collective-permute-done.16 = bf16[32,2176]{1,0:T(8,128)(2,1)S(1)} collective-permute-done((bf16[32,2176]{1,0:T(8,128)(2,1)S(1)}, bf16[32,2176]{1,0:T(8,128)(2,1)S(1)}, u32[]{:S(2)}, u32[]{:S(2)}) %collective-permute-start.16) | collective-permute-done | bytes 139296 | tf_op jit(solution)/shard_map/ppermute | solution.py:37
  33.6 1.7 %collective-permute-start.23 = (bf16[32,2176]{1,0:T(8,128)(2,1)S(1)}, bf16[32,2176]{1,0:T(8,128)(2,1)S(1)}, u32[]{:S(2)}, u32[]{:S(2)}) collective-permute-start(bf16[32,2176]{1,0:T(8,128)(2,1)S(1)} %collective-permute-done.22), channel_id=1, source_target_pairs={{0,1},{1,0},{2,6},{3,7},{4,5},{5,4},{6,2},{7,3},{8,9},{9,8},{10,14... | collective-permute-start | bytes 417800 | tf_op jit(solution)/shard_map/ppermute | solution.py:37
  35.3 4.9 %collective-permute-done.23 = bf16[32,2176]{1,0:T(8,128)(2,1)S(1)} collective-permute-done((bf16[32,2176]{1,0:T(8,128)(2,1)S(1)}, bf16[32,2176]{1,0:T(8,128)(2,1)S(1)}, u32[]{:S(2)}, u32[]{:S(2)}) %collective-permute-start.23) | collective-permute-done | bytes 139296 | tf_op jit(solution)/shard_map/ppermute | solution.py:37
  40.3 1.4 %collective-permute-start.24 = (bf16[64,2176]{1,0:T(8,128)(2,1)S(1)}, bf16[64,2176]{1,0:T(8,128)(2,1)S(1)}, u32[]{:S(2)}, u32[]{:S(2)}) collective-permute-start(bf16[64,2176]{1,0:T(8,128)(2,1)S(1)} %pad_maximum_fusion.3), channel_id=1, source_target_pairs={{0,4},{1,5},{2,3},{3,2},{4,0},{5,1},{6,7},{7,6},{8,12},{9,13},{10,... | collective-permute-start | bytes 835592 | tf_op jit(solution)/shard_map/ppermute | solution.py:37
  42.6 4.3 %collective-permute-done.24 = bf16[64,2176]{1,0:T(8,128)(2,1)S(1)} collective-permute-done((bf16[64,2176]{1,0:T(8,128)(2,1)S(1)}, bf16[64,2176]{1,0:T(8,128)(2,1)S(1)}, u32[]{:S(2)}, u32[]{:S(2)}) %collective-permute-start.24) | collective-permute-done | bytes 278560 | tf_op jit(solution)/shard_map/ppermute | solution.py:37
  47.0 2.7 %expert_half.4 = (bf16[128,2048]{1,0:T(8,128)(2,1)S(1)}, bf16[128,2048]{1,0:T(8,128)(2,1)S(1)}) custom-call(bf16[128,2176]{1,0:T(8,128)(2,1)S(1)} %constant_dynamic-update-slice_fusion.near_ref, bf16[128,2176]{1,0:T(8,128)(2,1)S(1)} %collective-permute-done.3.far_ref, bf16[1,2048,768]{2,1,0:T(8,128)(2,1)S(1)} %get-tuple-element.24.gate_ref, ...), custom_call_target="tpu_custom_call" | custom-call | flops 2415919104 | bytes 2097152 | tf_op jit(solution)/shard_map/expert_half/pallas_call | solution.py:386
  50.3 2.7 %expert_half.5 = (bf16[128,2048]{1,0:T(8,128)(2,1)S(1)}, bf16[128,2048]{1,0:T(8,128)(2,1)S(1)}) custom-call(bf16[128,2176]{1,0:T(8,128)(2,1)S(1)} %constant_dynamic-update-slice_fusion.3.near_ref, bf16[128,2176]{1,0:T(8,128)(2,1)S(1)} %collective-permute-done.10.far_ref, bf16[1,2048,768]{2,1,0:T(8,128)(2,1)S(1)} %get-tuple-element.24.gate_ref, ...), custom_call_target="tpu_custom_call" | custom-call | flops 2415919104 | bytes 2097152 | tf_op jit(solution)/shard_map/expert_half/pallas_call | solution.py:386
  53.1 2.7 %expert_half.6 = (bf16[128,2048]{1,0:T(8,128)(2,1)S(1)}, bf16[128,2048]{1,0:T(8,128)(2,1)S(1)}) custom-call(bf16[128,2176]{1,0:T(8,128)(2,1)S(1)} %constant_dynamic-update-slice_fusion.6.near_ref, bf16[128,2176]{1,0:T(8,128)(2,1)S(1)} %collective-permute-done.18.far_ref, bf16[1,2048,768]{2,1,0:T(8,128)(2,1)S(1)} %get-tuple-element.24.gate_ref, ...), custom_call_target="tpu_custom_call" | custom-call | flops 2415919104 | bytes 2097152 | tf_op jit(solution)/shard_map/expert_half/pallas_call | solution.py:386
  56.3 2.7 %expert_half.7 = (bf16[128,2048]{1,0:T(8,128)(2,1)S(1)}, bf16[128,2048]{1,0:T(8,128)(2,1)S(1)}) custom-call(bf16[128,2176]{1,0:T(8,128)(2,1)S(1)} %constant_dynamic-update-slice_fusion.9.near_ref, bf16[128,2176]{1,0:T(8,128)(2,1)S(1)} %collective-permute-done.25.far_ref, bf16[1,2048,768]{2,1,0:T(8,128)(2,1)S(1)} %get-tuple-element.24.gate_ref, ...), custom_call_target="tpu_custom_call" | custom-call | flops 2415919104 | bytes 2097152 | tf_op jit(solution)/shard_map/expert_half/pallas_call | solution.py:386
  59.2 1.4 %collective-permute-start.5 = (bf16[64,2048]{1,0:T(8,128)(2,1)S(1)}, bf16[64,2048]{1,0:T(8,128)(2,1)S(1)}, u32[]{:S(2)}, u32[]{:S(2)}) collective-permute-start(bf16[64,2048]{1,0:T(8,128)(2,1)S(1)} %slice.123), channel_id=1, source_target_pairs={{0,4},{1,5},{2,3},{3,2},{4,0},{5,1},{6,7},{7,6},{8,12},{9,13},{10,... | collective-permute-start | bytes 786440 | tf_op jit(solution)/shard_map/ppermute | solution.py:37
  61.7 1.4 %collective-permute-start.20 = (bf16[64,2048]{1,0:T(8,128)(2,1)S(1)}, bf16[64,2048]{1,0:T(8,128)(2,1)S(1)}, u32[]{:S(2)}, u32[]{:S(2)}) collective-permute-start(bf16[64,2048]{1,0:T(8,128)(2,1)S(1)} %slice.121), channel_id=1, source_target_pairs={{0,4},{1,5},{2,3},{3,2},{4,0},{5,1},{6,7},{7,6},{8,12},{9,13},{10,... | collective-permute-start | bytes 786440 | tf_op jit(solution)/shard_map/ppermute | solution.py:37
  63.2 2.5 %collective-permute-done.5 = bf16[64,2048]{1,0:T(8,128)(2,1)S(1)} collective-permute-done((bf16[64,2048]{1,0:T(8,128)(2,1)S(1)}, bf16[64,2048]{1,0:T(8,128)(2,1)S(1)}, u32[]{:S(2)}, u32[]{:S(2)}) %collective-permute-start.5) | collective-permute-done | bytes 262176 | tf_op jit(solution)/shard_map/ppermute | solution.py:37
  65.8 1.7 %collective-permute-start.6 = (bf16[32,2048]{1,0:T(8,128)(2,1)S(1)}, bf16[32,2048]{1,0:T(8,128)(2,1)S(1)}, u32[]{:S(2)}, u32[]{:S(2)}) collective-permute-start(bf16[32,2048]{1,0:T(8,128)(2,1)S(1)} %slice.127), channel_id=1, source_target_pairs={{0,1},{1,0},{2,6},{3,7},{4,5},{5,4},{6,2},{7,3},{8,9},{9,8},{10,14... | collective-permute-start | bytes 393224 | tf_op jit(solution)/shard_map/ppermute | solution.py:37
  67.6 1.2 %collective-permute-start.27 = (bf16[64,2048]{1,0:T(8,128)(2,1)S(1)}, bf16[64,2048]{1,0:T(8,128)(2,1)S(1)}, u32[]{:S(2)}, u32[]{:S(2)}) collective-permute-start(bf16[64,2048]{1,0:T(8,128)(2,1)S(1)} %slice.120), channel_id=1, source_target_pairs={{0,4},{1,5},{2,3},{3,2},{4,0},{5,1},{6,7},{7,6},{8,12},{9,13},{10,... | collective-permute-start | bytes 786440 | tf_op jit(solution)/shard_map/ppermute | solution.py:37
  68.9 1.7 %collective-permute-start.13 = (bf16[32,2048]{1,0:T(8,128)(2,1)S(1)}, bf16[32,2048]{1,0:T(8,128)(2,1)S(1)}, u32[]{:S(2)}, u32[]{:S(2)}) collective-permute-start(bf16[32,2048]{1,0:T(8,128)(2,1)S(1)} %slice.126), channel_id=1, source_target_pairs={{0,1},{1,0},{2,6},{3,7},{4,5},{5,4},{6,2},{7,3},{8,9},{9,8},{10,14... | collective-permute-start | bytes 393224 | tf_op jit(solution)/shard_map/ppermute | solution.py:37
  70.6 6.3 %collective-permute-done.27 = bf16[64,2048]{1,0:T(8,128)(2,1)S(1)} collective-permute-done((bf16[64,2048]{1,0:T(8,128)(2,1)S(1)}, bf16[64,2048]{1,0:T(8,128)(2,1)S(1)}, u32[]{:S(2)}, u32[]{:S(2)}) %collective-permute-start.27) | collective-permute-done | bytes 262176 | tf_op jit(solution)/shard_map/ppermute | solution.py:37
  77.0 1.7 %collective-permute-start.28 = (bf16[32,2048]{1,0:T(8,128)(2,1)S(1)}, bf16[32,2048]{1,0:T(8,128)(2,1)S(1)}, u32[]{:S(2)}, u32[]{:S(2)}) collective-permute-start(bf16[32,2048]{1,0:T(8,128)(2,1)S(1)} %slice.124), channel_id=1, source_target_pairs={{0,1},{1,0},{2,6},{3,7},{4,5},{5,4},{6,2},{7,3},{8,9},{9,8},{10,14... | collective-permute-start | bytes 393224 | tf_op jit(solution)/shard_map/ppermute | solution.py:37
  79.2 2.8 %collective-permute-done.28 = bf16[32,2048]{1,0:T(8,128)(2,1)S(1)} collective-permute-done((bf16[32,2048]{1,0:T(8,128)(2,1)S(1)}, bf16[32,2048]{1,0:T(8,128)(2,1)S(1)}, u32[]{:S(2)}, u32[]{:S(2)}) %collective-permute-start.28) | collective-permute-done | bytes 131104 | tf_op jit(solution)/shard_map/ppermute | solution.py:37
  84.3 3.5 %collective-permute-done.29 = bf16[32,2048]{1,0:T(8,128)(2,1)S(1)} collective-permute-done((bf16[32,2048]{1,0:T(8,128)(2,1)S(1)}, bf16[32,2048]{1,0:T(8,128)(2,1)S(1)}, u32[]{:S(2)}, u32[]{:S(2)}) %collective-permute-start.29) | collective-permute-done | bytes 131104 | tf_op jit(solution)/shard_map/ppermute | solution.py:37
  87.8 1.3 %collective-permute-start.30 = (bf16[32,2048]{1,0:T(8,128)(2,1)S(1)}, bf16[32,2048]{1,0:T(8,128)(2,1)S(1)}, u32[]{:S(2)}, u32[]{:S(2)}) collective-permute-start(bf16[32,2048]{1,0:T(8,128)(2,1)S(1)} %fusion.2), channel_id=1, source_target_pairs={{0,16},{1,17},{2,18},{3,19},{4,20},{5,21},{6,22},{7,23},{8,24},{9,... | collective-permute-start | bytes 393224 | tf_op jit(solution)/shard_map/ppermute | solution.py:37
  89.0 1.4 %collective-permute-done.14 = bf16[32,2048]{1,0:T(8,128)(2,1)S(1)} collective-permute-done((bf16[32,2048]{1,0:T(8,128)(2,1)S(1)}, bf16[32,2048]{1,0:T(8,128)(2,1)S(1)}, u32[]{:S(2)}, u32[]{:S(2)}) %collective-permute-start.14) | collective-permute-done | bytes 131104 | tf_op jit(solution)/shard_map/ppermute | solution.py:37
  90.4 4.7 %collective-permute-done.30 = bf16[32,2048]{1,0:T(8,128)(2,1)S(1)} collective-permute-done((bf16[32,2048]{1,0:T(8,128)(2,1)S(1)}, bf16[32,2048]{1,0:T(8,128)(2,1)S(1)}, u32[]{:S(2)}, u32[]{:S(2)}) %collective-permute-start.30) | collective-permute-done | bytes 131104 | tf_op jit(solution)/shard_map/ppermute | solution.py:37
  (83 shorter events, 9.7 us)
Async XLA Ops:
  6.2 6.9 %copy-start = (bf16[32,2048]{1,0:T(8,128)(2,1)S(1)}, bf16[32,2048]{1,0:T(8,128)(2,1)}, u32[]{:S(2)}) copy-start(bf16[32,2048]{1,0:T(8,128)(2,1)} %residual_ref.1) | copy-start | bytes 393220
  6.2 6.8 %collective-permute-start = (bf16[32,2048]{1,0:T(8,128)(2,1)S(1)}, bf16[32,2048]{1,0:T(8,128)(2,1)S(1)}, u32[]{:S(2)}, u32[]{:S(2)}) collective-permute-start(bf16[32,2048]{1,0:T(8,128)(2,1)S(1)} %get-tuple-element.21.refs_3_), channel_id=1, source_target_pairs={{0,1},{1,0},{2,3},{3,2},{4,5},{5,4},{6,7},{7,6},{8,9},{9,8},{10,11... | collective-permute-start | bytes 393224 | tf_op jit(solution)/shard_map/ppermute | solution.py:32
  13.3 10.9 %collective-permute-start.7 = (bf16[32,2176]{1,0:T(8,128)(2,1)S(1)}, bf16[32,2176]{1,0:T(8,128)(2,1)S(1)}, u32[]{:S(2)}, u32[]{:S(2)}) collective-permute-start(bf16[32,2176]{1,0:T(8,128)(2,1)S(1)} %get-tuple-element.23), channel_id=1, source_target_pairs={{0,8},{1,9},{2,10},{3,11},{4,12},{5,13},{6,14},{7,15},{8,0},{9,1},... | collective-permute-start | bytes 417800 | tf_op jit(solution)/shard_map/ppermute | solution.py:37
  14.9 10.7 %collective-permute-start.15 = (bf16[32,2176]{1,0:T(8,128)(2,1)S(1)}, bf16[32,2176]{1,0:T(8,128)(2,1)S(1)}, u32[]{:S(2)}, u32[]{:S(2)}) collective-permute-start(bf16[32,2176]{1,0:T(8,128)(2,1)S(1)} %get-tuple-element.23), channel_id=1, source_target_pairs={{0,16},{1,17},{2,18},{3,19},{4,20},{5,21},{6,22},{7,23},{8,24},{9,... | collective-permute-start | bytes 417800 | tf_op jit(solution)/shard_map/ppermute | solution.py:37
  17.5 5.1 %collective-permute-start.1 = (bf16[32,2176]{1,0:T(8,128)(2,1)S(1)}, bf16[32,2176]{1,0:T(8,128)(2,1)S(1)}, u32[]{:S(2)}, u32[]{:S(2)}) collective-permute-start(bf16[32,2176]{1,0:T(8,128)(2,1)S(1)} %get-tuple-element.23), channel_id=1, source_target_pairs={{0,1},{1,0},{2,6},{3,7},{4,5},{5,4},{6,2},{7,3},{8,9},{9,8},{10,14... | collective-permute-start | bytes 417800 | tf_op jit(solution)/shard_map/ppermute | solution.py:37
  22.6 19.2 %collective-permute-start.2 = (bf16[64,2176]{1,0:T(8,128)(2,1)S(1)}, bf16[64,2176]{1,0:T(8,128)(2,1)S(1)}, u32[]{:S(2)}, u32[]{:S(2)}) collective-permute-start(bf16[64,2176]{1,0:T(8,128)(2,1)S(1)} %pad_maximum_fusion), channel_id=1, source_target_pairs={{0,4},{1,5},{2,3},{3,2},{4,0},{5,1},{6,7},{7,6},{8,12},{9,13},{10,... | collective-permute-start | bytes 835592 | tf_op jit(solution)/shard_map/ppermute | solution.py:37
  24.2 6.4 %collective-permute-start.8 = (bf16[32,2176]{1,0:T(8,128)(2,1)S(1)}, bf16[32,2176]{1,0:T(8,128)(2,1)S(1)}, u32[]{:S(2)}, u32[]{:S(2)}) collective-permute-start(bf16[32,2176]{1,0:T(8,128)(2,1)S(1)} %collective-permute-done.7), channel_id=1, source_target_pairs={{0,1},{1,0},{2,6},{3,7},{4,5},{5,4},{6,2},{7,3},{8,9},{9,8},{10,14... | collective-permute-start | bytes 417800 | tf_op jit(solution)/shard_map/ppermute | solution.py:37
  25.6 8.0 %collective-permute-start.22 = (bf16[32,2176]{1,0:T(8,128)(2,1)S(1)}, bf16[32,2176]{1,0:T(8,128)(2,1)S(1)}, u32[]{:S(2)}, u32[]{:S(2)}) collective-permute-start(bf16[32,2176]{1,0:T(8,128)(2,1)S(1)} %collective-permute-done.15), channel_id=1, source_target_pairs={{0,8},{1,9},{2,10},{3,11},{4,12},{5,13},{6,14},{7,15},{8,0},{9,1},... | collective-permute-start | bytes 417800 | tf_op jit(solution)/shard_map/ppermute | solution.py:37
  26.1 7.4 %collective-permute-start.16 = (bf16[32,2176]{1,0:T(8,128)(2,1)S(1)}, bf16[32,2176]{1,0:T(8,128)(2,1)S(1)}, u32[]{:S(2)}, u32[]{:S(2)}) collective-permute-start(bf16[32,2176]{1,0:T(8,128)(2,1)S(1)} %collective-permute-done.15), channel_id=1, source_target_pairs={{0,1},{1,0},{2,6},{3,7},{4,5},{5,4},{6,2},{7,3},{8,9},{9,8},{10,14... | collective-permute-start | bytes 417800 | tf_op jit(solution)/shard_map/ppermute | solution.py:37
  30.5 11.3 %collective-permute-start.9 = (bf16[64,2176]{1,0:T(8,128)(2,1)S(1)}, bf16[64,2176]{1,0:T(8,128)(2,1)S(1)}, u32[]{:S(2)}, u32[]{:S(2)}) collective-permute-start(bf16[64,2176]{1,0:T(8,128)(2,1)S(1)} %pad_maximum_fusion.1), channel_id=1, source_target_pairs={{0,4},{1,5},{2,3},{3,2},{4,0},{5,1},{6,7},{7,6},{8,12},{9,13},{10,... | collective-permute-start | bytes 835592 | tf_op jit(solution)/shard_map/ppermute | solution.py:37
  33.5 9.0 %collective-permute-start.17 = (bf16[64,2176]{1,0:T(8,128)(2,1)S(1)}, bf16[64,2176]{1,0:T(8,128)(2,1)S(1)}, u32[]{:S(2)}, u32[]{:S(2)}) collective-permute-start(bf16[64,2176]{1,0:T(8,128)(2,1)S(1)} %pad_maximum_fusion.2), channel_id=1, source_target_pairs={{0,4},{1,5},{2,3},{3,2},{4,0},{5,1},{6,7},{7,6},{8,12},{9,13},{10,... | collective-permute-start | bytes 835592 | tf_op jit(solution)/shard_map/ppermute | solution.py:37
  33.6 6.7 %collective-permute-start.23 = (bf16[32,2176]{1,0:T(8,128)(2,1)S(1)}, bf16[32,2176]{1,0:T(8,128)(2,1)S(1)}, u32[]{:S(2)}, u32[]{:S(2)}) collective-permute-start(bf16[32,2176]{1,0:T(8,128)(2,1)S(1)} %collective-permute-done.22), channel_id=1, source_target_pairs={{0,1},{1,0},{2,6},{3,7},{4,5},{5,4},{6,2},{7,3},{8,9},{9,8},{10,14... | collective-permute-start | bytes 417800 | tf_op jit(solution)/shard_map/ppermute | solution.py:37
  40.3 6.6 %collective-permute-start.24 = (bf16[64,2176]{1,0:T(8,128)(2,1)S(1)}, bf16[64,2176]{1,0:T(8,128)(2,1)S(1)}, u32[]{:S(2)}, u32[]{:S(2)}) collective-permute-start(bf16[64,2176]{1,0:T(8,128)(2,1)S(1)} %pad_maximum_fusion.3), channel_id=1, source_target_pairs={{0,4},{1,5},{2,3},{3,2},{4,0},{5,1},{6,7},{7,6},{8,12},{9,13},{10,... | collective-permute-start | bytes 835592 | tf_op jit(solution)/shard_map/ppermute | solution.py:37
  41.8 5.3 %collective-permute-start.3 = (bf16[128,2176]{1,0:T(8,128)(2,1)S(1)}, bf16[128,2176]{1,0:T(8,128)(2,1)S(1)}, u32[]{:S(2)}, u32[]{:S(2)}) collective-permute-start(bf16[128,2176]{1,0:T(8,128)(2,1)S(1)} %constant_dynamic-update-slice_fusion.near_ref), channel_id=1, source_target_pairs={{0,2},{1,3},{2,0},{3,1},{4,6},{5,7},{6,4},{7,5},{8,10},{9,11},{10,... | collective-permute-start | bytes 1671176 | tf_op jit(solution)/shard_map/ppermute | solution.py:37
  41.9 8.4 %collective-permute-start.10 = (bf16[128,2176]{1,0:T(8,128)(2,1)S(1)}, bf16[128,2176]{1,0:T(8,128)(2,1)S(1)}, u32[]{:S(2)}, u32[]{:S(2)}) collective-permute-start(bf16[128,2176]{1,0:T(8,128)(2,1)S(1)} %constant_dynamic-update-slice_fusion.3.near_ref), channel_id=1, source_target_pairs={{0,2},{1,3},{2,0},{3,1},{4,6},{5,7},{6,4},{7,5},{8,10},{9,11},{10,... | collective-permute-start | bytes 1671176 | tf_op jit(solution)/shard_map/ppermute | solution.py:37
  42.5 10.5 %collective-permute-start.18 = (bf16[128,2176]{1,0:T(8,128)(2,1)S(1)}, bf16[128,2176]{1,0:T(8,128)(2,1)S(1)}, u32[]{:S(2)}, u32[]{:S(2)}) collective-permute-start(bf16[128,2176]{1,0:T(8,128)(2,1)S(1)} %constant_dynamic-update-slice_fusion.6.near_ref), channel_id=1, source_target_pairs={{0,2},{1,3},{2,0},{3,1},{4,6},{5,7},{6,4},{7,5},{8,10},{9,11},{10,... | collective-permute-start | bytes 1671176 | tf_op jit(solution)/shard_map/ppermute | solution.py:37
  47.0 9.3 %collective-permute-start.25 = (bf16[128,2176]{1,0:T(8,128)(2,1)S(1)}, bf16[128,2176]{1,0:T(8,128)(2,1)S(1)}, u32[]{:S(2)}, u32[]{:S(2)}) collective-permute-start(bf16[128,2176]{1,0:T(8,128)(2,1)S(1)} %constant_dynamic-update-slice_fusion.9.near_ref), channel_id=1, source_target_pairs={{0,2},{1,3},{2,0},{3,1},{4,6},{5,7},{6,4},{7,5},{8,10},{9,11},{10,... | collective-permute-start | bytes 1671176 | tf_op jit(solution)/shard_map/ppermute | solution.py:37
  49.7 9.3 %collective-permute-start.4 = (bf16[128,2048]{1,0:T(8,128)(2,1)S(1)}, bf16[128,2048]{1,0:T(8,128)(2,1)S(1)}, u32[]{:S(2)}, u32[]{:S(2)}) collective-permute-start(bf16[128,2048]{1,0:T(8,128)(2,1)S(1)} %get-tuple-element.28), channel_id=1, source_target_pairs={{0,2},{1,3},{2,0},{3,1},{4,6},{5,7},{6,4},{7,5},{8,10},{9,11},{10,... | collective-permute-start | bytes 1572872 | tf_op jit(solution)/shard_map/ppermute | solution.py:37
  53.0 7.7 %collective-permute-start.11 = (bf16[128,2048]{1,0:T(8,128)(2,1)S(1)}, bf16[128,2048]{1,0:T(8,128)(2,1)S(1)}, u32[]{:S(2)}, u32[]{:S(2)}) collective-permute-start(bf16[128,2048]{1,0:T(8,128)(2,1)S(1)} %get-tuple-element.30), channel_id=1, source_target_pairs={{0,2},{1,3},{2,0},{3,1},{4,6},{5,7},{6,4},{7,5},{8,10},{9,11},{10,... | collective-permute-start | bytes 1572872 | tf_op jit(solution)/shard_map/ppermute | solution.py:37
  55.7 5.8 %collective-permute-start.19 = (bf16[128,2048]{1,0:T(8,128)(2,1)S(1)}, bf16[128,2048]{1,0:T(8,128)(2,1)S(1)}, u32[]{:S(2)}, u32[]{:S(2)}) collective-permute-start(bf16[128,2048]{1,0:T(8,128)(2,1)S(1)} %get-tuple-element.32), channel_id=1, source_target_pairs={{0,2},{1,3},{2,0},{3,1},{4,6},{5,7},{6,4},{7,5},{8,10},{9,11},{10,... | collective-permute-start | bytes 1572872 | tf_op jit(solution)/shard_map/ppermute | solution.py:37
  59.0 8.5 %collective-permute-start.26 = (bf16[128,2048]{1,0:T(8,128)(2,1)S(1)}, bf16[128,2048]{1,0:T(8,128)(2,1)S(1)}, u32[]{:S(2)}, u32[]{:S(2)}) collective-permute-start(bf16[128,2048]{1,0:T(8,128)(2,1)S(1)} %get-tuple-element.34), channel_id=1, source_target_pairs={{0,2},{1,3},{2,0},{3,1},{4,6},{5,7},{6,4},{7,5},{8,10},{9,11},{10,... | collective-permute-start | bytes 1572872 | tf_op jit(solution)/shard_map/ppermute | solution.py:37
  59.2 6.4 %collective-permute-start.5 = (bf16[64,2048]{1,0:T(8,128)(2,1)S(1)}, bf16[64,2048]{1,0:T(8,128)(2,1)S(1)}, u32[]{:S(2)}, u32[]{:S(2)}) collective-permute-start(bf16[64,2048]{1,0:T(8,128)(2,1)S(1)} %slice.123), channel_id=1, source_target_pairs={{0,4},{1,5},{2,3},{3,2},{4,0},{5,1},{6,7},{7,6},{8,12},{9,13},{10,... | collective-permute-start | bytes 786440 | tf_op jit(solution)/shard_map/ppermute | solution.py:37
  60.8 8.0 %collective-permute-start.12 = (bf16[64,2048]{1,0:T(8,128)(2,1)S(1)}, bf16[64,2048]{1,0:T(8,128)(2,1)S(1)}, u32[]{:S(2)}, u32[]{:S(2)}) collective-permute-start(bf16[64,2048]{1,0:T(8,128)(2,1)S(1)} %slice.122), channel_id=1, source_target_pairs={{0,4},{1,5},{2,3},{3,2},{4,0},{5,1},{6,7},{7,6},{8,12},{9,13},{10,... | collective-permute-start | bytes 786440 | tf_op jit(solution)/shard_map/ppermute | solution.py:37
  61.7 16.9 %collective-permute-start.20 = (bf16[64,2048]{1,0:T(8,128)(2,1)S(1)}, bf16[64,2048]{1,0:T(8,128)(2,1)S(1)}, u32[]{:S(2)}, u32[]{:S(2)}) collective-permute-start(bf16[64,2048]{1,0:T(8,128)(2,1)S(1)} %slice.121), channel_id=1, source_target_pairs={{0,4},{1,5},{2,3},{3,2},{4,0},{5,1},{6,7},{7,6},{8,12},{9,13},{10,... | collective-permute-start | bytes 786440 | tf_op jit(solution)/shard_map/ppermute | solution.py:37
  65.8 23.3 %collective-permute-start.6 = (bf16[32,2048]{1,0:T(8,128)(2,1)S(1)}, bf16[32,2048]{1,0:T(8,128)(2,1)S(1)}, u32[]{:S(2)}, u32[]{:S(2)}) collective-permute-start(bf16[32,2048]{1,0:T(8,128)(2,1)S(1)} %slice.127), channel_id=1, source_target_pairs={{0,1},{1,0},{2,6},{3,7},{4,5},{5,4},{6,2},{7,3},{8,9},{9,8},{10,14... | collective-permute-start | bytes 393224 | tf_op jit(solution)/shard_map/ppermute | solution.py:37
  67.6 9.3 %collective-permute-start.27 = (bf16[64,2048]{1,0:T(8,128)(2,1)S(1)}, bf16[64,2048]{1,0:T(8,128)(2,1)S(1)}, u32[]{:S(2)}, u32[]{:S(2)}) collective-permute-start(bf16[64,2048]{1,0:T(8,128)(2,1)S(1)} %slice.120), channel_id=1, source_target_pairs={{0,4},{1,5},{2,3},{3,2},{4,0},{5,1},{6,7},{7,6},{8,12},{9,13},{10,... | collective-permute-start | bytes 786440 | tf_op jit(solution)/shard_map/ppermute | solution.py:37
  68.9 14.2 %collective-permute-start.13 = (bf16[32,2048]{1,0:T(8,128)(2,1)S(1)}, bf16[32,2048]{1,0:T(8,128)(2,1)S(1)}, u32[]{:S(2)}, u32[]{:S(2)}) collective-permute-start(bf16[32,2048]{1,0:T(8,128)(2,1)S(1)} %slice.126), channel_id=1, source_target_pairs={{0,1},{1,0},{2,6},{3,7},{4,5},{5,4},{6,2},{7,3},{8,9},{9,8},{10,14... | collective-permute-start | bytes 393224 | tf_op jit(solution)/shard_map/ppermute | solution.py:37
  77.0 5.0 %collective-permute-start.28 = (bf16[32,2048]{1,0:T(8,128)(2,1)S(1)}, bf16[32,2048]{1,0:T(8,128)(2,1)S(1)}, u32[]{:S(2)}, u32[]{:S(2)}) collective-permute-start(bf16[32,2048]{1,0:T(8,128)(2,1)S(1)} %slice.124), channel_id=1, source_target_pairs={{0,1},{1,0},{2,6},{3,7},{4,5},{5,4},{6,2},{7,3},{8,9},{9,8},{10,14... | collective-permute-start | bytes 393224 | tf_op jit(solution)/shard_map/ppermute | solution.py:37
  78.8 5.5 %collective-permute-start.21 = (bf16[32,2048]{1,0:T(8,128)(2,1)S(1)}, bf16[32,2048]{1,0:T(8,128)(2,1)S(1)}, u32[]{:S(2)}, u32[]{:S(2)}) collective-permute-start(bf16[32,2048]{1,0:T(8,128)(2,1)S(1)} %slice.125), channel_id=1, source_target_pairs={{0,1},{1,0},{2,6},{3,7},{4,5},{5,4},{6,2},{7,3},{8,9},{9,8},{10,14... | collective-permute-start | bytes 393224 | tf_op jit(solution)/shard_map/ppermute | solution.py:37
  82.1 5.7 %collective-permute-start.29 = (bf16[32,2048]{1,0:T(8,128)(2,1)S(1)}, bf16[32,2048]{1,0:T(8,128)(2,1)S(1)}, u32[]{:S(2)}, u32[]{:S(2)}) collective-permute-start(bf16[32,2048]{1,0:T(8,128)(2,1)S(1)} %fusion), channel_id=1, source_target_pairs={{0,8},{1,9},{2,10},{3,11},{4,12},{5,13},{6,14},{7,15},{8,0},{9,1},... | collective-permute-start | bytes 393224 | tf_op jit(solution)/shard_map/ppermute | solution.py:37
  83.2 7.2 %collective-permute-start.14 = (bf16[32,2048]{1,0:T(8,128)(2,1)S(1)}, bf16[32,2048]{1,0:T(8,128)(2,1)S(1)}, u32[]{:S(2)}, u32[]{:S(2)}) collective-permute-start(bf16[32,2048]{1,0:T(8,128)(2,1)S(1)} %fusion.3), channel_id=1, source_target_pairs={{0,8},{1,9},{2,10},{3,11},{4,12},{5,13},{6,14},{7,15},{8,0},{9,1},... | collective-permute-start | bytes 393224 | tf_op jit(solution)/shard_map/ppermute | solution.py:37
  87.8 7.3 %collective-permute-start.30 = (bf16[32,2048]{1,0:T(8,128)(2,1)S(1)}, bf16[32,2048]{1,0:T(8,128)(2,1)S(1)}, u32[]{:S(2)}, u32[]{:S(2)}) collective-permute-start(bf16[32,2048]{1,0:T(8,128)(2,1)S(1)} %fusion.2), channel_id=1, source_target_pairs={{0,16},{1,17},{2,18},{3,19},{4,20},{5,21},{6,22},{7,23},{8,24},{9,... | collective-permute-start | bytes 393224 | tf_op jit(solution)/shard_map/ppermute | solution.py:37
  (4 other events, 21.2 us)

commit v3 on v2

--- a/solution.py
+++ b/solution.py
@@ -23,6 +23,7 @@
 BIT_X, BIT_CORE, BIT_Y, BIT_Z0, BIT_Z1 = 1, 2, 4, 8, 16
 NEAR_PLANE, FAR_PLANE = (BIT_X, BIT_Y), (BIT_Y, BIT_X)
 NEAR_LINE, FAR_LINE = (BIT_Z0, BIT_Z0), (BIT_Z1, BIT_Z1)
+BOTH_LINE = (BIT_Z0 | BIT_Z1, BIT_Z0 | BIT_Z1)
 CORE = (BIT_CORE, BIT_CORE)
 FIRST_BLOCK = 256
 SECOND_BLOCK = 512
@@ -402,26 +403,99 @@
     )(near, far, *[pltpu.with_memory_space_constraint(w, pltpu.VMEM) for w in weights])
 
 
+class Order:
+    def __init__(self):
+        self.last = None
+
+    def __call__(self, value):
+        if self.last is not None:
+            value, _ = lax.optimization_barrier((value, self.last))
+        self.last = value
+        return value
+
+
 def dense_experts(middle_own, block, weights):
-    def plane_sum(rows):
-        pair = jnp.concatenate([rows, exchanged(rows, NEAR_PLANE)], axis=0)
-        near = jnp.concatenate([pair, exchanged(pair, FAR_PLANE)], axis=0)
-        near_out, far_out = weighted_expert(near, exchanged(near, CORE), weights)
-        total = widened(near_out) + widened(exchanged(far_out, CORE))
-        for masks in (FAR_PLANE, NEAR_PLANE):
-            half = total.shape[0] // 2
-            total = total[:half] + widened(exchanged(narrowed(total[half:]), masks))
-        return total
-
-    far_line = exchanged(block, FAR_LINE)
-    own_sum = plane_sum(block)
-    far_sum = plane_sum(far_line)
-    both_sum = plane_sum(exchanged(far_line, NEAR_LINE))
-    near_sum = plane_sum(exchanged(block, NEAR_LINE))
-    far_sum += widened(exchanged(narrowed(both_sum), NEAR_LINE))
-    own_sum += widened(exchanged(narrowed(near_sum), NEAR_LINE))
-    own_sum += widened(exchanged(narrowed(far_sum), FAR_LINE))
-    return (middle_own + own_sum).astype(jnp.bfloat16)
+    then = Order()
+
+    def joined(rows, taken):
+        then.last = jnp.concatenate([rows, then(taken)], axis=0)
+        return then.last
+
+    def expert(near, far):
+        outs = weighted_expert(near, then(far), weights)
+        then.last = outs[0]
+        return outs
+
+    def added(rows, taken):
+        then.last = rows + widened(then(taken))
+        return then.last
+
+    def sent(total, masks):
+        half = total.shape[0] // 2
+        return exchanged(narrowed(total[half:]), masks)
+
+    def kept(total):
+        return total[: total.shape[0] // 2]
+
+    near_0 = exchanged(block, NEAR_PLANE)
+    set_1 = exchanged(block, NEAR_LINE)
+    set_2 = exchanged(block, FAR_LINE)
+    pair_0 = joined(block, near_0)
+    far_0 = exchanged(pair_0, FAR_PLANE)
+    set_1 = then(set_1)
+    near_1 = exchanged(set_1, NEAR_PLANE)
+    quad_0 = joined(pair_0, far_0)
+    other_0 = exchanged(quad_0, CORE)
+    pair_1 = joined(set_1, near_1)
+    far_1 = exchanged(pair_1, FAR_PLANE)
+    set_2 = then(set_2)
+    set_3 = exchanged(set_2, NEAR_LINE)
+    near_2 = exchanged(set_2, NEAR_PLANE)
+    mine_0, back_0 = expert(quad_0, other_0)
+    back_0 = exchanged(back_0, CORE)
+    quad_1 = joined(pair_1, far_1)
+    other_1 = exchanged(quad_1, CORE)
+    set_3 = then(set_3)
+    near_3 = exchanged(set_3, NEAR_PLANE)
+    pair_2 = joined(set_2, near_2)
+    far_2 = exchanged(pair_2, FAR_PLANE)
+    mine_1, back_1 = expert(quad_1, other_1)
+    back_1 = exchanged(back_1, CORE)
+    pair_3 = joined(set_3, near_3)
+    far_3 = exchanged(pair_3, FAR_PLANE)
+    quad_2 = joined(pair_2, far_2)
+    other_2 = exchanged(quad_2, CORE)
+    total_1 = added(widened(mine_1), back_1)
+    sent_1 = sent(total_1, FAR_PLANE)
+    mine_2, back_2 = expert(quad_2, other_2)
+    back_2 = exchanged(back_2, CORE)
+    quad_3 = joined(pair_3, far_3)
+    other_3 = exchanged(quad_3, CORE)
+    total_1 = added(kept(total_1), sent_1)
+    sent_1 = sent(total_1, NEAR_PLANE)
+    total_2 = added(widened(mine_2), back_2)
+    sent_2 = sent(total_2, FAR_PLANE)
+    mine_3, back_3 = expert(quad_3, other_3)
+    back_3 = exchanged(back_3, CORE)
+    total_1 = added(kept(total_1), sent_1)
+    home_1 = exchanged(narrowed(total_1), NEAR_LINE)
+    total_2 = added(kept(total_2), sent_2)
+    sent_2 = sent(total_2, NEAR_PLANE)
+    total_3 = added(widened(mine_3), back_3)
+    sent_3 = sent(total_3, FAR_PLANE)
+    total_0 = added(widened(mine_0), back_0)
+    sent_0 = sent(total_0, FAR_PLANE)
+    total_2 = added(kept(total_2), sent_2)
+    home_2 = exchanged(narrowed(total_2), FAR_LINE)
+    total_3 = added(kept(total_3), sent_3)
+    sent_3 = sent(total_3, NEAR_PLANE)
+    total_0 = added(kept(total_0), sent_0)
+    sent_0 = sent(total_0, NEAR_PLANE)
+    total_3 = added(kept(total_3), sent_3)
+    home_3 = exchanged(narrowed(total_3), BOTH_LINE)
+    total_0 = added(kept(total_0), sent_0)
+    mixture = total_0 + widened(home_1) + widened(home_2) + widened(home_3)
+    return (middle_own + mixture).astype(jnp.bfloat16)
 
 
 def routed_experts(middle_own, normed_own, own_routes, own_probs, gate_weight, up_weight, down_weight):

time: 96 us -> 84.2 us (0.88)
  waiting for transfers between devices: 40.7 us -> 26.2 us
  starting transfers between devices: 31.9 us -> 34.7 us
    ppermute x30, waiting for transfers between devices: 40.7 us -> 26.2 us  [exchanged(): lax.ppermute(shard, BOTH, [(i, i ^ masks[1 if i & BIT_CORE else 0]) for i...]
    ppermute x30, starting transfers between devices: 28.9 us -> 31.7 us  [exchanged(): lax.ppermute(shard, BOTH, [(i, i ^ masks[1 if i & BIT_CORE else 0]) for i...]
  transfers between devices with their start and end apart: 31 -> 31, of which waited for: 11 -> 14; matrix products, arithmetic and copies ran while one was open for 1% -> 2% of each run, Pallas kernels for 15% -> 17%
where the time goes in v3:
time: 84.2 us; the launch traced here: 84 us
  starting transfers between devices  34.7 us (41%)
  waiting for transfers between devices  26.2 us (31%)
  Pallas kernels  20.1 us (24%)
  other arithmetic  1.56 us (2%)
  local copies, waits for them, and re-layouts  1.16 us (1%)
    ppermute x30, starting transfers between devices, exchanged(): lax.ppermute(shard, BOTH, [(i, i ^ masks[1 if i & BIT_CORE else 0]) for i...  31.7 us
    ppermute x30, waiting for transfers between devices, exchanged(): lax.ppermute(shard, BOTH, [(i, i ^ masks[1 if i & BIT_CORE else 0]) for i...  26.2 us
    pallas_call x4, Pallas kernels, weighted_expert(): pl.pallas_call(expert_kernel, in_specs=[whole] * 5, out_specs=[whole] * 2...  10.6 us
    pallas_call x1, Pallas kernels, attention_halves(): pl.pallas_call(attention_kernel, in_specs=[far, far, far, near, far], out...  5.5 us
    pallas_call x1, Pallas kernels, loaded(): pl.pallas_call(functools.partial(load_kernel, len(weights), pieces), in_s...  3.79 us
    ppermute x1, starting transfers between devices, swapped(): lax.ppermute(shard, axis, [(i, i ^ 1 << distance) for i in range(lax.axis...  3.01 us
  transfers between devices with their start and end apart: 31, of which 14 were waited for; matrix products, arithmetic and copies ran while one was open for 2% of the time, Pallas kernels for 17%

profile of v3, /device:TPU:0, one launch (start us, length us, event | category | flops | bytes accessed | tf_op | source)
XLA Modules:
  0.0 84.0 jit_solution(13589626304900334941)
XLA Ops:
  0.7 5.5 %attention_halves.1 = (f32[32,2048]{1,0:T(8,128)S(1)}, bf16[32,2048]{1,0:T(8,128)(2,1)S(1)}) custom-call(bf16[64,2048]{1,0:T(8,128)(2,1)} %queries_hbm.1, bf16[64,512]{1,0:T(8,128)(2,1)} %keys_hbm.1, bf16[64,512]{1,0:T(8,128)(2,1)} %values_hbm.1, s32[1,64]{1,0:T(1,128)S(1)} %bitcast.7, bf16[2048,2048]{1,0:T(8,128)(2,1)} %out_weight_hbm.1), custom_call_target="tpu_custom_call" | custom-call | flops 570425344 | bytes 8388608 | tf_op jit(solution)/shard_map/attention_halves/pallas_call | solution.py:219
  6.2 3.0 %collective-permute-start = (bf16[32,2048]{1,0:T(8,128)(2,1)S(1)}, bf16[32,2048]{1,0:T(8,128)(2,1)S(1)}, u32[]{:S(2)}, u32[]{:S(2)}) collective-permute-start(bf16[32,2048]{1,0:T(8,128)(2,1)S(1)} %get-tuple-element.47.refs_3_), channel_id=1, source_target_pairs={{0,1},{1,0},{2,3},{3,2},{4,5},{5,4},{6,7},{7,6},{8,9},{9,8},{10,11... | collective-permute-start | bytes 393224 | tf_op jit(solution)/shard_map/ppermute | solution.py:33
  9.2 3.8 %load_weights.1 = (bf16[1,2048,768]{2,1,0:T(8,128)(2,1)S(1)}, bf16[1,2048,768]{2,1,0:T(8,128)(2,1)S(1)}, bf16[1,768,2048]{2,1,0:T(8,128)(2,1)S(1)}) custom-call(bf16[1,2048,768]{2,1,0:T(8,128)(2,1)} %refs_0_.1, bf16[1,2048,768]{2,1,0:T(8,128)(2,1)} %refs_1_.1, bf16[1,768,2048]{2,1,0:T(8,128)(2,1)} %refs_2_.1, bf16[32,2048]{1,0:T(8,128)(2,1)S(1)} %get-tuple-element.47.refs_3_), custom_call_target="tpu_custom_call" | custom-call | bytes 9437184 | tf_op jit(solution)/shard_map/load_weights/pallas_call | solution.py:273
  13.3 1.5 %collective-permute-start.1 = (bf16[32,2176]{1,0:T(8,128)(2,1)S(1)}, bf16[32,2176]{1,0:T(8,128)(2,1)S(1)}, u32[]{:S(2)}, u32[]{:S(2)}) collective-permute-start(bf16[32,2176]{1,0:T(8,128)(2,1)S(1)} %get-tuple-element.49), channel_id=1, source_target_pairs={{0,1},{1,0},{2,6},{3,7},{4,5},{5,4},{6,2},{7,3},{8,9},{9,8},{10,14... | collective-permute-start | bytes 417800 | tf_op jit(solution)/shard_map/ppermute | solution.py:38
  14.8 1.6 %collective-permute-start.3 = (bf16[32,2176]{1,0:T(8,128)(2,1)S(1)}, bf16[32,2176]{1,0:T(8,128)(2,1)S(1)}, u32[]{:S(2)}, u32[]{:S(2)}) collective-permute-start(bf16[32,2176]{1,0:T(8,128)(2,1)S(1)} %get-tuple-element.49), channel_id=1, source_target_pairs={{0,8},{1,9},{2,10},{3,11},{4,12},{5,13},{6,14},{7,15},{8,0},{9,1},... | collective-permute-start | bytes 417800 | tf_op jit(solution)/shard_map/ppermute | solution.py:38
  16.4 2.6 %collective-permute-start.5 = (bf16[32,2176]{1,0:T(8,128)(2,1)S(1)}, bf16[32,2176]{1,0:T(8,128)(2,1)S(1)}, u32[]{:S(2)}, u32[]{:S(2)}) collective-permute-start(bf16[32,2176]{1,0:T(8,128)(2,1)S(1)} %get-tuple-element.49), channel_id=1, source_target_pairs={{0,16},{1,17},{2,18},{3,19},{4,20},{5,21},{6,22},{7,23},{8,24},{9,... | collective-permute-start | bytes 417800 | tf_op jit(solution)/shard_map/ppermute | solution.py:38
  19.0 1.6 %collective-permute-start.2 = (bf16[64,2176]{1,0:T(8,128)(2,1)S(1)}, bf16[64,2176]{1,0:T(8,128)(2,1)S(1)}, u32[]{:S(2)}, u32[]{:S(2)}) collective-permute-start(bf16[64,2176]{1,0:T(8,128)(2,1)S(1)} %get-tuple-element.99), channel_id=1, source_target_pairs={{0,4},{1,5},{2,3},{3,2},{4,0},{5,1},{6,7},{7,6},{8,12},{9,13},{10,... | collective-permute-start | bytes 835592 | tf_op jit(solution)/shard_map/ppermute | solution.py:38
  20.6 1.2 %collective-permute-done.3 = bf16[32,2176]{1,0:T(8,128)(2,1)S(1)} collective-permute-done((bf16[32,2176]{1,0:T(8,128)(2,1)S(1)}, bf16[32,2176]{1,0:T(8,128)(2,1)S(1)}, u32[]{:S(2)}, u32[]{:S(2)}) %collective-permute-start.3) | collective-permute-done | bytes 139296 | tf_op jit(solution)/shard_map/ppermute | solution.py:38
  22.7 2.9 %collective-permute-done.2 = bf16[64,2176]{1,0:T(8,128)(2,1)S(1)} collective-permute-done((bf16[64,2176]{1,0:T(8,128)(2,1)S(1)}, bf16[64,2176]{1,0:T(8,128)(2,1)S(1)}, u32[]{:S(2)}, u32[]{:S(2)}) %collective-permute-start.2) | collective-permute-done | bytes 278560 | tf_op jit(solution)/shard_map/ppermute | solution.py:38
  25.7 1.1 %collective-permute-done.6 = bf16[32,2176]{1,0:T(8,128)(2,1)S(1)} collective-permute-done((bf16[32,2176]{1,0:T(8,128)(2,1)S(1)}, bf16[32,2176]{1,0:T(8,128)(2,1)S(1)}, u32[]{:S(2)}, u32[]{:S(2)}) %collective-permute-start.6) | collective-permute-done | bytes 139296 | tf_op jit(solution)/shard_map/ppermute | solution.py:38
  27.7 1.6 %collective-permute-start.8 = (bf16[32,2176]{1,0:T(8,128)(2,1)S(1)}, bf16[32,2176]{1,0:T(8,128)(2,1)S(1)}, u32[]{:S(2)}, u32[]{:S(2)}) collective-permute-start(bf16[32,2176]{1,0:T(8,128)(2,1)S(1)} %collective-permute-done.5), channel_id=1, source_target_pairs={{0,8},{1,9},{2,10},{3,11},{4,12},{5,13},{6,14},{7,15},{8,0},{9,1},... | collective-permute-start | bytes 417800 | tf_op jit(solution)/shard_map/ppermute | solution.py:38
  30.3 2.7 %expert_half.4 = (bf16[128,2048]{1,0:T(8,128)(2,1)S(1)}, bf16[128,2048]{1,0:T(8,128)(2,1)S(1)}) custom-call(bf16[128,2176]{1,0:T(8,128)(2,1)S(1)} %constant_dynamic-update-slice_fusion.2.near_ref, bf16[128,2176]{1,0:T(8,128)(2,1)S(1)} %collective-permute-done.4.far_ref, bf16[1,2048,768]{2,1,0:T(8,128)(2,1)S(1)} %get-tuple-element.55.gate_ref, ...), custom_call_target="tpu_custom_call" | custom-call | flops 2415919104 | bytes 2097152 | tf_op jit(solution)/shard_map/expert_half/pallas_call | solution.py:387
  32.9 2.1 %collective-permute-done.9 = bf16[64,2176]{1,0:T(8,128)(2,1)S(1)} collective-permute-done((bf16[64,2176]{1,0:T(8,128)(2,1)S(1)}, bf16[64,2176]{1,0:T(8,128)(2,1)S(1)}, u32[]{:S(2)}, u32[]{:S(2)}) %collective-permute-start.9) | collective-permute-done | bytes 278560 | tf_op jit(solution)/shard_map/ppermute | solution.py:38
  36.1 1.0 %collective-permute-start.14 = (bf16[64,2176]{1,0:T(8,128)(2,1)S(1)}, bf16[64,2176]{1,0:T(8,128)(2,1)S(1)}, u32[]{:S(2)}, u32[]{:S(2)}) collective-permute-start(bf16[64,2176]{1,0:T(8,128)(2,1)S(1)} %get-tuple-element.88), channel_id=1, source_target_pairs={{0,4},{1,5},{2,3},{3,2},{4,0},{5,1},{6,7},{7,6},{8,12},{9,13},{10,... | collective-permute-start | bytes 835592 | tf_op jit(solution)/shard_map/ppermute | solution.py:38
  37.1 2.7 %expert_half.5 = (bf16[128,2048]{1,0:T(8,128)(2,1)S(1)}, bf16[128,2048]{1,0:T(8,128)(2,1)S(1)}) custom-call(bf16[128,2176]{1,0:T(8,128)(2,1)S(1)} %constant_dynamic-update-slice_fusion.7.near_ref, bf16[128,2176]{1,0:T(8,128)(2,1)S(1)} %collective-permute-done.11.far_ref, bf16[1,2048,768]{2,1,0:T(8,128)(2,1)S(1)} %get-tuple-element.55.gate_ref, ...), custom_call_target="tpu_custom_call" | custom-call | flops 2415919104 | bytes 2097152 | tf_op jit(solution)/shard_map/expert_half/pallas_call | solution.py:387
  39.8 1.9 %collective-permute-done.10 = bf16[32,2176]{1,0:T(8,128)(2,1)S(1)} collective-permute-done((bf16[32,2176]{1,0:T(8,128)(2,1)S(1)}, bf16[32,2176]{1,0:T(8,128)(2,1)S(1)}, u32[]{:S(2)}, u32[]{:S(2)}) %collective-permute-start.10) | collective-permute-done | bytes 139296 | tf_op jit(solution)/shard_map/ppermute | solution.py:38
  41.8 0.9 %collective-permute-done.14 = bf16[64,2176]{1,0:T(8,128)(2,1)S(1)} collective-permute-done((bf16[64,2176]{1,0:T(8,128)(2,1)S(1)}, bf16[64,2176]{1,0:T(8,128)(2,1)S(1)}, u32[]{:S(2)}, u32[]{:S(2)}) %collective-permute-start.14) | collective-permute-done | bytes 278560 | tf_op jit(solution)/shard_map/ppermute | solution.py:38
  43.3 0.9 %collective-permute-start.13 = (bf16[64,2176]{1,0:T(8,128)(2,1)S(1)}, bf16[64,2176]{1,0:T(8,128)(2,1)S(1)}, u32[]{:S(2)}, u32[]{:S(2)}) collective-permute-start(bf16[64,2176]{1,0:T(8,128)(2,1)S(1)} %get-tuple-element.91), channel_id=1, source_target_pairs={{0,4},{1,5},{2,3},{3,2},{4,0},{5,1},{6,7},{7,6},{8,12},{9,13},{10,... | collective-permute-start | bytes 835592 | tf_op jit(solution)/shard_map/ppermute | solution.py:38
  44.4 1.2 %collective-permute-start.19 = (bf16[64,2048]{1,0:T(8,128)(2,1)S(1)}, bf16[64,2048]{1,0:T(8,128)(2,1)S(1)}, u32[]{:S(2)}, u32[]{:S(2)}) collective-permute-start(bf16[64,2048]{1,0:T(8,128)(2,1)S(1)} %slice.117), channel_id=1, source_target_pairs={{0,4},{1,5},{2,3},{3,2},{4,0},{5,1},{6,7},{7,6},{8,12},{9,13},{10,... | collective-permute-start | bytes 786440 | tf_op jit(solution)/shard_map/ppermute | solution.py:38
  45.6 2.6 %expert_half.6 = (bf16[128,2048]{1,0:T(8,128)(2,1)S(1)}, bf16[128,2048]{1,0:T(8,128)(2,1)S(1)}) custom-call(bf16[128,2176]{1,0:T(8,128)(2,1)S(1)} %constant_dynamic-update-slice_fusion.14.near_ref, bf16[128,2176]{1,0:T(8,128)(2,1)S(1)} %collective-permute-done.15.far_ref, bf16[1,2048,768]{2,1,0:T(8,128)(2,1)S(1)} %get-tuple-element.55.gate_ref, ...), custom_call_target="tpu_custom_call" | custom-call | flops 2415919104 | bytes 2097152 | tf_op jit(solution)/shard_map/expert_half/pallas_call | solution.py:387
  48.2 1.6 %collective-permute-done.13 = bf16[64,2176]{1,0:T(8,128)(2,1)S(1)} collective-permute-done((bf16[64,2176]{1,0:T(8,128)(2,1)S(1)}, bf16[64,2176]{1,0:T(8,128)(2,1)S(1)}, u32[]{:S(2)}, u32[]{:S(2)}) %collective-permute-start.13) | collective-permute-done | bytes 278560 | tf_op jit(solution)/shard_map/ppermute | solution.py:38
  50.5 2.2 %collective-permute-done.19 = bf16[64,2048]{1,0:T(8,128)(2,1)S(1)} collective-permute-done((bf16[64,2048]{1,0:T(8,128)(2,1)S(1)}, bf16[64,2048]{1,0:T(8,128)(2,1)S(1)}, u32[]{:S(2)}, u32[]{:S(2)}) %collective-permute-start.19) | collective-permute-done | bytes 262176 | tf_op jit(solution)/shard_map/ppermute | solution.py:38
  52.7 1.2 %collective-permute-start.22 = (bf16[32,2048]{1,0:T(8,128)(2,1)S(1)}, bf16[32,2048]{1,0:T(8,128)(2,1)S(1)}, u32[]{:S(2)}, u32[]{:S(2)}) collective-permute-start(bf16[32,2048]{1,0:T(8,128)(2,1)S(1)} %slice.121), channel_id=1, source_target_pairs={{0,1},{1,0},{2,6},{3,7},{4,5},{5,4},{6,2},{7,3},{8,9},{9,8},{10,14... | collective-permute-start | bytes 393224 | tf_op jit(solution)/shard_map/ppermute | solution.py:38
  55.0 2.6 %expert_half.7 = (bf16[128,2048]{1,0:T(8,128)(2,1)S(1)}, bf16[128,2048]{1,0:T(8,128)(2,1)S(1)}) custom-call(bf16[128,2176]{1,0:T(8,128)(2,1)S(1)} %constant_dynamic-update-slice_fusion.17.near_ref, bf16[128,2176]{1,0:T(8,128)(2,1)S(1)} %collective-permute-done.17.far_ref, bf16[1,2048,768]{2,1,0:T(8,128)(2,1)S(1)} %get-tuple-element.55.gate_ref, ...), custom_call_target="tpu_custom_call" | custom-call | flops 2415919104 | bytes 2097152 | tf_op jit(solution)/shard_map/expert_half/pallas_call | solution.py:387
  57.7 1.4 %collective-permute-done.22 = bf16[32,2048]{1,0:T(8,128)(2,1)S(1)} collective-permute-done((bf16[32,2048]{1,0:T(8,128)(2,1)S(1)}, bf16[32,2048]{1,0:T(8,128)(2,1)S(1)}, u32[]{:S(2)}, u32[]{:S(2)}) %collective-permute-start.22) | collective-permute-done | bytes 131104 | tf_op jit(solution)/shard_map/ppermute | solution.py:38
  61.9 1.3 %collective-permute-start.23 = (bf16[64,2048]{1,0:T(8,128)(2,1)S(1)}, bf16[64,2048]{1,0:T(8,128)(2,1)S(1)}, u32[]{:S(2)}, u32[]{:S(2)}) collective-permute-start(bf16[64,2048]{1,0:T(8,128)(2,1)S(1)} %slice.115), channel_id=1, source_target_pairs={{0,4},{1,5},{2,3},{3,2},{4,0},{5,1},{6,7},{7,6},{8,12},{9,13},{10,... | collective-permute-start | bytes 786440 | tf_op jit(solution)/shard_map/ppermute | solution.py:38
  64.0 3.1 %collective-permute-done.25 = bf16[32,2048]{1,0:T(8,128)(2,1)S(1)} collective-permute-done((bf16[32,2048]{1,0:T(8,128)(2,1)S(1)}, bf16[32,2048]{1,0:T(8,128)(2,1)S(1)}, u32[]{:S(2)}, u32[]{:S(2)}) %collective-permute-start.25) | collective-permute-done | bytes 131104 | tf_op jit(solution)/shard_map/ppermute | solution.py:38
  67.1 3.2 %collective-permute-start.29 = (bf16[32,2048]{1,0:T(8,128)(2,1)S(1)}, bf16[32,2048]{1,0:T(8,128)(2,1)S(1)}, u32[]{:S(2)}, u32[]{:S(2)}) collective-permute-start(bf16[32,2048]{1,0:T(8,128)(2,1)S(1)} %slice_add_fusion.6), channel_id=1, source_target_pairs={{0,16},{1,17},{2,18},{3,19},{4,20},{5,21},{6,22},{7,23},{8,24},{9,... | collective-permute-start | bytes 393224 | tf_op jit(solution)/shard_map/ppermute | solution.py:38
  71.3 1.2 %collective-permute-start.27 = (bf16[32,2048]{1,0:T(8,128)(2,1)S(1)}, bf16[32,2048]{1,0:T(8,128)(2,1)S(1)}, u32[]{:S(2)}, u32[]{:S(2)}) collective-permute-start(bf16[32,2048]{1,0:T(8,128)(2,1)S(1)} %slice.118), channel_id=1, source_target_pairs={{0,1},{1,0},{2,6},{3,7},{4,5},{5,4},{6,2},{7,3},{8,9},{9,8},{10,14... | collective-permute-start | bytes 393224 | tf_op jit(solution)/shard_map/ppermute | solution.py:38
  73.5 2.8 %collective-permute-done.27 = bf16[32,2048]{1,0:T(8,128)(2,1)S(1)} collective-permute-done((bf16[32,2048]{1,0:T(8,128)(2,1)S(1)}, bf16[32,2048]{1,0:T(8,128)(2,1)S(1)}, u32[]{:S(2)}, u32[]{:S(2)}) %collective-permute-start.27) | collective-permute-done | bytes 131104 | tf_op jit(solution)/shard_map/ppermute | solution.py:38
  76.4 3.9 %collective-permute-start.30 = (bf16[32,2048]{1,0:T(8,128)(2,1)S(1)}, bf16[32,2048]{1,0:T(8,128)(2,1)S(1)}, u32[]{:S(2)}, u32[]{:S(2)}) collective-permute-start(bf16[32,2048]{1,0:T(8,128)(2,1)S(1)} %slice_add_fusion.4), channel_id=1, source_target_pairs={{0,24},{1,25},{2,26},{3,27},{4,28},{5,29},{6,30},{7,31},{8,16},{9,... | collective-permute-start | bytes 393224 | tf_op jit(solution)/shard_map/ppermute | solution.py:38
  80.3 3.0 %collective-permute-done.30 = bf16[32,2048]{1,0:T(8,128)(2,1)S(1)} collective-permute-done((bf16[32,2048]{1,0:T(8,128)(2,1)S(1)}, bf16[32,2048]{1,0:T(8,128)(2,1)S(1)}, u32[]{:S(2)}, u32[]{:S(2)}) %collective-permute-start.30) | collective-permute-done | bytes 131104 | tf_op jit(solution)/shard_map/ppermute | solution.py:38
  (79 shorter events, 13.6 us)
Async XLA Ops:
  6.2 6.9 %copy-start = (bf16[32,2048]{1,0:T(8,128)(2,1)S(1)}, bf16[32,2048]{1,0:T(8,128)(2,1)}, u32[]{:S(2)}) copy-start(bf16[32,2048]{1,0:T(8,128)(2,1)} %residual_ref.1) | copy-start | bytes 393220
  6.2 6.8 %collective-permute-start = (bf16[32,2048]{1,0:T(8,128)(2,1)S(1)}, bf16[32,2048]{1,0:T(8,128)(2,1)S(1)}, u32[]{:S(2)}, u32[]{:S(2)}) collective-permute-start(bf16[32,2048]{1,0:T(8,128)(2,1)S(1)} %get-tuple-element.47.refs_3_), channel_id=1, source_target_pairs={{0,1},{1,0},{2,3},{3,2},{4,5},{5,4},{6,7},{7,6},{8,9},{9,8},{10,11... | collective-permute-start | bytes 393224 | tf_op jit(solution)/shard_map/ppermute | solution.py:33
  13.3 5.7 %collective-permute-start.1 = (bf16[32,2176]{1,0:T(8,128)(2,1)S(1)}, bf16[32,2176]{1,0:T(8,128)(2,1)S(1)}, u32[]{:S(2)}, u32[]{:S(2)}) collective-permute-start(bf16[32,2176]{1,0:T(8,128)(2,1)S(1)} %get-tuple-element.49), channel_id=1, source_target_pairs={{0,1},{1,0},{2,6},{3,7},{4,5},{5,4},{6,2},{7,3},{8,9},{9,8},{10,14... | collective-permute-start | bytes 417800 | tf_op jit(solution)/shard_map/ppermute | solution.py:38
  14.8 7.1 %collective-permute-start.3 = (bf16[32,2176]{1,0:T(8,128)(2,1)S(1)}, bf16[32,2176]{1,0:T(8,128)(2,1)S(1)}, u32[]{:S(2)}, u32[]{:S(2)}) collective-permute-start(bf16[32,2176]{1,0:T(8,128)(2,1)S(1)} %get-tuple-element.49), channel_id=1, source_target_pairs={{0,8},{1,9},{2,10},{3,11},{4,12},{5,13},{6,14},{7,15},{8,0},{9,1},... | collective-permute-start | bytes 417800 | tf_op jit(solution)/shard_map/ppermute | solution.py:38
  16.4 11.3 %collective-permute-start.5 = (bf16[32,2176]{1,0:T(8,128)(2,1)S(1)}, bf16[32,2176]{1,0:T(8,128)(2,1)S(1)}, u32[]{:S(2)}, u32[]{:S(2)}) collective-permute-start(bf16[32,2176]{1,0:T(8,128)(2,1)S(1)} %get-tuple-element.49), channel_id=1, source_target_pairs={{0,16},{1,17},{2,18},{3,19},{4,20},{5,21},{6,22},{7,23},{8,24},{9,... | collective-permute-start | bytes 417800 | tf_op jit(solution)/shard_map/ppermute | solution.py:38
  19.0 6.6 %collective-permute-start.2 = (bf16[64,2176]{1,0:T(8,128)(2,1)S(1)}, bf16[64,2176]{1,0:T(8,128)(2,1)S(1)}, u32[]{:S(2)}, u32[]{:S(2)}) collective-permute-start(bf16[64,2176]{1,0:T(8,128)(2,1)S(1)} %get-tuple-element.99), channel_id=1, source_target_pairs={{0,4},{1,5},{2,3},{3,2},{4,0},{5,1},{6,7},{7,6},{8,12},{9,13},{10,... | collective-permute-start | bytes 835592 | tf_op jit(solution)/shard_map/ppermute | solution.py:38
  21.8 5.1 %collective-permute-start.6 = (bf16[32,2176]{1,0:T(8,128)(2,1)S(1)}, bf16[32,2176]{1,0:T(8,128)(2,1)S(1)}, u32[]{:S(2)}, u32[]{:S(2)}) collective-permute-start(bf16[32,2176]{1,0:T(8,128)(2,1)S(1)} %collective-permute-done.3), channel_id=1, source_target_pairs={{0,1},{1,0},{2,6},{3,7},{4,5},{5,4},{6,2},{7,3},{8,9},{9,8},{10,14... | collective-permute-start | bytes 417800 | tf_op jit(solution)/shard_map/ppermute | solution.py:38
  25.7 4.6 %collective-permute-start.4 = (bf16[128,2176]{1,0:T(8,128)(2,1)S(1)}, bf16[128,2176]{1,0:T(8,128)(2,1)S(1)}, u32[]{:S(2)}, u32[]{:S(2)}) collective-permute-start(bf16[128,2176]{1,0:T(8,128)(2,1)S(1)} %constant_dynamic-update-slice_fusion.2.near_ref), channel_id=1, source_target_pairs={{0,2},{1,3},{2,0},{3,1},{4,6},{5,7},{6,4},{7,5},{8,10},{9,11},{10,... | collective-permute-start | bytes 1671176 | tf_op jit(solution)/shard_map/ppermute | solution.py:38
  26.9 8.1 %collective-permute-start.9 = (bf16[64,2176]{1,0:T(8,128)(2,1)S(1)}, bf16[64,2176]{1,0:T(8,128)(2,1)S(1)}, u32[]{:S(2)}, u32[]{:S(2)}) collective-permute-start(bf16[64,2176]{1,0:T(8,128)(2,1)S(1)} %get-tuple-element.96), channel_id=1, source_target_pairs={{0,4},{1,5},{2,3},{3,2},{4,0},{5,1},{6,7},{7,6},{8,12},{9,13},{10,... | collective-permute-start | bytes 835592 | tf_op jit(solution)/shard_map/ppermute | solution.py:38
  27.7 7.4 %collective-permute-start.8 = (bf16[32,2176]{1,0:T(8,128)(2,1)S(1)}, bf16[32,2176]{1,0:T(8,128)(2,1)S(1)}, u32[]{:S(2)}, u32[]{:S(2)}) collective-permute-start(bf16[32,2176]{1,0:T(8,128)(2,1)S(1)} %collective-permute-done.5), channel_id=1, source_target_pairs={{0,8},{1,9},{2,10},{3,11},{4,12},{5,13},{6,14},{7,15},{8,0},{9,1},... | collective-permute-start | bytes 417800 | tf_op jit(solution)/shard_map/ppermute | solution.py:38
  29.4 6.7 %collective-permute-start.12 = (bf16[32,2176]{1,0:T(8,128)(2,1)S(1)}, bf16[32,2176]{1,0:T(8,128)(2,1)S(1)}, u32[]{:S(2)}, u32[]{:S(2)}) collective-permute-start(bf16[32,2176]{1,0:T(8,128)(2,1)S(1)} %collective-permute-done.5), channel_id=1, source_target_pairs={{0,1},{1,0},{2,6},{3,7},{4,5},{5,4},{6,2},{7,3},{8,9},{9,8},{10,14... | collective-permute-start | bytes 417800 | tf_op jit(solution)/shard_map/ppermute | solution.py:38
  35.1 2.1 %collective-permute-start.11 = (bf16[128,2176]{1,0:T(8,128)(2,1)S(1)}, bf16[128,2176]{1,0:T(8,128)(2,1)S(1)}, u32[]{:S(2)}, u32[]{:S(2)}) collective-permute-start(bf16[128,2176]{1,0:T(8,128)(2,1)S(1)} %constant_dynamic-update-slice_fusion.7.near_ref), channel_id=1, source_target_pairs={{0,2},{1,3},{2,0},{3,1},{4,6},{5,7},{6,4},{7,5},{8,10},{9,11},{10,... | collective-permute-start | bytes 1671176 | tf_op jit(solution)/shard_map/ppermute | solution.py:38
  35.1 6.6 %collective-permute-start.10 = (bf16[32,2176]{1,0:T(8,128)(2,1)S(1)}, bf16[32,2176]{1,0:T(8,128)(2,1)S(1)}, u32[]{:S(2)}, u32[]{:S(2)}) collective-permute-start(bf16[32,2176]{1,0:T(8,128)(2,1)S(1)} %collective-permute-done.8), channel_id=1, source_target_pairs={{0,1},{1,0},{2,6},{3,7},{4,5},{5,4},{6,2},{7,3},{8,9},{9,8},{10,14... | collective-permute-start | bytes 417800 | tf_op jit(solution)/shard_map/ppermute | solution.py:38
  36.1 6.6 %collective-permute-start.14 = (bf16[64,2176]{1,0:T(8,128)(2,1)S(1)}, bf16[64,2176]{1,0:T(8,128)(2,1)S(1)}, u32[]{:S(2)}, u32[]{:S(2)}) collective-permute-start(bf16[64,2176]{1,0:T(8,128)(2,1)S(1)} %get-tuple-element.88), channel_id=1, source_target_pairs={{0,4},{1,5},{2,3},{3,2},{4,0},{5,1},{6,7},{7,6},{8,12},{9,13},{10,... | collective-permute-start | bytes 835592 | tf_op jit(solution)/shard_map/ppermute | solution.py:38
  41.7 2.5 %collective-permute-start.16 = (bf16[128,2048]{1,0:T(8,128)(2,1)S(1)}, bf16[128,2048]{1,0:T(8,128)(2,1)S(1)}, u32[]{:S(2)}, u32[]{:S(2)}) collective-permute-start(bf16[128,2048]{1,0:T(8,128)(2,1)S(1)} %get-tuple-element.67), channel_id=1, source_target_pairs={{0,2},{1,3},{2,0},{3,1},{4,6},{5,7},{6,4},{7,5},{8,10},{9,11},{10,... | collective-permute-start | bytes 1572872 | tf_op jit(solution)/shard_map/ppermute | solution.py:38
  42.7 2.8 %collective-permute-start.15 = (bf16[128,2176]{1,0:T(8,128)(2,1)S(1)}, bf16[128,2176]{1,0:T(8,128)(2,1)S(1)}, u32[]{:S(2)}, u32[]{:S(2)}) collective-permute-start(bf16[128,2176]{1,0:T(8,128)(2,1)S(1)} %constant_dynamic-update-slice_fusion.14.near_ref), channel_id=1, source_target_pairs={{0,2},{1,3},{2,0},{3,1},{4,6},{5,7},{6,4},{7,5},{8,10},{9,11},{10,... | collective-permute-start | bytes 1671176 | tf_op jit(solution)/shard_map/ppermute | solution.py:38
  43.2 18.6 %collective-permute-start.7 = (bf16[128,2048]{1,0:T(8,128)(2,1)S(1)}, bf16[128,2048]{1,0:T(8,128)(2,1)S(1)}, u32[]{:S(2)}, u32[]{:S(2)}) collective-permute-start(bf16[128,2048]{1,0:T(8,128)(2,1)S(1)} %get-tuple-element.59), channel_id=1, source_target_pairs={{0,2},{1,3},{2,0},{3,1},{4,6},{5,7},{6,4},{7,5},{8,10},{9,11},{10,... | collective-permute-start | bytes 1572872 | tf_op jit(solution)/shard_map/ppermute | solution.py:38
  43.3 6.5 %collective-permute-start.13 = (bf16[64,2176]{1,0:T(8,128)(2,1)S(1)}, bf16[64,2176]{1,0:T(8,128)(2,1)S(1)}, u32[]{:S(2)}, u32[]{:S(2)}) collective-permute-start(bf16[64,2176]{1,0:T(8,128)(2,1)S(1)} %get-tuple-element.91), channel_id=1, source_target_pairs={{0,4},{1,5},{2,3},{3,2},{4,0},{5,1},{6,7},{7,6},{8,12},{9,13},{10,... | collective-permute-start | bytes 835592 | tf_op jit(solution)/shard_map/ppermute | solution.py:38
  44.4 8.2 %collective-permute-start.19 = (bf16[64,2048]{1,0:T(8,128)(2,1)S(1)}, bf16[64,2048]{1,0:T(8,128)(2,1)S(1)}, u32[]{:S(2)}, u32[]{:S(2)}) collective-permute-start(bf16[64,2048]{1,0:T(8,128)(2,1)S(1)} %slice.117), channel_id=1, source_target_pairs={{0,4},{1,5},{2,3},{3,2},{4,0},{5,1},{6,7},{7,6},{8,12},{9,13},{10,... | collective-permute-start | bytes 786440 | tf_op jit(solution)/shard_map/ppermute | solution.py:38
  49.9 4.1 %collective-permute-start.18 = (bf16[128,2048]{1,0:T(8,128)(2,1)S(1)}, bf16[128,2048]{1,0:T(8,128)(2,1)S(1)}, u32[]{:S(2)}, u32[]{:S(2)}) collective-permute-start(bf16[128,2048]{1,0:T(8,128)(2,1)S(1)} %get-tuple-element.72), channel_id=1, source_target_pairs={{0,2},{1,3},{2,0},{3,1},{4,6},{5,7},{6,4},{7,5},{8,10},{9,11},{10,... | collective-permute-start | bytes 1572872 | tf_op jit(solution)/shard_map/ppermute | solution.py:38
  49.9 5.1 %collective-permute-start.17 = (bf16[128,2176]{1,0:T(8,128)(2,1)S(1)}, bf16[128,2176]{1,0:T(8,128)(2,1)S(1)}, u32[]{:S(2)}, u32[]{:S(2)}) collective-permute-start(bf16[128,2176]{1,0:T(8,128)(2,1)S(1)} %constant_dynamic-update-slice_fusion.17.near_ref), channel_id=1, source_target_pairs={{0,2},{1,3},{2,0},{3,1},{4,6},{5,7},{6,4},{7,5},{8,10},{9,11},{10,... | collective-permute-start | bytes 1671176 | tf_op jit(solution)/shard_map/ppermute | solution.py:38
  52.7 6.4 %collective-permute-start.22 = (bf16[32,2048]{1,0:T(8,128)(2,1)S(1)}, bf16[32,2048]{1,0:T(8,128)(2,1)S(1)}, u32[]{:S(2)}, u32[]{:S(2)}) collective-permute-start(bf16[32,2048]{1,0:T(8,128)(2,1)S(1)} %slice.121), channel_id=1, source_target_pairs={{0,1},{1,0},{2,6},{3,7},{4,5},{5,4},{6,2},{7,3},{8,9},{9,8},{10,14... | collective-permute-start | bytes 393224 | tf_op jit(solution)/shard_map/ppermute | solution.py:38
  54.2 6.4 %collective-permute-start.21 = (bf16[64,2048]{1,0:T(8,128)(2,1)S(1)}, bf16[64,2048]{1,0:T(8,128)(2,1)S(1)}, u32[]{:S(2)}, u32[]{:S(2)}) collective-permute-start(bf16[64,2048]{1,0:T(8,128)(2,1)S(1)} %slice.116), channel_id=1, source_target_pairs={{0,4},{1,5},{2,3},{3,2},{4,0},{5,1},{6,7},{7,6},{8,12},{9,13},{10,... | collective-permute-start | bytes 786440 | tf_op jit(solution)/shard_map/ppermute | solution.py:38
  57.6 4.0 %collective-permute-start.20 = (bf16[128,2048]{1,0:T(8,128)(2,1)S(1)}, bf16[128,2048]{1,0:T(8,128)(2,1)S(1)}, u32[]{:S(2)}, u32[]{:S(2)}) collective-permute-start(bf16[128,2048]{1,0:T(8,128)(2,1)S(1)} %get-tuple-element.77), channel_id=1, source_target_pairs={{0,2},{1,3},{2,0},{3,1},{4,6},{5,7},{6,4},{7,5},{8,10},{9,11},{10,... | collective-permute-start | bytes 1572872 | tf_op jit(solution)/shard_map/ppermute | solution.py:38
  59.2 21.1 %collective-permute-start.28 = (bf16[32,2048]{1,0:T(8,128)(2,1)S(1)}, bf16[32,2048]{1,0:T(8,128)(2,1)S(1)}, u32[]{:S(2)}, u32[]{:S(2)}) collective-permute-start(bf16[32,2048]{1,0:T(8,128)(2,1)S(1)} %slice_add_fusion.7), channel_id=1, source_target_pairs={{0,8},{1,9},{2,10},{3,11},{4,12},{5,13},{6,14},{7,15},{8,0},{9,1},... | collective-permute-start | bytes 393224 | tf_op jit(solution)/shard_map/ppermute | solution.py:38
  60.7 6.4 %collective-permute-start.25 = (bf16[32,2048]{1,0:T(8,128)(2,1)S(1)}, bf16[32,2048]{1,0:T(8,128)(2,1)S(1)}, u32[]{:S(2)}, u32[]{:S(2)}) collective-permute-start(bf16[32,2048]{1,0:T(8,128)(2,1)S(1)} %slice.120), channel_id=1, source_target_pairs={{0,1},{1,0},{2,6},{3,7},{4,5},{5,4},{6,2},{7,3},{8,9},{9,8},{10,14... | collective-permute-start | bytes 393224 | tf_op jit(solution)/shard_map/ppermute | solution.py:38
  61.9 9.3 %collective-permute-start.23 = (bf16[64,2048]{1,0:T(8,128)(2,1)S(1)}, bf16[64,2048]{1,0:T(8,128)(2,1)S(1)}, u32[]{:S(2)}, u32[]{:S(2)}) collective-permute-start(bf16[64,2048]{1,0:T(8,128)(2,1)S(1)} %slice.115), channel_id=1, source_target_pairs={{0,4},{1,5},{2,3},{3,2},{4,0},{5,1},{6,7},{7,6},{8,12},{9,13},{10,... | collective-permute-start | bytes 786440 | tf_op jit(solution)/shard_map/ppermute | solution.py:38
  63.2 8.0 %collective-permute-start.24 = (bf16[64,2048]{1,0:T(8,128)(2,1)S(1)}, bf16[64,2048]{1,0:T(8,128)(2,1)S(1)}, u32[]{:S(2)}, u32[]{:S(2)}) collective-permute-start(bf16[64,2048]{1,0:T(8,128)(2,1)S(1)} %slice.114), channel_id=1, source_target_pairs={{0,4},{1,5},{2,3},{3,2},{4,0},{5,1},{6,7},{7,6},{8,12},{9,13},{10,... | collective-permute-start | bytes 786440 | tf_op jit(solution)/shard_map/ppermute | solution.py:38
  67.1 13.2 %collective-permute-start.29 = (bf16[32,2048]{1,0:T(8,128)(2,1)S(1)}, bf16[32,2048]{1,0:T(8,128)(2,1)S(1)}, u32[]{:S(2)}, u32[]{:S(2)}) collective-permute-start(bf16[32,2048]{1,0:T(8,128)(2,1)S(1)} %slice_add_fusion.6), channel_id=1, source_target_pairs={{0,16},{1,17},{2,18},{3,19},{4,20},{5,21},{6,22},{7,23},{8,24},{9,... | collective-permute-start | bytes 393224 | tf_op jit(solution)/shard_map/ppermute | solution.py:38
  71.3 5.0 %collective-permute-start.27 = (bf16[32,2048]{1,0:T(8,128)(2,1)S(1)}, bf16[32,2048]{1,0:T(8,128)(2,1)S(1)}, u32[]{:S(2)}, u32[]{:S(2)}) collective-permute-start(bf16[32,2048]{1,0:T(8,128)(2,1)S(1)} %slice.118), channel_id=1, source_target_pairs={{0,1},{1,0},{2,6},{3,7},{4,5},{5,4},{6,2},{7,3},{8,9},{9,8},{10,14... | collective-permute-start | bytes 393224 | tf_op jit(solution)/shard_map/ppermute | solution.py:38
  72.6 7.7 %collective-permute-start.26 = (bf16[32,2048]{1,0:T(8,128)(2,1)S(1)}, bf16[32,2048]{1,0:T(8,128)(2,1)S(1)}, u32[]{:S(2)}, u32[]{:S(2)}) collective-permute-start(bf16[32,2048]{1,0:T(8,128)(2,1)S(1)} %slice.119), channel_id=1, source_target_pairs={{0,1},{1,0},{2,6},{3,7},{4,5},{5,4},{6,2},{7,3},{8,9},{9,8},{10,14... | collective-permute-start | bytes 393224 | tf_op jit(solution)/shard_map/ppermute | solution.py:38
  76.4 6.9 %collective-permute-start.30 = (bf16[32,2048]{1,0:T(8,128)(2,1)S(1)}, bf16[32,2048]{1,0:T(8,128)(2,1)S(1)}, u32[]{:S(2)}, u32[]{:S(2)}) collective-permute-start(bf16[32,2048]{1,0:T(8,128)(2,1)S(1)} %slice_add_fusion.4), channel_id=1, source_target_pairs={{0,24},{1,25},{2,26},{3,27},{4,28},{5,29},{6,30},{7,31},{8,16},{9,... | collective-permute-start | bytes 393224 | tf_op jit(solution)/shard_map/ppermute | solution.py:38
  (4 other events, 21.2 us)

commit v4 on v3

--- a/solution.py
+++ b/solution.py
@@ -413,6 +413,11 @@
         self.last = value
         return value
 
+    def after(self, value):
+        if self.last is None or self.last is value:
+            return value
+        return lax.optimization_barrier((value, self.last))[0]
+
 
 def dense_experts(middle_own, block, weights):
     then = Order()
@@ -437,63 +442,66 @@
     def kept(total):
         return total[: total.shape[0] // 2]
 
-    near_0 = exchanged(block, NEAR_PLANE)
-    set_1 = exchanged(block, NEAR_LINE)
-    set_2 = exchanged(block, FAR_LINE)
-    pair_0 = joined(block, near_0)
-    far_0 = exchanged(pair_0, FAR_PLANE)
+    taken_0 = exchanged(then.after(block), NEAR_PLANE)
+    set_1 = exchanged(then.after(block), NEAR_LINE)
+    set_2 = exchanged(then.after(block), FAR_LINE)
+    pair_0 = joined(block, taken_0)
+    taken_0 = exchanged(then.after(pair_0), FAR_PLANE)
     set_1 = then(set_1)
-    near_1 = exchanged(set_1, NEAR_PLANE)
-    quad_0 = joined(pair_0, far_0)
-    other_0 = exchanged(quad_0, CORE)
-    pair_1 = joined(set_1, near_1)
-    far_1 = exchanged(pair_1, FAR_PLANE)
+    taken_1 = exchanged(then.after(set_1), NEAR_PLANE)
     set_2 = then(set_2)
-    set_3 = exchanged(set_2, NEAR_LINE)
-    near_2 = exchanged(set_2, NEAR_PLANE)
+    set_3 = exchanged(then.after(set_2), NEAR_LINE)
+    taken_2 = exchanged(then.after(set_2), NEAR_PLANE)
+    quad_0 = joined(pair_0, taken_0)
+    other_0 = exchanged(then.after(quad_0), CORE)
+    pair_1 = joined(set_1, taken_1)
+    taken_1 = exchanged(then.after(pair_1), FAR_PLANE)
+    set_3 = then(set_3)
+    taken_3 = exchanged(then.after(set_3), NEAR_PLANE)
+    pair_2 = joined(set_2, taken_2)
+    taken_2 = exchanged(then.after(pair_2), FAR_PLANE)
     mine_0, back_0 = expert(quad_0, other_0)
-    back_0 = exchanged(back_0, CORE)
-    quad_1 = joined(pair_1, far_1)
-    other_1 = exchanged(quad_1, CORE)
-    set_3 = then(set_3)
-    near_3 = exchanged(set_3, NEAR_PLANE)
-    pair_2 = joined(set_2, near_2)
-    far_2 = exchanged(pair_2, FAR_PLANE)
+    back_0 = exchanged(then.after(back_0), CORE)
+    quad_1 = joined(pair_1, taken_1)
+    other_1 = exchanged(then.after(quad_1), CORE)
+    pair_3 = joined(set_3, taken_3)
+    taken_3 = exchanged(then.after(pair_3), FAR_PLANE)
+    quad_2 = joined(pair_2, taken_2)
+    other_2 = exchanged(then.after(quad_2), CORE)
+    total_0 = added(widened(mine_0), back_0)
+    sent_0 = sent(then.after(total_0), FAR_PLANE)
     mine_1, back_1 = expert(quad_1, other_1)
-    back_1 = exchanged(back_1, CORE)
-    pair_3 = joined(set_3, near_3)
-    far_3 = exchanged(pair_3, FAR_PLANE)
-    quad_2 = joined(pair_2, far_2)
-    other_2 = exchanged(quad_2, CORE)
+    back_1 = exchanged(then.after(back_1), CORE)
+    quad_3 = joined(pair_3, taken_3)
+    other_3 = exchanged(then.after(quad_3), CORE)
+    mine_2, back_2 = expert(quad_2, other_2)
+    back_2 = exchanged(then.after(back_2), CORE)
+    total_0 = added(kept(total_0), sent_0)
+    sent_0 = sent(then.after(total_0), NEAR_PLANE)
     total_1 = added(widened(mine_1), back_1)
-    sent_1 = sent(total_1, FAR_PLANE)
-    mine_2, back_2 = expert(quad_2, other_2)
-    back_2 = exchanged(back_2, CORE)
-    quad_3 = joined(pair_3, far_3)
-    other_3 = exchanged(quad_3, CORE)
+    sent_1 = sent(then.after(total_1), FAR_PLANE)
+    mine_3, back_3 = expert(quad_3, other_3)
+    back_3 = exchanged(then.after(back_3), CORE)
+    total_2 = added(widened(mine_2), back_2)
+    sent_2 = sent(then.after(total_2), FAR_PLANE)
     total_1 = added(kept(total_1), sent_1)
-    sent_1 = sent(total_1, NEAR_PLANE)
-    total_2 = added(widened(mine_2), back_2)
-    sent_2 = sent(total_2, FAR_PLANE)
-    mine_3, back_3 = expert(quad_3, other_3)
-    back_3 = exchanged(back_3, CORE)
+    sent_1 = sent(then.after(total_1), NEAR_PLANE)
+    total_3 = added(widened(mine_3), back_3)
+    sent_3 = sent(then.after(total_3), FAR_PLANE)
+    total_2 = added(kept(total_2), sent_2)
+    sent_2 = sent(then.after(total_2), NEAR_PLANE)
     total_1 = added(kept(total_1), sent_1)
-    home_1 = exchanged(narrowed(total_1), NEAR_LINE)
+    home_1 = exchanged(narrowed(then.after(total_1)), NEAR_LINE)
+    total_3 = added(kept(total_3), sent_3)
+    sent_3 = sent(then.after(total_3), NEAR_PLANE)
+    total_0 = added(kept(total_0), sent_0)
     total_2 = added(kept(total_2), sent_2)
-    sent_2 = sent(total_2, NEAR_PLANE)
-    total_3 = added(widened(mine_3), back_3)
-    sent_3 = sent(total_3, FAR_PLANE)
-    total_0 = added(widened(mine_0), back_0)
-    sent_0 = sent(total_0, FAR_PLANE)
-    total_2 = added(kept(total_2), sent_2)
-    home_2 = exchanged(narrowed(total_2), FAR_LINE)
+    home_2 = exchanged(narrowed(then.after(total_2)), FAR_LINE)
+    home_1 = then(home_1)
     total_3 = added(kept(total_3), sent_3)
-    sent_3 = sent(total_3, NEAR_PLANE)
-    total_0 = added(kept(total_0), sent_0)
-    sent_0 = sent(total_0, NEAR_PLANE)
-    total_3 = added(kept(total_3), sent_3)
-    home_3 = exchanged(narrowed(total_3), BOTH_LINE)
-    total_0 = added(kept(total_0), sent_0)
+    home_3 = exchanged(narrowed(then.after(total_3)), BOTH_LINE)
+    home_2 = then(home_2)
+    home_3 = then(home_3)
     mixture = total_0 + widened(home_1) + widened(home_2) + widened(home_3)
     return (middle_own + mixture).astype(jnp.bfloat16)
 

time: 84.2 us -> 81.2 us (0.964)
  starting transfers between devices: 34.7 us -> 32 us
    ppermute x30, starting transfers between devices: 31.7 us -> 29 us  [exchanged(): lax.ppermute(shard, BOTH, [(i, i ^ masks[1 if i & BIT_CORE else 0]) for i...]
  transfers between devices with their start and end apart: 31 -> 31, of which waited for: 14 -> 16; matrix products, arithmetic and copies ran while one was open for 2% -> 2% of each run, Pallas kernels for 17% -> 18%
where the time goes in v4:
time: 81.2 us; the launch traced here: 80.8 us
  starting transfers between devices  32 us (39%)
  waiting for transfers between devices  25.7 us (32%)
  Pallas kernels  20 us (25%)
  other arithmetic  1.55 us (2%)
  local copies, waits for them, and re-layouts  1.16 us (1%)
    ppermute x30, starting transfers between devices, exchanged(): lax.ppermute(shard, BOTH, [(i, i ^ masks[1 if i & BIT_CORE else 0]) for i...  29 us
    ppermute x30, waiting for transfers between devices, exchanged(): lax.ppermute(shard, BOTH, [(i, i ^ masks[1 if i & BIT_CORE else 0]) for i...  25.7 us
    pallas_call x4, Pallas kernels, weighted_expert(): pl.pallas_call(expert_kernel, in_specs=[whole] * 5, out_specs=[whole] * 2...  10.6 us
    pallas_call x1, Pallas kernels, attention_halves(): pl.pallas_call(attention_kernel, in_specs=[far, far, far, near, far], out...  5.5 us
    pallas_call x1, Pallas kernels, loaded(): pl.pallas_call(functools.partial(load_kernel, len(weights), pieces), in_s...  3.79 us
    ppermute x1, starting transfers between devices, swapped(): lax.ppermute(shard, axis, [(i, i ^ 1 << distance) for i in range(lax.axis...  3.01 us
  transfers between devices with their start and end apart: 31, of which 16 were waited for; matrix products, arithmetic and copies ran while one was open for 2% of the time, Pallas kernels for 18%

profile of v4, /device:TPU:0, one launch (start us, length us, event | category | flops | bytes accessed | tf_op | source)
XLA Modules:
  0.0 80.8 jit_solution(156441840342565001)
XLA Ops:
  0.7 5.5 %attention_halves.1 = (f32[32,2048]{1,0:T(8,128)S(1)}, bf16[32,2048]{1,0:T(8,128)(2,1)S(1)}) custom-call(bf16[64,2048]{1,0:T(8,128)(2,1)} %queries_hbm.1, bf16[64,512]{1,0:T(8,128)(2,1)} %keys_hbm.1, bf16[64,512]{1,0:T(8,128)(2,1)} %values_hbm.1, s32[1,64]{1,0:T(1,128)S(1)} %bitcast.7, bf16[2048,2048]{1,0:T(8,128)(2,1)} %out_weight_hbm.1), custom_call_target="tpu_custom_call" | custom-call | flops 570425344 | bytes 8388608 | tf_op jit(solution)/shard_map/attention_halves/pallas_call | solution.py:219
  6.2 3.0 %collective-permute-start = (bf16[32,2048]{1,0:T(8,128)(2,1)S(1)}, bf16[32,2048]{1,0:T(8,128)(2,1)S(1)}, u32[]{:S(2)}, u32[]{:S(2)}) collective-permute-start(bf16[32,2048]{1,0:T(8,128)(2,1)S(1)} %get-tuple-element.54.refs_3_), channel_id=1, source_target_pairs={{0,1},{1,0},{2,3},{3,2},{4,5},{5,4},{6,7},{7,6},{8,9},{9,8},{10,11... | collective-permute-start | bytes 393224 | tf_op jit(solution)/shard_map/ppermute | solution.py:33
  9.2 3.8 %load_weights.1 = (bf16[1,2048,768]{2,1,0:T(8,128)(2,1)S(1)}, bf16[1,2048,768]{2,1,0:T(8,128)(2,1)S(1)}, bf16[1,768,2048]{2,1,0:T(8,128)(2,1)S(1)}) custom-call(bf16[1,2048,768]{2,1,0:T(8,128)(2,1)} %refs_0_.1, bf16[1,2048,768]{2,1,0:T(8,128)(2,1)} %refs_1_.1, bf16[1,768,2048]{2,1,0:T(8,128)(2,1)} %refs_2_.1, bf16[32,2048]{1,0:T(8,128)(2,1)S(1)} %get-tuple-element.54.refs_3_), custom_call_target="tpu_custom_call" | custom-call | bytes 9437184 | tf_op jit(solution)/shard_map/load_weights/pallas_call | solution.py:273
  13.3 1.5 %collective-permute-start.1 = (bf16[32,2176]{1,0:T(8,128)(2,1)S(1)}, bf16[32,2176]{1,0:T(8,128)(2,1)S(1)}, u32[]{:S(2)}, u32[]{:S(2)}) collective-permute-start(bf16[32,2176]{1,0:T(8,128)(2,1)S(1)} %get-tuple-element.56), channel_id=1, source_target_pairs={{0,1},{1,0},{2,6},{3,7},{4,5},{5,4},{6,2},{7,3},{8,9},{9,8},{10,14... | collective-permute-start | bytes 417800 | tf_op jit(solution)/shard_map/ppermute | solution.py:38
  14.8 1.6 %collective-permute-start.4 = (bf16[32,2176]{1,0:T(8,128)(2,1)S(1)}, bf16[32,2176]{1,0:T(8,128)(2,1)S(1)}, u32[]{:S(2)}, u32[]{:S(2)}) collective-permute-start(bf16[32,2176]{1,0:T(8,128)(2,1)S(1)} %get-tuple-element.56), channel_id=1, source_target_pairs={{0,8},{1,9},{2,10},{3,11},{4,12},{5,13},{6,14},{7,15},{8,0},{9,1},... | collective-permute-start | bytes 417800 | tf_op jit(solution)/shard_map/ppermute | solution.py:38
  16.4 2.6 %collective-permute-start.3 = (bf16[32,2176]{1,0:T(8,128)(2,1)S(1)}, bf16[32,2176]{1,0:T(8,128)(2,1)S(1)}, u32[]{:S(2)}, u32[]{:S(2)}) collective-permute-start(bf16[32,2176]{1,0:T(8,128)(2,1)S(1)} %get-tuple-element.56), channel_id=1, source_target_pairs={{0,16},{1,17},{2,18},{3,19},{4,20},{5,21},{6,22},{7,23},{8,24},{9,... | collective-permute-start | bytes 417800 | tf_op jit(solution)/shard_map/ppermute | solution.py:38
  19.0 1.6 %collective-permute-start.2 = (bf16[64,2176]{1,0:T(8,128)(2,1)S(1)}, bf16[64,2176]{1,0:T(8,128)(2,1)S(1)}, u32[]{:S(2)}, u32[]{:S(2)}) collective-permute-start(bf16[64,2176]{1,0:T(8,128)(2,1)S(1)} %get-tuple-element.114), channel_id=1, source_target_pairs={{0,4},{1,5},{2,3},{3,2},{4,0},{5,1},{6,7},{7,6},{8,12},{9,13},{10,... | collective-permute-start | bytes 835592 | tf_op jit(solution)/shard_map/ppermute | solution.py:38
  20.6 1.2 %collective-permute-done.4 = bf16[32,2176]{1,0:T(8,128)(2,1)S(1)} collective-permute-done((bf16[32,2176]{1,0:T(8,128)(2,1)S(1)}, bf16[32,2176]{1,0:T(8,128)(2,1)S(1)}, u32[]{:S(2)}, u32[]{:S(2)}) %collective-permute-start.4) | collective-permute-done | bytes 139296 | tf_op jit(solution)/shard_map/ppermute | solution.py:38
  22.7 2.4 %collective-permute-done.3 = bf16[32,2176]{1,0:T(8,128)(2,1)S(1)} collective-permute-done((bf16[32,2176]{1,0:T(8,128)(2,1)S(1)}, bf16[32,2176]{1,0:T(8,128)(2,1)S(1)}, u32[]{:S(2)}, u32[]{:S(2)}) %collective-permute-start.3) | collective-permute-done | bytes 139296 | tf_op jit(solution)/shard_map/ppermute | solution.py:38
  25.4 0.9 %collective-permute-start.6 = (bf16[32,2176]{1,0:T(8,128)(2,1)S(1)}, bf16[32,2176]{1,0:T(8,128)(2,1)S(1)}, u32[]{:S(2)}, u32[]{:S(2)}) collective-permute-start(bf16[32,2176]{1,0:T(8,128)(2,1)S(1)} %collective-permute-done.3), channel_id=1, source_target_pairs={{0,1},{1,0},{2,6},{3,7},{4,5},{5,4},{6,2},{7,3},{8,9},{9,8},{10,14... | collective-permute-start | bytes 417800 | tf_op jit(solution)/shard_map/ppermute | solution.py:38
  26.9 1.4 %collective-permute-start.12 = (bf16[64,2176]{1,0:T(8,128)(2,1)S(1)}, bf16[64,2176]{1,0:T(8,128)(2,1)S(1)}, u32[]{:S(2)}, u32[]{:S(2)}) collective-permute-start(bf16[64,2176]{1,0:T(8,128)(2,1)S(1)} %get-tuple-element.110), channel_id=1, source_target_pairs={{0,4},{1,5},{2,3},{3,2},{4,0},{5,1},{6,7},{7,6},{8,12},{9,13},{10,... | collective-permute-start | bytes 835592 | tf_op jit(solution)/shard_map/ppermute | solution.py:38
  28.3 1.8 %collective-permute-done.7 = bf16[32,2176]{1,0:T(8,128)(2,1)S(1)} collective-permute-done((bf16[32,2176]{1,0:T(8,128)(2,1)S(1)}, bf16[32,2176]{1,0:T(8,128)(2,1)S(1)}, u32[]{:S(2)}, u32[]{:S(2)}) %collective-permute-start.7) | collective-permute-done | bytes 139296 | tf_op jit(solution)/shard_map/ppermute | solution.py:38
  31.6 2.7 %expert_half.4 = (bf16[128,2048]{1,0:T(8,128)(2,1)S(1)}, bf16[128,2048]{1,0:T(8,128)(2,1)S(1)}) custom-call(bf16[128,2176]{1,0:T(8,128)(2,1)S(1)} %constant_dynamic-update-slice_fusion.2.near_ref, bf16[128,2176]{1,0:T(8,128)(2,1)S(1)} %collective-permute-done.5.far_ref, bf16[1,2048,768]{2,1,0:T(8,128)(2,1)S(1)} %get-tuple-element.64.gate_ref, ...), custom_call_target="tpu_custom_call" | custom-call | flops 2415919104 | bytes 2097152 | tf_op jit(solution)/shard_map/expert_half/pallas_call | solution.py:387
  35.0 1.8 %collective-permute-done.11 = bf16[32,2176]{1,0:T(8,128)(2,1)S(1)} collective-permute-done((bf16[32,2176]{1,0:T(8,128)(2,1)S(1)}, bf16[32,2176]{1,0:T(8,128)(2,1)S(1)}, u32[]{:S(2)}, u32[]{:S(2)}) %collective-permute-start.11) | collective-permute-done | bytes 139296 | tf_op jit(solution)/shard_map/ppermute | solution.py:38
  39.5 2.6 %expert_half.5 = (bf16[128,2048]{1,0:T(8,128)(2,1)S(1)}, bf16[128,2048]{1,0:T(8,128)(2,1)S(1)}) custom-call(bf16[128,2176]{1,0:T(8,128)(2,1)S(1)} %constant_dynamic-update-slice_fusion.9.near_ref, bf16[128,2176]{1,0:T(8,128)(2,1)S(1)} %collective-permute-done.16.far_ref, bf16[1,2048,768]{2,1,0:T(8,128)(2,1)S(1)} %get-tuple-element.64.gate_ref, ...), custom_call_target="tpu_custom_call" | custom-call | flops 2415919104 | bytes 2097152 | tf_op jit(solution)/shard_map/expert_half/pallas_call | solution.py:387
  42.1 1.3 %collective-permute-done.15 = bf16[64,2176]{1,0:T(8,128)(2,1)S(1)} collective-permute-done((bf16[64,2176]{1,0:T(8,128)(2,1)S(1)}, bf16[64,2176]{1,0:T(8,128)(2,1)S(1)}, u32[]{:S(2)}, u32[]{:S(2)}) %collective-permute-start.15) | collective-permute-done | bytes 278560 | tf_op jit(solution)/shard_map/ppermute | solution.py:38
  44.0 2.6 %expert_half.6 = (bf16[128,2048]{1,0:T(8,128)(2,1)S(1)}, bf16[128,2048]{1,0:T(8,128)(2,1)S(1)}) custom-call(bf16[128,2176]{1,0:T(8,128)(2,1)S(1)} %constant_dynamic-update-slice_fusion.14.near_ref, bf16[128,2176]{1,0:T(8,128)(2,1)S(1)} %collective-permute-done.14.far_ref, bf16[1,2048,768]{2,1,0:T(8,128)(2,1)S(1)} %get-tuple-element.64.gate_ref, ...), custom_call_target="tpu_custom_call" | custom-call | flops 2415919104 | bytes 2097152 | tf_op jit(solution)/shard_map/expert_half/pallas_call | solution.py:387
  46.9 0.9 %collective-permute-start.17 = (bf16[32,2048]{1,0:T(8,128)(2,1)S(1)}, bf16[32,2048]{1,0:T(8,128)(2,1)S(1)}, u32[]{:S(2)}, u32[]{:S(2)}) collective-permute-start(bf16[32,2048]{1,0:T(8,128)(2,1)S(1)} %slice.111), channel_id=1, source_target_pairs={{0,1},{1,0},{2,6},{3,7},{4,5},{5,4},{6,2},{7,3},{8,9},{9,8},{10,14... | collective-permute-start | bytes 393224 | tf_op jit(solution)/shard_map/ppermute | solution.py:38
  48.6 2.6 %expert_half.7 = (bf16[128,2048]{1,0:T(8,128)(2,1)S(1)}, bf16[128,2048]{1,0:T(8,128)(2,1)S(1)}) custom-call(bf16[128,2176]{1,0:T(8,128)(2,1)S(1)} %constant_dynamic-update-slice_fusion.17.near_ref, bf16[128,2176]{1,0:T(8,128)(2,1)S(1)} %collective-permute-done.18.far_ref, bf16[1,2048,768]{2,1,0:T(8,128)(2,1)S(1)} %get-tuple-element.64.gate_ref, ...), custom_call_target="tpu_custom_call" | custom-call | flops 2415919104 | bytes 2097152 | tf_op jit(solution)/shard_map/expert_half/pallas_call | solution.py:387
  51.5 1.6 %collective-permute-start.25 = (bf16[64,2048]{1,0:T(8,128)(2,1)S(1)}, bf16[64,2048]{1,0:T(8,128)(2,1)S(1)}, u32[]{:S(2)}, u32[]{:S(2)}) collective-permute-start(bf16[64,2048]{1,0:T(8,128)(2,1)S(1)} %slice.104), channel_id=1, source_target_pairs={{0,4},{1,5},{2,3},{3,2},{4,0},{5,1},{6,7},{7,6},{8,12},{9,13},{10,... | collective-permute-start | bytes 786440 | tf_op jit(solution)/shard_map/ppermute | solution.py:38
  53.1 1.4 %collective-permute-done.21 = bf16[64,2048]{1,0:T(8,128)(2,1)S(1)} collective-permute-done((bf16[64,2048]{1,0:T(8,128)(2,1)S(1)}, bf16[64,2048]{1,0:T(8,128)(2,1)S(1)}, u32[]{:S(2)}, u32[]{:S(2)}) %collective-permute-start.21) | collective-permute-done | bytes 262176 | tf_op jit(solution)/shard_map/ppermute | solution.py:38
  54.5 1.3 %collective-permute-start.24 = (bf16[32,2048]{1,0:T(8,128)(2,1)S(1)}, bf16[32,2048]{1,0:T(8,128)(2,1)S(1)}, u32[]{:S(2)}, u32[]{:S(2)}) collective-permute-start(bf16[32,2048]{1,0:T(8,128)(2,1)S(1)} %slice.110), channel_id=1, source_target_pairs={{0,1},{1,0},{2,6},{3,7},{4,5},{5,4},{6,2},{7,3},{8,9},{9,8},{10,14... | collective-permute-start | bytes 393224 | tf_op jit(solution)/shard_map/ppermute | solution.py:38
  55.9 2.6 %collective-permute-done.25 = bf16[64,2048]{1,0:T(8,128)(2,1)S(1)} collective-permute-done((bf16[64,2048]{1,0:T(8,128)(2,1)S(1)}, bf16[64,2048]{1,0:T(8,128)(2,1)S(1)}, u32[]{:S(2)}, u32[]{:S(2)}) %collective-permute-start.25) | collective-permute-done | bytes 262176 | tf_op jit(solution)/shard_map/ppermute | solution.py:38
  58.6 1.0 %collective-permute-done.24 = bf16[32,2048]{1,0:T(8,128)(2,1)S(1)} collective-permute-done((bf16[32,2048]{1,0:T(8,128)(2,1)S(1)}, bf16[32,2048]{1,0:T(8,128)(2,1)S(1)}, u32[]{:S(2)}, u32[]{:S(2)}) %collective-permute-start.24) | collective-permute-done | bytes 131104 | tf_op jit(solution)/shard_map/ppermute | solution.py:38
  59.5 1.5 %collective-permute-start.23 = (bf16[64,2048]{1,0:T(8,128)(2,1)S(1)}, bf16[64,2048]{1,0:T(8,128)(2,1)S(1)}, u32[]{:S(2)}, u32[]{:S(2)}) collective-permute-start(bf16[64,2048]{1,0:T(8,128)(2,1)S(1)} %slice.105), channel_id=1, source_target_pairs={{0,4},{1,5},{2,3},{3,2},{4,0},{5,1},{6,7},{7,6},{8,12},{9,13},{10,... | collective-permute-start | bytes 786440 | tf_op jit(solution)/shard_map/ppermute | solution.py:38
  61.0 1.2 %collective-permute-start.27 = (bf16[32,2048]{1,0:T(8,128)(2,1)S(1)}, bf16[32,2048]{1,0:T(8,128)(2,1)S(1)}, u32[]{:S(2)}, u32[]{:S(2)}) collective-permute-start(bf16[32,2048]{1,0:T(8,128)(2,1)S(1)} %slice.109), channel_id=1, source_target_pairs={{0,1},{1,0},{2,6},{3,7},{4,5},{5,4},{6,2},{7,3},{8,9},{9,8},{10,14... | collective-permute-start | bytes 393224 | tf_op jit(solution)/shard_map/ppermute | solution.py:38
  62.7 4.5 %collective-permute-done.23 = bf16[64,2048]{1,0:T(8,128)(2,1)S(1)} collective-permute-done((bf16[64,2048]{1,0:T(8,128)(2,1)S(1)}, bf16[64,2048]{1,0:T(8,128)(2,1)S(1)}, u32[]{:S(2)}, u32[]{:S(2)}) %collective-permute-start.23) | collective-permute-done | bytes 262176 | tf_op jit(solution)/shard_map/ppermute | solution.py:38
  67.3 0.9 %collective-permute-start.29 = (bf16[32,2048]{1,0:T(8,128)(2,1)S(1)}, bf16[32,2048]{1,0:T(8,128)(2,1)S(1)}, u32[]{:S(2)}, u32[]{:S(2)}) collective-permute-start(bf16[32,2048]{1,0:T(8,128)(2,1)S(1)} %slice.108), channel_id=1, source_target_pairs={{0,1},{1,0},{2,6},{3,7},{4,5},{5,4},{6,2},{7,3},{8,9},{9,8},{10,14... | collective-permute-start | bytes 393224 | tf_op jit(solution)/shard_map/ppermute | solution.py:38
  68.2 2.4 %collective-permute-start.28 = (bf16[32,2048]{1,0:T(8,128)(2,1)S(1)}, bf16[32,2048]{1,0:T(8,128)(2,1)S(1)}, u32[]{:S(2)}, u32[]{:S(2)}) collective-permute-start(bf16[32,2048]{1,0:T(8,128)(2,1)S(1)} %slice_add_fusion.5), channel_id=1, source_target_pairs={{0,16},{1,17},{2,18},{3,19},{4,20},{5,21},{6,22},{7,23},{8,24},{9,... | collective-permute-start | bytes 393224 | tf_op jit(solution)/shard_map/ppermute | solution.py:38
  70.6 1.7 %collective-permute-done.29 = bf16[32,2048]{1,0:T(8,128)(2,1)S(1)} collective-permute-done((bf16[32,2048]{1,0:T(8,128)(2,1)S(1)}, bf16[32,2048]{1,0:T(8,128)(2,1)S(1)}, u32[]{:S(2)}, u32[]{:S(2)}) %collective-permute-start.29) | collective-permute-done | bytes 131104 | tf_op jit(solution)/shard_map/ppermute | solution.py:38
  72.4 4.2 %collective-permute-start.30 = (bf16[32,2048]{1,0:T(8,128)(2,1)S(1)}, bf16[32,2048]{1,0:T(8,128)(2,1)S(1)}, u32[]{:S(2)}, u32[]{:S(2)}) collective-permute-start(bf16[32,2048]{1,0:T(8,128)(2,1)S(1)} %slice_add_fusion.4), channel_id=1, source_target_pairs={{0,24},{1,25},{2,26},{3,27},{4,28},{5,29},{6,30},{7,31},{8,16},{9,... | collective-permute-start | bytes 393224 | tf_op jit(solution)/shard_map/ppermute | solution.py:38
  76.6 3.5 %collective-permute-done.28 = bf16[32,2048]{1,0:T(8,128)(2,1)S(1)} collective-permute-done((bf16[32,2048]{1,0:T(8,128)(2,1)S(1)}, bf16[32,2048]{1,0:T(8,128)(2,1)S(1)}, u32[]{:S(2)}, u32[]{:S(2)}) %collective-permute-start.28) | collective-permute-done | bytes 131104 | tf_op jit(solution)/shard_map/ppermute | solution.py:38
  (80 shorter events, 10.8 us)
Async XLA Ops:
  6.2 6.9 %copy-start = (bf16[32,2048]{1,0:T(8,128)(2,1)S(1)}, bf16[32,2048]{1,0:T(8,128)(2,1)}, u32[]{:S(2)}) copy-start(bf16[32,2048]{1,0:T(8,128)(2,1)} %residual_ref.1) | copy-start | bytes 393220
  6.2 6.8 %collective-permute-start = (bf16[32,2048]{1,0:T(8,128)(2,1)S(1)}, bf16[32,2048]{1,0:T(8,128)(2,1)S(1)}, u32[]{:S(2)}, u32[]{:S(2)}) collective-permute-start(bf16[32,2048]{1,0:T(8,128)(2,1)S(1)} %get-tuple-element.54.refs_3_), channel_id=1, source_target_pairs={{0,1},{1,0},{2,3},{3,2},{4,5},{5,4},{6,7},{7,6},{8,9},{9,8},{10,11... | collective-permute-start | bytes 393224 | tf_op jit(solution)/shard_map/ppermute | solution.py:33
  13.3 5.7 %collective-permute-start.1 = (bf16[32,2176]{1,0:T(8,128)(2,1)S(1)}, bf16[32,2176]{1,0:T(8,128)(2,1)S(1)}, u32[]{:S(2)}, u32[]{:S(2)}) collective-permute-start(bf16[32,2176]{1,0:T(8,128)(2,1)S(1)} %get-tuple-element.56), channel_id=1, source_target_pairs={{0,1},{1,0},{2,6},{3,7},{4,5},{5,4},{6,2},{7,3},{8,9},{9,8},{10,14... | collective-permute-start | bytes 417800 | tf_op jit(solution)/shard_map/ppermute | solution.py:38
  14.8 7.1 %collective-permute-start.4 = (bf16[32,2176]{1,0:T(8,128)(2,1)S(1)}, bf16[32,2176]{1,0:T(8,128)(2,1)S(1)}, u32[]{:S(2)}, u32[]{:S(2)}) collective-permute-start(bf16[32,2176]{1,0:T(8,128)(2,1)S(1)} %get-tuple-element.56), channel_id=1, source_target_pairs={{0,8},{1,9},{2,10},{3,11},{4,12},{5,13},{6,14},{7,15},{8,0},{9,1},... | collective-permute-start | bytes 417800 | tf_op jit(solution)/shard_map/ppermute | solution.py:38
  16.4 8.7 %collective-permute-start.3 = (bf16[32,2176]{1,0:T(8,128)(2,1)S(1)}, bf16[32,2176]{1,0:T(8,128)(2,1)S(1)}, u32[]{:S(2)}, u32[]{:S(2)}) collective-permute-start(bf16[32,2176]{1,0:T(8,128)(2,1)S(1)} %get-tuple-element.56), channel_id=1, source_target_pairs={{0,16},{1,17},{2,18},{3,19},{4,20},{5,21},{6,22},{7,23},{8,24},{9,... | collective-permute-start | bytes 417800 | tf_op jit(solution)/shard_map/ppermute | solution.py:38
  19.0 7.3 %collective-permute-start.2 = (bf16[64,2176]{1,0:T(8,128)(2,1)S(1)}, bf16[64,2176]{1,0:T(8,128)(2,1)S(1)}, u32[]{:S(2)}, u32[]{:S(2)}) collective-permute-start(bf16[64,2176]{1,0:T(8,128)(2,1)S(1)} %get-tuple-element.114), channel_id=1, source_target_pairs={{0,4},{1,5},{2,3},{3,2},{4,0},{5,1},{6,7},{7,6},{8,12},{9,13},{10,... | collective-permute-start | bytes 835592 | tf_op jit(solution)/shard_map/ppermute | solution.py:38
  21.8 5.1 %collective-permute-start.8 = (bf16[32,2176]{1,0:T(8,128)(2,1)S(1)}, bf16[32,2176]{1,0:T(8,128)(2,1)S(1)}, u32[]{:S(2)}, u32[]{:S(2)}) collective-permute-start(bf16[32,2176]{1,0:T(8,128)(2,1)S(1)} %collective-permute-done.4), channel_id=1, source_target_pairs={{0,1},{1,0},{2,6},{3,7},{4,5},{5,4},{6,2},{7,3},{8,9},{9,8},{10,14... | collective-permute-start | bytes 417800 | tf_op jit(solution)/shard_map/ppermute | solution.py:38
  25.1 5.1 %collective-permute-start.7 = (bf16[32,2176]{1,0:T(8,128)(2,1)S(1)}, bf16[32,2176]{1,0:T(8,128)(2,1)S(1)}, u32[]{:S(2)}, u32[]{:S(2)}) collective-permute-start(bf16[32,2176]{1,0:T(8,128)(2,1)S(1)} %collective-permute-done.3), channel_id=1, source_target_pairs={{0,8},{1,9},{2,10},{3,11},{4,12},{5,13},{6,14},{7,15},{8,0},{9,1},... | collective-permute-start | bytes 417800 | tf_op jit(solution)/shard_map/ppermute | solution.py:38
  25.4 5.9 %collective-permute-start.6 = (bf16[32,2176]{1,0:T(8,128)(2,1)S(1)}, bf16[32,2176]{1,0:T(8,128)(2,1)S(1)}, u32[]{:S(2)}, u32[]{:S(2)}) collective-permute-start(bf16[32,2176]{1,0:T(8,128)(2,1)S(1)} %collective-permute-done.3), channel_id=1, source_target_pairs={{0,1},{1,0},{2,6},{3,7},{4,5},{5,4},{6,2},{7,3},{8,9},{9,8},{10,14... | collective-permute-start | bytes 417800 | tf_op jit(solution)/shard_map/ppermute | solution.py:38
  26.4 5.3 %collective-permute-start.5 = (bf16[128,2176]{1,0:T(8,128)(2,1)S(1)}, bf16[128,2176]{1,0:T(8,128)(2,1)S(1)}, u32[]{:S(2)}, u32[]{:S(2)}) collective-permute-start(bf16[128,2176]{1,0:T(8,128)(2,1)S(1)} %constant_dynamic-update-slice_fusion.2.near_ref), channel_id=1, source_target_pairs={{0,2},{1,3},{2,0},{3,1},{4,6},{5,7},{6,4},{7,5},{8,10},{9,11},{10,... | collective-permute-start | bytes 1671176 | tf_op jit(solution)/shard_map/ppermute | solution.py:38
  26.9 8.0 %collective-permute-start.12 = (bf16[64,2176]{1,0:T(8,128)(2,1)S(1)}, bf16[64,2176]{1,0:T(8,128)(2,1)S(1)}, u32[]{:S(2)}, u32[]{:S(2)}) collective-permute-start(bf16[64,2176]{1,0:T(8,128)(2,1)S(1)} %get-tuple-element.110), channel_id=1, source_target_pairs={{0,4},{1,5},{2,3},{3,2},{4,0},{5,1},{6,7},{7,6},{8,12},{9,13},{10,... | collective-permute-start | bytes 835592 | tf_op jit(solution)/shard_map/ppermute | solution.py:38
  30.2 6.6 %collective-permute-start.11 = (bf16[32,2176]{1,0:T(8,128)(2,1)S(1)}, bf16[32,2176]{1,0:T(8,128)(2,1)S(1)}, u32[]{:S(2)}, u32[]{:S(2)}) collective-permute-start(bf16[32,2176]{1,0:T(8,128)(2,1)S(1)} %collective-permute-done.7), channel_id=1, source_target_pairs={{0,1},{1,0},{2,6},{3,7},{4,5},{5,4},{6,2},{7,3},{8,9},{9,8},{10,14... | collective-permute-start | bytes 417800 | tf_op jit(solution)/shard_map/ppermute | solution.py:38
  31.3 6.6 %collective-permute-start.10 = (bf16[64,2176]{1,0:T(8,128)(2,1)S(1)}, bf16[64,2176]{1,0:T(8,128)(2,1)S(1)}, u32[]{:S(2)}, u32[]{:S(2)}) collective-permute-start(bf16[64,2176]{1,0:T(8,128)(2,1)S(1)} %get-tuple-element.102), channel_id=1, source_target_pairs={{0,4},{1,5},{2,3},{3,2},{4,0},{5,1},{6,7},{7,6},{8,12},{9,13},{10,... | collective-permute-start | bytes 835592 | tf_op jit(solution)/shard_map/ppermute | solution.py:38
  35.0 4.5 %collective-permute-start.16 = (bf16[128,2176]{1,0:T(8,128)(2,1)S(1)}, bf16[128,2176]{1,0:T(8,128)(2,1)S(1)}, u32[]{:S(2)}, u32[]{:S(2)}) collective-permute-start(bf16[128,2176]{1,0:T(8,128)(2,1)S(1)} %constant_dynamic-update-slice_fusion.9.near_ref), channel_id=1, source_target_pairs={{0,2},{1,3},{2,0},{3,1},{4,6},{5,7},{6,4},{7,5},{8,10},{9,11},{10,... | collective-permute-start | bytes 1671176 | tf_op jit(solution)/shard_map/ppermute | solution.py:38
  36.8 1.9 %collective-permute-start.9 = (bf16[128,2048]{1,0:T(8,128)(2,1)S(1)}, bf16[128,2048]{1,0:T(8,128)(2,1)S(1)}, u32[]{:S(2)}, u32[]{:S(2)}) collective-permute-start(bf16[128,2048]{1,0:T(8,128)(2,1)S(1)} %get-tuple-element.69), channel_id=1, source_target_pairs={{0,2},{1,3},{2,0},{3,1},{4,6},{5,7},{6,4},{7,5},{8,10},{9,11},{10,... | collective-permute-start | bytes 1572872 | tf_op jit(solution)/shard_map/ppermute | solution.py:38
  36.8 6.6 %collective-permute-start.15 = (bf16[64,2176]{1,0:T(8,128)(2,1)S(1)}, bf16[64,2176]{1,0:T(8,128)(2,1)S(1)}, u32[]{:S(2)}, u32[]{:S(2)}) collective-permute-start(bf16[64,2176]{1,0:T(8,128)(2,1)S(1)} %get-tuple-element.105), channel_id=1, source_target_pairs={{0,4},{1,5},{2,3},{3,2},{4,0},{5,1},{6,7},{7,6},{8,12},{9,13},{10,... | collective-permute-start | bytes 835592 | tf_op jit(solution)/shard_map/ppermute | solution.py:38
  38.0 5.6 %collective-permute-start.14 = (bf16[128,2176]{1,0:T(8,128)(2,1)S(1)}, bf16[128,2176]{1,0:T(8,128)(2,1)S(1)}, u32[]{:S(2)}, u32[]{:S(2)}) collective-permute-start(bf16[128,2176]{1,0:T(8,128)(2,1)S(1)} %constant_dynamic-update-slice_fusion.14.near_ref), channel_id=1, source_target_pairs={{0,2},{1,3},{2,0},{3,1},{4,6},{5,7},{6,4},{7,5},{8,10},{9,11},{10,... | collective-permute-start | bytes 1671176 | tf_op jit(solution)/shard_map/ppermute | solution.py:38
  38.9 8.0 %collective-permute-start.13 = (bf16[64,2048]{1,0:T(8,128)(2,1)S(1)}, bf16[64,2048]{1,0:T(8,128)(2,1)S(1)}, u32[]{:S(2)}, u32[]{:S(2)}) collective-permute-start(bf16[64,2048]{1,0:T(8,128)(2,1)S(1)} %slice.107), channel_id=1, source_target_pairs={{0,4},{1,5},{2,3},{3,2},{4,0},{5,1},{6,7},{7,6},{8,12},{9,13},{10,... | collective-permute-start | bytes 786440 | tf_op jit(solution)/shard_map/ppermute | solution.py:38
  43.5 5.1 %collective-permute-start.18 = (bf16[128,2176]{1,0:T(8,128)(2,1)S(1)}, bf16[128,2176]{1,0:T(8,128)(2,1)S(1)}, u32[]{:S(2)}, u32[]{:S(2)}) collective-permute-start(bf16[128,2176]{1,0:T(8,128)(2,1)S(1)} %constant_dynamic-update-slice_fusion.17.near_ref), channel_id=1, source_target_pairs={{0,2},{1,3},{2,0},{3,1},{4,6},{5,7},{6,4},{7,5},{8,10},{9,11},{10,... | collective-permute-start | bytes 1671176 | tf_op jit(solution)/shard_map/ppermute | solution.py:38
  43.6 4.3 %collective-permute-start.19 = (bf16[128,2048]{1,0:T(8,128)(2,1)S(1)}, bf16[128,2048]{1,0:T(8,128)(2,1)S(1)}, u32[]{:S(2)}, u32[]{:S(2)}) collective-permute-start(bf16[128,2048]{1,0:T(8,128)(2,1)S(1)} %get-tuple-element.81), channel_id=1, source_target_pairs={{0,2},{1,3},{2,0},{3,1},{4,6},{5,7},{6,4},{7,5},{8,10},{9,11},{10,... | collective-permute-start | bytes 1572872 | tf_op jit(solution)/shard_map/ppermute | solution.py:38
  46.7 4.5 %collective-permute-start.22 = (bf16[128,2048]{1,0:T(8,128)(2,1)S(1)}, bf16[128,2048]{1,0:T(8,128)(2,1)S(1)}, u32[]{:S(2)}, u32[]{:S(2)}) collective-permute-start(bf16[128,2048]{1,0:T(8,128)(2,1)S(1)} %get-tuple-element.88), channel_id=1, source_target_pairs={{0,2},{1,3},{2,0},{3,1},{4,6},{5,7},{6,4},{7,5},{8,10},{9,11},{10,... | collective-permute-start | bytes 1572872 | tf_op jit(solution)/shard_map/ppermute | solution.py:38
  46.9 20.3 %collective-permute-start.17 = (bf16[32,2048]{1,0:T(8,128)(2,1)S(1)}, bf16[32,2048]{1,0:T(8,128)(2,1)S(1)}, u32[]{:S(2)}, u32[]{:S(2)}) collective-permute-start(bf16[32,2048]{1,0:T(8,128)(2,1)S(1)} %slice.111), channel_id=1, source_target_pairs={{0,1},{1,0},{2,6},{3,7},{4,5},{5,4},{6,2},{7,3},{8,9},{9,8},{10,14... | collective-permute-start | bytes 393224 | tf_op jit(solution)/shard_map/ppermute | solution.py:38
  48.0 6.4 %collective-permute-start.21 = (bf16[64,2048]{1,0:T(8,128)(2,1)S(1)}, bf16[64,2048]{1,0:T(8,128)(2,1)S(1)}, u32[]{:S(2)}, u32[]{:S(2)}) collective-permute-start(bf16[64,2048]{1,0:T(8,128)(2,1)S(1)} %slice.106), channel_id=1, source_target_pairs={{0,4},{1,5},{2,3},{3,2},{4,0},{5,1},{6,7},{7,6},{8,12},{9,13},{10,... | collective-permute-start | bytes 786440 | tf_op jit(solution)/shard_map/ppermute | solution.py:38
  51.2 4.6 %collective-permute-start.20 = (bf16[128,2048]{1,0:T(8,128)(2,1)S(1)}, bf16[128,2048]{1,0:T(8,128)(2,1)S(1)}, u32[]{:S(2)}, u32[]{:S(2)}) collective-permute-start(bf16[128,2048]{1,0:T(8,128)(2,1)S(1)} %get-tuple-element.86), channel_id=1, source_target_pairs={{0,2},{1,3},{2,0},{3,1},{4,6},{5,7},{6,4},{7,5},{8,10},{9,11},{10,... | collective-permute-start | bytes 1572872 | tf_op jit(solution)/shard_map/ppermute | solution.py:38
  51.5 7.0 %collective-permute-start.25 = (bf16[64,2048]{1,0:T(8,128)(2,1)S(1)}, bf16[64,2048]{1,0:T(8,128)(2,1)S(1)}, u32[]{:S(2)}, u32[]{:S(2)}) collective-permute-start(bf16[64,2048]{1,0:T(8,128)(2,1)S(1)} %slice.104), channel_id=1, source_target_pairs={{0,4},{1,5},{2,3},{3,2},{4,0},{5,1},{6,7},{7,6},{8,12},{9,13},{10,... | collective-permute-start | bytes 786440 | tf_op jit(solution)/shard_map/ppermute | solution.py:38
  54.5 5.0 %collective-permute-start.24 = (bf16[32,2048]{1,0:T(8,128)(2,1)S(1)}, bf16[32,2048]{1,0:T(8,128)(2,1)S(1)}, u32[]{:S(2)}, u32[]{:S(2)}) collective-permute-start(bf16[32,2048]{1,0:T(8,128)(2,1)S(1)} %slice.110), channel_id=1, source_target_pairs={{0,1},{1,0},{2,6},{3,7},{4,5},{5,4},{6,2},{7,3},{8,9},{9,8},{10,14... | collective-permute-start | bytes 393224 | tf_op jit(solution)/shard_map/ppermute | solution.py:38
  59.5 7.6 %collective-permute-start.23 = (bf16[64,2048]{1,0:T(8,128)(2,1)S(1)}, bf16[64,2048]{1,0:T(8,128)(2,1)S(1)}, u32[]{:S(2)}, u32[]{:S(2)}) collective-permute-start(bf16[64,2048]{1,0:T(8,128)(2,1)S(1)} %slice.105), channel_id=1, source_target_pairs={{0,4},{1,5},{2,3},{3,2},{4,0},{5,1},{6,7},{7,6},{8,12},{9,13},{10,... | collective-permute-start | bytes 786440 | tf_op jit(solution)/shard_map/ppermute | solution.py:38
  61.0 6.3 %collective-permute-start.27 = (bf16[32,2048]{1,0:T(8,128)(2,1)S(1)}, bf16[32,2048]{1,0:T(8,128)(2,1)S(1)}, u32[]{:S(2)}, u32[]{:S(2)}) collective-permute-start(bf16[32,2048]{1,0:T(8,128)(2,1)S(1)} %slice.109), channel_id=1, source_target_pairs={{0,1},{1,0},{2,6},{3,7},{4,5},{5,4},{6,2},{7,3},{8,9},{9,8},{10,14... | collective-permute-start | bytes 393224 | tf_op jit(solution)/shard_map/ppermute | solution.py:38
  62.3 8.4 %collective-permute-start.26 = (bf16[32,2048]{1,0:T(8,128)(2,1)S(1)}, bf16[32,2048]{1,0:T(8,128)(2,1)S(1)}, u32[]{:S(2)}, u32[]{:S(2)}) collective-permute-start(bf16[32,2048]{1,0:T(8,128)(2,1)S(1)} %slice_add_fusion.6), channel_id=1, source_target_pairs={{0,8},{1,9},{2,10},{3,11},{4,12},{5,13},{6,14},{7,15},{8,0},{9,1},... | collective-permute-start | bytes 393224 | tf_op jit(solution)/shard_map/ppermute | solution.py:38
  67.3 5.0 %collective-permute-start.29 = (bf16[32,2048]{1,0:T(8,128)(2,1)S(1)}, bf16[32,2048]{1,0:T(8,128)(2,1)S(1)}, u32[]{:S(2)}, u32[]{:S(2)}) collective-permute-start(bf16[32,2048]{1,0:T(8,128)(2,1)S(1)} %slice.108), channel_id=1, source_target_pairs={{0,1},{1,0},{2,6},{3,7},{4,5},{5,4},{6,2},{7,3},{8,9},{9,8},{10,14... | collective-permute-start | bytes 393224 | tf_op jit(solution)/shard_map/ppermute | solution.py:38
  68.2 11.9 %collective-permute-start.28 = (bf16[32,2048]{1,0:T(8,128)(2,1)S(1)}, bf16[32,2048]{1,0:T(8,128)(2,1)S(1)}, u32[]{:S(2)}, u32[]{:S(2)}) collective-permute-start(bf16[32,2048]{1,0:T(8,128)(2,1)S(1)} %slice_add_fusion.5), channel_id=1, source_target_pairs={{0,16},{1,17},{2,18},{3,19},{4,20},{5,21},{6,22},{7,23},{8,24},{9,... | collective-permute-start | bytes 393224 | tf_op jit(solution)/shard_map/ppermute | solution.py:38
  72.4 7.7 %collective-permute-start.30 = (bf16[32,2048]{1,0:T(8,128)(2,1)S(1)}, bf16[32,2048]{1,0:T(8,128)(2,1)S(1)}, u32[]{:S(2)}, u32[]{:S(2)}) collective-permute-start(bf16[32,2048]{1,0:T(8,128)(2,1)S(1)} %slice_add_fusion.4), channel_id=1, source_target_pairs={{0,24},{1,25},{2,26},{3,27},{4,28},{5,29},{6,30},{7,31},{8,16},{9,... | collective-permute-start | bytes 393224 | tf_op jit(solution)/shard_map/ppermute | solution.py:38
  (4 other events, 21.2 us)

commit v5 on v4

--- a/solution.py
+++ b/solution.py
@@ -121,13 +121,14 @@
     queries_hbm,
     keys_hbm,
     values_hbm,
-    positions_ref,
+    positions_hbm,
     out_weight_hbm,
     kept_ref,
     given_ref,
     queries_ref,
     keys_ref,
     values_ref,
+    positions_ref,
     weight_ref,
     total_ref,
     input_sems,
@@ -137,7 +138,12 @@
     input_copies = [
         pltpu.make_async_copy(source, target, input_sems.at[place])
         for place, (source, target) in enumerate(
-            ((keys_hbm, keys_ref), (queries_hbm, queries_ref), (values_hbm, values_ref))
+            (
+                (positions_hbm, positions_ref),
+                (keys_hbm, keys_ref),
+                (queries_hbm, queries_ref),
+                (values_hbm, values_ref),
+            )
         )
     ]
     weight_copies = [
@@ -150,6 +156,8 @@
     ]
     for copy in input_copies + weight_copies:
         copy.start()
+    for copy in input_copies:
+        copy.wait()
     rows = queries_ref.shape[0]
     own_rows = kept_ref.shape[0]
     rank = lax.axis_index("tensor")
@@ -165,8 +173,6 @@
     score_scale = 1.0 / math.sqrt(HEAD_WIDTH)
     per_group = chunks // groups
     heads_chunk = group_heads // per_group
-    for copy in input_copies:
-        copy.wait()
     for group in range(groups):
         place = pl.multiple_of((rank * groups + group) * HEAD_WIDTH, HEAD_WIDTH)
         key = keys_ref[:, pl.ds(place, HEAD_WIDTH)]
@@ -218,7 +224,7 @@
     far = pl.BlockSpec(memory_space=pltpu.HBM)
     return pl.pallas_call(
         attention_kernel,
-        in_specs=[far, far, far, near, far],
+        in_specs=[far] * 5,
         out_specs=[near] * 2,
         out_shape=[
             jax.ShapeDtypeStruct((rows // 2, D), jnp.float32),
@@ -228,9 +234,10 @@
             pltpu.VMEM(queries.shape, queries.dtype),
             pltpu.VMEM(keys.shape, keys.dtype),
             pltpu.VMEM(values.shape, values.dtype),
+            pltpu.VMEM((1, rows), positions.dtype),
             pltpu.VMEM((chunks, width // chunks, D), jnp.bfloat16),
             pltpu.VMEM((rows, D), jnp.float32),
-            pltpu.SemaphoreType.DMA((3,)),
+            pltpu.SemaphoreType.DMA((4,)),
             pltpu.SemaphoreType.DMA((chunks,)),
         ],
         compiler_params=pltpu.CompilerParams(vmem_limit_bytes=24 * 2**20),
@@ -241,9 +248,10 @@
         ),
         name="attention_halves",
     )(
-        *[pltpu.with_memory_space_constraint(x, pltpu.HBM) for x in (queries, keys, values)],
-        positions.reshape(1, rows),
-        pltpu.with_memory_space_constraint(out_weight, pltpu.HBM),
+        *[
+            pltpu.with_memory_space_constraint(x, pltpu.HBM)
+            for x in (queries, keys, values, positions.reshape(1, rows), out_weight)
+        ]
     )
 
 
@@ -342,65 +350,61 @@
     )(kept, taken, residual, norm_gain.reshape(1, D), routes.T, route_probs.T)
 
 
-def expert_kernel(
-    near_ref,
-    far_ref,
-    gate_ref,
-    up_ref,
-    down_ref,
-    near_out_ref,
-    far_out_ref,
-    feed_ref,
-    hidden_ref,
-):
-    rows = near_ref.shape[0]
-    units = gate_ref.shape[2]
+def expert_kernel(rows_ref, *refs):
+    weights, (kept_ref, given_ref, hidden_ref) = (refs[:3], refs[3:6]), refs[6:]
+    units = weights[0][0].shape[2]
     lane = lax.broadcasted_iota(jnp.int32, (1, LANES), 1)
     mine = lax.axis_index("expert")
-    pick = jnp.where((lane == mine) | (lane == mine + lax.axis_size("expert")), 1.0, 0.0)
-    weights = []
-    for place, source in enumerate((near_ref, far_ref)):
-        feed_ref[place * rows : (place + 1) * rows, :] = source[:, :D]
-        weights.append(
-            jnp.sum(source[:, D:].astype(jnp.float32) * pick, axis=1, keepdims=True)
-        )
-    weight = jnp.concatenate(weights, axis=0)
-    for first in range(0, units, FIRST_BLOCK):
-        cols = slice(first, first + FIRST_BLOCK)
-        gate = jnp.dot(feed_ref[...], gate_ref[0, :, cols], preferred_element_type=jnp.float32)
-        up = jnp.dot(feed_ref[...], up_ref[0, :, cols], preferred_element_type=jnp.float32)
-        hidden = gate / (1.0 + jnp.exp(-gate)) * up * weight
-        hidden_ref[:, cols] = hidden.astype(jnp.bfloat16)
+    expert_size = lax.axis_size("expert")
+    table = rows_ref[:, D:].astype(jnp.float32)
+    for place, (gate_ref, up_ref, _) in enumerate(weights):
+        number = mine if place == 0 else mine + 1 - 2 * (mine % 2)
+        pick = jnp.where((lane == number) | (lane == number + expert_size), 1.0, 0.0)
+        weight = jnp.sum(table * pick, axis=1, keepdims=True)
+        for first in range(0, units, FIRST_BLOCK):
+            cols = slice(first, first + FIRST_BLOCK)
+            feed = rows_ref[:, :D]
+            gate = jnp.dot(feed, gate_ref[0, :, cols], preferred_element_type=jnp.float32)
+            up = jnp.dot(feed, up_ref[0, :, cols], preferred_element_type=jnp.float32)
+            hidden = gate / (1.0 + jnp.exp(-gate)) * up * weight
+            target = slice(place * units + first, place * units + first + FIRST_BLOCK)
+            hidden_ref[:, target] = hidden.astype(jnp.bfloat16)
+    half = kept_ref.shape[0]
     for first in range(0, D, SECOND_BLOCK):
         cols = slice(first, first + SECOND_BLOCK)
-        part = jnp.dot(
-            hidden_ref[...], down_ref[0, :, cols], preferred_element_type=jnp.float32
-        ).astype(jnp.bfloat16)
-        near_out_ref[:, cols] = part[:rows]
-        far_out_ref[:, cols] = part[rows:]
-
-
-def weighted_expert(near, far, weights):
-    rows = near.shape[0]
+        part = None
+        for place, (_, _, down_ref) in enumerate(weights):
+            product = jnp.dot(
+                hidden_ref[:, place * units : (place + 1) * units],
+                down_ref[0, :, cols],
+                preferred_element_type=jnp.float32,
+            )
+            part = product if part is None else part + product
+        kept_ref[:, cols] = part[:half]
+        given_ref[:, cols] = part[half:].astype(jnp.bfloat16)
+
+
+def weighted_experts(rows, weights):
+    count = rows.shape[0]
     units = weights[0].shape[2]
     whole = pl.BlockSpec(memory_space=pltpu.VMEM)
     return pl.pallas_call(
         expert_kernel,
-        in_specs=[whole] * 5,
+        in_specs=[whole] * 7,
         out_specs=[whole] * 2,
-        out_shape=[jax.ShapeDtypeStruct((rows, D), jnp.bfloat16)] * 2,
-        scratch_shapes=[
-            pltpu.VMEM((2 * rows, D), jnp.bfloat16),
-            pltpu.VMEM((2 * rows, units), jnp.bfloat16),
+        out_shape=[
+            jax.ShapeDtypeStruct((count // 2, D), jnp.float32),
+            jax.ShapeDtypeStruct((count // 2, D), jnp.bfloat16),
         ],
+        scratch_shapes=[pltpu.VMEM((count, 2 * units), jnp.bfloat16)],
         compiler_params=pltpu.CompilerParams(vmem_limit_bytes=12 * 2**20),
         cost_estimate=pl.CostEstimate(
-            flops=2 * 2 * rows * 3 * D * units,
-            bytes_accessed=8 * rows * D,
-            transcendentals=2 * rows * units,
+            flops=2 * 2 * count * 3 * D * units,
+            bytes_accessed=8 * count * D,
+            transcendentals=2 * count * units,
         ),
-        name="expert_half",
-    )(near, far, *[pltpu.with_memory_space_constraint(w, pltpu.VMEM) for w in weights])
+        name="expert_halves",
+    )(rows, *[pltpu.with_memory_space_constraint(w, pltpu.VMEM) for w in weights])
 
 
 class Order:
@@ -426,8 +430,8 @@
         then.last = jnp.concatenate([rows, then(taken)], axis=0)
         return then.last
 
-    def expert(near, far):
-        outs = weighted_expert(near, then(far), weights)
+    def expert(rows):
+        outs = weighted_experts(rows, weights)
         then.last = outs[0]
         return outs
 
@@ -445,6 +449,7 @@
     taken_0 = exchanged(then.after(block), NEAR_PLANE)
     set_1 = exchanged(then.after(block), NEAR_LINE)
     set_2 = exchanged(then.after(block), FAR_LINE)
+    taken_0, weights = lax.optimization_barrier((taken_0, weights))
     pair_0 = joined(block, taken_0)
     taken_0 = exchanged(then.after(pair_0), FAR_PLANE)
     set_1 = then(set_1)
@@ -453,48 +458,36 @@
     set_3 = exchanged(then.after(set_2), NEAR_LINE)
     taken_2 = exchanged(then.after(set_2), NEAR_PLANE)
     quad_0 = joined(pair_0, taken_0)
-    other_0 = exchanged(then.after(quad_0), CORE)
     pair_1 = joined(set_1, taken_1)
     taken_1 = exchanged(then.after(pair_1), FAR_PLANE)
     set_3 = then(set_3)
     taken_3 = exchanged(then.after(set_3), NEAR_PLANE)
     pair_2 = joined(set_2, taken_2)
     taken_2 = exchanged(then.after(pair_2), FAR_PLANE)
-    mine_0, back_0 = expert(quad_0, other_0)
-    back_0 = exchanged(then.after(back_0), CORE)
-    quad_1 = joined(pair_1, taken_1)
-    other_1 = exchanged(then.after(quad_1), CORE)
+    kept_0, given_0 = expert(quad_0)
     pair_3 = joined(set_3, taken_3)
     taken_3 = exchanged(then.after(pair_3), FAR_PLANE)
+    sent_0 = exchanged(then.after(given_0), FAR_PLANE)
+    quad_1 = joined(pair_1, taken_1)
+    kept_1, given_1 = expert(quad_1)
+    sent_1 = exchanged(then.after(given_1), FAR_PLANE)
     quad_2 = joined(pair_2, taken_2)
-    other_2 = exchanged(then.after(quad_2), CORE)
-    total_0 = added(widened(mine_0), back_0)
-    sent_0 = sent(then.after(total_0), FAR_PLANE)
-    mine_1, back_1 = expert(quad_1, other_1)
-    back_1 = exchanged(then.after(back_1), CORE)
+    kept_2, given_2 = expert(quad_2)
+    sent_2 = exchanged(then.after(given_2), FAR_PLANE)
+    total_0 = added(kept_0, sent_0)
+    sent_0 = sent(then.after(total_0), NEAR_PLANE)
     quad_3 = joined(pair_3, taken_3)
-    other_3 = exchanged(then.after(quad_3), CORE)
-    mine_2, back_2 = expert(quad_2, other_2)
-    back_2 = exchanged(then.after(back_2), CORE)
+    kept_3, given_3 = expert(quad_3)
+    sent_3 = exchanged(then.after(given_3), FAR_PLANE)
+    total_1 = added(kept_1, sent_1)
+    sent_1 = sent(then.after(total_1), NEAR_PLANE)
     total_0 = added(kept(total_0), sent_0)
-    sent_0 = sent(then.after(total_0), NEAR_PLANE)
-    total_1 = added(widened(mine_1), back_1)
-    sent_1 = sent(then.after(total_1), FAR_PLANE)
-    mine_3, back_3 = expert(quad_3, other_3)
-    back_3 = exchanged(then.after(back_3), CORE)
-    total_2 = added(widened(mine_2), back_2)
-    sent_2 = sent(then.after(total_2), FAR_PLANE)
-    total_1 = added(kept(total_1), sent_1)
-    sent_1 = sent(then.after(total_1), NEAR_PLANE)
-    total_3 = added(widened(mine_3), back_3)
-    sent_3 = sent(then.after(total_3), FAR_PLANE)
-    total_2 = added(kept(total_2), sent_2)
+    total_2 = added(kept_2, sent_2)
     sent_2 = sent(then.after(total_2), NEAR_PLANE)
     total_1 = added(kept(total_1), sent_1)
     home_1 = exchanged(narrowed(then.after(total_1)), NEAR_LINE)
-    total_3 = added(kept(total_3), sent_3)
+    total_3 = added(kept_3, sent_3)
     sent_3 = sent(then.after(total_3), NEAR_PLANE)
-    total_0 = added(kept(total_0), sent_0)
     total_2 = added(kept(total_2), sent_2)
     home_2 = exchanged(narrowed(then.after(total_2)), FAR_LINE)
     home_1 = then(home_1)
@@ -573,9 +566,15 @@
     token_rows = queries.shape[0] // tensor_size
     if tensor_size == 2 and expert_size == 16:
         kept, given = attention_halves(queries, keys, values, positions, out_weight)
-        weights = loaded((gate_weight, up_weight, down_weight), given)
+        weights = (gate_weight, up_weight, down_weight)
+        others = tuple(exchanged(weight, CORE) for weight in weights)
+        taken = swapped(given, "tensor", 0)
+        weights = loaded(weights, given)
+        *others, last = others
+        taken, weights, others = lax.optimization_barrier((taken, weights, others))
+        weights = (*weights, *others, last)
         middle_own, block = normed_block(
-            kept, swapped(given, "tensor", 0), residual, norm_gain, routes, route_probs
+            kept, taken, residual, norm_gain, routes, route_probs
         )
         return dense_experts(middle_own, block, weights)
     own_routes = lax.dynamic_slice_in_dim(routes, tensor_rank * token_rows, token_rows, 0)

time: 81.2 us -> 76.2 us (0.938)
  starting transfers between devices: 32 us -> 27.6 us
  local copies, waits for them, and re-layouts: 1.16 us -> 0.22 us
    ppermute x30 -> x25, starting transfers between devices: 29 us -> 25.1 us  [exchanged(): lax.ppermute(shard, BOTH, [(i, i ^ masks[1 if i & BIT_CORE else 0]) for i...]
    ppermute x30 -> x25, waiting for transfers between devices: 25.7 us -> 25.8 us  [exchanged(): lax.ppermute(shard, BOTH, [(i, i ^ masks[1 if i & BIT_CORE else 0]) for i...]
  transfers between devices with their start and end apart: 31 -> 26, of which waited for: 16 -> 11; matrix products, arithmetic and copies ran while one was open for 2% -> 1% of each run, Pallas kernels for 18% -> 27%
where the time goes in v5:
time: 76.2 us; the launch traced here: 76.1 us
  starting transfers between devices  27.6 us (36%)
  waiting for transfers between devices  26.1 us (34%)
  Pallas kernels  20.6 us (27%)
  other arithmetic  1.2 us (2%)
    ppermute x25, waiting for transfers between devices, exchanged(): lax.ppermute(shard, BOTH, [(i, i ^ masks[1 if i & BIT_CORE else 0]) for i...  25.8 us
    ppermute x25, starting transfers between devices, exchanged(): lax.ppermute(shard, BOTH, [(i, i ^ masks[1 if i & BIT_CORE else 0]) for i...  25.1 us
    pallas_call x4, Pallas kernels, weighted_experts(): pl.pallas_call(expert_kernel, in_specs=[whole] * 7, out_specs=[whole] * 2...  11.1 us
    pallas_call x1, Pallas kernels, attention_halves(): pl.pallas_call(attention_kernel, in_specs=[far] * 5, out_specs=[near] * 2...  5.52 us
    pallas_call x1, Pallas kernels, loaded(): pl.pallas_call(functools.partial(load_kernel, len(weights), pieces), in_s...  3.79 us
    ppermute x1, starting transfers between devices, swapped(): lax.ppermute(shard, axis, [(i, i ^ 1 << distance) for i in range(lax.axis...  2.56 us
  transfers between devices with their start and end apart: 26, of which 11 were waited for; matrix products, arithmetic and copies ran while one was open for 1% of the time, Pallas kernels for 27%

profile of v5, /device:TPU:0, one launch (start us, length us, event | category | flops | bytes accessed | tf_op | source)
XLA Modules:
  0.0 76.1 jit_solution(16544633737542460775)
XLA Ops:
  1.0 5.5 %attention_halves.1 = (f32[32,2048]{1,0:T(8,128)S(1)}, bf16[32,2048]{1,0:T(8,128)(2,1)S(1)}) custom-call(bf16[64,2048]{1,0:T(8,128)(2,1)} %queries_hbm.1, bf16[64,512]{1,0:T(8,128)(2,1)} %keys_hbm.1, bf16[64,512]{1,0:T(8,128)(2,1)} %values_hbm.1, s32[1,64]{1,0:T(1,128)} %bitcast.7, bf16[2048,2048]{1,0:T(8,128)(2,1)} %out_weight_hbm.1), custom_call_target="tpu_custom_call" | custom-call | flops 570425344 | bytes 8388608 | tf_op jit(solution)/shard_map/attention_halves/pallas_call | solution.py:225
  6.5 2.6 %collective-permute-start = (bf16[32,2048]{1,0:T(8,128)(2,1)S(1)}, bf16[32,2048]{1,0:T(8,128)(2,1)S(1)}, u32[]{:S(2)}, u32[]{:S(2)}) collective-permute-start(bf16[32,2048]{1,0:T(8,128)(2,1)S(1)} %get-tuple-element.59.refs_3_), channel_id=1, source_target_pairs={{0,1},{1,0},{2,3},{3,2},{4,5},{5,4},{6,7},{7,6},{8,9},{9,8},{10,11... | collective-permute-start | bytes 393224 | tf_op jit(solution)/shard_map/ppermute | solution.py:33
  9.1 3.8 %load_weights.1 = (bf16[1,2048,768]{2,1,0:T(8,128)(2,1)S(1)}, bf16[1,2048,768]{2,1,0:T(8,128)(2,1)S(1)}, bf16[1,768,2048]{2,1,0:T(8,128)(2,1)S(1)}) custom-call(bf16[1,2048,768]{2,1,0:T(8,128)(2,1)} %refs_0_.1, bf16[1,2048,768]{2,1,0:T(8,128)(2,1)} %refs_1_.1, bf16[1,768,2048]{2,1,0:T(8,128)(2,1)} %refs_2_.1, bf16[32,2048]{1,0:T(8,128)(2,1)S(1)} %get-tuple-element.59.refs_3_), custom_call_target="tpu_custom_call" | custom-call | bytes 9437184 | tf_op jit(solution)/shard_map/load_weights/pallas_call | solution.py:281
  13.5 2.9 %collective-permute-start.6 = (bf16[32,2176]{1,0:T(8,128)(2,1)S(1)}, bf16[32,2176]{1,0:T(8,128)(2,1)S(1)}, u32[]{:S(2)}, u32[]{:S(2)}) collective-permute-start(bf16[32,2176]{1,0:T(8,128)(2,1)S(1)} %get-tuple-element.65), channel_id=1, source_target_pairs={{0,16},{1,17},{2,18},{3,19},{4,20},{5,21},{6,22},{7,23},{8,24},{9,... | collective-permute-start | bytes 417800 | tf_op jit(solution)/shard_map/ppermute | solution.py:38
  16.4 1.6 %collective-permute-start.7 = (bf16[32,2176]{1,0:T(8,128)(2,1)S(1)}, bf16[32,2176]{1,0:T(8,128)(2,1)S(1)}, u32[]{:S(2)}, u32[]{:S(2)}) collective-permute-start(bf16[32,2176]{1,0:T(8,128)(2,1)S(1)} %get-tuple-element.65), channel_id=1, source_target_pairs={{0,8},{1,9},{2,10},{3,11},{4,12},{5,13},{6,14},{7,15},{8,0},{9,1},... | collective-permute-start | bytes 417800 | tf_op jit(solution)/shard_map/ppermute | solution.py:38
  18.0 1.5 %collective-permute-start.3 = (bf16[32,2176]{1,0:T(8,128)(2,1)S(1)}, bf16[32,2176]{1,0:T(8,128)(2,1)S(1)}, u32[]{:S(2)}, u32[]{:S(2)}) collective-permute-start(bf16[32,2176]{1,0:T(8,128)(2,1)S(1)} %get-tuple-element.65), channel_id=1, source_target_pairs={{0,1},{1,0},{2,6},{3,7},{4,5},{5,4},{6,2},{7,3},{8,9},{9,8},{10,14... | collective-permute-start | bytes 417800 | tf_op jit(solution)/shard_map/ppermute | solution.py:38
  19.5 3.5 %collective-permute-done.3 = bf16[32,2176]{1,0:T(8,128)(2,1)S(1)} collective-permute-done((bf16[32,2176]{1,0:T(8,128)(2,1)S(1)}, bf16[32,2176]{1,0:T(8,128)(2,1)S(1)}, u32[]{:S(2)}, u32[]{:S(2)}) %collective-permute-start.3) | collective-permute-done | bytes 139296 | tf_op jit(solution)/shard_map/ppermute | solution.py:38
  23.1 1.6 %collective-permute-start.5 = (bf16[64,2176]{1,0:T(8,128)(2,1)S(1)}, bf16[64,2176]{1,0:T(8,128)(2,1)S(1)}, u32[]{:S(2)}, u32[]{:S(2)}) collective-permute-start(bf16[64,2176]{1,0:T(8,128)(2,1)S(1)} %get-tuple-element.112), channel_id=1, source_target_pairs={{0,4},{1,5},{2,3},{3,2},{4,0},{5,1},{6,7},{7,6},{8,12},{9,13},{10,... | collective-permute-start | bytes 835592 | tf_op jit(solution)/shard_map/ppermute | solution.py:38
  24.7 1.5 %collective-permute-start.9 = (bf16[32,2176]{1,0:T(8,128)(2,1)S(1)}, bf16[32,2176]{1,0:T(8,128)(2,1)S(1)}, u32[]{:S(2)}, u32[]{:S(2)}) collective-permute-start(bf16[32,2176]{1,0:T(8,128)(2,1)S(1)} %collective-permute-done.7), channel_id=1, source_target_pairs={{0,1},{1,0},{2,6},{3,7},{4,5},{5,4},{6,2},{7,3},{8,9},{9,8},{10,14... | collective-permute-start | bytes 417800 | tf_op jit(solution)/shard_map/ppermute | solution.py:38
  27.2 4.4 %collective-permute-done.5 = bf16[64,2176]{1,0:T(8,128)(2,1)S(1)} collective-permute-done((bf16[64,2176]{1,0:T(8,128)(2,1)S(1)}, bf16[64,2176]{1,0:T(8,128)(2,1)S(1)}, u32[]{:S(2)}, u32[]{:S(2)}) %collective-permute-start.5) | collective-permute-done | bytes 278560 | tf_op jit(solution)/shard_map/ppermute | solution.py:38
  31.7 2.3 %collective-permute-start.10 = (bf16[32,2176]{1,0:T(8,128)(2,1)S(1)}, bf16[32,2176]{1,0:T(8,128)(2,1)S(1)}, u32[]{:S(2)}, u32[]{:S(2)}) collective-permute-start(bf16[32,2176]{1,0:T(8,128)(2,1)S(1)} %collective-permute-done.8), channel_id=1, source_target_pairs={{0,1},{1,0},{2,6},{3,7},{4,5},{5,4},{6,2},{7,3},{8,9},{9,8},{10,14... | collective-permute-start | bytes 417800 | tf_op jit(solution)/shard_map/ppermute | solution.py:38
  34.4 1.7 %collective-permute-start.13 = (bf16[64,2176]{1,0:T(8,128)(2,1)S(1)}, bf16[64,2176]{1,0:T(8,128)(2,1)S(1)}, u32[]{:S(2)}, u32[]{:S(2)}) collective-permute-start(bf16[64,2176]{1,0:T(8,128)(2,1)S(1)} %pad_maximum_fusion.3), channel_id=1, source_target_pairs={{0,4},{1,5},{2,3},{3,2},{4,0},{5,1},{6,7},{7,6},{8,12},{9,13},{10,... | collective-permute-start | bytes 835592 | tf_op jit(solution)/shard_map/ppermute | solution.py:38
  36.1 2.8 %expert_halves.4 = (f32[64,2048]{1,0:T(8,128)S(1)}, bf16[64,2048]{1,0:T(8,128)(2,1)S(1)}) custom-call(bf16[128,2176]{1,0:T(8,128)(2,1)S(1)} %constant_dynamic-update-slice_fusion.2.rows_ref, bf16[1,2048,768]{2,1,0:T(8,128)(2,1)S(1)} %get-tuple-element.75.refs_0_, bf16[1,2048,768]{2,1,0:T(8,128)(2,1)S(1)} %get-tuple-element.76.refs_1_, ...), custom_call_target="tpu_custom_call" | custom-call | flops 2415919104 | bytes 2097152 | tf_op jit(solution)/shard_map/expert_halves/pallas_call | solution.py:391
  38.9 2.0 %collective-permute-start.17 = (bf16[64,2176]{1,0:T(8,128)(2,1)S(1)}, bf16[64,2176]{1,0:T(8,128)(2,1)S(1)}, u32[]{:S(2)}, u32[]{:S(2)}) collective-permute-start(bf16[64,2176]{1,0:T(8,128)(2,1)S(1)} %constant_dynamic-update-slice_fusion.7), channel_id=1, source_target_pairs={{0,4},{1,5},{2,3},{3,2},{4,0},{5,1},{6,7},{7,6},{8,12},{9,13},{10,... | collective-permute-start | bytes 835592 | tf_op jit(solution)/shard_map/ppermute | solution.py:38
  41.0 2.7 %expert_halves.5 = (f32[64,2048]{1,0:T(8,128)S(1)}, bf16[64,2048]{1,0:T(8,128)(2,1)S(1)}) custom-call(bf16[128,2176]{1,0:T(8,128)(2,1)S(1)} %pad_maximum_fusion.rows_ref, bf16[1,2048,768]{2,1,0:T(8,128)(2,1)S(1)} %get-tuple-element.75.refs_0_, bf16[1,2048,768]{2,1,0:T(8,128)(2,1)S(1)} %get-tuple-element.76.refs_1_, ...), custom_call_target="tpu_custom_call" | custom-call | flops 2415919104 | bytes 2097152 | tf_op jit(solution)/shard_map/expert_halves/pallas_call | solution.py:391
  43.8 2.0 %collective-permute-start.16 = (bf16[64,2048]{1,0:T(8,128)(2,1)S(1)}, bf16[64,2048]{1,0:T(8,128)(2,1)S(1)}, u32[]{:S(2)}, u32[]{:S(2)}) collective-permute-start(bf16[64,2048]{1,0:T(8,128)(2,1)S(1)} %get-tuple-element.94), channel_id=1, source_target_pairs={{0,4},{1,5},{2,3},{3,2},{4,0},{5,1},{6,7},{7,6},{8,12},{9,13},{10,... | collective-permute-start | bytes 786440 | tf_op jit(solution)/shard_map/ppermute | solution.py:38
  45.8 2.7 %expert_halves.6 = (f32[64,2048]{1,0:T(8,128)S(1)}, bf16[64,2048]{1,0:T(8,128)(2,1)S(1)}) custom-call(bf16[128,2176]{1,0:T(8,128)(2,1)S(1)} %pad_maximum_fusion.1.rows_ref, bf16[1,2048,768]{2,1,0:T(8,128)(2,1)S(1)} %get-tuple-element.75.refs_0_, bf16[1,2048,768]{2,1,0:T(8,128)(2,1)S(1)} %get-tuple-element.76.refs_1_, ...), custom_call_target="tpu_custom_call" | custom-call | flops 2415919104 | bytes 2097152 | tf_op jit(solution)/shard_map/expert_halves/pallas_call | solution.py:391
  48.7 2.0 %collective-permute-done.11 = bf16[64,2048]{1,0:T(8,128)(2,1)S(1)} collective-permute-done((bf16[64,2048]{1,0:T(8,128)(2,1)S(1)}, bf16[64,2048]{1,0:T(8,128)(2,1)S(1)}, u32[]{:S(2)}, u32[]{:S(2)}) %collective-permute-start.11) | collective-permute-done | bytes 262176 | tf_op jit(solution)/shard_map/ppermute | solution.py:38
  51.3 2.9 %expert_halves.7 = (f32[64,2048]{1,0:T(8,128)S(1)}, bf16[64,2048]{1,0:T(8,128)(2,1)S(1)}) custom-call(bf16[128,2176]{1,0:T(8,128)(2,1)S(1)} %pad_maximum_fusion.2.rows_ref, bf16[1,2048,768]{2,1,0:T(8,128)(2,1)S(1)} %get-tuple-element.75.refs_0_, bf16[1,2048,768]{2,1,0:T(8,128)(2,1)S(1)} %get-tuple-element.76.refs_1_, ...), custom_call_target="tpu_custom_call" | custom-call | flops 2415919104 | bytes 2097152 | tf_op jit(solution)/shard_map/expert_halves/pallas_call | solution.py:391
  54.3 1.9 %collective-permute-start.22 = (bf16[64,2048]{1,0:T(8,128)(2,1)S(1)}, bf16[64,2048]{1,0:T(8,128)(2,1)S(1)}, u32[]{:S(2)}, u32[]{:S(2)}) collective-permute-start(bf16[64,2048]{1,0:T(8,128)(2,1)S(1)} %get-tuple-element.104), channel_id=1, source_target_pairs={{0,4},{1,5},{2,3},{3,2},{4,0},{5,1},{6,7},{7,6},{8,12},{9,13},{10,... | collective-permute-start | bytes 786440 | tf_op jit(solution)/shard_map/ppermute | solution.py:38
  56.2 0.6 collective-permute-start.18
  56.9 2.2 %collective-permute-done.19 = bf16[64,2048]{1,0:T(8,128)(2,1)S(1)} collective-permute-done((bf16[64,2048]{1,0:T(8,128)(2,1)S(1)}, bf16[64,2048]{1,0:T(8,128)(2,1)S(1)}, u32[]{:S(2)}, u32[]{:S(2)}) %collective-permute-start.19) | collective-permute-done | bytes 262176 | tf_op jit(solution)/shard_map/ppermute | solution.py:38
  59.2 0.8 %collective-permute-start.21 = (bf16[32,2048]{1,0:T(8,128)(2,1)S(1)}, bf16[32,2048]{1,0:T(8,128)(2,1)S(1)}, u32[]{:S(2)}, u32[]{:S(2)}) collective-permute-start(bf16[32,2048]{1,0:T(8,128)(2,1)S(1)} %slice.53), channel_id=1, source_target_pairs={{0,1},{1,0},{2,6},{3,7},{4,5},{5,4},{6,2},{7,3},{8,9},{9,8},{10,14... | collective-permute-start | bytes 393224 | tf_op jit(solution)/shard_map/ppermute | solution.py:38
  60.0 1.2 %collective-permute-done.18 = bf16[32,2048]{1,0:T(8,128)(2,1)S(1)} collective-permute-done((bf16[32,2048]{1,0:T(8,128)(2,1)S(1)}, bf16[32,2048]{1,0:T(8,128)(2,1)S(1)}, u32[]{:S(2)}, u32[]{:S(2)}) %collective-permute-start.18) | collective-permute-done | bytes 131104 | tf_op jit(solution)/shard_map/ppermute | solution.py:38
  61.3 0.7 collective-permute-start.20
  62.0 1.4 %collective-permute-done.22 = bf16[64,2048]{1,0:T(8,128)(2,1)S(1)} collective-permute-done((bf16[64,2048]{1,0:T(8,128)(2,1)S(1)}, bf16[64,2048]{1,0:T(8,128)(2,1)S(1)}, u32[]{:S(2)}, u32[]{:S(2)}) %collective-permute-start.22) | collective-permute-done | bytes 262176 | tf_op jit(solution)/shard_map/ppermute | solution.py:38
  63.4 0.8 %collective-permute-start.24 = (bf16[32,2048]{1,0:T(8,128)(2,1)S(1)}, bf16[32,2048]{1,0:T(8,128)(2,1)S(1)}, u32[]{:S(2)}, u32[]{:S(2)}) collective-permute-start(bf16[32,2048]{1,0:T(8,128)(2,1)S(1)} %slice.52), channel_id=1, source_target_pairs={{0,1},{1,0},{2,6},{3,7},{4,5},{5,4},{6,2},{7,3},{8,9},{9,8},{10,14... | collective-permute-start | bytes 393224 | tf_op jit(solution)/shard_map/ppermute | solution.py:38
  64.3 2.0 %collective-permute-done.20 = bf16[32,2048]{1,0:T(8,128)(2,1)S(1)} collective-permute-done((bf16[32,2048]{1,0:T(8,128)(2,1)S(1)}, bf16[32,2048]{1,0:T(8,128)(2,1)S(1)}, u32[]{:S(2)}, u32[]{:S(2)}) %collective-permute-start.20) | collective-permute-done | bytes 131104 | tf_op jit(solution)/shard_map/ppermute | solution.py:38
  66.3 2.1 %collective-permute-done.24 = bf16[32,2048]{1,0:T(8,128)(2,1)S(1)} collective-permute-done((bf16[32,2048]{1,0:T(8,128)(2,1)S(1)}, bf16[32,2048]{1,0:T(8,128)(2,1)S(1)}, u32[]{:S(2)}, u32[]{:S(2)}) %collective-permute-start.24) | collective-permute-done | bytes 131104 | tf_op jit(solution)/shard_map/ppermute | solution.py:38
  68.6 2.8 %collective-permute-done.23 = bf16[32,2048]{1,0:T(8,128)(2,1)S(1)} collective-permute-done((bf16[32,2048]{1,0:T(8,128)(2,1)S(1)}, bf16[32,2048]{1,0:T(8,128)(2,1)S(1)}, u32[]{:S(2)}, u32[]{:S(2)}) %collective-permute-start.23) | collective-permute-done | bytes 131104 | tf_op jit(solution)/shard_map/ppermute | solution.py:38
  71.3 4.0 %collective-permute-done.25 = bf16[32,2048]{1,0:T(8,128)(2,1)S(1)} collective-permute-done((bf16[32,2048]{1,0:T(8,128)(2,1)S(1)}, bf16[32,2048]{1,0:T(8,128)(2,1)S(1)}, u32[]{:S(2)}, u32[]{:S(2)}) %collective-permute-start.25) | collective-permute-done | bytes 131104 | tf_op jit(solution)/shard_map/ppermute | solution.py:38
  75.3 0.7 add_convert_fusion
  (59 shorter events, 4.6 us)
Async XLA Ops:
  0.0 13.3 %collective-permute-start.1 = (bf16[1,2048,768]{2,1,0:T(8,128)(2,1)}, bf16[1,2048,768]{2,1,0:T(8,128)(2,1)S(1)}, u32[]{:S(2)}, u32[]{:S(2)}) collective-permute-start(bf16[1,2048,768]{2,1,0:T(8,128)(2,1)} %refs_0_.1), channel_id=1, source_target_pairs={{0,2},{1,3},{2,0},{3,1},{4,6},{5,7},{6,4},{7,5},{8,10},{9,11},{10,... | collective-permute-start | bytes 9437192 | tf_op jit(solution)/shard_map/ppermute | solution.py:38
  0.5 12.8 %collective-permute-start.2 = (bf16[1,2048,768]{2,1,0:T(8,128)(2,1)}, bf16[1,2048,768]{2,1,0:T(8,128)(2,1)S(1)}, u32[]{:S(2)}, u32[]{:S(2)}) collective-permute-start(bf16[1,2048,768]{2,1,0:T(8,128)(2,1)} %refs_1_.1), channel_id=1, source_target_pairs={{0,2},{1,3},{2,0},{3,1},{4,6},{5,7},{6,4},{7,5},{8,10},{9,11},{10,... | collective-permute-start | bytes 9437192 | tf_op jit(solution)/shard_map/ppermute | solution.py:38
  0.5 19.0 %collective-permute-start.4 = (bf16[1,768,2048]{2,1,0:T(8,128)(2,1)}, bf16[1,768,2048]{2,1,0:T(8,128)(2,1)S(1)}, u32[]{:S(2)}, u32[]{:S(2)}) collective-permute-start(bf16[1,768,2048]{2,1,0:T(8,128)(2,1)} %refs_2_.1), channel_id=1, source_target_pairs={{0,2},{1,3},{2,0},{3,1},{4,6},{5,7},{6,4},{7,5},{8,10},{9,11},{10,... | collective-permute-start | bytes 9437192 | tf_op jit(solution)/shard_map/ppermute | solution.py:38
  6.5 6.8 %copy-start = (bf16[32,2048]{1,0:T(8,128)(2,1)S(1)}, bf16[32,2048]{1,0:T(8,128)(2,1)}, u32[]{:S(2)}) copy-start(bf16[32,2048]{1,0:T(8,128)(2,1)} %residual_ref.1) | copy-start | bytes 393220
  6.5 6.8 %copy-start.1 = (f32[2048]{0:T(1024)S(1)}, f32[2048]{0:T(1024)}, u32[]{:S(2)}) copy-start(f32[2048]{0:T(1024)} %param.18) | copy-start | bytes 24580
  6.5 6.8 %copy-start.2 = (s32[64,8]{0,1:T(8,128)S(1)}, s32[64,8]{0,1:T(8,128)}, u32[]{:S(2)}) copy-start(s32[64,8]{0,1:T(8,128)} %param.19) | copy-start | bytes 6148
  6.5 6.8 %copy-start.3 = (f32[64,8]{0,1:T(8,128)S(1)}, f32[64,8]{0,1:T(8,128)}, u32[]{:S(2)}) copy-start(f32[64,8]{0,1:T(8,128)} %param.20) | copy-start | bytes 6148
  6.5 6.7 %collective-permute-start = (bf16[32,2048]{1,0:T(8,128)(2,1)S(1)}, bf16[32,2048]{1,0:T(8,128)(2,1)S(1)}, u32[]{:S(2)}, u32[]{:S(2)}) collective-permute-start(bf16[32,2048]{1,0:T(8,128)(2,1)S(1)} %get-tuple-element.59.refs_3_), channel_id=1, source_target_pairs={{0,1},{1,0},{2,3},{3,2},{4,5},{5,4},{6,7},{7,6},{8,9},{9,8},{10,11... | collective-permute-start | bytes 393224 | tf_op jit(solution)/shard_map/ppermute | solution.py:33
  13.5 12.7 %collective-permute-start.6 = (bf16[32,2176]{1,0:T(8,128)(2,1)S(1)}, bf16[32,2176]{1,0:T(8,128)(2,1)S(1)}, u32[]{:S(2)}, u32[]{:S(2)}) collective-permute-start(bf16[32,2176]{1,0:T(8,128)(2,1)S(1)} %get-tuple-element.65), channel_id=1, source_target_pairs={{0,16},{1,17},{2,18},{3,19},{4,20},{5,21},{6,22},{7,23},{8,24},{9,... | collective-permute-start | bytes 417800 | tf_op jit(solution)/shard_map/ppermute | solution.py:38
  16.4 8.3 %collective-permute-start.7 = (bf16[32,2176]{1,0:T(8,128)(2,1)S(1)}, bf16[32,2176]{1,0:T(8,128)(2,1)S(1)}, u32[]{:S(2)}, u32[]{:S(2)}) collective-permute-start(bf16[32,2176]{1,0:T(8,128)(2,1)S(1)} %get-tuple-element.65), channel_id=1, source_target_pairs={{0,8},{1,9},{2,10},{3,11},{4,12},{5,13},{6,14},{7,15},{8,0},{9,1},... | collective-permute-start | bytes 417800 | tf_op jit(solution)/shard_map/ppermute | solution.py:38
  18.0 5.1 %collective-permute-start.3 = (bf16[32,2176]{1,0:T(8,128)(2,1)S(1)}, bf16[32,2176]{1,0:T(8,128)(2,1)S(1)}, u32[]{:S(2)}, u32[]{:S(2)}) collective-permute-start(bf16[32,2176]{1,0:T(8,128)(2,1)S(1)} %get-tuple-element.65), channel_id=1, source_target_pairs={{0,1},{1,0},{2,6},{3,7},{4,5},{5,4},{6,2},{7,3},{8,9},{9,8},{10,14... | collective-permute-start | bytes 417800 | tf_op jit(solution)/shard_map/ppermute | solution.py:38
  23.1 8.5 %collective-permute-start.5 = (bf16[64,2176]{1,0:T(8,128)(2,1)S(1)}, bf16[64,2176]{1,0:T(8,128)(2,1)S(1)}, u32[]{:S(2)}, u32[]{:S(2)}) collective-permute-start(bf16[64,2176]{1,0:T(8,128)(2,1)S(1)} %get-tuple-element.112), channel_id=1, source_target_pairs={{0,4},{1,5},{2,3},{3,2},{4,0},{5,1},{6,7},{7,6},{8,12},{9,13},{10,... | collective-permute-start | bytes 835592 | tf_op jit(solution)/shard_map/ppermute | solution.py:38
  24.7 6.9 %collective-permute-start.9 = (bf16[32,2176]{1,0:T(8,128)(2,1)S(1)}, bf16[32,2176]{1,0:T(8,128)(2,1)S(1)}, u32[]{:S(2)}, u32[]{:S(2)}) collective-permute-start(bf16[32,2176]{1,0:T(8,128)(2,1)S(1)} %collective-permute-done.7), channel_id=1, source_target_pairs={{0,1},{1,0},{2,6},{3,7},{4,5},{5,4},{6,2},{7,3},{8,9},{9,8},{10,14... | collective-permute-start | bytes 417800 | tf_op jit(solution)/shard_map/ppermute | solution.py:38
  26.2 5.5 %collective-permute-start.8 = (bf16[32,2176]{1,0:T(8,128)(2,1)S(1)}, bf16[32,2176]{1,0:T(8,128)(2,1)S(1)}, u32[]{:S(2)}, u32[]{:S(2)}) collective-permute-start(bf16[32,2176]{1,0:T(8,128)(2,1)S(1)} %collective-permute-done.6), channel_id=1, source_target_pairs={{0,8},{1,9},{2,10},{3,11},{4,12},{5,13},{6,14},{7,15},{8,0},{9,1},... | collective-permute-start | bytes 417800 | tf_op jit(solution)/shard_map/ppermute | solution.py:38
  26.6 7.8 %collective-permute-start.12 = (bf16[32,2176]{1,0:T(8,128)(2,1)S(1)}, bf16[32,2176]{1,0:T(8,128)(2,1)S(1)}, u32[]{:S(2)}, u32[]{:S(2)}) collective-permute-start(bf16[32,2176]{1,0:T(8,128)(2,1)S(1)} %collective-permute-done.6), channel_id=1, source_target_pairs={{0,1},{1,0},{2,6},{3,7},{4,5},{5,4},{6,2},{7,3},{8,9},{9,8},{10,14... | collective-permute-start | bytes 417800 | tf_op jit(solution)/shard_map/ppermute | solution.py:38
  31.7 7.2 %collective-permute-start.10 = (bf16[32,2176]{1,0:T(8,128)(2,1)S(1)}, bf16[32,2176]{1,0:T(8,128)(2,1)S(1)}, u32[]{:S(2)}, u32[]{:S(2)}) collective-permute-start(bf16[32,2176]{1,0:T(8,128)(2,1)S(1)} %collective-permute-done.8), channel_id=1, source_target_pairs={{0,1},{1,0},{2,6},{3,7},{4,5},{5,4},{6,2},{7,3},{8,9},{9,8},{10,14... | collective-permute-start | bytes 417800 | tf_op jit(solution)/shard_map/ppermute | solution.py:38
  34.0 7.0 %collective-permute-start.14 = (bf16[64,2176]{1,0:T(8,128)(2,1)S(1)}, bf16[64,2176]{1,0:T(8,128)(2,1)S(1)}, u32[]{:S(2)}, u32[]{:S(2)}) collective-permute-start(bf16[64,2176]{1,0:T(8,128)(2,1)S(1)} %constant_dynamic-update-slice_fusion.5), channel_id=1, source_target_pairs={{0,4},{1,5},{2,3},{3,2},{4,0},{5,1},{6,7},{7,6},{8,12},{9,13},{10,... | collective-permute-start | bytes 835592 | tf_op jit(solution)/shard_map/ppermute | solution.py:38
  34.4 9.4 %collective-permute-start.13 = (bf16[64,2176]{1,0:T(8,128)(2,1)S(1)}, bf16[64,2176]{1,0:T(8,128)(2,1)S(1)}, u32[]{:S(2)}, u32[]{:S(2)}) collective-permute-start(bf16[64,2176]{1,0:T(8,128)(2,1)S(1)} %pad_maximum_fusion.3), channel_id=1, source_target_pairs={{0,4},{1,5},{2,3},{3,2},{4,0},{5,1},{6,7},{7,6},{8,12},{9,13},{10,... | collective-permute-start | bytes 835592 | tf_op jit(solution)/shard_map/ppermute | solution.py:38
  38.9 12.4 %collective-permute-start.17 = (bf16[64,2176]{1,0:T(8,128)(2,1)S(1)}, bf16[64,2176]{1,0:T(8,128)(2,1)S(1)}, u32[]{:S(2)}, u32[]{:S(2)}) collective-permute-start(bf16[64,2176]{1,0:T(8,128)(2,1)S(1)} %constant_dynamic-update-slice_fusion.7), channel_id=1, source_target_pairs={{0,4},{1,5},{2,3},{3,2},{4,0},{5,1},{6,7},{7,6},{8,12},{9,13},{10,... | collective-permute-start | bytes 835592 | tf_op jit(solution)/shard_map/ppermute | solution.py:38
  40.9 9.8 %collective-permute-start.11 = (bf16[64,2048]{1,0:T(8,128)(2,1)S(1)}, bf16[64,2048]{1,0:T(8,128)(2,1)S(1)}, u32[]{:S(2)}, u32[]{:S(2)}) collective-permute-start(bf16[64,2048]{1,0:T(8,128)(2,1)S(1)} %get-tuple-element.86), channel_id=1, source_target_pairs={{0,4},{1,5},{2,3},{3,2},{4,0},{5,1},{6,7},{7,6},{8,12},{9,13},{10,... | collective-permute-start | bytes 786440 | tf_op jit(solution)/shard_map/ppermute | solution.py:38
  43.8 12.3 %collective-permute-start.16 = (bf16[64,2048]{1,0:T(8,128)(2,1)S(1)}, bf16[64,2048]{1,0:T(8,128)(2,1)S(1)}, u32[]{:S(2)}, u32[]{:S(2)}) collective-permute-start(bf16[64,2048]{1,0:T(8,128)(2,1)S(1)} %get-tuple-element.94), channel_id=1, source_target_pairs={{0,4},{1,5},{2,3},{3,2},{4,0},{5,1},{6,7},{7,6},{8,12},{9,13},{10,... | collective-permute-start | bytes 786440 | tf_op jit(solution)/shard_map/ppermute | solution.py:38
  48.5 10.6 %collective-permute-start.19 = (bf16[64,2048]{1,0:T(8,128)(2,1)S(1)}, bf16[64,2048]{1,0:T(8,128)(2,1)S(1)}, u32[]{:S(2)}, u32[]{:S(2)}) collective-permute-start(bf16[64,2048]{1,0:T(8,128)(2,1)S(1)} %get-tuple-element.100), channel_id=1, source_target_pairs={{0,4},{1,5},{2,3},{3,2},{4,0},{5,1},{6,7},{7,6},{8,12},{9,13},{10,... | collective-permute-start | bytes 786440 | tf_op jit(solution)/shard_map/ppermute | solution.py:38
  50.8 6.1 %collective-permute-start.15 = (bf16[32,2048]{1,0:T(8,128)(2,1)S(1)}, bf16[32,2048]{1,0:T(8,128)(2,1)S(1)}, u32[]{:S(2)}, u32[]{:S(2)}) collective-permute-start(bf16[32,2048]{1,0:T(8,128)(2,1)S(1)} %slice.55), channel_id=1, source_target_pairs={{0,1},{1,0},{2,6},{3,7},{4,5},{5,4},{6,2},{7,3},{8,9},{9,8},{10,14... | collective-permute-start | bytes 393224 | tf_op jit(solution)/shard_map/ppermute | solution.py:38
  54.3 9.1 %collective-permute-start.22 = (bf16[64,2048]{1,0:T(8,128)(2,1)S(1)}, bf16[64,2048]{1,0:T(8,128)(2,1)S(1)}, u32[]{:S(2)}, u32[]{:S(2)}) collective-permute-start(bf16[64,2048]{1,0:T(8,128)(2,1)S(1)} %get-tuple-element.104), channel_id=1, source_target_pairs={{0,4},{1,5},{2,3},{3,2},{4,0},{5,1},{6,7},{7,6},{8,12},{9,13},{10,... | collective-permute-start | bytes 786440 | tf_op jit(solution)/shard_map/ppermute | solution.py:38
  56.2 5.0 %collective-permute-start.18 = (bf16[32,2048]{1,0:T(8,128)(2,1)S(1)}, bf16[32,2048]{1,0:T(8,128)(2,1)S(1)}, u32[]{:S(2)}, u32[]{:S(2)}) collective-permute-start(bf16[32,2048]{1,0:T(8,128)(2,1)S(1)} %slice.54), channel_id=1, source_target_pairs={{0,1},{1,0},{2,6},{3,7},{4,5},{5,4},{6,2},{7,3},{8,9},{9,8},{10,14... | collective-permute-start | bytes 393224 | tf_op jit(solution)/shard_map/ppermute | solution.py:38
  59.2 5.0 %collective-permute-start.21 = (bf16[32,2048]{1,0:T(8,128)(2,1)S(1)}, bf16[32,2048]{1,0:T(8,128)(2,1)S(1)}, u32[]{:S(2)}, u32[]{:S(2)}) collective-permute-start(bf16[32,2048]{1,0:T(8,128)(2,1)S(1)} %slice.53), channel_id=1, source_target_pairs={{0,1},{1,0},{2,6},{3,7},{4,5},{5,4},{6,2},{7,3},{8,9},{9,8},{10,14... | collective-permute-start | bytes 393224 | tf_op jit(solution)/shard_map/ppermute | solution.py:38
  61.3 5.0 %collective-permute-start.20 = (bf16[32,2048]{1,0:T(8,128)(2,1)S(1)}, bf16[32,2048]{1,0:T(8,128)(2,1)S(1)}, u32[]{:S(2)}, u32[]{:S(2)}) collective-permute-start(bf16[32,2048]{1,0:T(8,128)(2,1)S(1)} %slice_add_fusion.2), channel_id=1, source_target_pairs={{0,8},{1,9},{2,10},{3,11},{4,12},{5,13},{6,14},{7,15},{8,0},{9,1},... | collective-permute-start | bytes 393224 | tf_op jit(solution)/shard_map/ppermute | solution.py:38
  63.4 5.0 %collective-permute-start.24 = (bf16[32,2048]{1,0:T(8,128)(2,1)S(1)}, bf16[32,2048]{1,0:T(8,128)(2,1)S(1)}, u32[]{:S(2)}, u32[]{:S(2)}) collective-permute-start(bf16[32,2048]{1,0:T(8,128)(2,1)S(1)} %slice.52), channel_id=1, source_target_pairs={{0,1},{1,0},{2,6},{3,7},{4,5},{5,4},{6,2},{7,3},{8,9},{9,8},{10,14... | collective-permute-start | bytes 393224 | tf_op jit(solution)/shard_map/ppermute | solution.py:38
  64.3 7.1 %collective-permute-start.23 = (bf16[32,2048]{1,0:T(8,128)(2,1)S(1)}, bf16[32,2048]{1,0:T(8,128)(2,1)S(1)}, u32[]{:S(2)}, u32[]{:S(2)}) collective-permute-start(bf16[32,2048]{1,0:T(8,128)(2,1)S(1)} %slice_add_fusion.1), channel_id=1, source_target_pairs={{0,16},{1,17},{2,18},{3,19},{4,20},{5,21},{6,22},{7,23},{8,24},{9,... | collective-permute-start | bytes 393224 | tf_op jit(solution)/shard_map/ppermute | solution.py:38
  68.5 6.8 %collective-permute-start.25 = (bf16[32,2048]{1,0:T(8,128)(2,1)S(1)}, bf16[32,2048]{1,0:T(8,128)(2,1)S(1)}, u32[]{:S(2)}, u32[]{:S(2)}) collective-permute-start(bf16[32,2048]{1,0:T(8,128)(2,1)S(1)} %slice_add_fusion), channel_id=1, source_target_pairs={{0,24},{1,25},{2,26},{3,27},{4,28},{5,29},{6,30},{7,31},{8,16},{9,... | collective-permute-start | bytes 393224 | tf_op jit(solution)/shard_map/ppermute | solution.py:38

commit v6 on v5

--- a/solution.py
+++ b/solution.py
@@ -457,42 +457,42 @@
     set_2 = then(set_2)
     set_3 = exchanged(then.after(set_2), NEAR_LINE)
     taken_2 = exchanged(then.after(set_2), NEAR_PLANE)
-    quad_0 = joined(pair_0, taken_0)
     pair_1 = joined(set_1, taken_1)
     taken_1 = exchanged(then.after(pair_1), FAR_PLANE)
     set_3 = then(set_3)
     taken_3 = exchanged(then.after(set_3), NEAR_PLANE)
     pair_2 = joined(set_2, taken_2)
     taken_2 = exchanged(then.after(pair_2), FAR_PLANE)
+    quad_0 = joined(pair_0, taken_0)
     kept_0, given_0 = expert(quad_0)
     pair_3 = joined(set_3, taken_3)
     taken_3 = exchanged(then.after(pair_3), FAR_PLANE)
     sent_0 = exchanged(then.after(given_0), FAR_PLANE)
+    quad_2 = joined(pair_2, taken_2)
+    kept_2, given_2 = expert(quad_2)
+    sent_2 = exchanged(then.after(given_2), FAR_PLANE)
     quad_1 = joined(pair_1, taken_1)
     kept_1, given_1 = expert(quad_1)
     sent_1 = exchanged(then.after(given_1), FAR_PLANE)
-    quad_2 = joined(pair_2, taken_2)
-    kept_2, given_2 = expert(quad_2)
-    sent_2 = exchanged(then.after(given_2), FAR_PLANE)
     total_0 = added(kept_0, sent_0)
     sent_0 = sent(then.after(total_0), NEAR_PLANE)
     quad_3 = joined(pair_3, taken_3)
     kept_3, given_3 = expert(quad_3)
     sent_3 = exchanged(then.after(given_3), FAR_PLANE)
+    total_2 = added(kept_2, sent_2)
+    sent_2 = sent(then.after(total_2), NEAR_PLANE)
     total_1 = added(kept_1, sent_1)
     sent_1 = sent(then.after(total_1), NEAR_PLANE)
     total_0 = added(kept(total_0), sent_0)
-    total_2 = added(kept_2, sent_2)
-    sent_2 = sent(then.after(total_2), NEAR_PLANE)
+    total_2 = added(kept(total_2), sent_2)
+    home_2 = exchanged(narrowed(then.after(total_2)), FAR_LINE)
+    total_3 = added(kept_3, sent_3)
+    sent_3 = sent(then.after(total_3), NEAR_PLANE)
     total_1 = added(kept(total_1), sent_1)
     home_1 = exchanged(narrowed(then.after(total_1)), NEAR_LINE)
-    total_3 = added(kept_3, sent_3)
-    sent_3 = sent(then.after(total_3), NEAR_PLANE)
-    total_2 = added(kept(total_2), sent_2)
-    home_2 = exchanged(narrowed(then.after(total_2)), FAR_LINE)
-    home_1 = then(home_1)
     total_3 = added(kept(total_3), sent_3)
     home_3 = exchanged(narrowed(then.after(total_3)), BOTH_LINE)
+    home_1 = then(home_1)
     home_2 = then(home_2)
     home_3 = then(home_3)
     mixture = total_0 + widened(home_1) + widened(home_2) + widened(home_3)

time: 76.2 us -> 73.3 us (0.962)
  waiting for transfers between devices: 26.1 us -> 16.9 us
  starting transfers between devices: 27.6 us -> 34 us
    ppermute x25, waiting for transfers between devices: 25.8 us -> 16.6 us  [exchanged(): lax.ppermute(shard, BOTH, [(i, i ^ masks[1 if i & BIT_CORE else 0]) for i...]
    ppermute x25, starting transfers between devices: 25.1 us -> 31.4 us  [exchanged(): lax.ppermute(shard, BOTH, [(i, i ^ masks[1 if i & BIT_CORE else 0]) for i...]
  transfers between devices with their start and end apart: 26 -> 26, of which waited for: 11 -> 14; matrix products, arithmetic and copies ran while one was open for 1% -> 1% of each run, Pallas kernels for 27% -> 28%
where the time goes in v6:
time: 73.3 us; the launch traced here: 73.1 us
  starting transfers between devices  34 us (46%)
  Pallas kernels  20.5 us (28%)
  waiting for transfers between devices  16.9 us (23%)
  other arithmetic  1.21 us (2%)
    ppermute x25, starting transfers between devices, exchanged(): lax.ppermute(shard, BOTH, [(i, i ^ masks[1 if i & BIT_CORE else 0]) for i...  31.4 us
    ppermute x25, waiting for transfers between devices, exchanged(): lax.ppermute(shard, BOTH, [(i, i ^ masks[1 if i & BIT_CORE else 0]) for i...  16.6 us
    pallas_call x4, Pallas kernels, weighted_experts(): pl.pallas_call(expert_kernel, in_specs=[whole] * 7, out_specs=[whole] * 2...  11 us
    pallas_call x1, Pallas kernels, attention_halves(): pl.pallas_call(attention_kernel, in_specs=[far] * 5, out_specs=[near] * 2...  5.52 us
    pallas_call x1, Pallas kernels, loaded(): pl.pallas_call(functools.partial(load_kernel, len(weights), pieces), in_s...  3.79 us
    ppermute x1, starting transfers between devices, swapped(): lax.ppermute(shard, axis, [(i, i ^ 1 << distance) for i in range(lax.axis...  2.56 us
  transfers between devices with their start and end apart: 26, of which 14 were waited for; matrix products, arithmetic and copies ran while one was open for 1% of the time, Pallas kernels for 28%

profile of v6, /device:TPU:0, one launch (start us, length us, event | category | flops | bytes accessed | tf_op | source)
XLA Modules:
  0.0 73.1 jit_solution(1909745396266323218)
XLA Ops:
  1.0 5.5 %attention_halves.1 = (f32[32,2048]{1,0:T(8,128)S(1)}, bf16[32,2048]{1,0:T(8,128)(2,1)S(1)}) custom-call(bf16[64,2048]{1,0:T(8,128)(2,1)} %queries_hbm.1, bf16[64,512]{1,0:T(8,128)(2,1)} %keys_hbm.1, bf16[64,512]{1,0:T(8,128)(2,1)} %values_hbm.1, s32[1,64]{1,0:T(1,128)} %bitcast.7, bf16[2048,2048]{1,0:T(8,128)(2,1)} %out_weight_hbm.1), custom_call_target="tpu_custom_call" | custom-call | flops 570425344 | bytes 8388608 | tf_op jit(solution)/shard_map/attention_halves/pallas_call | solution.py:225
  6.5 2.6 %collective-permute-start = (bf16[32,2048]{1,0:T(8,128)(2,1)S(1)}, bf16[32,2048]{1,0:T(8,128)(2,1)S(1)}, u32[]{:S(2)}, u32[]{:S(2)}) collective-permute-start(bf16[32,2048]{1,0:T(8,128)(2,1)S(1)} %get-tuple-element.59.refs_3_), channel_id=1, source_target_pairs={{0,1},{1,0},{2,3},{3,2},{4,5},{5,4},{6,7},{7,6},{8,9},{9,8},{10,11... | collective-permute-start | bytes 393224 | tf_op jit(solution)/shard_map/ppermute | solution.py:33
  9.1 3.8 %load_weights.1 = (bf16[1,2048,768]{2,1,0:T(8,128)(2,1)S(1)}, bf16[1,2048,768]{2,1,0:T(8,128)(2,1)S(1)}, bf16[1,768,2048]{2,1,0:T(8,128)(2,1)S(1)}) custom-call(bf16[1,2048,768]{2,1,0:T(8,128)(2,1)} %refs_0_.1, bf16[1,2048,768]{2,1,0:T(8,128)(2,1)} %refs_1_.1, bf16[1,768,2048]{2,1,0:T(8,128)(2,1)} %refs_2_.1, bf16[32,2048]{1,0:T(8,128)(2,1)S(1)} %get-tuple-element.59.refs_3_), custom_call_target="tpu_custom_call" | custom-call | bytes 9437184 | tf_op jit(solution)/shard_map/load_weights/pallas_call | solution.py:281
  13.5 2.9 %collective-permute-start.6 = (bf16[32,2176]{1,0:T(8,128)(2,1)S(1)}, bf16[32,2176]{1,0:T(8,128)(2,1)S(1)}, u32[]{:S(2)}, u32[]{:S(2)}) collective-permute-start(bf16[32,2176]{1,0:T(8,128)(2,1)S(1)} %get-tuple-element.65), channel_id=1, source_target_pairs={{0,16},{1,17},{2,18},{3,19},{4,20},{5,21},{6,22},{7,23},{8,24},{9,... | collective-permute-start | bytes 417800 | tf_op jit(solution)/shard_map/ppermute | solution.py:38
  16.4 1.6 %collective-permute-start.7 = (bf16[32,2176]{1,0:T(8,128)(2,1)S(1)}, bf16[32,2176]{1,0:T(8,128)(2,1)S(1)}, u32[]{:S(2)}, u32[]{:S(2)}) collective-permute-start(bf16[32,2176]{1,0:T(8,128)(2,1)S(1)} %get-tuple-element.65), channel_id=1, source_target_pairs={{0,8},{1,9},{2,10},{3,11},{4,12},{5,13},{6,14},{7,15},{8,0},{9,1},... | collective-permute-start | bytes 417800 | tf_op jit(solution)/shard_map/ppermute | solution.py:38
  18.0 1.5 %collective-permute-start.3 = (bf16[32,2176]{1,0:T(8,128)(2,1)S(1)}, bf16[32,2176]{1,0:T(8,128)(2,1)S(1)}, u32[]{:S(2)}, u32[]{:S(2)}) collective-permute-start(bf16[32,2176]{1,0:T(8,128)(2,1)S(1)} %get-tuple-element.65), channel_id=1, source_target_pairs={{0,1},{1,0},{2,6},{3,7},{4,5},{5,4},{6,2},{7,3},{8,9},{9,8},{10,14... | collective-permute-start | bytes 417800 | tf_op jit(solution)/shard_map/ppermute | solution.py:38
  19.5 3.5 %collective-permute-done.3 = bf16[32,2176]{1,0:T(8,128)(2,1)S(1)} collective-permute-done((bf16[32,2176]{1,0:T(8,128)(2,1)S(1)}, bf16[32,2176]{1,0:T(8,128)(2,1)S(1)}, u32[]{:S(2)}, u32[]{:S(2)}) %collective-permute-start.3) | collective-permute-done | bytes 139296 | tf_op jit(solution)/shard_map/ppermute | solution.py:38
  23.3 1.6 %collective-permute-start.10 = (bf16[32,2176]{1,0:T(8,128)(2,1)S(1)}, bf16[32,2176]{1,0:T(8,128)(2,1)S(1)}, u32[]{:S(2)}, u32[]{:S(2)}) collective-permute-start(bf16[32,2176]{1,0:T(8,128)(2,1)S(1)} %collective-permute-done.7), channel_id=1, source_target_pairs={{0,1},{1,0},{2,6},{3,7},{4,5},{5,4},{6,2},{7,3},{8,9},{9,8},{10,14... | collective-permute-start | bytes 417800 | tf_op jit(solution)/shard_map/ppermute | solution.py:38
  24.9 1.5 %collective-permute-start.5 = (bf16[64,2176]{1,0:T(8,128)(2,1)S(1)}, bf16[64,2176]{1,0:T(8,128)(2,1)S(1)}, u32[]{:S(2)}, u32[]{:S(2)}) collective-permute-start(bf16[64,2176]{1,0:T(8,128)(2,1)S(1)} %constant_dynamic-update-slice_fusion), channel_id=1, source_target_pairs={{0,4},{1,5},{2,3},{3,2},{4,0},{5,1},{6,7},{7,6},{8,12},{9,13},{10,... | collective-permute-start | bytes 835592 | tf_op jit(solution)/shard_map/ppermute | solution.py:38
  26.4 1.4 %collective-permute-start.9 = (bf16[32,2176]{1,0:T(8,128)(2,1)S(1)}, bf16[32,2176]{1,0:T(8,128)(2,1)S(1)}, u32[]{:S(2)}, u32[]{:S(2)}) collective-permute-start(bf16[32,2176]{1,0:T(8,128)(2,1)S(1)} %collective-permute-done.6), channel_id=1, source_target_pairs={{0,8},{1,9},{2,10},{3,11},{4,12},{5,13},{6,14},{7,15},{8,0},{9,1},... | collective-permute-start | bytes 417800 | tf_op jit(solution)/shard_map/ppermute | solution.py:38
  28.4 1.6 %collective-permute-done.10 = bf16[32,2176]{1,0:T(8,128)(2,1)S(1)} collective-permute-done((bf16[32,2176]{1,0:T(8,128)(2,1)S(1)}, bf16[32,2176]{1,0:T(8,128)(2,1)S(1)}, u32[]{:S(2)}, u32[]{:S(2)}) %collective-permute-start.10) | collective-permute-done | bytes 139296 | tf_op jit(solution)/shard_map/ppermute | solution.py:38
  30.4 1.1 %collective-permute-done.9 = bf16[32,2176]{1,0:T(8,128)(2,1)S(1)} collective-permute-done((bf16[32,2176]{1,0:T(8,128)(2,1)S(1)}, bf16[32,2176]{1,0:T(8,128)(2,1)S(1)}, u32[]{:S(2)}, u32[]{:S(2)}) %collective-permute-start.9) | collective-permute-done | bytes 139296 | tf_op jit(solution)/shard_map/ppermute | solution.py:38
  31.5 1.1 %collective-permute-start.11 = (bf16[32,2176]{1,0:T(8,128)(2,1)S(1)}, bf16[32,2176]{1,0:T(8,128)(2,1)S(1)}, u32[]{:S(2)}, u32[]{:S(2)}) collective-permute-start(bf16[32,2176]{1,0:T(8,128)(2,1)S(1)} %collective-permute-done.9), channel_id=1, source_target_pairs={{0,1},{1,0},{2,6},{3,7},{4,5},{5,4},{6,2},{7,3},{8,9},{9,8},{10,14... | collective-permute-start | bytes 417800 | tf_op jit(solution)/shard_map/ppermute | solution.py:38
  32.6 1.7 %collective-permute-done.8 = bf16[32,2176]{1,0:T(8,128)(2,1)S(1)} collective-permute-done((bf16[32,2176]{1,0:T(8,128)(2,1)S(1)}, bf16[32,2176]{1,0:T(8,128)(2,1)S(1)}, u32[]{:S(2)}, u32[]{:S(2)}) %collective-permute-start.8) | collective-permute-done | bytes 139296 | tf_op jit(solution)/shard_map/ppermute | solution.py:38
  35.2 2.7 %expert_halves.4 = (f32[64,2048]{1,0:T(8,128)S(1)}, bf16[64,2048]{1,0:T(8,128)(2,1)S(1)}) custom-call(bf16[128,2176]{1,0:T(8,128)(2,1)S(1)} %pad_maximum_fusion.rows_ref, bf16[1,2048,768]{2,1,0:T(8,128)(2,1)S(1)} %get-tuple-element.78.refs_0_, bf16[1,2048,768]{2,1,0:T(8,128)(2,1)S(1)} %get-tuple-element.79.refs_1_, ...), custom_call_target="tpu_custom_call" | custom-call | flops 2415919104 | bytes 2097152 | tf_op jit(solution)/shard_map/expert_halves/pallas_call | solution.py:391
  38.0 1.2 %collective-permute-start.18 = (bf16[64,2176]{1,0:T(8,128)(2,1)S(1)}, bf16[64,2176]{1,0:T(8,128)(2,1)S(1)}, u32[]{:S(2)}, u32[]{:S(2)}) collective-permute-start(bf16[64,2176]{1,0:T(8,128)(2,1)S(1)} %constant_dynamic-update-slice_fusion.6), channel_id=1, source_target_pairs={{0,4},{1,5},{2,3},{3,2},{4,0},{5,1},{6,7},{7,6},{8,12},{9,13},{10,... | collective-permute-start | bytes 835592 | tf_op jit(solution)/shard_map/ppermute | solution.py:38
  39.3 0.9 %collective-permute-start.12 = (bf16[64,2048]{1,0:T(8,128)(2,1)S(1)}, bf16[64,2048]{1,0:T(8,128)(2,1)S(1)}, u32[]{:S(2)}, u32[]{:S(2)}) collective-permute-start(bf16[64,2048]{1,0:T(8,128)(2,1)S(1)} %get-tuple-element.87), channel_id=1, source_target_pairs={{0,4},{1,5},{2,3},{3,2},{4,0},{5,1},{6,7},{7,6},{8,12},{9,13},{10,... | collective-permute-start | bytes 786440 | tf_op jit(solution)/shard_map/ppermute | solution.py:38
  40.9 2.7 %expert_halves.5 = (f32[64,2048]{1,0:T(8,128)S(1)}, bf16[64,2048]{1,0:T(8,128)(2,1)S(1)}) custom-call(bf16[128,2176]{1,0:T(8,128)(2,1)S(1)} %pad_maximum_fusion.1.rows_ref, bf16[1,2048,768]{2,1,0:T(8,128)(2,1)S(1)} %get-tuple-element.78.refs_0_, bf16[1,2048,768]{2,1,0:T(8,128)(2,1)S(1)} %get-tuple-element.79.refs_1_, ...), custom_call_target="tpu_custom_call" | custom-call | flops 2415919104 | bytes 2097152 | tf_op jit(solution)/shard_map/expert_halves/pallas_call | solution.py:391
  43.7 0.8 %collective-permute-start.17 = (bf16[64,2048]{1,0:T(8,128)(2,1)S(1)}, bf16[64,2048]{1,0:T(8,128)(2,1)S(1)}, u32[]{:S(2)}, u32[]{:S(2)}) collective-permute-start(bf16[64,2048]{1,0:T(8,128)(2,1)S(1)} %get-tuple-element.96), channel_id=1, source_target_pairs={{0,4},{1,5},{2,3},{3,2},{4,0},{5,1},{6,7},{7,6},{8,12},{9,13},{10,... | collective-permute-start | bytes 786440 | tf_op jit(solution)/shard_map/ppermute | solution.py:38
  44.5 2.7 %expert_halves.6 = (f32[64,2048]{1,0:T(8,128)S(1)}, bf16[64,2048]{1,0:T(8,128)(2,1)S(1)}) custom-call(bf16[128,2176]{1,0:T(8,128)(2,1)S(1)} %pad_maximum_fusion.2.rows_ref, bf16[1,2048,768]{2,1,0:T(8,128)(2,1)S(1)} %get-tuple-element.78.refs_0_, bf16[1,2048,768]{2,1,0:T(8,128)(2,1)S(1)} %get-tuple-element.79.refs_1_, ...), custom_call_target="tpu_custom_call" | custom-call | flops 2415919104 | bytes 2097152 | tf_op jit(solution)/shard_map/expert_halves/pallas_call | solution.py:391
  47.2 1.3 %collective-permute-start.16 = (bf16[64,2048]{1,0:T(8,128)(2,1)S(1)}, bf16[64,2048]{1,0:T(8,128)(2,1)S(1)}, u32[]{:S(2)}, u32[]{:S(2)}) collective-permute-start(bf16[64,2048]{1,0:T(8,128)(2,1)S(1)} %get-tuple-element.94), channel_id=1, source_target_pairs={{0,4},{1,5},{2,3},{3,2},{4,0},{5,1},{6,7},{7,6},{8,12},{9,13},{10,... | collective-permute-start | bytes 786440 | tf_op jit(solution)/shard_map/ppermute | solution.py:38
  49.5 2.9 %expert_halves.7 = (f32[64,2048]{1,0:T(8,128)S(1)}, bf16[64,2048]{1,0:T(8,128)(2,1)S(1)}) custom-call(bf16[128,2176]{1,0:T(8,128)(2,1)S(1)} %pad_maximum_fusion.3.rows_ref, bf16[1,2048,768]{2,1,0:T(8,128)(2,1)S(1)} %get-tuple-element.78.refs_0_, bf16[1,2048,768]{2,1,0:T(8,128)(2,1)S(1)} %get-tuple-element.79.refs_1_, ...), custom_call_target="tpu_custom_call" | custom-call | flops 2415919104 | bytes 2097152 | tf_op jit(solution)/shard_map/expert_halves/pallas_call | solution.py:391
  53.3 1.4 %collective-permute-start.21 = (bf16[32,2048]{1,0:T(8,128)(2,1)S(1)}, bf16[32,2048]{1,0:T(8,128)(2,1)S(1)}, u32[]{:S(2)}, u32[]{:S(2)}) collective-permute-start(bf16[32,2048]{1,0:T(8,128)(2,1)S(1)} %slice.53), channel_id=1, source_target_pairs={{0,1},{1,0},{2,6},{3,7},{4,5},{5,4},{6,2},{7,3},{8,9},{9,8},{10,14... | collective-permute-start | bytes 393224 | tf_op jit(solution)/shard_map/ppermute | solution.py:38
  54.7 0.9 %collective-permute-done.16 = bf16[64,2048]{1,0:T(8,128)(2,1)S(1)} collective-permute-done((bf16[64,2048]{1,0:T(8,128)(2,1)S(1)}, bf16[64,2048]{1,0:T(8,128)(2,1)S(1)}, u32[]{:S(2)}, u32[]{:S(2)}) %collective-permute-start.16) | collective-permute-done | bytes 262176 | tf_op jit(solution)/shard_map/ppermute | solution.py:38
  55.7 1.8 %collective-permute-start.19 = (bf16[32,2048]{1,0:T(8,128)(2,1)S(1)}, bf16[32,2048]{1,0:T(8,128)(2,1)S(1)}, u32[]{:S(2)}, u32[]{:S(2)}) collective-permute-start(bf16[32,2048]{1,0:T(8,128)(2,1)S(1)} %slice.54), channel_id=1, source_target_pairs={{0,1},{1,0},{2,6},{3,7},{4,5},{5,4},{6,2},{7,3},{8,9},{9,8},{10,14... | collective-permute-start | bytes 393224 | tf_op jit(solution)/shard_map/ppermute | solution.py:38
  57.5 0.9 %collective-permute-done.21 = bf16[32,2048]{1,0:T(8,128)(2,1)S(1)} collective-permute-done((bf16[32,2048]{1,0:T(8,128)(2,1)S(1)}, bf16[32,2048]{1,0:T(8,128)(2,1)S(1)}, u32[]{:S(2)}, u32[]{:S(2)}) %collective-permute-start.21) | collective-permute-done | bytes 131104 | tf_op jit(solution)/shard_map/ppermute | solution.py:38
  58.4 1.7 %collective-permute-start.24 = (bf16[32,2048]{1,0:T(8,128)(2,1)S(1)}, bf16[32,2048]{1,0:T(8,128)(2,1)S(1)}, u32[]{:S(2)}, u32[]{:S(2)}) collective-permute-start(bf16[32,2048]{1,0:T(8,128)(2,1)S(1)} %slice_add_fusion.1), channel_id=1, source_target_pairs={{0,16},{1,17},{2,18},{3,19},{4,20},{5,21},{6,22},{7,23},{8,24},{9,... | collective-permute-start | bytes 393224 | tf_op jit(solution)/shard_map/ppermute | solution.py:38
  60.4 1.0 %collective-permute-start.23 = (bf16[32,2048]{1,0:T(8,128)(2,1)S(1)}, bf16[32,2048]{1,0:T(8,128)(2,1)S(1)}, u32[]{:S(2)}, u32[]{:S(2)}) collective-permute-start(bf16[32,2048]{1,0:T(8,128)(2,1)S(1)} %slice.52), channel_id=1, source_target_pairs={{0,1},{1,0},{2,6},{3,7},{4,5},{5,4},{6,2},{7,3},{8,9},{9,8},{10,14... | collective-permute-start | bytes 393224 | tf_op jit(solution)/shard_map/ppermute | solution.py:38
  61.4 3.3 %collective-permute-start.22 = (bf16[32,2048]{1,0:T(8,128)(2,1)S(1)}, bf16[32,2048]{1,0:T(8,128)(2,1)S(1)}, u32[]{:S(2)}, u32[]{:S(2)}) collective-permute-start(bf16[32,2048]{1,0:T(8,128)(2,1)S(1)} %slice_add_fusion.2), channel_id=1, source_target_pairs={{0,8},{1,9},{2,10},{3,11},{4,12},{5,13},{6,14},{7,15},{8,0},{9,1},... | collective-permute-start | bytes 393224 | tf_op jit(solution)/shard_map/ppermute | solution.py:38
  65.5 2.2 %collective-permute-start.25 = (bf16[32,2048]{1,0:T(8,128)(2,1)S(1)}, bf16[32,2048]{1,0:T(8,128)(2,1)S(1)}, u32[]{:S(2)}, u32[]{:S(2)}) collective-permute-start(bf16[32,2048]{1,0:T(8,128)(2,1)S(1)} %slice_add_fusion), channel_id=1, source_target_pairs={{0,24},{1,25},{2,26},{3,27},{4,28},{5,29},{6,30},{7,31},{8,16},{9,... | collective-permute-start | bytes 393224 | tf_op jit(solution)/shard_map/ppermute | solution.py:38
  67.7 0.9 %collective-permute-done.22 = bf16[32,2048]{1,0:T(8,128)(2,1)S(1)} collective-permute-done((bf16[32,2048]{1,0:T(8,128)(2,1)S(1)}, bf16[32,2048]{1,0:T(8,128)(2,1)S(1)}, u32[]{:S(2)}, u32[]{:S(2)}) %collective-permute-start.22) | collective-permute-done | bytes 131104 | tf_op jit(solution)/shard_map/ppermute | solution.py:38
  68.6 3.8 %collective-permute-done.25 = bf16[32,2048]{1,0:T(8,128)(2,1)S(1)} collective-permute-done((bf16[32,2048]{1,0:T(8,128)(2,1)S(1)}, bf16[32,2048]{1,0:T(8,128)(2,1)S(1)}, u32[]{:S(2)}, u32[]{:S(2)}) %collective-permute-start.25) | collective-permute-done | bytes 131104 | tf_op jit(solution)/shard_map/ppermute | solution.py:38
  (60 shorter events, 8.5 us)
Async XLA Ops:
  0.0 13.3 %collective-permute-start.1 = (bf16[1,2048,768]{2,1,0:T(8,128)(2,1)}, bf16[1,2048,768]{2,1,0:T(8,128)(2,1)S(1)}, u32[]{:S(2)}, u32[]{:S(2)}) collective-permute-start(bf16[1,2048,768]{2,1,0:T(8,128)(2,1)} %refs_0_.1), channel_id=1, source_target_pairs={{0,2},{1,3},{2,0},{3,1},{4,6},{5,7},{6,4},{7,5},{8,10},{9,11},{10,... | collective-permute-start | bytes 9437192 | tf_op jit(solution)/shard_map/ppermute | solution.py:38
  0.5 12.8 %collective-permute-start.2 = (bf16[1,2048,768]{2,1,0:T(8,128)(2,1)}, bf16[1,2048,768]{2,1,0:T(8,128)(2,1)S(1)}, u32[]{:S(2)}, u32[]{:S(2)}) collective-permute-start(bf16[1,2048,768]{2,1,0:T(8,128)(2,1)} %refs_1_.1), channel_id=1, source_target_pairs={{0,2},{1,3},{2,0},{3,1},{4,6},{5,7},{6,4},{7,5},{8,10},{9,11},{10,... | collective-permute-start | bytes 9437192 | tf_op jit(solution)/shard_map/ppermute | solution.py:38
  0.5 19.0 %collective-permute-start.4 = (bf16[1,768,2048]{2,1,0:T(8,128)(2,1)}, bf16[1,768,2048]{2,1,0:T(8,128)(2,1)S(1)}, u32[]{:S(2)}, u32[]{:S(2)}) collective-permute-start(bf16[1,768,2048]{2,1,0:T(8,128)(2,1)} %refs_2_.1), channel_id=1, source_target_pairs={{0,2},{1,3},{2,0},{3,1},{4,6},{5,7},{6,4},{7,5},{8,10},{9,11},{10,... | collective-permute-start | bytes 9437192 | tf_op jit(solution)/shard_map/ppermute | solution.py:38
  6.5 6.8 %copy-start = (bf16[32,2048]{1,0:T(8,128)(2,1)S(1)}, bf16[32,2048]{1,0:T(8,128)(2,1)}, u32[]{:S(2)}) copy-start(bf16[32,2048]{1,0:T(8,128)(2,1)} %residual_ref.1) | copy-start | bytes 393220
  6.5 6.8 %copy-start.1 = (f32[2048]{0:T(1024)S(1)}, f32[2048]{0:T(1024)}, u32[]{:S(2)}) copy-start(f32[2048]{0:T(1024)} %param.18) | copy-start | bytes 24580
  6.5 6.8 %copy-start.2 = (s32[64,8]{0,1:T(8,128)S(1)}, s32[64,8]{0,1:T(8,128)}, u32[]{:S(2)}) copy-start(s32[64,8]{0,1:T(8,128)} %param.19) | copy-start | bytes 6148
  6.5 6.8 %copy-start.3 = (f32[64,8]{0,1:T(8,128)S(1)}, f32[64,8]{0,1:T(8,128)}, u32[]{:S(2)}) copy-start(f32[64,8]{0,1:T(8,128)} %param.20) | copy-start | bytes 6148
  6.5 6.7 %collective-permute-start = (bf16[32,2048]{1,0:T(8,128)(2,1)S(1)}, bf16[32,2048]{1,0:T(8,128)(2,1)S(1)}, u32[]{:S(2)}, u32[]{:S(2)}) collective-permute-start(bf16[32,2048]{1,0:T(8,128)(2,1)S(1)} %get-tuple-element.59.refs_3_), channel_id=1, source_target_pairs={{0,1},{1,0},{2,3},{3,2},{4,5},{5,4},{6,7},{7,6},{8,9},{9,8},{10,11... | collective-permute-start | bytes 393224 | tf_op jit(solution)/shard_map/ppermute | solution.py:33
  13.5 12.9 %collective-permute-start.6 = (bf16[32,2176]{1,0:T(8,128)(2,1)S(1)}, bf16[32,2176]{1,0:T(8,128)(2,1)S(1)}, u32[]{:S(2)}, u32[]{:S(2)}) collective-permute-start(bf16[32,2176]{1,0:T(8,128)(2,1)S(1)} %get-tuple-element.65), channel_id=1, source_target_pairs={{0,16},{1,17},{2,18},{3,19},{4,20},{5,21},{6,22},{7,23},{8,24},{9,... | collective-permute-start | bytes 417800 | tf_op jit(solution)/shard_map/ppermute | solution.py:38
  16.4 6.9 %collective-permute-start.7 = (bf16[32,2176]{1,0:T(8,128)(2,1)S(1)}, bf16[32,2176]{1,0:T(8,128)(2,1)S(1)}, u32[]{:S(2)}, u32[]{:S(2)}) collective-permute-start(bf16[32,2176]{1,0:T(8,128)(2,1)S(1)} %get-tuple-element.65), channel_id=1, source_target_pairs={{0,8},{1,9},{2,10},{3,11},{4,12},{5,13},{6,14},{7,15},{8,0},{9,1},... | collective-permute-start | bytes 417800 | tf_op jit(solution)/shard_map/ppermute | solution.py:38
  18.0 5.1 %collective-permute-start.3 = (bf16[32,2176]{1,0:T(8,128)(2,1)S(1)}, bf16[32,2176]{1,0:T(8,128)(2,1)S(1)}, u32[]{:S(2)}, u32[]{:S(2)}) collective-permute-start(bf16[32,2176]{1,0:T(8,128)(2,1)S(1)} %get-tuple-element.65), channel_id=1, source_target_pairs={{0,1},{1,0},{2,6},{3,7},{4,5},{5,4},{6,2},{7,3},{8,9},{9,8},{10,14... | collective-permute-start | bytes 417800 | tf_op jit(solution)/shard_map/ppermute | solution.py:38
  23.3 6.7 %collective-permute-start.10 = (bf16[32,2176]{1,0:T(8,128)(2,1)S(1)}, bf16[32,2176]{1,0:T(8,128)(2,1)S(1)}, u32[]{:S(2)}, u32[]{:S(2)}) collective-permute-start(bf16[32,2176]{1,0:T(8,128)(2,1)S(1)} %collective-permute-done.7), channel_id=1, source_target_pairs={{0,1},{1,0},{2,6},{3,7},{4,5},{5,4},{6,2},{7,3},{8,9},{9,8},{10,14... | collective-permute-start | bytes 417800 | tf_op jit(solution)/shard_map/ppermute | solution.py:38
  24.9 10.2 %collective-permute-start.5 = (bf16[64,2176]{1,0:T(8,128)(2,1)S(1)}, bf16[64,2176]{1,0:T(8,128)(2,1)S(1)}, u32[]{:S(2)}, u32[]{:S(2)}) collective-permute-start(bf16[64,2176]{1,0:T(8,128)(2,1)S(1)} %constant_dynamic-update-slice_fusion), channel_id=1, source_target_pairs={{0,4},{1,5},{2,3},{3,2},{4,0},{5,1},{6,7},{7,6},{8,12},{9,13},{10,... | collective-permute-start | bytes 835592 | tf_op jit(solution)/shard_map/ppermute | solution.py:38
  26.4 5.1 %collective-permute-start.9 = (bf16[32,2176]{1,0:T(8,128)(2,1)S(1)}, bf16[32,2176]{1,0:T(8,128)(2,1)S(1)}, u32[]{:S(2)}, u32[]{:S(2)}) collective-permute-start(bf16[32,2176]{1,0:T(8,128)(2,1)S(1)} %collective-permute-done.6), channel_id=1, source_target_pairs={{0,8},{1,9},{2,10},{3,11},{4,12},{5,13},{6,14},{7,15},{8,0},{9,1},... | collective-permute-start | bytes 417800 | tf_op jit(solution)/shard_map/ppermute | solution.py:38
  27.8 6.4 %collective-permute-start.8 = (bf16[32,2176]{1,0:T(8,128)(2,1)S(1)}, bf16[32,2176]{1,0:T(8,128)(2,1)S(1)}, u32[]{:S(2)}, u32[]{:S(2)}) collective-permute-start(bf16[32,2176]{1,0:T(8,128)(2,1)S(1)} %collective-permute-done.6), channel_id=1, source_target_pairs={{0,1},{1,0},{2,6},{3,7},{4,5},{5,4},{6,2},{7,3},{8,9},{9,8},{10,14... | collective-permute-start | bytes 417800 | tf_op jit(solution)/shard_map/ppermute | solution.py:38
  30.0 13.6 %collective-permute-start.13 = (bf16[64,2176]{1,0:T(8,128)(2,1)S(1)}, bf16[64,2176]{1,0:T(8,128)(2,1)S(1)}, u32[]{:S(2)}, u32[]{:S(2)}) collective-permute-start(bf16[64,2176]{1,0:T(8,128)(2,1)S(1)} %constant_dynamic-update-slice_fusion.2), channel_id=1, source_target_pairs={{0,4},{1,5},{2,3},{3,2},{4,0},{5,1},{6,7},{7,6},{8,12},{9,13},{10,... | collective-permute-start | bytes 835592 | tf_op jit(solution)/shard_map/ppermute | solution.py:38
  31.5 6.5 %collective-permute-start.11 = (bf16[32,2176]{1,0:T(8,128)(2,1)S(1)}, bf16[32,2176]{1,0:T(8,128)(2,1)S(1)}, u32[]{:S(2)}, u32[]{:S(2)}) collective-permute-start(bf16[32,2176]{1,0:T(8,128)(2,1)S(1)} %collective-permute-done.9), channel_id=1, source_target_pairs={{0,1},{1,0},{2,6},{3,7},{4,5},{5,4},{6,2},{7,3},{8,9},{9,8},{10,14... | collective-permute-start | bytes 417800 | tf_op jit(solution)/shard_map/ppermute | solution.py:38
  34.3 6.6 %collective-permute-start.14 = (bf16[64,2176]{1,0:T(8,128)(2,1)S(1)}, bf16[64,2176]{1,0:T(8,128)(2,1)S(1)}, u32[]{:S(2)}, u32[]{:S(2)}) collective-permute-start(bf16[64,2176]{1,0:T(8,128)(2,1)S(1)} %constant_dynamic-update-slice_fusion.4), channel_id=1, source_target_pairs={{0,4},{1,5},{2,3},{3,2},{4,0},{5,1},{6,7},{7,6},{8,12},{9,13},{10,... | collective-permute-start | bytes 835592 | tf_op jit(solution)/shard_map/ppermute | solution.py:38
  38.0 11.5 %collective-permute-start.18 = (bf16[64,2176]{1,0:T(8,128)(2,1)S(1)}, bf16[64,2176]{1,0:T(8,128)(2,1)S(1)}, u32[]{:S(2)}, u32[]{:S(2)}) collective-permute-start(bf16[64,2176]{1,0:T(8,128)(2,1)S(1)} %constant_dynamic-update-slice_fusion.6), channel_id=1, source_target_pairs={{0,4},{1,5},{2,3},{3,2},{4,0},{5,1},{6,7},{7,6},{8,12},{9,13},{10,... | collective-permute-start | bytes 835592 | tf_op jit(solution)/shard_map/ppermute | solution.py:38
  39.3 9.3 %collective-permute-start.12 = (bf16[64,2048]{1,0:T(8,128)(2,1)S(1)}, bf16[64,2048]{1,0:T(8,128)(2,1)S(1)}, u32[]{:S(2)}, u32[]{:S(2)}) collective-permute-start(bf16[64,2048]{1,0:T(8,128)(2,1)S(1)} %get-tuple-element.87), channel_id=1, source_target_pairs={{0,4},{1,5},{2,3},{3,2},{4,0},{5,1},{6,7},{7,6},{8,12},{9,13},{10,... | collective-permute-start | bytes 786440 | tf_op jit(solution)/shard_map/ppermute | solution.py:38
  43.7 9.5 %collective-permute-start.17 = (bf16[64,2048]{1,0:T(8,128)(2,1)S(1)}, bf16[64,2048]{1,0:T(8,128)(2,1)S(1)}, u32[]{:S(2)}, u32[]{:S(2)}) collective-permute-start(bf16[64,2048]{1,0:T(8,128)(2,1)S(1)} %get-tuple-element.96), channel_id=1, source_target_pairs={{0,4},{1,5},{2,3},{3,2},{4,0},{5,1},{6,7},{7,6},{8,12},{9,13},{10,... | collective-permute-start | bytes 786440 | tf_op jit(solution)/shard_map/ppermute | solution.py:38
  47.2 8.3 %collective-permute-start.16 = (bf16[64,2048]{1,0:T(8,128)(2,1)S(1)}, bf16[64,2048]{1,0:T(8,128)(2,1)S(1)}, u32[]{:S(2)}, u32[]{:S(2)}) collective-permute-start(bf16[64,2048]{1,0:T(8,128)(2,1)S(1)} %get-tuple-element.94), channel_id=1, source_target_pairs={{0,4},{1,5},{2,3},{3,2},{4,0},{5,1},{6,7},{7,6},{8,12},{9,13},{10,... | collective-permute-start | bytes 786440 | tf_op jit(solution)/shard_map/ppermute | solution.py:38
  48.7 7.0 %collective-permute-start.15 = (bf16[32,2048]{1,0:T(8,128)(2,1)S(1)}, bf16[32,2048]{1,0:T(8,128)(2,1)S(1)}, u32[]{:S(2)}, u32[]{:S(2)}) collective-permute-start(bf16[32,2048]{1,0:T(8,128)(2,1)S(1)} %slice.55), channel_id=1, source_target_pairs={{0,1},{1,0},{2,6},{3,7},{4,5},{5,4},{6,2},{7,3},{8,9},{9,8},{10,14... | collective-permute-start | bytes 393224 | tf_op jit(solution)/shard_map/ppermute | solution.py:38
  52.4 7.9 %collective-permute-start.20 = (bf16[64,2048]{1,0:T(8,128)(2,1)S(1)}, bf16[64,2048]{1,0:T(8,128)(2,1)S(1)}, u32[]{:S(2)}, u32[]{:S(2)}) collective-permute-start(bf16[64,2048]{1,0:T(8,128)(2,1)S(1)} %get-tuple-element.103), channel_id=1, source_target_pairs={{0,4},{1,5},{2,3},{3,2},{4,0},{5,1},{6,7},{7,6},{8,12},{9,13},{10,... | collective-permute-start | bytes 786440 | tf_op jit(solution)/shard_map/ppermute | solution.py:38
  53.3 5.0 %collective-permute-start.21 = (bf16[32,2048]{1,0:T(8,128)(2,1)S(1)}, bf16[32,2048]{1,0:T(8,128)(2,1)S(1)}, u32[]{:S(2)}, u32[]{:S(2)}) collective-permute-start(bf16[32,2048]{1,0:T(8,128)(2,1)S(1)} %slice.53), channel_id=1, source_target_pairs={{0,1},{1,0},{2,6},{3,7},{4,5},{5,4},{6,2},{7,3},{8,9},{9,8},{10,14... | collective-permute-start | bytes 393224 | tf_op jit(solution)/shard_map/ppermute | solution.py:38
  55.7 5.7 %collective-permute-start.19 = (bf16[32,2048]{1,0:T(8,128)(2,1)S(1)}, bf16[32,2048]{1,0:T(8,128)(2,1)S(1)}, u32[]{:S(2)}, u32[]{:S(2)}) collective-permute-start(bf16[32,2048]{1,0:T(8,128)(2,1)S(1)} %slice.54), channel_id=1, source_target_pairs={{0,1},{1,0},{2,6},{3,7},{4,5},{5,4},{6,2},{7,3},{8,9},{9,8},{10,14... | collective-permute-start | bytes 393224 | tf_op jit(solution)/shard_map/ppermute | solution.py:38
  58.4 10.2 %collective-permute-start.24 = (bf16[32,2048]{1,0:T(8,128)(2,1)S(1)}, bf16[32,2048]{1,0:T(8,128)(2,1)S(1)}, u32[]{:S(2)}, u32[]{:S(2)}) collective-permute-start(bf16[32,2048]{1,0:T(8,128)(2,1)S(1)} %slice_add_fusion.1), channel_id=1, source_target_pairs={{0,16},{1,17},{2,18},{3,19},{4,20},{5,21},{6,22},{7,23},{8,24},{9,... | collective-permute-start | bytes 393224 | tf_op jit(solution)/shard_map/ppermute | solution.py:38
  60.4 5.0 %collective-permute-start.23 = (bf16[32,2048]{1,0:T(8,128)(2,1)S(1)}, bf16[32,2048]{1,0:T(8,128)(2,1)S(1)}, u32[]{:S(2)}, u32[]{:S(2)}) collective-permute-start(bf16[32,2048]{1,0:T(8,128)(2,1)S(1)} %slice.52), channel_id=1, source_target_pairs={{0,1},{1,0},{2,6},{3,7},{4,5},{5,4},{6,2},{7,3},{8,9},{9,8},{10,14... | collective-permute-start | bytes 393224 | tf_op jit(solution)/shard_map/ppermute | solution.py:38
  61.4 7.2 %collective-permute-start.22 = (bf16[32,2048]{1,0:T(8,128)(2,1)S(1)}, bf16[32,2048]{1,0:T(8,128)(2,1)S(1)}, u32[]{:S(2)}, u32[]{:S(2)}) collective-permute-start(bf16[32,2048]{1,0:T(8,128)(2,1)S(1)} %slice_add_fusion.2), channel_id=1, source_target_pairs={{0,8},{1,9},{2,10},{3,11},{4,12},{5,13},{6,14},{7,15},{8,0},{9,1},... | collective-permute-start | bytes 393224 | tf_op jit(solution)/shard_map/ppermute | solution.py:38
  65.5 6.9 %collective-permute-start.25 = (bf16[32,2048]{1,0:T(8,128)(2,1)S(1)}, bf16[32,2048]{1,0:T(8,128)(2,1)S(1)}, u32[]{:S(2)}, u32[]{:S(2)}) collective-permute-start(bf16[32,2048]{1,0:T(8,128)(2,1)S(1)} %slice_add_fusion), channel_id=1, source_target_pairs={{0,24},{1,25},{2,26},{3,27},{4,28},{5,29},{6,30},{7,31},{8,16},{9,... | collective-permute-start | bytes 393224 | tf_op jit(solution)/shard_map/ppermute | solution.py:38

commit v7 on v6

--- a/solution.py
+++ b/solution.py
@@ -219,7 +219,7 @@
 
 def attention_halves(queries, keys, values, positions, out_weight):
     rows, width = queries.shape
-    chunks = 4
+    chunks = 2
     near = pl.BlockSpec(memory_space=pltpu.VMEM)
     far = pl.BlockSpec(memory_space=pltpu.HBM)
     return pl.pallas_call(
@@ -276,7 +276,7 @@
 
 
 def loaded(weights, after):
-    pieces = 2
+    pieces = 1
     far = pl.BlockSpec(memory_space=pltpu.HBM)
     return pl.pallas_call(
         functools.partial(load_kernel, len(weights), pieces),
@@ -472,14 +472,14 @@
     kept_2, given_2 = expert(quad_2)
     sent_2 = exchanged(then.after(given_2), FAR_PLANE)
     quad_1 = joined(pair_1, taken_1)
-    kept_1, given_1 = expert(quad_1)
-    sent_1 = exchanged(then.after(given_1), FAR_PLANE)
     total_0 = added(kept_0, sent_0)
     sent_0 = sent(then.after(total_0), NEAR_PLANE)
     quad_3 = joined(pair_3, taken_3)
     kept_3, given_3 = expert(quad_3)
     sent_3 = exchanged(then.after(given_3), FAR_PLANE)
     total_2 = added(kept_2, sent_2)
+    kept_1, given_1 = expert(quad_1)
+    sent_1 = exchanged(then.after(given_1), FAR_PLANE)
     sent_2 = sent(then.after(total_2), NEAR_PLANE)
     total_1 = added(kept_1, sent_1)
     sent_1 = sent(then.after(total_1), NEAR_PLANE)

time: 73.3 us -> 72.5 us (0.989)
  transfers between devices with their start and end apart: 26 -> 26, of which waited for: 14 -> 14; matrix products, arithmetic and copies ran while one was open for 1% -> 1% of each run, Pallas kernels for 28% -> 27%
where the time goes in v7:
time: 72.5 us; the launch traced here: 72.4 us
  starting transfers between devices  34.2 us (47%)
  Pallas kernels  19.8 us (27%)
  waiting for transfers between devices  16.6 us (23%)
  other arithmetic  1.22 us (2%)
    ppermute x25, starting transfers between devices, exchanged(): lax.ppermute(shard, BOTH, [(i, i ^ masks[1 if i & BIT_CORE else 0]) for i...  31.7 us
    ppermute x25, waiting for transfers between devices, exchanged(): lax.ppermute(shard, BOTH, [(i, i ^ masks[1 if i & BIT_CORE else 0]) for i...  16.3 us
    pallas_call x4, Pallas kernels, weighted_experts(): pl.pallas_call(expert_kernel, in_specs=[whole] * 7, out_specs=[whole] * 2...  11 us
    pallas_call x1, Pallas kernels, attention_halves(): pl.pallas_call(attention_kernel, in_specs=[far] * 5, out_specs=[near] * 2...  4.81 us
    pallas_call x1, Pallas kernels, loaded(): pl.pallas_call(functools.partial(load_kernel, len(weights), pieces), in_s...  3.78 us
    ppermute x1, starting transfers between devices, swapped(): lax.ppermute(shard, axis, [(i, i ^ 1 << distance) for i in range(lax.axis...  2.56 us
  transfers between devices with their start and end apart: 26, of which 14 were waited for; matrix products, arithmetic and copies ran while one was open for 1% of the time, Pallas kernels for 27%

profile of v7, /device:TPU:0, one launch (start us, length us, event | category | flops | bytes accessed | tf_op | source)
XLA Modules:
  0.0 72.4 jit_solution(17071127550217651212)
XLA Ops:
  1.0 4.8 %attention_halves.1 = (f32[32,2048]{1,0:T(8,128)S(1)}, bf16[32,2048]{1,0:T(8,128)(2,1)S(1)}) custom-call(bf16[64,2048]{1,0:T(8,128)(2,1)} %queries_hbm.1, bf16[64,512]{1,0:T(8,128)(2,1)} %keys_hbm.1, bf16[64,512]{1,0:T(8,128)(2,1)} %values_hbm.1, s32[1,64]{1,0:T(1,128)} %bitcast.7, bf16[2048,2048]{1,0:T(8,128)(2,1)} %out_weight_hbm.1), custom_call_target="tpu_custom_call" | custom-call | flops 570425344 | bytes 8388608 | tf_op jit(solution)/shard_map/attention_halves/pallas_call | solution.py:225
  5.8 2.6 %collective-permute-start = (bf16[32,2048]{1,0:T(8,128)(2,1)S(1)}, bf16[32,2048]{1,0:T(8,128)(2,1)S(1)}, u32[]{:S(2)}, u32[]{:S(2)}) collective-permute-start(bf16[32,2048]{1,0:T(8,128)(2,1)S(1)} %get-tuple-element.60.refs_3_), channel_id=1, source_target_pairs={{0,1},{1,0},{2,3},{3,2},{4,5},{5,4},{6,7},{7,6},{8,9},{9,8},{10,11... | collective-permute-start | bytes 393224 | tf_op jit(solution)/shard_map/ppermute | solution.py:33
  8.4 3.8 %load_weights.1 = (bf16[1,2048,768]{2,1,0:T(8,128)(2,1)S(1)}, bf16[1,2048,768]{2,1,0:T(8,128)(2,1)S(1)}, bf16[1,768,2048]{2,1,0:T(8,128)(2,1)S(1)}) custom-call(bf16[1,2048,768]{2,1,0:T(8,128)(2,1)} %refs_0_.1, bf16[1,2048,768]{2,1,0:T(8,128)(2,1)} %refs_1_.1, bf16[1,768,2048]{2,1,0:T(8,128)(2,1)} %refs_2_.1, bf16[32,2048]{1,0:T(8,128)(2,1)S(1)} %get-tuple-element.60.refs_3_), custom_call_target="tpu_custom_call" | custom-call | bytes 9437184 | tf_op jit(solution)/shard_map/load_weights/pallas_call | solution.py:281
  12.8 2.9 %collective-permute-start.6 = (bf16[32,2176]{1,0:T(8,128)(2,1)S(1)}, bf16[32,2176]{1,0:T(8,128)(2,1)S(1)}, u32[]{:S(2)}, u32[]{:S(2)}) collective-permute-start(bf16[32,2176]{1,0:T(8,128)(2,1)S(1)} %get-tuple-element.66), channel_id=1, source_target_pairs={{0,16},{1,17},{2,18},{3,19},{4,20},{5,21},{6,22},{7,23},{8,24},{9,... | collective-permute-start | bytes 417800 | tf_op jit(solution)/shard_map/ppermute | solution.py:38
  15.7 1.6 %collective-permute-start.7 = (bf16[32,2176]{1,0:T(8,128)(2,1)S(1)}, bf16[32,2176]{1,0:T(8,128)(2,1)S(1)}, u32[]{:S(2)}, u32[]{:S(2)}) collective-permute-start(bf16[32,2176]{1,0:T(8,128)(2,1)S(1)} %get-tuple-element.66), channel_id=1, source_target_pairs={{0,8},{1,9},{2,10},{3,11},{4,12},{5,13},{6,14},{7,15},{8,0},{9,1},... | collective-permute-start | bytes 417800 | tf_op jit(solution)/shard_map/ppermute | solution.py:38
  17.3 1.5 %collective-permute-start.3 = (bf16[32,2176]{1,0:T(8,128)(2,1)S(1)}, bf16[32,2176]{1,0:T(8,128)(2,1)S(1)}, u32[]{:S(2)}, u32[]{:S(2)}) collective-permute-start(bf16[32,2176]{1,0:T(8,128)(2,1)S(1)} %get-tuple-element.66), channel_id=1, source_target_pairs={{0,1},{1,0},{2,6},{3,7},{4,5},{5,4},{6,2},{7,3},{8,9},{9,8},{10,14... | collective-permute-start | bytes 417800 | tf_op jit(solution)/shard_map/ppermute | solution.py:38
  18.8 3.5 %collective-permute-done.3 = bf16[32,2176]{1,0:T(8,128)(2,1)S(1)} collective-permute-done((bf16[32,2176]{1,0:T(8,128)(2,1)S(1)}, bf16[32,2176]{1,0:T(8,128)(2,1)S(1)}, u32[]{:S(2)}, u32[]{:S(2)}) %collective-permute-start.3) | collective-permute-done | bytes 139296 | tf_op jit(solution)/shard_map/ppermute | solution.py:38
  22.6 1.6 %collective-permute-start.10 = (bf16[32,2176]{1,0:T(8,128)(2,1)S(1)}, bf16[32,2176]{1,0:T(8,128)(2,1)S(1)}, u32[]{:S(2)}, u32[]{:S(2)}) collective-permute-start(bf16[32,2176]{1,0:T(8,128)(2,1)S(1)} %collective-permute-done.7), channel_id=1, source_target_pairs={{0,1},{1,0},{2,6},{3,7},{4,5},{5,4},{6,2},{7,3},{8,9},{9,8},{10,14... | collective-permute-start | bytes 417800 | tf_op jit(solution)/shard_map/ppermute | solution.py:38
  24.2 1.5 %collective-permute-start.5 = (bf16[64,2176]{1,0:T(8,128)(2,1)S(1)}, bf16[64,2176]{1,0:T(8,128)(2,1)S(1)}, u32[]{:S(2)}, u32[]{:S(2)}) collective-permute-start(bf16[64,2176]{1,0:T(8,128)(2,1)S(1)} %constant_dynamic-update-slice_fusion), channel_id=1, source_target_pairs={{0,4},{1,5},{2,3},{3,2},{4,0},{5,1},{6,7},{7,6},{8,12},{9,13},{10,... | collective-permute-start | bytes 835592 | tf_op jit(solution)/shard_map/ppermute | solution.py:38
  25.7 1.4 %collective-permute-start.9 = (bf16[32,2176]{1,0:T(8,128)(2,1)S(1)}, bf16[32,2176]{1,0:T(8,128)(2,1)S(1)}, u32[]{:S(2)}, u32[]{:S(2)}) collective-permute-start(bf16[32,2176]{1,0:T(8,128)(2,1)S(1)} %collective-permute-done.6), channel_id=1, source_target_pairs={{0,8},{1,9},{2,10},{3,11},{4,12},{5,13},{6,14},{7,15},{8,0},{9,1},... | collective-permute-start | bytes 417800 | tf_op jit(solution)/shard_map/ppermute | solution.py:38
  27.7 1.6 %collective-permute-done.10 = bf16[32,2176]{1,0:T(8,128)(2,1)S(1)} collective-permute-done((bf16[32,2176]{1,0:T(8,128)(2,1)S(1)}, bf16[32,2176]{1,0:T(8,128)(2,1)S(1)}, u32[]{:S(2)}, u32[]{:S(2)}) %collective-permute-start.10) | collective-permute-done | bytes 139296 | tf_op jit(solution)/shard_map/ppermute | solution.py:38
  29.7 1.1 %collective-permute-done.9 = bf16[32,2176]{1,0:T(8,128)(2,1)S(1)} collective-permute-done((bf16[32,2176]{1,0:T(8,128)(2,1)S(1)}, bf16[32,2176]{1,0:T(8,128)(2,1)S(1)}, u32[]{:S(2)}, u32[]{:S(2)}) %collective-permute-start.9) | collective-permute-done | bytes 139296 | tf_op jit(solution)/shard_map/ppermute | solution.py:38
  30.8 1.1 %collective-permute-start.11 = (bf16[32,2176]{1,0:T(8,128)(2,1)S(1)}, bf16[32,2176]{1,0:T(8,128)(2,1)S(1)}, u32[]{:S(2)}, u32[]{:S(2)}) collective-permute-start(bf16[32,2176]{1,0:T(8,128)(2,1)S(1)} %collective-permute-done.9), channel_id=1, source_target_pairs={{0,1},{1,0},{2,6},{3,7},{4,5},{5,4},{6,2},{7,3},{8,9},{9,8},{10,14... | collective-permute-start | bytes 417800 | tf_op jit(solution)/shard_map/ppermute | solution.py:38
  31.9 1.7 %collective-permute-done.8 = bf16[32,2176]{1,0:T(8,128)(2,1)S(1)} collective-permute-done((bf16[32,2176]{1,0:T(8,128)(2,1)S(1)}, bf16[32,2176]{1,0:T(8,128)(2,1)S(1)}, u32[]{:S(2)}, u32[]{:S(2)}) %collective-permute-start.8) | collective-permute-done | bytes 139296 | tf_op jit(solution)/shard_map/ppermute | solution.py:38
  33.6 0.8 %collective-permute-start.14 = (bf16[64,2176]{1,0:T(8,128)(2,1)S(1)}, bf16[64,2176]{1,0:T(8,128)(2,1)S(1)}, u32[]{:S(2)}, u32[]{:S(2)}) collective-permute-start(bf16[64,2176]{1,0:T(8,128)(2,1)S(1)} %constant_dynamic-update-slice_fusion.4), channel_id=1, source_target_pairs={{0,4},{1,5},{2,3},{3,2},{4,0},{5,1},{6,7},{7,6},{8,12},{9,13},{10,... | collective-permute-start | bytes 835592 | tf_op jit(solution)/shard_map/ppermute | solution.py:38
  34.5 2.7 %expert_halves.4 = (f32[64,2048]{1,0:T(8,128)S(1)}, bf16[64,2048]{1,0:T(8,128)(2,1)S(1)}) custom-call(bf16[128,2176]{1,0:T(8,128)(2,1)S(1)} %pad_maximum_fusion.rows_ref, bf16[1,2048,768]{2,1,0:T(8,128)(2,1)S(1)} %get-tuple-element.79.refs_0_, bf16[1,2048,768]{2,1,0:T(8,128)(2,1)S(1)} %get-tuple-element.80.refs_1_, ...), custom_call_target="tpu_custom_call" | custom-call | flops 2415919104 | bytes 2097152 | tf_op jit(solution)/shard_map/expert_halves/pallas_call | solution.py:391
  37.3 1.2 %collective-permute-start.18 = (bf16[64,2176]{1,0:T(8,128)(2,1)S(1)}, bf16[64,2176]{1,0:T(8,128)(2,1)S(1)}, u32[]{:S(2)}, u32[]{:S(2)}) collective-permute-start(bf16[64,2176]{1,0:T(8,128)(2,1)S(1)} %constant_dynamic-update-slice_fusion.6), channel_id=1, source_target_pairs={{0,4},{1,5},{2,3},{3,2},{4,0},{5,1},{6,7},{7,6},{8,12},{9,13},{10,... | collective-permute-start | bytes 835592 | tf_op jit(solution)/shard_map/ppermute | solution.py:38
  38.5 0.9 %collective-permute-start.12 = (bf16[64,2048]{1,0:T(8,128)(2,1)S(1)}, bf16[64,2048]{1,0:T(8,128)(2,1)S(1)}, u32[]{:S(2)}, u32[]{:S(2)}) collective-permute-start(bf16[64,2048]{1,0:T(8,128)(2,1)S(1)} %get-tuple-element.88), channel_id=1, source_target_pairs={{0,4},{1,5},{2,3},{3,2},{4,0},{5,1},{6,7},{7,6},{8,12},{9,13},{10,... | collective-permute-start | bytes 786440 | tf_op jit(solution)/shard_map/ppermute | solution.py:38
  40.2 2.7 %expert_halves.5 = (f32[64,2048]{1,0:T(8,128)S(1)}, bf16[64,2048]{1,0:T(8,128)(2,1)S(1)}) custom-call(bf16[128,2176]{1,0:T(8,128)(2,1)S(1)} %pad_maximum_fusion.1.rows_ref, bf16[1,2048,768]{2,1,0:T(8,128)(2,1)S(1)} %get-tuple-element.79.refs_0_, bf16[1,2048,768]{2,1,0:T(8,128)(2,1)S(1)} %get-tuple-element.80.refs_1_, ...), custom_call_target="tpu_custom_call" | custom-call | flops 2415919104 | bytes 2097152 | tf_op jit(solution)/shard_map/expert_halves/pallas_call | solution.py:391
  43.0 0.8 %collective-permute-start.20 = (bf16[64,2048]{1,0:T(8,128)(2,1)S(1)}, bf16[64,2048]{1,0:T(8,128)(2,1)S(1)}, u32[]{:S(2)}, u32[]{:S(2)}) collective-permute-start(bf16[64,2048]{1,0:T(8,128)(2,1)S(1)} %get-tuple-element.103), channel_id=1, source_target_pairs={{0,4},{1,5},{2,3},{3,2},{4,0},{5,1},{6,7},{7,6},{8,12},{9,13},{10,... | collective-permute-start | bytes 786440 | tf_op jit(solution)/shard_map/ppermute | solution.py:38
  43.8 2.7 %expert_halves.6 = (f32[64,2048]{1,0:T(8,128)S(1)}, bf16[64,2048]{1,0:T(8,128)(2,1)S(1)}) custom-call(bf16[128,2176]{1,0:T(8,128)(2,1)S(1)} %constant_dynamic-update-slice_fusion.8.rows_ref, bf16[1,2048,768]{2,1,0:T(8,128)(2,1)S(1)} %get-tuple-element.79.refs_0_, bf16[1,2048,768]{2,1,0:T(8,128)(2,1)S(1)} %get-tuple-element.80.refs_1_, ...), custom_call_target="tpu_custom_call" | custom-call | flops 2415919104 | bytes 2097152 | tf_op jit(solution)/shard_map/expert_halves/pallas_call | solution.py:391
  46.5 1.3 %collective-permute-start.16 = (bf16[64,2048]{1,0:T(8,128)(2,1)S(1)}, bf16[64,2048]{1,0:T(8,128)(2,1)S(1)}, u32[]{:S(2)}, u32[]{:S(2)}) collective-permute-start(bf16[64,2048]{1,0:T(8,128)(2,1)S(1)} %get-tuple-element.95), channel_id=1, source_target_pairs={{0,4},{1,5},{2,3},{3,2},{4,0},{5,1},{6,7},{7,6},{8,12},{9,13},{10,... | collective-permute-start | bytes 786440 | tf_op jit(solution)/shard_map/ppermute | solution.py:38
  48.8 2.9 %expert_halves.7 = (f32[64,2048]{1,0:T(8,128)S(1)}, bf16[64,2048]{1,0:T(8,128)(2,1)S(1)}) custom-call(bf16[128,2176]{1,0:T(8,128)(2,1)S(1)} %pad_maximum_fusion.2.rows_ref, bf16[1,2048,768]{2,1,0:T(8,128)(2,1)S(1)} %get-tuple-element.79.refs_0_, bf16[1,2048,768]{2,1,0:T(8,128)(2,1)S(1)} %get-tuple-element.80.refs_1_, ...), custom_call_target="tpu_custom_call" | custom-call | flops 2415919104 | bytes 2097152 | tf_op jit(solution)/shard_map/expert_halves/pallas_call | solution.py:391
  52.6 1.4 %collective-permute-start.21 = (bf16[32,2048]{1,0:T(8,128)(2,1)S(1)}, bf16[32,2048]{1,0:T(8,128)(2,1)S(1)}, u32[]{:S(2)}, u32[]{:S(2)}) collective-permute-start(bf16[32,2048]{1,0:T(8,128)(2,1)S(1)} %slice.53), channel_id=1, source_target_pairs={{0,1},{1,0},{2,6},{3,7},{4,5},{5,4},{6,2},{7,3},{8,9},{9,8},{10,14... | collective-permute-start | bytes 393224 | tf_op jit(solution)/shard_map/ppermute | solution.py:38
  54.9 1.9 %collective-permute-start.17 = (bf16[32,2048]{1,0:T(8,128)(2,1)S(1)}, bf16[32,2048]{1,0:T(8,128)(2,1)S(1)}, u32[]{:S(2)}, u32[]{:S(2)}) collective-permute-start(bf16[32,2048]{1,0:T(8,128)(2,1)S(1)} %slice.54), channel_id=1, source_target_pairs={{0,1},{1,0},{2,6},{3,7},{4,5},{5,4},{6,2},{7,3},{8,9},{9,8},{10,14... | collective-permute-start | bytes 393224 | tf_op jit(solution)/shard_map/ppermute | solution.py:38
  56.8 0.9 %collective-permute-done.21 = bf16[32,2048]{1,0:T(8,128)(2,1)S(1)} collective-permute-done((bf16[32,2048]{1,0:T(8,128)(2,1)S(1)}, bf16[32,2048]{1,0:T(8,128)(2,1)S(1)}, u32[]{:S(2)}, u32[]{:S(2)}) %collective-permute-start.21) | collective-permute-done | bytes 131104 | tf_op jit(solution)/shard_map/ppermute | solution.py:38
  57.7 1.6 %collective-permute-start.24 = (bf16[32,2048]{1,0:T(8,128)(2,1)S(1)}, bf16[32,2048]{1,0:T(8,128)(2,1)S(1)}, u32[]{:S(2)}, u32[]{:S(2)}) collective-permute-start(bf16[32,2048]{1,0:T(8,128)(2,1)S(1)} %slice_add_fusion.1), channel_id=1, source_target_pairs={{0,16},{1,17},{2,18},{3,19},{4,20},{5,21},{6,22},{7,23},{8,24},{9,... | collective-permute-start | bytes 393224 | tf_op jit(solution)/shard_map/ppermute | solution.py:38
  59.7 1.0 %collective-permute-start.23 = (bf16[32,2048]{1,0:T(8,128)(2,1)S(1)}, bf16[32,2048]{1,0:T(8,128)(2,1)S(1)}, u32[]{:S(2)}, u32[]{:S(2)}) collective-permute-start(bf16[32,2048]{1,0:T(8,128)(2,1)S(1)} %slice.52), channel_id=1, source_target_pairs={{0,1},{1,0},{2,6},{3,7},{4,5},{5,4},{6,2},{7,3},{8,9},{9,8},{10,14... | collective-permute-start | bytes 393224 | tf_op jit(solution)/shard_map/ppermute | solution.py:38
  60.7 3.3 %collective-permute-start.22 = (bf16[32,2048]{1,0:T(8,128)(2,1)S(1)}, bf16[32,2048]{1,0:T(8,128)(2,1)S(1)}, u32[]{:S(2)}, u32[]{:S(2)}) collective-permute-start(bf16[32,2048]{1,0:T(8,128)(2,1)S(1)} %slice_add_fusion.2), channel_id=1, source_target_pairs={{0,8},{1,9},{2,10},{3,11},{4,12},{5,13},{6,14},{7,15},{8,0},{9,1},... | collective-permute-start | bytes 393224 | tf_op jit(solution)/shard_map/ppermute | solution.py:38
  64.7 2.3 %collective-permute-start.25 = (bf16[32,2048]{1,0:T(8,128)(2,1)S(1)}, bf16[32,2048]{1,0:T(8,128)(2,1)S(1)}, u32[]{:S(2)}, u32[]{:S(2)}) collective-permute-start(bf16[32,2048]{1,0:T(8,128)(2,1)S(1)} %slice_add_fusion), channel_id=1, source_target_pairs={{0,24},{1,25},{2,26},{3,27},{4,28},{5,29},{6,30},{7,31},{8,16},{9,... | collective-permute-start | bytes 393224 | tf_op jit(solution)/shard_map/ppermute | solution.py:38
  67.0 0.9 %collective-permute-done.22 = bf16[32,2048]{1,0:T(8,128)(2,1)S(1)} collective-permute-done((bf16[32,2048]{1,0:T(8,128)(2,1)S(1)}, bf16[32,2048]{1,0:T(8,128)(2,1)S(1)}, u32[]{:S(2)}, u32[]{:S(2)}) %collective-permute-start.22) | collective-permute-done | bytes 131104 | tf_op jit(solution)/shard_map/ppermute | solution.py:38
  67.9 3.7 %collective-permute-done.25 = bf16[32,2048]{1,0:T(8,128)(2,1)S(1)} collective-permute-done((bf16[32,2048]{1,0:T(8,128)(2,1)S(1)}, bf16[32,2048]{1,0:T(8,128)(2,1)S(1)}, u32[]{:S(2)}, u32[]{:S(2)}) %collective-permute-start.25) | collective-permute-done | bytes 131104 | tf_op jit(solution)/shard_map/ppermute | solution.py:38
  (60 shorter events, 8.4 us)
Async XLA Ops:
  0.0 12.6 %collective-permute-start.1 = (bf16[1,2048,768]{2,1,0:T(8,128)(2,1)}, bf16[1,2048,768]{2,1,0:T(8,128)(2,1)S(1)}, u32[]{:S(2)}, u32[]{:S(2)}) collective-permute-start(bf16[1,2048,768]{2,1,0:T(8,128)(2,1)} %refs_0_.1), channel_id=1, source_target_pairs={{0,2},{1,3},{2,0},{3,1},{4,6},{5,7},{6,4},{7,5},{8,10},{9,11},{10,... | collective-permute-start | bytes 9437192 | tf_op jit(solution)/shard_map/ppermute | solution.py:38
  0.5 12.1 %collective-permute-start.2 = (bf16[1,2048,768]{2,1,0:T(8,128)(2,1)}, bf16[1,2048,768]{2,1,0:T(8,128)(2,1)S(1)}, u32[]{:S(2)}, u32[]{:S(2)}) collective-permute-start(bf16[1,2048,768]{2,1,0:T(8,128)(2,1)} %refs_1_.1), channel_id=1, source_target_pairs={{0,2},{1,3},{2,0},{3,1},{4,6},{5,7},{6,4},{7,5},{8,10},{9,11},{10,... | collective-permute-start | bytes 9437192 | tf_op jit(solution)/shard_map/ppermute | solution.py:38
  0.5 18.3 %collective-permute-start.4 = (bf16[1,768,2048]{2,1,0:T(8,128)(2,1)}, bf16[1,768,2048]{2,1,0:T(8,128)(2,1)S(1)}, u32[]{:S(2)}, u32[]{:S(2)}) collective-permute-start(bf16[1,768,2048]{2,1,0:T(8,128)(2,1)} %refs_2_.1), channel_id=1, source_target_pairs={{0,2},{1,3},{2,0},{3,1},{4,6},{5,7},{6,4},{7,5},{8,10},{9,11},{10,... | collective-permute-start | bytes 9437192 | tf_op jit(solution)/shard_map/ppermute | solution.py:38
  5.8 6.8 %copy-start = (bf16[32,2048]{1,0:T(8,128)(2,1)S(1)}, bf16[32,2048]{1,0:T(8,128)(2,1)}, u32[]{:S(2)}) copy-start(bf16[32,2048]{1,0:T(8,128)(2,1)} %residual_ref.1) | copy-start | bytes 393220
  5.8 6.8 %copy-start.1 = (f32[2048]{0:T(1024)S(1)}, f32[2048]{0:T(1024)}, u32[]{:S(2)}) copy-start(f32[2048]{0:T(1024)} %param.18) | copy-start | bytes 24580
  5.8 6.8 %copy-start.2 = (s32[64,8]{0,1:T(8,128)S(1)}, s32[64,8]{0,1:T(8,128)}, u32[]{:S(2)}) copy-start(s32[64,8]{0,1:T(8,128)} %param.19) | copy-start | bytes 6148
  5.8 6.8 %copy-start.3 = (f32[64,8]{0,1:T(8,128)S(1)}, f32[64,8]{0,1:T(8,128)}, u32[]{:S(2)}) copy-start(f32[64,8]{0,1:T(8,128)} %param.20) | copy-start | bytes 6148
  5.8 6.7 %collective-permute-start = (bf16[32,2048]{1,0:T(8,128)(2,1)S(1)}, bf16[32,2048]{1,0:T(8,128)(2,1)S(1)}, u32[]{:S(2)}, u32[]{:S(2)}) collective-permute-start(bf16[32,2048]{1,0:T(8,128)(2,1)S(1)} %get-tuple-element.60.refs_3_), channel_id=1, source_target_pairs={{0,1},{1,0},{2,3},{3,2},{4,5},{5,4},{6,7},{7,6},{8,9},{9,8},{10,11... | collective-permute-start | bytes 393224 | tf_op jit(solution)/shard_map/ppermute | solution.py:33
  12.8 12.9 %collective-permute-start.6 = (bf16[32,2176]{1,0:T(8,128)(2,1)S(1)}, bf16[32,2176]{1,0:T(8,128)(2,1)S(1)}, u32[]{:S(2)}, u32[]{:S(2)}) collective-permute-start(bf16[32,2176]{1,0:T(8,128)(2,1)S(1)} %get-tuple-element.66), channel_id=1, source_target_pairs={{0,16},{1,17},{2,18},{3,19},{4,20},{5,21},{6,22},{7,23},{8,24},{9,... | collective-permute-start | bytes 417800 | tf_op jit(solution)/shard_map/ppermute | solution.py:38
  15.7 6.9 %collective-permute-start.7 = (bf16[32,2176]{1,0:T(8,128)(2,1)S(1)}, bf16[32,2176]{1,0:T(8,128)(2,1)S(1)}, u32[]{:S(2)}, u32[]{:S(2)}) collective-permute-start(bf16[32,2176]{1,0:T(8,128)(2,1)S(1)} %get-tuple-element.66), channel_id=1, source_target_pairs={{0,8},{1,9},{2,10},{3,11},{4,12},{5,13},{6,14},{7,15},{8,0},{9,1},... | collective-permute-start | bytes 417800 | tf_op jit(solution)/shard_map/ppermute | solution.py:38
  17.3 5.1 %collective-permute-start.3 = (bf16[32,2176]{1,0:T(8,128)(2,1)S(1)}, bf16[32,2176]{1,0:T(8,128)(2,1)S(1)}, u32[]{:S(2)}, u32[]{:S(2)}) collective-permute-start(bf16[32,2176]{1,0:T(8,128)(2,1)S(1)} %get-tuple-element.66), channel_id=1, source_target_pairs={{0,1},{1,0},{2,6},{3,7},{4,5},{5,4},{6,2},{7,3},{8,9},{9,8},{10,14... | collective-permute-start | bytes 417800 | tf_op jit(solution)/shard_map/ppermute | solution.py:38
  22.6 6.7 %collective-permute-start.10 = (bf16[32,2176]{1,0:T(8,128)(2,1)S(1)}, bf16[32,2176]{1,0:T(8,128)(2,1)S(1)}, u32[]{:S(2)}, u32[]{:S(2)}) collective-permute-start(bf16[32,2176]{1,0:T(8,128)(2,1)S(1)} %collective-permute-done.7), channel_id=1, source_target_pairs={{0,1},{1,0},{2,6},{3,7},{4,5},{5,4},{6,2},{7,3},{8,9},{9,8},{10,14... | collective-permute-start | bytes 417800 | tf_op jit(solution)/shard_map/ppermute | solution.py:38
  24.2 10.2 %collective-permute-start.5 = (bf16[64,2176]{1,0:T(8,128)(2,1)S(1)}, bf16[64,2176]{1,0:T(8,128)(2,1)S(1)}, u32[]{:S(2)}, u32[]{:S(2)}) collective-permute-start(bf16[64,2176]{1,0:T(8,128)(2,1)S(1)} %constant_dynamic-update-slice_fusion), channel_id=1, source_target_pairs={{0,4},{1,5},{2,3},{3,2},{4,0},{5,1},{6,7},{7,6},{8,12},{9,13},{10,... | collective-permute-start | bytes 835592 | tf_op jit(solution)/shard_map/ppermute | solution.py:38
  25.7 5.1 %collective-permute-start.9 = (bf16[32,2176]{1,0:T(8,128)(2,1)S(1)}, bf16[32,2176]{1,0:T(8,128)(2,1)S(1)}, u32[]{:S(2)}, u32[]{:S(2)}) collective-permute-start(bf16[32,2176]{1,0:T(8,128)(2,1)S(1)} %collective-permute-done.6), channel_id=1, source_target_pairs={{0,8},{1,9},{2,10},{3,11},{4,12},{5,13},{6,14},{7,15},{8,0},{9,1},... | collective-permute-start | bytes 417800 | tf_op jit(solution)/shard_map/ppermute | solution.py:38
  27.1 6.4 %collective-permute-start.8 = (bf16[32,2176]{1,0:T(8,128)(2,1)S(1)}, bf16[32,2176]{1,0:T(8,128)(2,1)S(1)}, u32[]{:S(2)}, u32[]{:S(2)}) collective-permute-start(bf16[32,2176]{1,0:T(8,128)(2,1)S(1)} %collective-permute-done.6), channel_id=1, source_target_pairs={{0,1},{1,0},{2,6},{3,7},{4,5},{5,4},{6,2},{7,3},{8,9},{9,8},{10,14... | collective-permute-start | bytes 417800 | tf_op jit(solution)/shard_map/ppermute | solution.py:38
  29.3 13.6 %collective-permute-start.13 = (bf16[64,2176]{1,0:T(8,128)(2,1)S(1)}, bf16[64,2176]{1,0:T(8,128)(2,1)S(1)}, u32[]{:S(2)}, u32[]{:S(2)}) collective-permute-start(bf16[64,2176]{1,0:T(8,128)(2,1)S(1)} %get-tuple-element.114), channel_id=1, source_target_pairs={{0,4},{1,5},{2,3},{3,2},{4,0},{5,1},{6,7},{7,6},{8,12},{9,13},{10,... | collective-permute-start | bytes 835592 | tf_op jit(solution)/shard_map/ppermute | solution.py:38
  30.8 6.5 %collective-permute-start.11 = (bf16[32,2176]{1,0:T(8,128)(2,1)S(1)}, bf16[32,2176]{1,0:T(8,128)(2,1)S(1)}, u32[]{:S(2)}, u32[]{:S(2)}) collective-permute-start(bf16[32,2176]{1,0:T(8,128)(2,1)S(1)} %collective-permute-done.9), channel_id=1, source_target_pairs={{0,1},{1,0},{2,6},{3,7},{4,5},{5,4},{6,2},{7,3},{8,9},{9,8},{10,14... | collective-permute-start | bytes 417800 | tf_op jit(solution)/shard_map/ppermute | solution.py:38
  33.6 6.6 %collective-permute-start.14 = (bf16[64,2176]{1,0:T(8,128)(2,1)S(1)}, bf16[64,2176]{1,0:T(8,128)(2,1)S(1)}, u32[]{:S(2)}, u32[]{:S(2)}) collective-permute-start(bf16[64,2176]{1,0:T(8,128)(2,1)S(1)} %constant_dynamic-update-slice_fusion.4), channel_id=1, source_target_pairs={{0,4},{1,5},{2,3},{3,2},{4,0},{5,1},{6,7},{7,6},{8,12},{9,13},{10,... | collective-permute-start | bytes 835592 | tf_op jit(solution)/shard_map/ppermute | solution.py:38
  37.3 11.5 %collective-permute-start.18 = (bf16[64,2176]{1,0:T(8,128)(2,1)S(1)}, bf16[64,2176]{1,0:T(8,128)(2,1)S(1)}, u32[]{:S(2)}, u32[]{:S(2)}) collective-permute-start(bf16[64,2176]{1,0:T(8,128)(2,1)S(1)} %constant_dynamic-update-slice_fusion.6), channel_id=1, source_target_pairs={{0,4},{1,5},{2,3},{3,2},{4,0},{5,1},{6,7},{7,6},{8,12},{9,13},{10,... | collective-permute-start | bytes 835592 | tf_op jit(solution)/shard_map/ppermute | solution.py:38
  38.5 9.3 %collective-permute-start.12 = (bf16[64,2048]{1,0:T(8,128)(2,1)S(1)}, bf16[64,2048]{1,0:T(8,128)(2,1)S(1)}, u32[]{:S(2)}, u32[]{:S(2)}) collective-permute-start(bf16[64,2048]{1,0:T(8,128)(2,1)S(1)} %get-tuple-element.88), channel_id=1, source_target_pairs={{0,4},{1,5},{2,3},{3,2},{4,0},{5,1},{6,7},{7,6},{8,12},{9,13},{10,... | collective-permute-start | bytes 786440 | tf_op jit(solution)/shard_map/ppermute | solution.py:38
  43.0 9.6 %collective-permute-start.20 = (bf16[64,2048]{1,0:T(8,128)(2,1)S(1)}, bf16[64,2048]{1,0:T(8,128)(2,1)S(1)}, u32[]{:S(2)}, u32[]{:S(2)}) collective-permute-start(bf16[64,2048]{1,0:T(8,128)(2,1)S(1)} %get-tuple-element.103), channel_id=1, source_target_pairs={{0,4},{1,5},{2,3},{3,2},{4,0},{5,1},{6,7},{7,6},{8,12},{9,13},{10,... | collective-permute-start | bytes 786440 | tf_op jit(solution)/shard_map/ppermute | solution.py:38
  46.5 8.3 %collective-permute-start.16 = (bf16[64,2048]{1,0:T(8,128)(2,1)S(1)}, bf16[64,2048]{1,0:T(8,128)(2,1)S(1)}, u32[]{:S(2)}, u32[]{:S(2)}) collective-permute-start(bf16[64,2048]{1,0:T(8,128)(2,1)S(1)} %get-tuple-element.95), channel_id=1, source_target_pairs={{0,4},{1,5},{2,3},{3,2},{4,0},{5,1},{6,7},{7,6},{8,12},{9,13},{10,... | collective-permute-start | bytes 786440 | tf_op jit(solution)/shard_map/ppermute | solution.py:38
  48.0 6.9 %collective-permute-start.15 = (bf16[32,2048]{1,0:T(8,128)(2,1)S(1)}, bf16[32,2048]{1,0:T(8,128)(2,1)S(1)}, u32[]{:S(2)}, u32[]{:S(2)}) collective-permute-start(bf16[32,2048]{1,0:T(8,128)(2,1)S(1)} %slice.55), channel_id=1, source_target_pairs={{0,1},{1,0},{2,6},{3,7},{4,5},{5,4},{6,2},{7,3},{8,9},{9,8},{10,14... | collective-permute-start | bytes 393224 | tf_op jit(solution)/shard_map/ppermute | solution.py:38
  51.7 7.9 %collective-permute-start.19 = (bf16[64,2048]{1,0:T(8,128)(2,1)S(1)}, bf16[64,2048]{1,0:T(8,128)(2,1)S(1)}, u32[]{:S(2)}, u32[]{:S(2)}) collective-permute-start(bf16[64,2048]{1,0:T(8,128)(2,1)S(1)} %get-tuple-element.101), channel_id=1, source_target_pairs={{0,4},{1,5},{2,3},{3,2},{4,0},{5,1},{6,7},{7,6},{8,12},{9,13},{10,... | collective-permute-start | bytes 786440 | tf_op jit(solution)/shard_map/ppermute | solution.py:38
  52.6 5.0 %collective-permute-start.21 = (bf16[32,2048]{1,0:T(8,128)(2,1)S(1)}, bf16[32,2048]{1,0:T(8,128)(2,1)S(1)}, u32[]{:S(2)}, u32[]{:S(2)}) collective-permute-start(bf16[32,2048]{1,0:T(8,128)(2,1)S(1)} %slice.53), channel_id=1, source_target_pairs={{0,1},{1,0},{2,6},{3,7},{4,5},{5,4},{6,2},{7,3},{8,9},{9,8},{10,14... | collective-permute-start | bytes 393224 | tf_op jit(solution)/shard_map/ppermute | solution.py:38
  54.9 5.8 %collective-permute-start.17 = (bf16[32,2048]{1,0:T(8,128)(2,1)S(1)}, bf16[32,2048]{1,0:T(8,128)(2,1)S(1)}, u32[]{:S(2)}, u32[]{:S(2)}) collective-permute-start(bf16[32,2048]{1,0:T(8,128)(2,1)S(1)} %slice.54), channel_id=1, source_target_pairs={{0,1},{1,0},{2,6},{3,7},{4,5},{5,4},{6,2},{7,3},{8,9},{9,8},{10,14... | collective-permute-start | bytes 393224 | tf_op jit(solution)/shard_map/ppermute | solution.py:38
  57.7 10.2 %collective-permute-start.24 = (bf16[32,2048]{1,0:T(8,128)(2,1)S(1)}, bf16[32,2048]{1,0:T(8,128)(2,1)S(1)}, u32[]{:S(2)}, u32[]{:S(2)}) collective-permute-start(bf16[32,2048]{1,0:T(8,128)(2,1)S(1)} %slice_add_fusion.1), channel_id=1, source_target_pairs={{0,16},{1,17},{2,18},{3,19},{4,20},{5,21},{6,22},{7,23},{8,24},{9,... | collective-permute-start | bytes 393224 | tf_op jit(solution)/shard_map/ppermute | solution.py:38
  59.7 5.0 %collective-permute-start.23 = (bf16[32,2048]{1,0:T(8,128)(2,1)S(1)}, bf16[32,2048]{1,0:T(8,128)(2,1)S(1)}, u32[]{:S(2)}, u32[]{:S(2)}) collective-permute-start(bf16[32,2048]{1,0:T(8,128)(2,1)S(1)} %slice.52), channel_id=1, source_target_pairs={{0,1},{1,0},{2,6},{3,7},{4,5},{5,4},{6,2},{7,3},{8,9},{9,8},{10,14... | collective-permute-start | bytes 393224 | tf_op jit(solution)/shard_map/ppermute | solution.py:38
  60.7 7.2 %collective-permute-start.22 = (bf16[32,2048]{1,0:T(8,128)(2,1)S(1)}, bf16[32,2048]{1,0:T(8,128)(2,1)S(1)}, u32[]{:S(2)}, u32[]{:S(2)}) collective-permute-start(bf16[32,2048]{1,0:T(8,128)(2,1)S(1)} %slice_add_fusion.2), channel_id=1, source_target_pairs={{0,8},{1,9},{2,10},{3,11},{4,12},{5,13},{6,14},{7,15},{8,0},{9,1},... | collective-permute-start | bytes 393224 | tf_op jit(solution)/shard_map/ppermute | solution.py:38
  64.7 6.9 %collective-permute-start.25 = (bf16[32,2048]{1,0:T(8,128)(2,1)S(1)}, bf16[32,2048]{1,0:T(8,128)(2,1)S(1)}, u32[]{:S(2)}, u32[]{:S(2)}) collective-permute-start(bf16[32,2048]{1,0:T(8,128)(2,1)S(1)} %slice_add_fusion), channel_id=1, source_target_pairs={{0,24},{1,25},{2,26},{3,27},{4,28},{5,29},{6,30},{7,31},{8,16},{9,... | collective-permute-start | bytes 393224 | tf_op jit(solution)/shard_map/ppermute | solution.py:38

commit v8 on v7

--- a/solution.py
+++ b/solution.py
@@ -492,8 +492,8 @@
     home_1 = exchanged(narrowed(then.after(total_1)), NEAR_LINE)
     total_3 = added(kept(total_3), sent_3)
     home_3 = exchanged(narrowed(then.after(total_3)), BOTH_LINE)
+    home_2 = then(home_2)
     home_1 = then(home_1)
-    home_2 = then(home_2)
     home_3 = then(home_3)
     mixture = total_0 + widened(home_1) + widened(home_2) + widened(home_3)
     return (middle_own + mixture).astype(jnp.bfloat16)

time: 72.5 us -> 72.6 us (level)
  no operation moved by 1% of the time
where the time goes in v8:
time: 72.6 us; the launch traced here: 72.4 us
  starting transfers between devices  34.2 us (47%)
  Pallas kernels  19.8 us (27%)
  waiting for transfers between devices  16.6 us (23%)
  other arithmetic  1.23 us (2%)
    ppermute x25, starting transfers between devices, exchanged(): lax.ppermute(shard, BOTH, [(i, i ^ masks[1 if i & BIT_CORE else 0]) for i...  31.7 us
    ppermute x25, waiting for transfers between devices, exchanged(): lax.ppermute(shard, BOTH, [(i, i ^ masks[1 if i & BIT_CORE else 0]) for i...  16.3 us
    pallas_call x4, Pallas kernels, weighted_experts(): pl.pallas_call(expert_kernel, in_specs=[whole] * 7, out_specs=[whole] * 2...  11 us
    pallas_call x1, Pallas kernels, attention_halves(): pl.pallas_call(attention_kernel, in_specs=[far] * 5, out_specs=[near] * 2...  4.81 us
    pallas_call x1, Pallas kernels, loaded(): pl.pallas_call(functools.partial(load_kernel, len(weights), pieces), in_s...  3.78 us
    ppermute x1, starting transfers between devices, swapped(): lax.ppermute(shard, axis, [(i, i ^ 1 << distance) for i in range(lax.axis...  2.56 us
  transfers between devices with their start and end apart: 26, of which 14 were waited for; matrix products, arithmetic and copies ran while one was open for 1% of the time, Pallas kernels for 27%

profile of v8, /device:TPU:0, one launch (start us, length us, event | category | flops | bytes accessed | tf_op | source)
XLA Modules:
  0.0 72.4 jit_solution(6636028292055357891)
XLA Ops:
  1.0 4.8 %attention_halves.1 = (f32[32,2048]{1,0:T(8,128)S(1)}, bf16[32,2048]{1,0:T(8,128)(2,1)S(1)}) custom-call(bf16[64,2048]{1,0:T(8,128)(2,1)} %queries_hbm.1, bf16[64,512]{1,0:T(8,128)(2,1)} %keys_hbm.1, bf16[64,512]{1,0:T(8,128)(2,1)} %values_hbm.1, s32[1,64]{1,0:T(1,128)} %bitcast.7, bf16[2048,2048]{1,0:T(8,128)(2,1)} %out_weight_hbm.1), custom_call_target="tpu_custom_call" | custom-call | flops 570425344 | bytes 8388608 | tf_op jit(solution)/shard_map/attention_halves/pallas_call | solution.py:225
  5.8 2.6 %collective-permute-start = (bf16[32,2048]{1,0:T(8,128)(2,1)S(1)}, bf16[32,2048]{1,0:T(8,128)(2,1)S(1)}, u32[]{:S(2)}, u32[]{:S(2)}) collective-permute-start(bf16[32,2048]{1,0:T(8,128)(2,1)S(1)} %get-tuple-element.60.refs_3_), channel_id=1, source_target_pairs={{0,1},{1,0},{2,3},{3,2},{4,5},{5,4},{6,7},{7,6},{8,9},{9,8},{10,11... | collective-permute-start | bytes 393224 | tf_op jit(solution)/shard_map/ppermute | solution.py:33
  8.4 3.8 %load_weights.1 = (bf16[1,2048,768]{2,1,0:T(8,128)(2,1)S(1)}, bf16[1,2048,768]{2,1,0:T(8,128)(2,1)S(1)}, bf16[1,768,2048]{2,1,0:T(8,128)(2,1)S(1)}) custom-call(bf16[1,2048,768]{2,1,0:T(8,128)(2,1)} %refs_0_.1, bf16[1,2048,768]{2,1,0:T(8,128)(2,1)} %refs_1_.1, bf16[1,768,2048]{2,1,0:T(8,128)(2,1)} %refs_2_.1, bf16[32,2048]{1,0:T(8,128)(2,1)S(1)} %get-tuple-element.60.refs_3_), custom_call_target="tpu_custom_call" | custom-call | bytes 9437184 | tf_op jit(solution)/shard_map/load_weights/pallas_call | solution.py:281
  12.8 2.9 %collective-permute-start.6 = (bf16[32,2176]{1,0:T(8,128)(2,1)S(1)}, bf16[32,2176]{1,0:T(8,128)(2,1)S(1)}, u32[]{:S(2)}, u32[]{:S(2)}) collective-permute-start(bf16[32,2176]{1,0:T(8,128)(2,1)S(1)} %get-tuple-element.66), channel_id=1, source_target_pairs={{0,16},{1,17},{2,18},{3,19},{4,20},{5,21},{6,22},{7,23},{8,24},{9,... | collective-permute-start | bytes 417800 | tf_op jit(solution)/shard_map/ppermute | solution.py:38
  15.7 1.6 %collective-permute-start.7 = (bf16[32,2176]{1,0:T(8,128)(2,1)S(1)}, bf16[32,2176]{1,0:T(8,128)(2,1)S(1)}, u32[]{:S(2)}, u32[]{:S(2)}) collective-permute-start(bf16[32,2176]{1,0:T(8,128)(2,1)S(1)} %get-tuple-element.66), channel_id=1, source_target_pairs={{0,8},{1,9},{2,10},{3,11},{4,12},{5,13},{6,14},{7,15},{8,0},{9,1},... | collective-permute-start | bytes 417800 | tf_op jit(solution)/shard_map/ppermute | solution.py:38
  17.3 1.5 %collective-permute-start.3 = (bf16[32,2176]{1,0:T(8,128)(2,1)S(1)}, bf16[32,2176]{1,0:T(8,128)(2,1)S(1)}, u32[]{:S(2)}, u32[]{:S(2)}) collective-permute-start(bf16[32,2176]{1,0:T(8,128)(2,1)S(1)} %get-tuple-element.66), channel_id=1, source_target_pairs={{0,1},{1,0},{2,6},{3,7},{4,5},{5,4},{6,2},{7,3},{8,9},{9,8},{10,14... | collective-permute-start | bytes 417800 | tf_op jit(solution)/shard_map/ppermute | solution.py:38
  18.8 3.5 %collective-permute-done.3 = bf16[32,2176]{1,0:T(8,128)(2,1)S(1)} collective-permute-done((bf16[32,2176]{1,0:T(8,128)(2,1)S(1)}, bf16[32,2176]{1,0:T(8,128)(2,1)S(1)}, u32[]{:S(2)}, u32[]{:S(2)}) %collective-permute-start.3) | collective-permute-done | bytes 139296 | tf_op jit(solution)/shard_map/ppermute | solution.py:38
  22.6 1.6 %collective-permute-start.10 = (bf16[32,2176]{1,0:T(8,128)(2,1)S(1)}, bf16[32,2176]{1,0:T(8,128)(2,1)S(1)}, u32[]{:S(2)}, u32[]{:S(2)}) collective-permute-start(bf16[32,2176]{1,0:T(8,128)(2,1)S(1)} %collective-permute-done.7), channel_id=1, source_target_pairs={{0,1},{1,0},{2,6},{3,7},{4,5},{5,4},{6,2},{7,3},{8,9},{9,8},{10,14... | collective-permute-start | bytes 417800 | tf_op jit(solution)/shard_map/ppermute | solution.py:38
  24.2 1.5 %collective-permute-start.5 = (bf16[64,2176]{1,0:T(8,128)(2,1)S(1)}, bf16[64,2176]{1,0:T(8,128)(2,1)S(1)}, u32[]{:S(2)}, u32[]{:S(2)}) collective-permute-start(bf16[64,2176]{1,0:T(8,128)(2,1)S(1)} %constant_dynamic-update-slice_fusion), channel_id=1, source_target_pairs={{0,4},{1,5},{2,3},{3,2},{4,0},{5,1},{6,7},{7,6},{8,12},{9,13},{10,... | collective-permute-start | bytes 835592 | tf_op jit(solution)/shard_map/ppermute | solution.py:38
  25.7 1.4 %collective-permute-start.9 = (bf16[32,2176]{1,0:T(8,128)(2,1)S(1)}, bf16[32,2176]{1,0:T(8,128)(2,1)S(1)}, u32[]{:S(2)}, u32[]{:S(2)}) collective-permute-start(bf16[32,2176]{1,0:T(8,128)(2,1)S(1)} %collective-permute-done.6), channel_id=1, source_target_pairs={{0,8},{1,9},{2,10},{3,11},{4,12},{5,13},{6,14},{7,15},{8,0},{9,1},... | collective-permute-start | bytes 417800 | tf_op jit(solution)/shard_map/ppermute | solution.py:38
  27.7 1.6 %collective-permute-done.10 = bf16[32,2176]{1,0:T(8,128)(2,1)S(1)} collective-permute-done((bf16[32,2176]{1,0:T(8,128)(2,1)S(1)}, bf16[32,2176]{1,0:T(8,128)(2,1)S(1)}, u32[]{:S(2)}, u32[]{:S(2)}) %collective-permute-start.10) | collective-permute-done | bytes 139296 | tf_op jit(solution)/shard_map/ppermute | solution.py:38
  29.7 1.1 %collective-permute-done.9 = bf16[32,2176]{1,0:T(8,128)(2,1)S(1)} collective-permute-done((bf16[32,2176]{1,0:T(8,128)(2,1)S(1)}, bf16[32,2176]{1,0:T(8,128)(2,1)S(1)}, u32[]{:S(2)}, u32[]{:S(2)}) %collective-permute-start.9) | collective-permute-done | bytes 139296 | tf_op jit(solution)/shard_map/ppermute | solution.py:38
  30.8 1.1 %collective-permute-start.11 = (bf16[32,2176]{1,0:T(8,128)(2,1)S(1)}, bf16[32,2176]{1,0:T(8,128)(2,1)S(1)}, u32[]{:S(2)}, u32[]{:S(2)}) collective-permute-start(bf16[32,2176]{1,0:T(8,128)(2,1)S(1)} %collective-permute-done.9), channel_id=1, source_target_pairs={{0,1},{1,0},{2,6},{3,7},{4,5},{5,4},{6,2},{7,3},{8,9},{9,8},{10,14... | collective-permute-start | bytes 417800 | tf_op jit(solution)/shard_map/ppermute | solution.py:38
  31.9 1.7 %collective-permute-done.8 = bf16[32,2176]{1,0:T(8,128)(2,1)S(1)} collective-permute-done((bf16[32,2176]{1,0:T(8,128)(2,1)S(1)}, bf16[32,2176]{1,0:T(8,128)(2,1)S(1)}, u32[]{:S(2)}, u32[]{:S(2)}) %collective-permute-start.8) | collective-permute-done | bytes 139296 | tf_op jit(solution)/shard_map/ppermute | solution.py:38
  33.6 0.8 %collective-permute-start.14 = (bf16[64,2176]{1,0:T(8,128)(2,1)S(1)}, bf16[64,2176]{1,0:T(8,128)(2,1)S(1)}, u32[]{:S(2)}, u32[]{:S(2)}) collective-permute-start(bf16[64,2176]{1,0:T(8,128)(2,1)S(1)} %constant_dynamic-update-slice_fusion.4), channel_id=1, source_target_pairs={{0,4},{1,5},{2,3},{3,2},{4,0},{5,1},{6,7},{7,6},{8,12},{9,13},{10,... | collective-permute-start | bytes 835592 | tf_op jit(solution)/shard_map/ppermute | solution.py:38
  34.5 2.7 %expert_halves.4 = (f32[64,2048]{1,0:T(8,128)S(1)}, bf16[64,2048]{1,0:T(8,128)(2,1)S(1)}) custom-call(bf16[128,2176]{1,0:T(8,128)(2,1)S(1)} %pad_maximum_fusion.rows_ref, bf16[1,2048,768]{2,1,0:T(8,128)(2,1)S(1)} %get-tuple-element.79.refs_0_, bf16[1,2048,768]{2,1,0:T(8,128)(2,1)S(1)} %get-tuple-element.80.refs_1_, ...), custom_call_target="tpu_custom_call" | custom-call | flops 2415919104 | bytes 2097152 | tf_op jit(solution)/shard_map/expert_halves/pallas_call | solution.py:391
  37.3 1.2 %collective-permute-start.18 = (bf16[64,2176]{1,0:T(8,128)(2,1)S(1)}, bf16[64,2176]{1,0:T(8,128)(2,1)S(1)}, u32[]{:S(2)}, u32[]{:S(2)}) collective-permute-start(bf16[64,2176]{1,0:T(8,128)(2,1)S(1)} %constant_dynamic-update-slice_fusion.6), channel_id=1, source_target_pairs={{0,4},{1,5},{2,3},{3,2},{4,0},{5,1},{6,7},{7,6},{8,12},{9,13},{10,... | collective-permute-start | bytes 835592 | tf_op jit(solution)/shard_map/ppermute | solution.py:38
  38.5 0.9 %collective-permute-start.12 = (bf16[64,2048]{1,0:T(8,128)(2,1)S(1)}, bf16[64,2048]{1,0:T(8,128)(2,1)S(1)}, u32[]{:S(2)}, u32[]{:S(2)}) collective-permute-start(bf16[64,2048]{1,0:T(8,128)(2,1)S(1)} %get-tuple-element.88), channel_id=1, source_target_pairs={{0,4},{1,5},{2,3},{3,2},{4,0},{5,1},{6,7},{7,6},{8,12},{9,13},{10,... | collective-permute-start | bytes 786440 | tf_op jit(solution)/shard_map/ppermute | solution.py:38
  40.2 2.7 %expert_halves.5 = (f32[64,2048]{1,0:T(8,128)S(1)}, bf16[64,2048]{1,0:T(8,128)(2,1)S(1)}) custom-call(bf16[128,2176]{1,0:T(8,128)(2,1)S(1)} %pad_maximum_fusion.1.rows_ref, bf16[1,2048,768]{2,1,0:T(8,128)(2,1)S(1)} %get-tuple-element.79.refs_0_, bf16[1,2048,768]{2,1,0:T(8,128)(2,1)S(1)} %get-tuple-element.80.refs_1_, ...), custom_call_target="tpu_custom_call" | custom-call | flops 2415919104 | bytes 2097152 | tf_op jit(solution)/shard_map/expert_halves/pallas_call | solution.py:391
  43.0 0.8 %collective-permute-start.20 = (bf16[64,2048]{1,0:T(8,128)(2,1)S(1)}, bf16[64,2048]{1,0:T(8,128)(2,1)S(1)}, u32[]{:S(2)}, u32[]{:S(2)}) collective-permute-start(bf16[64,2048]{1,0:T(8,128)(2,1)S(1)} %get-tuple-element.103), channel_id=1, source_target_pairs={{0,4},{1,5},{2,3},{3,2},{4,0},{5,1},{6,7},{7,6},{8,12},{9,13},{10,... | collective-permute-start | bytes 786440 | tf_op jit(solution)/shard_map/ppermute | solution.py:38
  43.8 2.7 %expert_halves.6 = (f32[64,2048]{1,0:T(8,128)S(1)}, bf16[64,2048]{1,0:T(8,128)(2,1)S(1)}) custom-call(bf16[128,2176]{1,0:T(8,128)(2,1)S(1)} %constant_dynamic-update-slice_fusion.8.rows_ref, bf16[1,2048,768]{2,1,0:T(8,128)(2,1)S(1)} %get-tuple-element.79.refs_0_, bf16[1,2048,768]{2,1,0:T(8,128)(2,1)S(1)} %get-tuple-element.80.refs_1_, ...), custom_call_target="tpu_custom_call" | custom-call | flops 2415919104 | bytes 2097152 | tf_op jit(solution)/shard_map/expert_halves/pallas_call | solution.py:391
  46.5 1.3 %collective-permute-start.16 = (bf16[64,2048]{1,0:T(8,128)(2,1)S(1)}, bf16[64,2048]{1,0:T(8,128)(2,1)S(1)}, u32[]{:S(2)}, u32[]{:S(2)}) collective-permute-start(bf16[64,2048]{1,0:T(8,128)(2,1)S(1)} %get-tuple-element.95), channel_id=1, source_target_pairs={{0,4},{1,5},{2,3},{3,2},{4,0},{5,1},{6,7},{7,6},{8,12},{9,13},{10,... | collective-permute-start | bytes 786440 | tf_op jit(solution)/shard_map/ppermute | solution.py:38
  48.8 2.9 %expert_halves.7 = (f32[64,2048]{1,0:T(8,128)S(1)}, bf16[64,2048]{1,0:T(8,128)(2,1)S(1)}) custom-call(bf16[128,2176]{1,0:T(8,128)(2,1)S(1)} %pad_maximum_fusion.2.rows_ref, bf16[1,2048,768]{2,1,0:T(8,128)(2,1)S(1)} %get-tuple-element.79.refs_0_, bf16[1,2048,768]{2,1,0:T(8,128)(2,1)S(1)} %get-tuple-element.80.refs_1_, ...), custom_call_target="tpu_custom_call" | custom-call | flops 2415919104 | bytes 2097152 | tf_op jit(solution)/shard_map/expert_halves/pallas_call | solution.py:391
  52.6 1.4 %collective-permute-start.21 = (bf16[32,2048]{1,0:T(8,128)(2,1)S(1)}, bf16[32,2048]{1,0:T(8,128)(2,1)S(1)}, u32[]{:S(2)}, u32[]{:S(2)}) collective-permute-start(bf16[32,2048]{1,0:T(8,128)(2,1)S(1)} %slice.53), channel_id=1, source_target_pairs={{0,1},{1,0},{2,6},{3,7},{4,5},{5,4},{6,2},{7,3},{8,9},{9,8},{10,14... | collective-permute-start | bytes 393224 | tf_op jit(solution)/shard_map/ppermute | solution.py:38
  54.9 1.9 %collective-permute-start.17 = (bf16[32,2048]{1,0:T(8,128)(2,1)S(1)}, bf16[32,2048]{1,0:T(8,128)(2,1)S(1)}, u32[]{:S(2)}, u32[]{:S(2)}) collective-permute-start(bf16[32,2048]{1,0:T(8,128)(2,1)S(1)} %slice.54), channel_id=1, source_target_pairs={{0,1},{1,0},{2,6},{3,7},{4,5},{5,4},{6,2},{7,3},{8,9},{9,8},{10,14... | collective-permute-start | bytes 393224 | tf_op jit(solution)/shard_map/ppermute | solution.py:38
  56.8 0.9 %collective-permute-done.21 = bf16[32,2048]{1,0:T(8,128)(2,1)S(1)} collective-permute-done((bf16[32,2048]{1,0:T(8,128)(2,1)S(1)}, bf16[32,2048]{1,0:T(8,128)(2,1)S(1)}, u32[]{:S(2)}, u32[]{:S(2)}) %collective-permute-start.21) | collective-permute-done | bytes 131104 | tf_op jit(solution)/shard_map/ppermute | solution.py:38
  57.7 1.6 %collective-permute-start.23 = (bf16[32,2048]{1,0:T(8,128)(2,1)S(1)}, bf16[32,2048]{1,0:T(8,128)(2,1)S(1)}, u32[]{:S(2)}, u32[]{:S(2)}) collective-permute-start(bf16[32,2048]{1,0:T(8,128)(2,1)S(1)} %slice_add_fusion.1), channel_id=1, source_target_pairs={{0,16},{1,17},{2,18},{3,19},{4,20},{5,21},{6,22},{7,23},{8,24},{9,... | collective-permute-start | bytes 393224 | tf_op jit(solution)/shard_map/ppermute | solution.py:38
  59.7 1.0 %collective-permute-start.24 = (bf16[32,2048]{1,0:T(8,128)(2,1)S(1)}, bf16[32,2048]{1,0:T(8,128)(2,1)S(1)}, u32[]{:S(2)}, u32[]{:S(2)}) collective-permute-start(bf16[32,2048]{1,0:T(8,128)(2,1)S(1)} %slice.52), channel_id=1, source_target_pairs={{0,1},{1,0},{2,6},{3,7},{4,5},{5,4},{6,2},{7,3},{8,9},{9,8},{10,14... | collective-permute-start | bytes 393224 | tf_op jit(solution)/shard_map/ppermute | solution.py:38
  60.7 3.3 %collective-permute-start.22 = (bf16[32,2048]{1,0:T(8,128)(2,1)S(1)}, bf16[32,2048]{1,0:T(8,128)(2,1)S(1)}, u32[]{:S(2)}, u32[]{:S(2)}) collective-permute-start(bf16[32,2048]{1,0:T(8,128)(2,1)S(1)} %slice_add_fusion.2), channel_id=1, source_target_pairs={{0,8},{1,9},{2,10},{3,11},{4,12},{5,13},{6,14},{7,15},{8,0},{9,1},... | collective-permute-start | bytes 393224 | tf_op jit(solution)/shard_map/ppermute | solution.py:38
  64.7 2.3 %collective-permute-start.25 = (bf16[32,2048]{1,0:T(8,128)(2,1)S(1)}, bf16[32,2048]{1,0:T(8,128)(2,1)S(1)}, u32[]{:S(2)}, u32[]{:S(2)}) collective-permute-start(bf16[32,2048]{1,0:T(8,128)(2,1)S(1)} %slice_add_fusion), channel_id=1, source_target_pairs={{0,24},{1,25},{2,26},{3,27},{4,28},{5,29},{6,30},{7,31},{8,16},{9,... | collective-permute-start | bytes 393224 | tf_op jit(solution)/shard_map/ppermute | solution.py:38
  67.0 0.9 %collective-permute-done.22 = bf16[32,2048]{1,0:T(8,128)(2,1)S(1)} collective-permute-done((bf16[32,2048]{1,0:T(8,128)(2,1)S(1)}, bf16[32,2048]{1,0:T(8,128)(2,1)S(1)}, u32[]{:S(2)}, u32[]{:S(2)}) %collective-permute-start.22) | collective-permute-done | bytes 131104 | tf_op jit(solution)/shard_map/ppermute | solution.py:38
  67.9 3.7 %collective-permute-done.25 = bf16[32,2048]{1,0:T(8,128)(2,1)S(1)} collective-permute-done((bf16[32,2048]{1,0:T(8,128)(2,1)S(1)}, bf16[32,2048]{1,0:T(8,128)(2,1)S(1)}, u32[]{:S(2)}, u32[]{:S(2)}) %collective-permute-start.25) | collective-permute-done | bytes 131104 | tf_op jit(solution)/shard_map/ppermute | solution.py:38
  (60 shorter events, 8.4 us)
Async XLA Ops:
  0.0 12.6 %collective-permute-start.1 = (bf16[1,2048,768]{2,1,0:T(8,128)(2,1)}, bf16[1,2048,768]{2,1,0:T(8,128)(2,1)S(1)}, u32[]{:S(2)}, u32[]{:S(2)}) collective-permute-start(bf16[1,2048,768]{2,1,0:T(8,128)(2,1)} %refs_0_.1), channel_id=1, source_target_pairs={{0,2},{1,3},{2,0},{3,1},{4,6},{5,7},{6,4},{7,5},{8,10},{9,11},{10,... | collective-permute-start | bytes 9437192 | tf_op jit(solution)/shard_map/ppermute | solution.py:38
  0.5 12.1 %collective-permute-start.2 = (bf16[1,2048,768]{2,1,0:T(8,128)(2,1)}, bf16[1,2048,768]{2,1,0:T(8,128)(2,1)S(1)}, u32[]{:S(2)}, u32[]{:S(2)}) collective-permute-start(bf16[1,2048,768]{2,1,0:T(8,128)(2,1)} %refs_1_.1), channel_id=1, source_target_pairs={{0,2},{1,3},{2,0},{3,1},{4,6},{5,7},{6,4},{7,5},{8,10},{9,11},{10,... | collective-permute-start | bytes 9437192 | tf_op jit(solution)/shard_map/ppermute | solution.py:38
  0.5 18.3 %collective-permute-start.4 = (bf16[1,768,2048]{2,1,0:T(8,128)(2,1)}, bf16[1,768,2048]{2,1,0:T(8,128)(2,1)S(1)}, u32[]{:S(2)}, u32[]{:S(2)}) collective-permute-start(bf16[1,768,2048]{2,1,0:T(8,128)(2,1)} %refs_2_.1), channel_id=1, source_target_pairs={{0,2},{1,3},{2,0},{3,1},{4,6},{5,7},{6,4},{7,5},{8,10},{9,11},{10,... | collective-permute-start | bytes 9437192 | tf_op jit(solution)/shard_map/ppermute | solution.py:38
  5.8 6.8 %copy-start = (bf16[32,2048]{1,0:T(8,128)(2,1)S(1)}, bf16[32,2048]{1,0:T(8,128)(2,1)}, u32[]{:S(2)}) copy-start(bf16[32,2048]{1,0:T(8,128)(2,1)} %residual_ref.1) | copy-start | bytes 393220
  5.8 6.8 %copy-start.1 = (f32[2048]{0:T(1024)S(1)}, f32[2048]{0:T(1024)}, u32[]{:S(2)}) copy-start(f32[2048]{0:T(1024)} %param.18) | copy-start | bytes 24580
  5.8 6.8 %copy-start.2 = (s32[64,8]{0,1:T(8,128)S(1)}, s32[64,8]{0,1:T(8,128)}, u32[]{:S(2)}) copy-start(s32[64,8]{0,1:T(8,128)} %param.19) | copy-start | bytes 6148
  5.8 6.8 %copy-start.3 = (f32[64,8]{0,1:T(8,128)S(1)}, f32[64,8]{0,1:T(8,128)}, u32[]{:S(2)}) copy-start(f32[64,8]{0,1:T(8,128)} %param.20) | copy-start | bytes 6148
  5.8 6.7 %collective-permute-start = (bf16[32,2048]{1,0:T(8,128)(2,1)S(1)}, bf16[32,2048]{1,0:T(8,128)(2,1)S(1)}, u32[]{:S(2)}, u32[]{:S(2)}) collective-permute-start(bf16[32,2048]{1,0:T(8,128)(2,1)S(1)} %get-tuple-element.60.refs_3_), channel_id=1, source_target_pairs={{0,1},{1,0},{2,3},{3,2},{4,5},{5,4},{6,7},{7,6},{8,9},{9,8},{10,11... | collective-permute-start | bytes 393224 | tf_op jit(solution)/shard_map/ppermute | solution.py:33
  12.8 12.9 %collective-permute-start.6 = (bf16[32,2176]{1,0:T(8,128)(2,1)S(1)}, bf16[32,2176]{1,0:T(8,128)(2,1)S(1)}, u32[]{:S(2)}, u32[]{:S(2)}) collective-permute-start(bf16[32,2176]{1,0:T(8,128)(2,1)S(1)} %get-tuple-element.66), channel_id=1, source_target_pairs={{0,16},{1,17},{2,18},{3,19},{4,20},{5,21},{6,22},{7,23},{8,24},{9,... | collective-permute-start | bytes 417800 | tf_op jit(solution)/shard_map/ppermute | solution.py:38
  15.7 6.9 %collective-permute-start.7 = (bf16[32,2176]{1,0:T(8,128)(2,1)S(1)}, bf16[32,2176]{1,0:T(8,128)(2,1)S(1)}, u32[]{:S(2)}, u32[]{:S(2)}) collective-permute-start(bf16[32,2176]{1,0:T(8,128)(2,1)S(1)} %get-tuple-element.66), channel_id=1, source_target_pairs={{0,8},{1,9},{2,10},{3,11},{4,12},{5,13},{6,14},{7,15},{8,0},{9,1},... | collective-permute-start | bytes 417800 | tf_op jit(solution)/shard_map/ppermute | solution.py:38
  17.3 5.1 %collective-permute-start.3 = (bf16[32,2176]{1,0:T(8,128)(2,1)S(1)}, bf16[32,2176]{1,0:T(8,128)(2,1)S(1)}, u32[]{:S(2)}, u32[]{:S(2)}) collective-permute-start(bf16[32,2176]{1,0:T(8,128)(2,1)S(1)} %get-tuple-element.66), channel_id=1, source_target_pairs={{0,1},{1,0},{2,6},{3,7},{4,5},{5,4},{6,2},{7,3},{8,9},{9,8},{10,14... | collective-permute-start | bytes 417800 | tf_op jit(solution)/shard_map/ppermute | solution.py:38
  22.6 6.7 %collective-permute-start.10 = (bf16[32,2176]{1,0:T(8,128)(2,1)S(1)}, bf16[32,2176]{1,0:T(8,128)(2,1)S(1)}, u32[]{:S(2)}, u32[]{:S(2)}) collective-permute-start(bf16[32,2176]{1,0:T(8,128)(2,1)S(1)} %collective-permute-done.7), channel_id=1, source_target_pairs={{0,1},{1,0},{2,6},{3,7},{4,5},{5,4},{6,2},{7,3},{8,9},{9,8},{10,14... | collective-permute-start | bytes 417800 | tf_op jit(solution)/shard_map/ppermute | solution.py:38
  24.2 10.2 %collective-permute-start.5 = (bf16[64,2176]{1,0:T(8,128)(2,1)S(1)}, bf16[64,2176]{1,0:T(8,128)(2,1)S(1)}, u32[]{:S(2)}, u32[]{:S(2)}) collective-permute-start(bf16[64,2176]{1,0:T(8,128)(2,1)S(1)} %constant_dynamic-update-slice_fusion), channel_id=1, source_target_pairs={{0,4},{1,5},{2,3},{3,2},{4,0},{5,1},{6,7},{7,6},{8,12},{9,13},{10,... | collective-permute-start | bytes 835592 | tf_op jit(solution)/shard_map/ppermute | solution.py:38
  25.7 5.1 %collective-permute-start.9 = (bf16[32,2176]{1,0:T(8,128)(2,1)S(1)}, bf16[32,2176]{1,0:T(8,128)(2,1)S(1)}, u32[]{:S(2)}, u32[]{:S(2)}) collective-permute-start(bf16[32,2176]{1,0:T(8,128)(2,1)S(1)} %collective-permute-done.6), channel_id=1, source_target_pairs={{0,8},{1,9},{2,10},{3,11},{4,12},{5,13},{6,14},{7,15},{8,0},{9,1},... | collective-permute-start | bytes 417800 | tf_op jit(solution)/shard_map/ppermute | solution.py:38
  27.1 6.4 %collective-permute-start.8 = (bf16[32,2176]{1,0:T(8,128)(2,1)S(1)}, bf16[32,2176]{1,0:T(8,128)(2,1)S(1)}, u32[]{:S(2)}, u32[]{:S(2)}) collective-permute-start(bf16[32,2176]{1,0:T(8,128)(2,1)S(1)} %collective-permute-done.6), channel_id=1, source_target_pairs={{0,1},{1,0},{2,6},{3,7},{4,5},{5,4},{6,2},{7,3},{8,9},{9,8},{10,14... | collective-permute-start | bytes 417800 | tf_op jit(solution)/shard_map/ppermute | solution.py:38
  29.3 13.6 %collective-permute-start.13 = (bf16[64,2176]{1,0:T(8,128)(2,1)S(1)}, bf16[64,2176]{1,0:T(8,128)(2,1)S(1)}, u32[]{:S(2)}, u32[]{:S(2)}) collective-permute-start(bf16[64,2176]{1,0:T(8,128)(2,1)S(1)} %get-tuple-element.114), channel_id=1, source_target_pairs={{0,4},{1,5},{2,3},{3,2},{4,0},{5,1},{6,7},{7,6},{8,12},{9,13},{10,... | collective-permute-start | bytes 835592 | tf_op jit(solution)/shard_map/ppermute | solution.py:38
  30.8 6.5 %collective-permute-start.11 = (bf16[32,2176]{1,0:T(8,128)(2,1)S(1)}, bf16[32,2176]{1,0:T(8,128)(2,1)S(1)}, u32[]{:S(2)}, u32[]{:S(2)}) collective-permute-start(bf16[32,2176]{1,0:T(8,128)(2,1)S(1)} %collective-permute-done.9), channel_id=1, source_target_pairs={{0,1},{1,0},{2,6},{3,7},{4,5},{5,4},{6,2},{7,3},{8,9},{9,8},{10,14... | collective-permute-start | bytes 417800 | tf_op jit(solution)/shard_map/ppermute | solution.py:38
  33.6 6.6 %collective-permute-start.14 = (bf16[64,2176]{1,0:T(8,128)(2,1)S(1)}, bf16[64,2176]{1,0:T(8,128)(2,1)S(1)}, u32[]{:S(2)}, u32[]{:S(2)}) collective-permute-start(bf16[64,2176]{1,0:T(8,128)(2,1)S(1)} %constant_dynamic-update-slice_fusion.4), channel_id=1, source_target_pairs={{0,4},{1,5},{2,3},{3,2},{4,0},{5,1},{6,7},{7,6},{8,12},{9,13},{10,... | collective-permute-start | bytes 835592 | tf_op jit(solution)/shard_map/ppermute | solution.py:38
  37.3 11.5 %collective-permute-start.18 = (bf16[64,2176]{1,0:T(8,128)(2,1)S(1)}, bf16[64,2176]{1,0:T(8,128)(2,1)S(1)}, u32[]{:S(2)}, u32[]{:S(2)}) collective-permute-start(bf16[64,2176]{1,0:T(8,128)(2,1)S(1)} %constant_dynamic-update-slice_fusion.6), channel_id=1, source_target_pairs={{0,4},{1,5},{2,3},{3,2},{4,0},{5,1},{6,7},{7,6},{8,12},{9,13},{10,... | collective-permute-start | bytes 835592 | tf_op jit(solution)/shard_map/ppermute | solution.py:38
  38.5 9.3 %collective-permute-start.12 = (bf16[64,2048]{1,0:T(8,128)(2,1)S(1)}, bf16[64,2048]{1,0:T(8,128)(2,1)S(1)}, u32[]{:S(2)}, u32[]{:S(2)}) collective-permute-start(bf16[64,2048]{1,0:T(8,128)(2,1)S(1)} %get-tuple-element.88), channel_id=1, source_target_pairs={{0,4},{1,5},{2,3},{3,2},{4,0},{5,1},{6,7},{7,6},{8,12},{9,13},{10,... | collective-permute-start | bytes 786440 | tf_op jit(solution)/shard_map/ppermute | solution.py:38
  43.0 9.6 %collective-permute-start.20 = (bf16[64,2048]{1,0:T(8,128)(2,1)S(1)}, bf16[64,2048]{1,0:T(8,128)(2,1)S(1)}, u32[]{:S(2)}, u32[]{:S(2)}) collective-permute-start(bf16[64,2048]{1,0:T(8,128)(2,1)S(1)} %get-tuple-element.103), channel_id=1, source_target_pairs={{0,4},{1,5},{2,3},{3,2},{4,0},{5,1},{6,7},{7,6},{8,12},{9,13},{10,... | collective-permute-start | bytes 786440 | tf_op jit(solution)/shard_map/ppermute | solution.py:38
  46.5 8.3 %collective-permute-start.16 = (bf16[64,2048]{1,0:T(8,128)(2,1)S(1)}, bf16[64,2048]{1,0:T(8,128)(2,1)S(1)}, u32[]{:S(2)}, u32[]{:S(2)}) collective-permute-start(bf16[64,2048]{1,0:T(8,128)(2,1)S(1)} %get-tuple-element.95), channel_id=1, source_target_pairs={{0,4},{1,5},{2,3},{3,2},{4,0},{5,1},{6,7},{7,6},{8,12},{9,13},{10,... | collective-permute-start | bytes 786440 | tf_op jit(solution)/shard_map/ppermute | solution.py:38
  48.0 6.9 %collective-permute-start.15 = (bf16[32,2048]{1,0:T(8,128)(2,1)S(1)}, bf16[32,2048]{1,0:T(8,128)(2,1)S(1)}, u32[]{:S(2)}, u32[]{:S(2)}) collective-permute-start(bf16[32,2048]{1,0:T(8,128)(2,1)S(1)} %slice.55), channel_id=1, source_target_pairs={{0,1},{1,0},{2,6},{3,7},{4,5},{5,4},{6,2},{7,3},{8,9},{9,8},{10,14... | collective-permute-start | bytes 393224 | tf_op jit(solution)/shard_map/ppermute | solution.py:38
  51.7 7.9 %collective-permute-start.19 = (bf16[64,2048]{1,0:T(8,128)(2,1)S(1)}, bf16[64,2048]{1,0:T(8,128)(2,1)S(1)}, u32[]{:S(2)}, u32[]{:S(2)}) collective-permute-start(bf16[64,2048]{1,0:T(8,128)(2,1)S(1)} %get-tuple-element.101), channel_id=1, source_target_pairs={{0,4},{1,5},{2,3},{3,2},{4,0},{5,1},{6,7},{7,6},{8,12},{9,13},{10,... | collective-permute-start | bytes 786440 | tf_op jit(solution)/shard_map/ppermute | solution.py:38
  52.6 5.0 %collective-permute-start.21 = (bf16[32,2048]{1,0:T(8,128)(2,1)S(1)}, bf16[32,2048]{1,0:T(8,128)(2,1)S(1)}, u32[]{:S(2)}, u32[]{:S(2)}) collective-permute-start(bf16[32,2048]{1,0:T(8,128)(2,1)S(1)} %slice.53), channel_id=1, source_target_pairs={{0,1},{1,0},{2,6},{3,7},{4,5},{5,4},{6,2},{7,3},{8,9},{9,8},{10,14... | collective-permute-start | bytes 393224 | tf_op jit(solution)/shard_map/ppermute | solution.py:38
  54.9 5.8 %collective-permute-start.17 = (bf16[32,2048]{1,0:T(8,128)(2,1)S(1)}, bf16[32,2048]{1,0:T(8,128)(2,1)S(1)}, u32[]{:S(2)}, u32[]{:S(2)}) collective-permute-start(bf16[32,2048]{1,0:T(8,128)(2,1)S(1)} %slice.54), channel_id=1, source_target_pairs={{0,1},{1,0},{2,6},{3,7},{4,5},{5,4},{6,2},{7,3},{8,9},{9,8},{10,14... | collective-permute-start | bytes 393224 | tf_op jit(solution)/shard_map/ppermute | solution.py:38
  57.7 9.3 %collective-permute-start.23 = (bf16[32,2048]{1,0:T(8,128)(2,1)S(1)}, bf16[32,2048]{1,0:T(8,128)(2,1)S(1)}, u32[]{:S(2)}, u32[]{:S(2)}) collective-permute-start(bf16[32,2048]{1,0:T(8,128)(2,1)S(1)} %slice_add_fusion.1), channel_id=1, source_target_pairs={{0,16},{1,17},{2,18},{3,19},{4,20},{5,21},{6,22},{7,23},{8,24},{9,... | collective-permute-start | bytes 393224 | tf_op jit(solution)/shard_map/ppermute | solution.py:38
  59.7 5.0 %collective-permute-start.24 = (bf16[32,2048]{1,0:T(8,128)(2,1)S(1)}, bf16[32,2048]{1,0:T(8,128)(2,1)S(1)}, u32[]{:S(2)}, u32[]{:S(2)}) collective-permute-start(bf16[32,2048]{1,0:T(8,128)(2,1)S(1)} %slice.52), channel_id=1, source_target_pairs={{0,1},{1,0},{2,6},{3,7},{4,5},{5,4},{6,2},{7,3},{8,9},{9,8},{10,14... | collective-permute-start | bytes 393224 | tf_op jit(solution)/shard_map/ppermute | solution.py:38
  60.7 7.2 %collective-permute-start.22 = (bf16[32,2048]{1,0:T(8,128)(2,1)S(1)}, bf16[32,2048]{1,0:T(8,128)(2,1)S(1)}, u32[]{:S(2)}, u32[]{:S(2)}) collective-permute-start(bf16[32,2048]{1,0:T(8,128)(2,1)S(1)} %slice_add_fusion.2), channel_id=1, source_target_pairs={{0,8},{1,9},{2,10},{3,11},{4,12},{5,13},{6,14},{7,15},{8,0},{9,1},... | collective-permute-start | bytes 393224 | tf_op jit(solution)/shard_map/ppermute | solution.py:38
  64.7 6.9 %collective-permute-start.25 = (bf16[32,2048]{1,0:T(8,128)(2,1)S(1)}, bf16[32,2048]{1,0:T(8,128)(2,1)S(1)}, u32[]{:S(2)}, u32[]{:S(2)}) collective-permute-start(bf16[32,2048]{1,0:T(8,128)(2,1)S(1)} %slice_add_fusion), channel_id=1, source_target_pairs={{0,24},{1,25},{2,26},{3,27},{4,28},{5,29},{6,30},{7,31},{8,16},{9,... | collective-permute-start | bytes 393224 | tf_op jit(solution)/shard_map/ppermute | solution.py:38
